TPU v7x, 32 devices: a whole 2x2x4 slice. The times are simulated.
32 devices in a mesh: clip: 8 (over y, x, core), feat: 4 (over z).
Axes of the slice: x: 2, y: 2, z: 4, core: 2. Of those that a mesh axis runs over, the one named last changes fastest.
Arguments:
- features: float32 [6144, 22528], P('clip', 'feat'), may hold values from -20 to 20
- weights: float32 [400, 22528], P(None, 'feat'), may hold values from -0.02665009 to 0.02665009
- labels: int32 [6144], P('clip'), may hold values from 0 to 399
Outputs:
- new_weights: float32 [400, 22528], P(None, 'feat')
- residual: float32 [400, 22528], P(None, 'feat')
All inputs are finite; a program needn't handle non-finite values.
Results may differ from a plain program's by a relative error of at most 0.0003.
Values sent between devices are 32-bit elements; how exact they have to be, the bound alone decides.
No kernel may reach another device: no remote copies, remote signals or barrier semaphores. Data moves between devices by JAX's collectives and lax.ppermute only.
A program may use at most 128 MiB of HBM per device.

v0:
```python
import functools

import jax
import jax.numpy as jnp
from jax import lax
from jax.experimental import pallas as pl
from jax.experimental.pallas import tpu as pltpu
from jax.sharding import PartitionSpec as P

damping = 0.01
F32, BF16 = jnp.float32, jnp.bfloat16
LANES, ROWS8, UNIT = 128, 8, 16
NT = (((1,), (1,)), ((), ()))
NN = (((1,), (0,)), ((), ()))
VMEM_LIMIT = 52 * 1024 * 1024


def parts_of(x):
    high = x.astype(BF16)
    return high, (x - high.astype(F32)).astype(BF16)


def dot3(x, high, low, dims):
    x_high, x_low = parts_of(x)
    n = x.shape[0]
    dot = functools.partial(lax.dot_general, dimension_numbers=dims, preferred_element_type=F32)
    both = dot(jnp.concatenate([x_high, x_low], axis=0), high)
    return both[:n] + (both[n:] + dot(x_high, low))


def dot3_stream(high, low, x):
    x_high, x_low = parts_of(x)
    dot = functools.partial(lax.dot_general, dimension_numbers=NT, preferred_element_type=F32)
    return dot(high, x_high) + (dot(high, x_low) + dot(low, x_high))


def params():
    return pltpu.CompilerParams(vmem_limit_bytes=VMEM_LIMIT)


class Plan:
    def __init__(self, rows, feats, classes, n_clip, n_feat):
        self.rows, self.feats, self.classes = rows, feats, classes
        self.n_clip, self.n_feat = n_clip, n_feat
        units = classes // UNIT
        sizes = [UNIT * (units // 4 + (k < units % 4)) for k in range(4)]
        starts = [sum(sizes[:k]) for k in range(4)]
        self.chunks = list(zip(starts, sizes))
        self.pairs = [(0, 1), (2, 3)]
        strides = [1 << k for k in range(1, n_clip.bit_length() - 1)]
        self.levels, block = [], feats
        while strides and block % (2 * LANES) == 0:
            self.levels.append(strides.pop(0))
            block //= 2
        self.doubled = strides
        self.block, self.nb = block, feats // block
        self.rows_step = next(n for n in (256, 128, rows) if rows % n == 0)

    def pair_range(self, pair):
        first, last = self.pairs[pair][0], self.pairs[pair][-1]
        start = self.chunks[first][0]
        return start, self.chunks[last][0] + self.chunks[last][1] - start


def swap(x, axis, stride):
    size = lax.axis_size(axis)
    return lax.ppermute(x, axis, [(i, i ^ stride) for i in range(size)])


def first_body(plan, s_ref, f_ref, w_ref, *rest):
    high_ref, low_ref, send_ref, keep_ref, acc = rest[-5:]
    p = pl.program_id(0)
    high, low = parts_of(f_ref[...])
    high_ref[...] = high
    low_ref[...] = low
    part = dot3(w_ref[...], high, low, NT)

    @pl.when(p == 0)
    def _():
        acc[...] = part

    @pl.when(p > 0)
    def _():
        acc[...] += part

    @pl.when(p == plan.nb - 1)
    def _():
        half = plan.classes // 2
        bit = s_ref[2]
        send_ref[...] = acc[pl.ds(pl.multiple_of((1 - bit) * half, ROWS8), half), :]
        keep_ref[...] = acc[pl.ds(pl.multiple_of(bit * half, ROWS8), half), :]


def first(plan, where, features, weights, part, split):
    rows, block, step = plan.rows, plan.block, plan.rows_step
    half = plan.classes // 2
    operands = [features, weights]
    in_specs = [
        pl.BlockSpec((step, block), lambda p, s: (part, p ^ s[0])),
        pl.BlockSpec((plan.classes, block), lambda p, s: (0, p ^ s[0])),
    ]
    aliases = {}
    if split is not None:
        aliases = {3: 0, 4: 1}
        operands += list(split)
        in_specs += [pl.BlockSpec(memory_space=pl.ANY)] * 2
    high, low, send, keep = pl.pallas_call(
        functools.partial(first_body, plan),
        out_shape=[jax.ShapeDtypeStruct((rows, plan.feats), BF16)] * 2
        + [jax.ShapeDtypeStruct((half, step), F32)] * 2,
        grid_spec=pltpu.PrefetchScalarGridSpec(
            num_scalar_prefetch=1,
            grid=(plan.nb,),
            in_specs=in_specs,
            out_specs=[pl.BlockSpec((step, block), lambda p, s: (part, p))] * 2
            + [pl.BlockSpec((half, step), lambda p, s: (0, 0))] * 2,
            scratch_shapes=[pltpu.VMEM((plan.classes, step), F32)],
        ),
        input_output_aliases=aliases,
        compiler_params=params(),
        cost_estimate=pl.CostEstimate(
            flops=6 * plan.classes * step * plan.feats,
            bytes_accessed=4 * plan.feats * (2 * step + plan.classes),
            transcendentals=0,
        ),
        name="split_and_logits",
    )(where, *operands)
    return (high, low), (send, keep)


def back_body(plan, pair, s_ref, g_ref, high_ref, low_ref, *rest):
    outs, acc = rest[:-1], rest[-1]
    acc[...] = dot3(g_ref[...], high_ref[...], low_ref[...], NN)
    core = s_ref[1]
    base = plan.pair_range(pair)[0]
    for k, c in enumerate(plan.pairs[pair]):
        a, n = plan.chunks[c]
        h = n // 2
        outs[2 * k][...] = acc[pl.ds(pl.multiple_of(a - base + core * h, ROWS8), h), :]
        outs[2 * k + 1][...] = acc[pl.ds(pl.multiple_of(a - base + (1 - core) * h, ROWS8), h), :]


def back(plan, where, pair, values, high, low):
    rows, block, feats = plan.rows, plan.block, plan.feats
    n_pair = plan.pair_range(pair)[1]
    outs, specs = [], []
    for c in plan.pairs[pair]:
        h = plan.chunks[c][1] // 2
        outs += [jax.ShapeDtypeStruct((h, feats), F32)] * 2
        specs += [pl.BlockSpec((h, block), lambda p, s: (0, p))] * 2
    result = pl.pallas_call(
        functools.partial(back_body, plan, pair),
        out_shape=outs,
        grid_spec=pltpu.PrefetchScalarGridSpec(
            num_scalar_prefetch=1,
            grid=(plan.nb,),
            in_specs=[
                pl.BlockSpec((n_pair, rows), lambda p, s: (0, 0)),
                pl.BlockSpec((rows, block), lambda p, s: (0, p)),
                pl.BlockSpec((rows, block), lambda p, s: (0, p)),
            ],
            out_specs=specs,
            scratch_shapes=[pltpu.VMEM((n_pair, block), F32)],
        ),
        compiler_params=params(),
        cost_estimate=pl.CostEstimate(
            flops=6 * n_pair * rows * feats, bytes_accessed=4 * feats * (rows + n_pair), transcendentals=0
        ),
        name="back_pair",
    )(where, values, high, low)
    return [tuple(result[2 * k : 2 * k + 2]) for k in range(len(plan.pairs[pair]))]


class Pieces:
    def __init__(self, places, mine, theirs):
        self.places, self.mine, self.theirs = places, mine, theirs

    def flat(self):
        return list(self.mine) + list(self.theirs)


def gather_rows(plan, pair, chunks, s_ref, refs, position, target):
    core = s_ref[1]
    base = plan.pair_range(pair)[0]
    refs = list(refs)
    for c, places in zip(plan.pairs[pair], chunks):
        a, n = plan.chunks[c]
        h = n // 2
        for side in (core, 1 - core):
            for place in places:
                ref = refs.pop(0)
                if position in place:
                    k = place.index(position) * plan.block
                    target[pl.ds(pl.multiple_of(a - base + side * h, ROWS8), h), :] = ref[:, k : k + plan.block]


def forth_body(plan, pair, step, chunks, s_ref, *refs):
    nb = plan.nb
    refs = list(refs)
    scalar_ref = refs.pop(0) if step else None
    n_pieces = 2 * sum(len(places) for places in chunks)
    pieces, refs = refs[:n_pieces], refs[n_pieces:]
    direction_ref = refs.pop(0) if step else None
    high_ref, low_ref = refs[:2]
    n_ranges = len(tangent_ranges(plan, pair))
    target, acc, turned, sums = refs[-4:]
    vector_ref, outs = refs[-5 - 2 * n_ranges], refs[-4 - 2 * n_ranges : -4]
    n_pair = plan.pair_range(pair)[1]
    p = pl.program_id(0)
    for position in range(nb):

        @pl.when(p == position)
        def _():
            gather_rows(plan, pair, chunks, s_ref, pieces, position, target)

    if step:
        direction = direction_ref[...]
        vector = direction - scalar_ref[0] * (target[...] + damping * direction)
    else:
        vector = -target[...]
    vector_ref[...] = vector
    part = dot3_stream(high_ref[...], low_ref[...], vector)
    square = jnp.sum(vector * vector).reshape(1, 1)
    cross = jnp.sum(vector * direction).reshape(1, 1) if step else square
    ids = lax.broadcasted_iota(jnp.int32, (ROWS8, plan.rows), 0)
    new = jnp.where(ids == 0, square, jnp.where(ids == 1, cross, 0.0))

    @pl.when(p == 0)
    def _():
        acc[...] = part
        sums[...] = new

    @pl.when(p > 0)
    def _():
        acc[...] += part
        sums[...] += new

    @pl.when(p == nb - 1)
    def _():
        turned[:n_pair, :] = acc[...].T
        turned[n_pair:, :] = sums[...]
        half = plan.rows // 2
        bit = s_ref[2]
        keep = pl.multiple_of(bit * half, LANES)
        send = pl.multiple_of((1 - bit) * half, LANES)
        for k, (a, n) in enumerate(tangent_ranges(plan, pair)):
            outs[2 * k][...] = turned[a : a + n, pl.ds(send, half)]
            outs[2 * k + 1][...] = turned[a : a + n, pl.ds(keep, half)]


def tangent_ranges(plan, pair):
    base, n_pair = plan.pair_range(pair)
    if pair == 0:
        return [(0, n_pair + ROWS8)]
    ranges = [(plan.chunks[c][0] - base, plan.chunks[c][1]) for c in plan.pairs[pair]]
    ranges[-1] = (ranges[-1][0], ranges[-1][1] + ROWS8)
    return ranges


def placed(plan, pair):
    base, n_pair = plan.pair_range(pair)
    return pl.BlockSpec(
        (pl.Element(n_pair), pl.Element(plan.block)), lambda p, s: (base, (p ^ s[0]) * plan.block)
    )


def forth(plan, where, pair, pieces, high, low, vectors, step=None, direction=None):
    rows, block, feats, nb = plan.rows, plan.block, plan.feats, plan.nb
    half = rows // 2
    n_pair = plan.pair_range(pair)[1]
    operands, in_specs = [], []
    if step is not None:
        operands.append(step.reshape(1))
        in_specs.append(pl.BlockSpec(memory_space=pltpu.SMEM))
    for piece in pieces:
        for x in piece.flat():
            operands.append(x)
            in_specs.append(pl.BlockSpec(x.shape, lambda p, s: (0, 0)))
    if step is not None:
        operands.append(direction)
        in_specs.append(placed(plan, pair))
    operands += [high, low]
    in_specs += [pl.BlockSpec((rows, block), lambda p, s: (0, p))] * 2
    aliases = {}
    if vectors is not None:
        aliases = {len(operands) + 1: 0}
        operands.append(vectors)
        in_specs.append(pl.BlockSpec(memory_space=pl.ANY))
    outs, specs = [jax.ShapeDtypeStruct((plan.classes, feats), F32)], [placed(plan, pair)]
    for _, n in tangent_ranges(plan, pair):
        outs += [jax.ShapeDtypeStruct((n, half), F32)] * 2
        specs += [pl.BlockSpec((n, half), lambda p, s: (0, 0))] * 2
    result = pl.pallas_call(
        functools.partial(forth_body, plan, pair, step is not None, [piece.places for piece in pieces]),
        out_shape=outs,
        grid_spec=pltpu.PrefetchScalarGridSpec(
            num_scalar_prefetch=1,
            grid=(nb,),
            in_specs=in_specs,
            out_specs=specs,
            scratch_shapes=[
                pltpu.VMEM((n_pair, block), F32),
                pltpu.VMEM((rows, n_pair), F32),
                pltpu.VMEM((n_pair + ROWS8, rows), F32),
                pltpu.VMEM((ROWS8, rows), F32),
            ],
        ),
        input_output_aliases=aliases,
        compiler_params=params(),
        cost_estimate=pl.CostEstimate(
            flops=6 * n_pair * rows * feats, bytes_accessed=4 * feats * (rows + 3 * n_pair), transcendentals=0
        ),
        name="forth_pair",
    )(where, *operands)
    return result[0], [tuple(result[1 + 2 * k : 3 + 2 * k]) for k in range(len(tangent_ranges(plan, pair)))]


def last_body(plan, pair, chunks, s_ref, scalar_ref, *refs):
    nb = plan.nb
    refs = list(refs)
    n_pieces = 2 * sum(len(places) for places in chunks)
    pieces = refs[:n_pieces]
    base_ref, out_ref, target, ready, arrived, left = refs[n_pieces:]
    base, n_pair = plan.pair_range(pair)

    def place(ref, position):
        column = pl.multiple_of((position ^ s_ref[0]) * plan.block, LANES)
        return ref.at[pl.ds(base, n_pair), pl.ds(column, plan.block)]

    reads = [
        pltpu.make_async_copy(place(base_ref, q), ready.at[q], arrived.at[q]) for q in range(nb)
    ]
    writes = [pltpu.make_async_copy(ready.at[q], place(out_ref, q), left.at[q]) for q in range(nb)]
    for read in reads:
        read.start()
    for position in range(nb):
        gather_rows(plan, pair, chunks, s_ref, pieces, position, target)
        reads[position].wait()
        ready[position] = ready[position] - scalar_ref[0] * target[...]
        writes[position].start()
    for write in writes:
        write.wait()


def last(plan, where, pair, step, pieces, base):
    block, nb = plan.block, plan.nb
    n_pair = plan.pair_range(pair)[1]
    operands, in_specs = [where, step.reshape(1)], [pl.BlockSpec(memory_space=pltpu.SMEM)] * 2
    for piece in pieces:
        for x in piece.flat():
            operands.append(x)
            in_specs.append(pl.BlockSpec(memory_space=pltpu.VMEM))
    operands.append(base)
    in_specs.append(pl.BlockSpec(memory_space=pl.ANY))
    return pl.pallas_call(
        functools.partial(last_body, plan, pair, [piece.places for piece in pieces]),
        out_shape=jax.ShapeDtypeStruct((plan.classes, plan.feats), F32),
        in_specs=in_specs,
        out_specs=pl.BlockSpec(memory_space=pl.ANY),
        scratch_shapes=[
            pltpu.VMEM((n_pair, block), F32),
            pltpu.VMEM((nb, n_pair, block), F32),
            pltpu.SemaphoreType.DMA((nb,)),
            pltpu.SemaphoreType.DMA((nb,)),
        ],
        input_output_aliases={len(operands) - 1: 0},
        compiler_params=params(),
        cost_estimate=pl.CostEstimate(
            flops=6 * n_pair * plan.feats, bytes_accessed=12 * n_pair * plan.feats, transcendentals=0
        ),
        name="last_pair",
    )(*operands)


def tie(*values):
    return lax.optimization_barrier(values)


def columns(plan, x, positions):
    if list(positions) == list(range(positions[0], positions[-1] + 1)):
        return x[:, positions[0] * plan.block : (positions[-1] + 1) * plan.block]
    return jnp.concatenate([x[:, p * plan.block : (p + 1) * plan.block] for p in positions], axis=1)


class ClipSum:
    def __init__(self, plan, sides, order):
        self.plan = plan
        self.own, self.other = sides
        levels = [(plan.levels[k], 1 << k) for k in range(len(plan.levels))]
        self.levels = levels[::-1] if order else levels

    def cores(self):
        if self.plan.n_clip > 1:
            self.own = self.own + swap(self.other, "clip", 1)
        self.active = list(range(self.plan.nb))

    def scatter(self, k):
        stride, bit = self.levels[k]
        rest = [p for p in self.active if not p & bit]
        sent = columns(self.plan, self.own, [self.active.index(p | bit) for p in rest])
        kept = columns(self.plan, self.own, [self.active.index(p) for p in rest])
        self.own = kept + swap(sent, "clip", stride)
        self.active = rest

    def double(self):
        for stride in self.plan.doubled:
            self.own = self.own + swap(self.own, "clip", stride)
        self.places, self.mine = [tuple(self.active)], [self.own]

    def gather(self, k):
        stride, bit = self.levels[k]
        whole = self.mine[0] if len(self.mine) == 1 else jnp.concatenate(self.mine, axis=1)
        self.mine.append(swap(whole, "clip", stride))
        self.places.append(tuple(p | bit for place in self.places for p in place))

    def pieces(self):
        theirs = [swap(x, "clip", 1) for x in self.mine] if self.plan.n_clip > 1 else self.mine
        return Pieces(self.places, self.mine, theirs)


def sum_clips(plan, sides, value, during):
    sums = [ClipSum(plan, side, k % 2) for k, side in enumerate(sides)]
    for s in sums:
        s.cores()
    sums[0].own, value = tie(sums[0].own, value)
    result = during(value)
    steps = len(plan.levels)
    for k in range(steps):
        for s in sums:
            s.scatter(k)
        if k == steps - 1:
            sums[0].own, result = tie(sums[0].own, result)
    for s in sums:
        s.double()
    for k in reversed(range(steps)):
        for s in sums:
            s.gather(k)
    return sums, result


def sum_feat(plan, halves, bit, axis):
    send, keep = halves
    if plan.n_feat == 1:
        return jnp.where(bit, jnp.concatenate([send, keep], axis), jnp.concatenate([keep, send], axis))
    total = keep + swap(send, "feat", 1)
    stride = 2
    while stride < plan.n_feat:
        total = total + swap(total, "feat", stride)
        stride *= 2
    away = swap(total, "feat", 1)
    return jnp.where(bit, jnp.concatenate([away, total], axis), jnp.concatenate([total, away], axis))


def sum_clip_scalar(plan, value):
    row = jnp.broadcast_to(value, (ROWS8, LANES))
    stride = 1
    while stride < plan.n_clip:
        row = row + swap(row, "clip", stride)
        stride *= 2
    return row[0, 0]


def local(features, weights, labels):
    rows, feats = features.shape
    classes = weights.shape[0]
    plan = Plan(rows, feats, classes, lax.axis_size("clip"), lax.axis_size("feat"))
    total_rows = rows * plan.n_clip
    me, bit = lax.axis_index("clip"), lax.axis_index("feat") & 1
    mask = sum(((me // stride) & 1) << k for k, stride in enumerate(plan.levels))
    where = jnp.stack([jnp.asarray(mask), me & 1, bit]).astype(jnp.int32)

    split, parts = None, []
    for part in range(rows // plan.rows_step):
        split, halves = first(plan, where, features, weights, part, split)
        parts.append(halves)
    high, low = split
    probs, values = [], []
    for part, halves in enumerate(parts):
        logits = sum_feat(plan, halves, bit, 0)
        top = jnp.max(logits, axis=0, keepdims=True)
        powers = jnp.exp(logits - top)
        some = powers / jnp.sum(powers, axis=0, keepdims=True)
        mine = labels[part * plan.rows_step : (part + 1) * plan.rows_step]
        onehot = (mine[None, :] == jnp.arange(classes, dtype=jnp.int32)[:, None]).astype(F32)
        probs.append(some)
        values.append((some - onehot) / total_rows)
    probs, values = jnp.concatenate(probs, axis=1), jnp.concatenate(values, axis=1)

    def backward(values, value=0.0, during=lambda value: value):
        sides = []
        for pair in range(len(plan.pairs)):
            a, n = plan.pair_range(pair)
            sides += back(plan, where, pair, values[a : a + n], high, low)
        return sum_clips(plan, sides, jnp.asarray(value, F32), during)

    def forward(sums, step=None, direction=None):
        vectors, tangents, inner, ahead = None, [], 0.0, None
        for pair, members in enumerate(plan.pairs):
            if ahead is not None:
                for c in members:
                    sums[c].mine[-1], halves[0] = tie(sums[c].mine[-1], halves[0])
            if pair:
                tangents.append((pair - 1, halves))
            pieces = [sums[c].pieces() for c in members]
            vectors, halves = forth(plan, where, pair, pieces, high, low, vectors, step, direction)
            ahead = halves
        tangents.append((len(plan.pairs) - 1, halves))
        found = []
        for pair, halves in tangents:
            some = [sum_feat(plan, half, bit, 1) for half in halves]
            n = some[-1].shape[0] - ROWS8
            inner = inner + some[-1][n : n + 2, 0]
            some[-1] = some[-1][:n]
            found += some
        return vectors, jnp.concatenate(found, axis=0), inner

    def bend(tangent):
        weighted = probs * tangent
        bent = (weighted - probs * jnp.sum(weighted, axis=0, keepdims=True)) / total_rows
        return bent, jnp.sum(bent * tangent)

    sums, _ = backward(values)
    direction, tangent, inner = forward(sums)
    norm0 = inner[0]
    bent, curvature = bend(tangent)

    def first_step(curvature):
        return norm0 / (sum_clip_scalar(plan, curvature) + damping * norm0)

    sums, step0 = backward(bent, curvature, first_step)
    residual, fresh, inner = forward(sums, step0, direction)
    norm1, cross = inner[0], inner[1]
    ratio = norm1 / norm0
    bent, curvature = bend(fresh + ratio * tangent)
    length = norm1 + 2.0 * ratio * cross + ratio * ratio * norm0

    def second_step(curvature):
        step1 = norm1 / (sum_clip_scalar(plan, curvature) + damping * length)
        moved = weights + (step0 + step1 * ratio) * direction + step1 * residual
        base = residual - (step1 * damping) * (residual + ratio * direction)
        return step1, moved, base

    sums, (step1, moved, base) = backward(bent, curvature, second_step)
    for pair, members in enumerate(plan.pairs):
        base = last(plan, where, pair, step1, [sums[c].pieces() for c in members], base)
    return moved, base


def solution(mesh):
    in_specs = (P("clip", "feat"), P(None, "feat"), P("clip"))
    out_specs = (P(None, "feat"), P(None, "feat"))
    return jax.shard_map(local, mesh=mesh, in_specs=in_specs, out_specs=out_specs, check_vma=False)
```

profile of v0, /device:TPU:0, one launch (start us, length us, event | category | flops | bytes accessed | tf_op | source)
XLA Modules:
  0.0 613.5 jit_solution(2384762363789583008)
XLA Ops:
  0.7 10.6 %split_and_logits.3 = (bf16[768,5632]{1,0:T(8,128)(2,1)}, bf16[768,5632]{1,0:T(8,128)(2,1)}, f32[200,256]{1,0:T(8,128)S(1)}, f32[200,256]{1,0:T(8,128)S(1)}) custom-call(s32[3]{0:T(128)S(1)} %pad_add_fusion.s_ref, f32[768,5632]{1,0:T(8,128)} %f_ref.5, f32[400,5632]{1,0:T(8,128)} %w_ref.5), custom_call_target="tpu_custom_call" | custom-call | flops 3460300800 | bytes 20545536 | tf_op jit(solution)/shard_map/split_and_logits/pallas_call | solution.py:107
  11.3 3.0 collective-permute-start
  14.3 10.6 %split_and_logits.4 = (bf16[768,5632]{1,0:T(8,128)(2,1)}, bf16[768,5632]{1,0:T(8,128)(2,1)}, f32[200,256]{1,0:T(8,128)S(1)}, f32[200,256]{1,0:T(8,128)S(1)}) custom-call(s32[3]{0:T(128)S(1)} %pad_add_fusion.s_ref, f32[768,5632]{1,0:T(8,128)} %f_ref.5, f32[400,5632]{1,0:T(8,128)} %w_ref.5, ...), custom_call_target="tpu_custom_call", output_to_operand_aliasing={{0}: (3, {}), {1}: (4, {})} | custom-call | flops 3460300800 | bytes 20545536 | tf_op jit(solution)/shard_map/split_and_logits/pallas_call | solution.py:107
  24.9 10.6 %split_and_logits.5 = (bf16[768,5632]{1,0:T(8,128)(2,1)}, bf16[768,5632]{1,0:T(8,128)(2,1)}, f32[200,256]{1,0:T(8,128)S(1)}, f32[200,256]{1,0:T(8,128)S(1)}) custom-call(s32[3]{0:T(128)S(1)} %pad_add_fusion.s_ref, f32[768,5632]{1,0:T(8,128)} %f_ref.5, f32[400,5632]{1,0:T(8,128)} %w_ref.5, ...), custom_call_target="tpu_custom_call", output_to_operand_aliasing={{0}: (3, {}), {1}: (4, {})} | custom-call | flops 3460300800 | bytes 20545536 | tf_op jit(solution)/shard_map/split_and_logits/pallas_call | solution.py:107
  35.5 2.0 collective-permute-start.6
  37.5 2.6 collective-permute-start.1
  40.6 5.6 collective-permute-done.6
  47.0 12.7 %collective-permute-done.1 = f32[200,256]{1,0:T(8,128)S(1)} collective-permute-done((f32[200,256]{1,0:T(8,128)S(1)}, f32[200,256]{1,0:T(8,128)S(1)}, u32[]{:S(2)}, u32[]{:S(2)}) %collective-permute-start.1) | collective-permute-done | bytes 204832 | tf_op jit(solution)/shard_map/ppermute | solution.py:67
  59.8 4.4 collective-permute-done.4
  64.3 2.3 collective-permute-done.7
  66.7 4.2 collective-permute-done.2
  71.0 4.3 collective-permute-done.5
  75.3 2.1 collective-permute-done.8
  78.3 11.5 %back_pair.6 = (f32[48,5632]{1,0:T(8,128)S(1)}, f32[48,5632]{1,0:T(8,128)}, f32[48,5632]{1,0:T(8,128)}, f32[48,5632]{1,0:T(8,128)}) custom-call(s32[3]{0:T(128)S(1)} %pad_add_fusion.s_ref, f32[192,768]{1,0:T(8,128)S(1)} %pad_maximum_fusion.10.g_ref, bf16[768,5632]{1,0:T(8,128)(2,1)} %get-tuple-element.87.high_ref.refs_12_.refs_14_, ...), custom_call_target="tpu_custom_call" | custom-call | flops 4982833152 | bytes 21626880 | tf_op jit(solution)/shard_map/back_pair/pallas_call | solution.py:151
  90.4 11.7 %back_pair.7 = (f32[56,5632]{1,0:T(8,128)}, f32[56,5632]{1,0:T(8,128)}, f32[48,5632]{1,0:T(8,128)S(1)}, f32[48,5632]{1,0:T(8,128)}) custom-call(s32[3]{0:T(128)S(1)} %pad_add_fusion.s_ref, f32[208,768]{1,0:T(8,128)S(1)} %pad_maximum_fusion.2.g_ref, bf16[768,5632]{1,0:T(8,128)(2,1)} %get-tuple-element.87.high_ref.refs_12_.refs_14_, ...), custom_call_target="tpu_custom_call" | custom-call | flops 5398069248 | bytes 21987328 | tf_op jit(solution)/shard_map/back_pair/pallas_call | solution.py:151
  110.4 7.5 %collective-permute-done.10 = f32[48,2816]{1,0:T(8,128)S(1)} collective-permute-done((f32[48,2816]{1,0:T(8,128)S(1)}, f32[48,2816]{1,0:T(8,128)S(1)}, u32[]{:S(2)}, u32[]{:S(2)}) %collective-permute-start.10) | collective-permute-done | bytes 540704 | tf_op jit(solution)/shard_map/ppermute | solution.py:67
  121.3 8.2 %collective-permute-done.28 = f32[48,2816]{1,0:T(8,128)S(1)} collective-permute-done((f32[48,2816]{1,0:T(8,128)S(1)}, f32[48,2816]{1,0:T(8,128)S(1)}, u32[]{:S(2)}, u32[]{:S(2)}) %collective-permute-start.28) | collective-permute-done | bytes 540704 | tf_op jit(solution)/shard_map/ppermute | solution.py:67
  131.2 2.1 collective-permute-done.20
  134.0 9.7 %collective-permute-done.29 = f32[48,1408]{1,0:T(8,128)S(1)} collective-permute-done((f32[48,1408]{1,0:T(8,128)S(1)}, f32[48,1408]{1,0:T(8,128)S(1)}, u32[]{:S(2)}, u32[]{:S(2)}) %collective-permute-start.29) | collective-permute-done | bytes 270368 | tf_op jit(solution)/shard_map/ppermute | solution.py:67
  146.0 6.7 %collective-permute-done.30.refs_7_ = f32[48,1408]{1,0:T(8,128)S(1)} collective-permute-done((f32[48,1408]{1,0:T(8,128)S(1)}, f32[48,1408]{1,0:T(8,128)S(1)}, u32[]{:S(2)}, u32[]{:S(2)}) %collective-permute-start.30) | collective-permute-done | bytes 270368 | tf_op jit(solution)/shard_map/ppermute | solution.py:67
  157.8 14.6 %collective-permute-done.17.refs_1_ = f32[48,1408]{1,0:T(8,128)S(1)} collective-permute-done((f32[48,1408]{1,0:T(8,128)S(1)}, f32[48,1408]{1,0:T(8,128)S(1)}, u32[]{:S(2)}, u32[]{:S(2)}) %collective-permute-start.17) | collective-permute-done | bytes 270368 | tf_op jit(solution)/shard_map/ppermute | solution.py:67
  173.1 3.3 collective-permute-done.12.refs_7_
  181.1 14.7 %forth_pair.4 = (f32[400,5632]{1,0:T(8,128)}, f32[216,384]{1,0:T(8,128)}, f32[216,384]{1,0:T(8,128)}) custom-call(s32[3]{0:T(128)S(1)} %pad_add_fusion.s_ref, f32[56,1408]{1,0:T(8,128)S(1)} %slice_add_fusion.8.refs_0_, f32[56,1408]{1,0:T(8,128)S(1)} %collective-permute-done.22.refs_1_, f32[56,2816]{1,0:T(8,128)} %copy-done.25, ...), custom_call_target="tpu_custom_call" | custom-call | flops 5398069248 | bytes 31358976 | tf_op jit(solution)/shard_map/forth_pair/pallas_call | solution.py:293
  197.6 8.0 %collective-permute-done.35 = f32[216,384]{1,0:T(8,128)S(1)} collective-permute-done((f32[216,384]{1,0:T(8,128)}, f32[216,384]{1,0:T(8,128)S(1)}, u32[]{:S(2)}, u32[]{:S(2)}) %collective-permute-start.35) | collective-permute-done | bytes 331808 | tf_op jit(solution)/shard_map/ppermute | solution.py:67
  209.1 14.3 %forth_pair.5 = (f32[400,5632]{1,0:T(8,128)}, f32[96,384]{1,0:T(8,128)S(1)}, f32[96,384]{1,0:T(8,128)S(1)}, f32[104,384]{1,0:T(8,128)S(1)}, f32[104,384]{1,0:T(8,128)S(1)}) custom-call(s32[3]{0:T(128)S(1)} %pad_add_fusion.s_ref, f32[48,1408]{1,0:T(8,128)S(1)} %slice_add_fusion.16.refs_0_, ...), custom_call_target="tpu_custom_call", output_to_operand_aliasing={{0}: (15, {})} | custom-call | flops 4982833152 | bytes 30277632 | tf_op jit(solution)/shard_map/forth_pair/pallas_call | solution.py:293
  223.4 1.7 collective-permute-start.44
  225.4 4.7 collective-permute-done.44
  232.4 2.2 collective-permute-done.47
  235.1 5.1 collective-permute-done.45
  240.3 6.4 %collective-permute-done.48 = f32[104,384]{1,0:T(8,128)S(1)} collective-permute-done((f32[104,384]{1,0:T(8,128)S(1)}, f32[104,384]{1,0:T(8,128)S(1)}, u32[]{:S(2)}, u32[]{:S(2)}) %collective-permute-start.48) | collective-permute-done | bytes 159776 | tf_op jit(solution)/shard_map/ppermute | solution.py:67
  246.7 3.1 collective-permute-start.49
  251.0 2.1 collective-permute-done.49
  255.0 11.5 %back_pair.8 = (f32[48,5632]{1,0:T(8,128)S(1)}, f32[48,5632]{1,0:T(8,128)}, f32[48,5632]{1,0:T(8,128)}, f32[48,5632]{1,0:T(8,128)}) custom-call(s32[3]{0:T(128)S(1)} %pad_add_fusion.s_ref, f32[192,768]{1,0:T(8,128)S(1)} %slice.349.g_ref, bf16[768,5632]{1,0:T(8,128)(2,1)} %get-tuple-element.87.high_ref.refs_12_.refs_14_, ...), custom_call_target="tpu_custom_call" | custom-call | flops 4982833152 | bytes 21626880 | tf_op jit(solution)/shard_map/back_pair/pallas_call | solution.py:151
  266.9 11.9 %back_pair.9 = (f32[56,5632]{1,0:T(8,128)}, f32[56,5632]{1,0:T(8,128)}, f32[48,5632]{1,0:T(8,128)S(1)}, f32[48,5632]{1,0:T(8,128)}) custom-call(s32[3]{0:T(128)S(1)} %pad_add_fusion.s_ref, f32[208,768]{1,0:T(8,128)S(1)} %slice.360.g_ref, bf16[768,5632]{1,0:T(8,128)(2,1)} %get-tuple-element.87.high_ref.refs_12_.refs_14_, ...), custom_call_target="tpu_custom_call" | custom-call | flops 5398069248 | bytes 21987328 | tf_op jit(solution)/shard_map/back_pair/pallas_call | solution.py:151
  297.0 8.3 %collective-permute-done.64 = f32[8,128]{1,0:T(8,128)S(1)} collective-permute-done((f32[8,128]{1,0:T(8,128)S(1)}, f32[8,128]{1,0:T(8,128)S(1)}, u32[]{:S(2)}, u32[]{:S(2)}) %collective-permute-start.64) | collective-permute-done | bytes 4128 | tf_op jit(solution)/shard_map/ppermute | solution.py:67
  318.1 7.0 %collective-permute-done.61 = f32[56,2816]{1,0:T(8,128)} collective-permute-done((f32[56,2816]{1,0:T(8,128)}, f32[56,2816]{1,0:T(8,128)}, u32[]{:S(2)}, u32[]{:S(2)}) %collective-permute-start.61) | collective-permute-done | bytes 630816 | tf_op jit(solution)/shard_map/ppermute | solution.py:67
  327.6 7.5 %collective-permute-done.73 = f32[48,1408]{1,0:T(8,128)S(1)} collective-permute-done((f32[48,1408]{1,0:T(8,128)S(1)}, f32[48,1408]{1,0:T(8,128)S(1)}, u32[]{:S(2)}, u32[]{:S(2)}) %collective-permute-start.73) | collective-permute-done | bytes 270368 | tf_op jit(solution)/shard_map/ppermute | solution.py:67
  338.0 6.0 collective-permute-done.74.refs_8_
  349.9 13.9 %collective-permute-done.58.refs_2_ = f32[48,1408]{1,0:T(8,128)S(1)} collective-permute-done((f32[48,1408]{1,0:T(8,128)S(1)}, f32[48,1408]{1,0:T(8,128)S(1)}, u32[]{:S(2)}, u32[]{:S(2)}) %collective-permute-start.58) | collective-permute-done | bytes 270368 | tf_op jit(solution)/shard_map/ppermute | solution.py:67
  364.4 3.1 collective-permute-done.53.refs_8_
  372.1 16.1 %forth_pair.6 = (f32[400,5632]{1,0:T(8,128)}, f32[216,384]{1,0:T(8,128)}, f32[216,384]{1,0:T(8,128)}) custom-call(s32[3]{0:T(128)S(1)} %pad_add_fusion.s_ref, f32[1]{0:T(128)} %bitcast.5.refs_0_, f32[56,1408]{1,0:T(8,128)S(1)} %slice_add_fusion.7.refs_1_, f32[56,1408]{1,0:T(8,128)S(1)} %collective-permute-done.66.refs_2_, f32[56,2816]{1,0:T(8,128)} %copy-done.28, ...), custom_call_target="tpu_custom_call" | custom-call | flops 5398069248 | bytes 31358976 | tf_op jit(solution)/shard_map/forth_pair/pallas_call | solution.py:293
  388.3 2.1 collective-permute-start.79
  392.0 6.4 %collective-permute-done.79 = f32[216,384]{1,0:T(8,128)S(1)} collective-permute-done((f32[216,384]{1,0:T(8,128)}, f32[216,384]{1,0:T(8,128)S(1)}, u32[]{:S(2)}, u32[]{:S(2)}) %collective-permute-start.79) | collective-permute-done | bytes 331808 | tf_op jit(solution)/shard_map/ppermute | solution.py:67
  399.4 2.1 collective-permute-start.80
  402.7 15.8 %forth_pair.7 = (f32[400,5632]{1,0:T(8,128)}, f32[96,384]{1,0:T(8,128)S(1)}, f32[96,384]{1,0:T(8,128)S(1)}, f32[104,384]{1,0:T(8,128)S(1)}, f32[104,384]{1,0:T(8,128)S(1)}) custom-call(s32[3]{0:T(128)S(1)} %pad_add_fusion.s_ref, f32[1]{0:T(128)} %bitcast.5.refs_0_, f32[48,1408]{1,0:T(8,128)S(1)} %slice_add_fusion.13.refs_1_, ...), custom_call_target="tpu_custom_call", output_to_operand_aliasing={{0}: (17, {})} | custom-call | flops 4982833152 | bytes 30277632 | tf_op jit(solution)/shard_map/forth_pair/pallas_call | solution.py:293
  420.5 4.7 collective-permute-done.88
  426.1 1.8 collective-permute-start.81
  429.5 5.2 collective-permute-done.89
  434.8 6.1 collective-permute-done.92
  440.9 2.9 collective-permute-start.93
  443.8 2.0 collective-permute-done.90
  452.3 11.7 %back_pair.11 = (f32[48,5632]{1,0:T(8,128)S(1)}, f32[48,5632]{1,0:T(8,128)}, f32[48,5632]{1,0:T(8,128)}, f32[48,5632]{1,0:T(8,128)}) custom-call(s32[3]{0:T(128)S(1)} %pad_add_fusion.s_ref, f32[192,768]{1,0:T(8,128)S(1)} %slice.376.g_ref, bf16[768,5632]{1,0:T(8,128)(2,1)} %get-tuple-element.87.high_ref.refs_12_.refs_14_, ...), custom_call_target="tpu_custom_call" | custom-call | flops 4982833152 | bytes 21626880 | tf_op jit(solution)/shard_map/back_pair/pallas_call | solution.py:151
  464.1 11.8 %back_pair.10 = (f32[56,5632]{1,0:T(8,128)}, f32[56,5632]{1,0:T(8,128)}, f32[48,5632]{1,0:T(8,128)S(1)}, f32[48,5632]{1,0:T(8,128)}) custom-call(s32[3]{0:T(128)S(1)} %pad_add_fusion.s_ref, f32[208,768]{1,0:T(8,128)S(1)} %slice.373.g_ref, bf16[768,5632]{1,0:T(8,128)(2,1)} %get-tuple-element.87.high_ref.refs_12_.refs_14_, ...), custom_call_target="tpu_custom_call" | custom-call | flops 5398069248 | bytes 21987328 | tf_op jit(solution)/shard_map/back_pair/pallas_call | solution.py:151
  495.9 3.9 collective-permute-done.98
  503.6 11.1 %collective-permute-done.99 = f32[8,128]{1,0:T(8,128)S(1)} collective-permute-done((f32[8,128]{1,0:T(8,128)S(1)}, f32[8,128]{1,0:T(8,128)S(1)}, u32[]{:S(2)}, u32[]{:S(2)}) %collective-permute-start.99) | collective-permute-done | bytes 4128 | tf_op jit(solution)/shard_map/ppermute | solution.py:67
  516.6 17.0 %multiply_subtract_fusion = (f32[400,5632]{1,0:T(8,128)}, f32[400,5632]{1,0:T(8,128)}) fusion(f32[400,5632]{1,0:T(8,128)} %get-tuple-element.141, f32[400,5632]{1,0:T(8,128)} %get-tuple-element.123.refs_13_, f32[]{:T(128)S(6)} %div.80, f32[]{:T(128)S(6)} %mul.99, f32[]{:T(128)} %div.82, f32[400,5632]{1,0:T(8,128)} %w_ref.5, f32[]{:T(128)S(6)} %add.279), kind=kLoop, calls=%fused_computation | loop fusion | flops 18022400 | bytes 45056016 | tf_op jit(solution)/shard_map/sub | solution.py:540
  540.2 2.4 collective-permute-done.102
  543.7 6.6 %collective-permute-done.123 = f32[48,1408]{1,0:T(8,128)S(1)} collective-permute-done((f32[48,1408]{1,0:T(8,128)S(1)}, f32[48,1408]{1,0:T(8,128)S(1)}, u32[]{:S(2)}, u32[]{:S(2)}) %collective-permute-start.123) | collective-permute-done | bytes 270368 | tf_op jit(solution)/shard_map/ppermute | solution.py:67
  553.5 8.4 %collective-permute-done.96 = f32[56,1408]{1,0:T(8,128)S(1)} collective-permute-done((f32[56,1408]{1,0:T(8,128)S(1)}, f32[56,1408]{1,0:T(8,128)S(1)}, u32[]{:S(2)}, u32[]{:S(2)}) %collective-permute-start.96) | collective-permute-done | bytes 315424 | tf_op jit(solution)/shard_map/ppermute | solution.py:67
  564.6 7.2 %collective-permute-done.116.refs_1_ = f32[56,1408]{1,0:T(8,128)S(1)} collective-permute-done((f32[56,1408]{1,0:T(8,128)S(1)}, f32[56,1408]{1,0:T(8,128)S(1)}, u32[]{:S(2)}, u32[]{:S(2)}) %collective-permute-start.116) | collective-permute-done | bytes 315424 | tf_op jit(solution)/shard_map/ppermute | solution.py:67
  576.2 14.0 %collective-permute-done.117.refs_2_ = f32[56,2816]{1,0:T(8,128)S(1)} collective-permute-done((f32[56,2816]{1,0:T(8,128)S(1)}, f32[56,2816]{1,0:T(8,128)S(1)}, u32[]{:S(2)}, u32[]{:S(2)}) %collective-permute-start.117) | collective-permute-done | bytes 630816 | tf_op jit(solution)/shard_map/ppermute | solution.py:67
  590.8 7.8 %collective-permute-done.104.refs_2_ = f32[48,2816]{1,0:T(8,128)S(1)} collective-permute-done((f32[48,2816]{1,0:T(8,128)S(1)}, f32[48,2816]{1,0:T(8,128)S(1)}, u32[]{:S(2)}, u32[]{:S(2)}) %collective-permute-start.104) | collective-permute-done | bytes 540704 | tf_op jit(solution)/shard_map/ppermute | solution.py:67
  600.5 5.6 last_pair.2.refs_12_
  607.8 5.2 last_pair.3
  (468 shorter events, 145.5 us)
Async XLA Ops:
  11.3 26.2 %collective-permute-start = (f32[200,256]{1,0:T(8,128)S(1)}, f32[200,256]{1,0:T(8,128)S(1)}, u32[]{:S(2)}, u32[]{:S(2)}) collective-permute-start(f32[200,256]{1,0:T(8,128)S(1)} %get-tuple-element.78), channel_id=1, source_target_pairs={{0,1},{1,0},{2,3},{3,2},{4,5},{5,4},{6,7},{7,6},{8,9},{9,8},{10,11... | collective-permute-start | bytes 614408 | tf_op jit(solution)/shard_map/ppermute | solution.py:67
  24.9 15.3 %collective-permute-start.3 = (f32[200,256]{1,0:T(8,128)S(1)}, f32[200,256]{1,0:T(8,128)S(1)}, u32[]{:S(2)}, u32[]{:S(2)}) collective-permute-start(f32[200,256]{1,0:T(8,128)S(1)} %get-tuple-element.82), channel_id=1, source_target_pairs={{0,1},{1,0},{2,3},{3,2},{4,5},{5,4},{6,7},{7,6},{8,9},{9,8},{10,11... | collective-permute-start | bytes 614408 | tf_op jit(solution)/shard_map/ppermute | solution.py:67
  37.5 22.1 %collective-permute-start.1 = (f32[200,256]{1,0:T(8,128)S(1)}, f32[200,256]{1,0:T(8,128)S(1)}, u32[]{:S(2)}, u32[]{:S(2)}) collective-permute-start(f32[200,256]{1,0:T(8,128)S(1)} %add.221), channel_id=1, source_target_pairs={{0,2},{1,3},{2,0},{3,1},{4,6},{5,7},{6,4},{7,5},{8,10},{9,11},{10,... | collective-permute-start | bytes 614408 | tf_op jit(solution)/shard_map/ppermute | solution.py:67
  40.2 24.0 %collective-permute-start.4 = (f32[200,256]{1,0:T(8,128)S(1)}, f32[200,256]{1,0:T(8,128)S(1)}, u32[]{:S(2)}, u32[]{:S(2)}) collective-permute-start(f32[200,256]{1,0:T(8,128)S(1)} %add.223), channel_id=1, source_target_pairs={{0,2},{1,3},{2,0},{3,1},{4,6},{5,7},{6,4},{7,5},{8,10},{9,11},{10,... | collective-permute-start | bytes 614408 | tf_op jit(solution)/shard_map/ppermute | solution.py:67
  46.2 20.3 %collective-permute-start.7 = (f32[200,256]{1,0:T(8,128)S(1)}, f32[200,256]{1,0:T(8,128)S(1)}, u32[]{:S(2)}, u32[]{:S(2)}) collective-permute-start(f32[200,256]{1,0:T(8,128)S(1)} %add.225), channel_id=1, source_target_pairs={{0,2},{1,3},{2,0},{3,1},{4,6},{5,7},{6,4},{7,5},{8,10},{9,11},{10,... | collective-permute-start | bytes 614408 | tf_op jit(solution)/shard_map/ppermute | solution.py:67
  89.8 12.8 %collective-permute-start.9 = (f32[48,5632]{1,0:T(8,128)}, f32[48,5632]{1,0:T(8,128)S(1)}, u32[]{:S(2)}, u32[]{:S(2)}) collective-permute-start(f32[48,5632]{1,0:T(8,128)} %get-tuple-element.90), channel_id=1, source_target_pairs={{0,4},{4,0},{8,12},{12,8},{16,20},{20,16},{24,28},{28,24},{1,5},{5... | collective-permute-start | bytes 3244040 | tf_op jit(solution)/shard_map/ppermute | solution.py:67
  89.8 14.6 %collective-permute-start.14 = (f32[48,5632]{1,0:T(8,128)}, f32[48,5632]{1,0:T(8,128)S(1)}, u32[]{:S(2)}, u32[]{:S(2)}) collective-permute-start(f32[48,5632]{1,0:T(8,128)} %get-tuple-element.92), channel_id=1, source_target_pairs={{0,4},{4,0},{8,12},{12,8},{16,20},{20,16},{24,28},{28,24},{1,5},{5... | collective-permute-start | bytes 3244040 | tf_op jit(solution)/shard_map/ppermute | solution.py:67
  102.7 15.2 %collective-permute-start.10 = (f32[48,2816]{1,0:T(8,128)S(1)}, f32[48,2816]{1,0:T(8,128)S(1)}, u32[]{:S(2)}, u32[]{:S(2)}) collective-permute-start(f32[48,2816]{1,0:T(8,128)S(1)} %slice.332), channel_id=1, source_target_pairs={{0,16},{4,20},{8,24},{12,28},{16,0},{20,4},{24,8},{28,12},{1,17},{... | collective-permute-start | bytes 1622024 | tf_op jit(solution)/shard_map/ppermute | solution.py:67
  104.6 15.2 %collective-permute-start.15 = (f32[48,2816]{1,0:T(8,128)S(1)}, f32[48,2816]{1,0:T(8,128)S(1)}, u32[]{:S(2)}, u32[]{:S(2)}) collective-permute-start(f32[48,2816]{1,0:T(8,128)S(1)} %pad_maximum_fusion.12), channel_id=1, source_target_pairs={{0,8},{4,12},{8,0},{12,4},{16,24},{20,28},{24,16},{28,20},{1,9},{5... | collective-permute-start | bytes 1622024 | tf_op jit(solution)/shard_map/ppermute | solution.py:67
  107.0 22.6 %collective-permute-start.28 = (f32[48,2816]{1,0:T(8,128)S(1)}, f32[48,2816]{1,0:T(8,128)S(1)}, u32[]{:S(2)}, u32[]{:S(2)}) collective-permute-start(f32[48,2816]{1,0:T(8,128)S(1)} %slice.344), channel_id=1, source_target_pairs={{0,16},{4,20},{8,24},{12,28},{16,0},{20,4},{24,8},{28,12},{1,17},{... | collective-permute-start | bytes 1622024 | tf_op jit(solution)/shard_map/ppermute | solution.py:67
  108.9 24.5 %collective-permute-start.20 = (f32[56,2816]{1,0:T(8,128)S(1)}, f32[56,2816]{1,0:T(8,128)S(1)}, u32[]{:S(2)}, u32[]{:S(2)}) collective-permute-start(f32[56,2816]{1,0:T(8,128)S(1)} %pad_maximum_fusion.4), channel_id=1, source_target_pairs={{0,8},{4,12},{8,0},{12,4},{16,24},{20,28},{24,16},{28,20},{1,9},{5... | collective-permute-start | bytes 1892360 | tf_op jit(solution)/shard_map/ppermute | solution.py:67
  118.0 38.5 %collective-permute-start.11 = (f32[48,1408]{1,0:T(8,128)S(1)}, f32[48,1408]{1,0:T(8,128)S(1)}, u32[]{:S(2)}, u32[]{:S(2)}) collective-permute-start(f32[48,1408]{1,0:T(8,128)S(1)} %slice.334), channel_id=1, source_target_pairs={{0,8},{4,12},{8,0},{12,4},{16,24},{20,28},{24,16},{28,20},{1,9},{5... | collective-permute-start | bytes 811016 | tf_op jit(solution)/shard_map/ppermute | solution.py:67
  120.0 35.7 %collective-permute-start.16 = (f32[48,1408]{1,0:T(8,128)S(1)}, f32[48,1408]{1,0:T(8,128)S(1)}, u32[]{:S(2)}, u32[]{:S(2)}) collective-permute-start(f32[48,1408]{1,0:T(8,128)S(1)} %slice.340), channel_id=1, source_target_pairs={{0,16},{4,20},{8,24},{12,28},{16,0},{20,4},{24,8},{28,12},{1,17},{... | collective-permute-start | bytes 811016 | tf_op jit(solution)/shard_map/ppermute | solution.py:67
  129.6 14.0 %collective-permute-start.29 = (f32[48,1408]{1,0:T(8,128)S(1)}, f32[48,1408]{1,0:T(8,128)S(1)}, u32[]{:S(2)}, u32[]{:S(2)}) collective-permute-start(f32[48,1408]{1,0:T(8,128)S(1)} %slice.346), channel_id=1, source_target_pairs={{0,8},{4,12},{8,0},{12,4},{16,24},{20,28},{24,16},{28,20},{1,9},{5... | collective-permute-start | bytes 811016 | tf_op jit(solution)/shard_map/ppermute | solution.py:67
  133.5 11.9 %collective-permute-start.21 = (f32[56,1408]{1,0:T(8,128)S(1)}, f32[56,1408]{1,0:T(8,128)S(1)}, u32[]{:S(2)}, u32[]{:S(2)}) collective-permute-start(f32[56,1408]{1,0:T(8,128)S(1)} %slice.342), channel_id=1, source_target_pairs={{0,16},{4,20},{8,24},{12,28},{16,0},{20,4},{24,8},{28,12},{1,17},{... | collective-permute-start | bytes 946184 | tf_op jit(solution)/shard_map/ppermute | solution.py:67
  143.7 33.2 %collective-permute-start.32 = (f32[48,1408]{1,0:T(8,128)S(1)}, f32[48,1408]{1,0:T(8,128)S(1)}, u32[]{:S(2)}, u32[]{:S(2)}) collective-permute-start(f32[48,1408]{1,0:T(8,128)S(1)} %slice_add_fusion.15.refs_6_), channel_id=1, source_target_pairs={{0,4},{4,0},{8,12},{12,8},{16,20},{20,16},{24,28},{28,24},{1,5},{5... | collective-permute-start | bytes 811016 | tf_op jit(solution)/shard_map/ppermute | solution.py:67
  152.7 19.7 %collective-permute-start.31 = (f32[48,2816]{1,0:T(8,128)S(1)}, f32[48,2816]{1,0:T(8,128)S(1)}, u32[]{:S(2)}, u32[]{:S(2)}) collective-permute-start(f32[48,2816]{1,0:T(8,128)S(1)} %pad_maximum_fusion.14), channel_id=1, source_target_pairs={{0,16},{4,20},{8,24},{12,28},{16,0},{20,4},{24,8},{28,12},{1,17},{... | collective-permute-start | bytes 1622024 | tf_op jit(solution)/shard_map/ppermute | solution.py:67
  155.0 17.9 %collective-permute-start.23 = (f32[56,2816]{1,0:T(8,128)S(1)}, f32[56,2816]{1,0:T(8,128)S(1)}, u32[]{:S(2)}, u32[]{:S(2)}) collective-permute-start(f32[56,2816]{1,0:T(8,128)S(1)} %pad_maximum_fusion.5), channel_id=1, source_target_pairs={{0,8},{4,12},{8,0},{12,4},{16,24},{20,28},{24,16},{28,20},{1,9},{5... | collective-permute-start | bytes 1892360 | tf_op jit(solution)/shard_map/ppermute | solution.py:67
  155.7 16.8 %collective-permute-start.17 = (f32[48,1408]{1,0:T(8,128)S(1)}, f32[48,1408]{1,0:T(8,128)S(1)}, u32[]{:S(2)}, u32[]{:S(2)}) collective-permute-start(f32[48,1408]{1,0:T(8,128)S(1)} %slice_add_fusion.16.refs_0_), channel_id=1, source_target_pairs={{0,16},{4,20},{8,24},{12,28},{16,0},{20,4},{24,8},{28,12},{1,17},{... | collective-permute-start | bytes 811016 | tf_op jit(solution)/shard_map/ppermute | solution.py:67
  156.6 19.8 %collective-permute-start.12 = (f32[48,1408]{1,0:T(8,128)S(1)}, f32[48,1408]{1,0:T(8,128)S(1)}, u32[]{:S(2)}, u32[]{:S(2)}) collective-permute-start(f32[48,1408]{1,0:T(8,128)S(1)} %slice_add_fusion.17.refs_6_), channel_id=1, source_target_pairs={{0,8},{4,12},{8,0},{12,4},{16,24},{20,28},{24,16},{28,20},{1,9},{5... | collective-permute-start | bytes 811016 | tf_op jit(solution)/shard_map/ppermute | solution.py:67
  176.3 19.4 %collective-permute-start.18 = (f32[48,2816]{1,0:T(8,128)S(1)}, f32[48,2816]{1,0:T(8,128)S(1)}, u32[]{:S(2)}, u32[]{:S(2)}) collective-permute-start(f32[48,2816]{1,0:T(8,128)S(1)} %pad_maximum_fusion.13), channel_id=1, source_target_pairs={{0,8},{4,12},{8,0},{12,4},{16,24},{20,28},{24,16},{28,20},{1,9},{5... | collective-permute-start | bytes 1622024 | tf_op jit(solution)/shard_map/ppermute | solution.py:67
  178.5 17.3 %collective-permute-start.13 = (f32[48,2816]{1,0:T(8,128)S(1)}, f32[48,2816]{1,0:T(8,128)S(1)}, u32[]{:S(2)}, u32[]{:S(2)}) collective-permute-start(f32[48,2816]{1,0:T(8,128)S(1)} %pad_maximum_fusion.11), channel_id=1, source_target_pairs={{0,16},{4,20},{8,24},{12,28},{16,0},{20,4},{24,8},{28,12},{1,17},{... | collective-permute-start | bytes 1622024 | tf_op jit(solution)/shard_map/ppermute | solution.py:67
  195.9 12.1 %collective-permute-start.43 = (f32[48,2816]{1,0:T(8,128)S(1)}, f32[48,2816]{1,0:T(8,128)S(1)}, u32[]{:S(2)}, u32[]{:S(2)}) collective-permute-start(f32[48,2816]{1,0:T(8,128)S(1)} %collective-permute-done.13.refs_8_), channel_id=1, source_target_pairs={{0,4},{4,0},{8,12},{12,8},{16,20},{20,16},{24,28},{28,24},{1,5},{5... | collective-permute-start | bytes 1622024 | tf_op jit(solution)/shard_map/ppermute | solution.py:67
  206.6 25.2 %collective-permute-start.36 = (f32[216,384]{1,0:T(8,128)S(1)}, f32[216,384]{1,0:T(8,128)S(1)}, u32[]{:S(2)}, u32[]{:S(2)}) collective-permute-start(f32[216,384]{1,0:T(8,128)S(1)} %add.239), channel_id=1, source_target_pairs={{0,2},{1,3},{2,0},{3,1},{4,6},{5,7},{6,4},{7,5},{8,10},{9,11},{10,... | collective-permute-start | bytes 995336 | tf_op jit(solution)/shard_map/ppermute | solution.py:67
  231.9 19.0 %collective-permute-start.37 = (f32[216,384]{1,0:T(8,128)S(1)}, f32[216,384]{1,0:T(8,128)S(1)}, u32[]{:S(2)}, u32[]{:S(2)}) collective-permute-start(f32[216,384]{1,0:T(8,128)S(1)} %add.240), channel_id=1, source_target_pairs={{0,1},{1,0},{2,3},{3,2},{4,5},{5,4},{6,7},{7,6},{8,9},{9,8},{10,11... | collective-permute-start | bytes 995336 | tf_op jit(solution)/shard_map/ppermute | solution.py:67
  234.7 12.0 %collective-permute-start.48 = (f32[104,384]{1,0:T(8,128)S(1)}, f32[104,384]{1,0:T(8,128)S(1)}, u32[]{:S(2)}, u32[]{:S(2)}) collective-permute-start(f32[104,384]{1,0:T(8,128)S(1)} %add.243), channel_id=1, source_target_pairs={{0,2},{1,3},{2,0},{3,1},{4,6},{5,7},{6,4},{7,5},{8,10},{9,11},{10,... | collective-permute-start | bytes 479240 | tf_op jit(solution)/shard_map/ppermute | solution.py:67
  266.4 14.1 %collective-permute-start.50 = (f32[48,5632]{1,0:T(8,128)}, f32[48,5632]{1,0:T(8,128)}, u32[]{:S(2)}, u32[]{:S(2)}) collective-permute-start(f32[48,5632]{1,0:T(8,128)} %get-tuple-element.112), channel_id=1, source_target_pairs={{0,4},{4,0},{8,12},{12,8},{16,20},{20,16},{24,28},{28,24},{1,5},{5... | collective-permute-start | bytes 3244040 | tf_op jit(solution)/shard_map/ppermute | solution.py:67
  266.4 17.8 %collective-permute-start.55 = (f32[48,5632]{1,0:T(8,128)}, f32[48,5632]{1,0:T(8,128)}, u32[]{:S(2)}, u32[]{:S(2)}) collective-permute-start(f32[48,5632]{1,0:T(8,128)} %get-tuple-element.114), channel_id=1, source_target_pairs={{0,4},{4,0},{8,12},{12,8},{16,20},{20,16},{24,28},{28,24},{1,5},{5... | collective-permute-start | bytes 3244040 | tf_op jit(solution)/shard_map/ppermute | solution.py:67
  278.9 12.8 %collective-permute-start.71 = (f32[48,5632]{1,0:T(8,128)}, f32[48,5632]{1,0:T(8,128)}, u32[]{:S(2)}, u32[]{:S(2)}) collective-permute-start(f32[48,5632]{1,0:T(8,128)} %get-tuple-element.122), channel_id=1, source_target_pairs={{0,4},{4,0},{8,12},{12,8},{16,20},{20,16},{24,28},{28,24},{1,5},{5... | collective-permute-start | bytes 3244040 | tf_op jit(solution)/shard_map/ppermute | solution.py:67
  283.1 28.3 %collective-permute-start.51 = (f32[48,2816]{1,0:T(8,128)}, f32[48,2816]{1,0:T(8,128)}, u32[]{:S(2)}, u32[]{:S(2)}) collective-permute-start(f32[48,2816]{1,0:T(8,128)} %slice.351), channel_id=1, source_target_pairs={{0,16},{4,20},{8,24},{12,28},{16,0},{20,4},{24,8},{28,12},{1,17},{... | collective-permute-start | bytes 1622024 | tf_op jit(solution)/shard_map/ppermute | solution.py:67
  290.2 23.9 %collective-permute-start.56 = (f32[48,2816]{1,0:T(8,128)}, f32[48,2816]{1,0:T(8,128)}, u32[]{:S(2)}, u32[]{:S(2)}) collective-permute-start(f32[48,2816]{1,0:T(8,128)} %pad_maximum_fusion.16), channel_id=1, source_target_pairs={{0,8},{4,12},{8,0},{12,4},{16,24},{20,28},{24,16},{28,20},{1,9},{5... | collective-permute-start | bytes 1622024 | tf_op jit(solution)/shard_map/ppermute | solution.py:67
  294.0 22.3 %collective-permute-start.72 = (f32[48,2816]{1,0:T(8,128)}, f32[48,2816]{1,0:T(8,128)}, u32[]{:S(2)}, u32[]{:S(2)}) collective-permute-start(f32[48,2816]{1,0:T(8,128)} %slice.366), channel_id=1, source_target_pairs={{0,16},{4,20},{8,24},{12,28},{16,0},{20,4},{24,8},{28,12},{1,17},{... | collective-permute-start | bytes 1622024 | tf_op jit(solution)/shard_map/ppermute | solution.py:67
  307.6 17.5 %collective-permute-start.61 = (f32[56,2816]{1,0:T(8,128)}, f32[56,2816]{1,0:T(8,128)}, u32[]{:S(2)}, u32[]{:S(2)}) collective-permute-start(f32[56,2816]{1,0:T(8,128)} %pad_maximum_fusion.6), channel_id=1, source_target_pairs={{0,8},{4,12},{8,0},{12,4},{16,24},{20,28},{24,16},{28,20},{1,9},{5... | collective-permute-start | bytes 1892360 | tf_op jit(solution)/shard_map/ppermute | solution.py:67
  312.6 35.7 %collective-permute-start.52 = (f32[48,1408]{1,0:T(8,128)S(1)}, f32[48,1408]{1,0:T(8,128)S(1)}, u32[]{:S(2)}, u32[]{:S(2)}) collective-permute-start(f32[48,1408]{1,0:T(8,128)S(1)} %slice.353), channel_id=1, source_target_pairs={{0,8},{4,12},{8,0},{12,4},{16,24},{20,28},{24,16},{28,20},{1,9},{5... | collective-permute-start | bytes 811016 | tf_op jit(solution)/shard_map/ppermute | solution.py:67
  315.3 31.7 %collective-permute-start.57 = (f32[48,1408]{1,0:T(8,128)S(1)}, f32[48,1408]{1,0:T(8,128)S(1)}, u32[]{:S(2)}, u32[]{:S(2)}) collective-permute-start(f32[48,1408]{1,0:T(8,128)S(1)} %slice.359), channel_id=1, source_target_pairs={{0,16},{4,20},{8,24},{12,28},{16,0},{20,4},{24,8},{28,12},{1,17},{... | collective-permute-start | bytes 811016 | tf_op jit(solution)/shard_map/ppermute | solution.py:67
  317.5 17.6 %collective-permute-start.73 = (f32[48,1408]{1,0:T(8,128)S(1)}, f32[48,1408]{1,0:T(8,128)S(1)}, u32[]{:S(2)}, u32[]{:S(2)}) collective-permute-start(f32[48,1408]{1,0:T(8,128)S(1)} %slice.368), channel_id=1, source_target_pairs={{0,8},{4,12},{8,0},{12,4},{16,24},{20,28},{24,16},{28,20},{1,9},{5... | collective-permute-start | bytes 811016 | tf_op jit(solution)/shard_map/ppermute | solution.py:67
  335.1 33.2 %collective-permute-start.76 = (f32[48,1408]{1,0:T(8,128)S(1)}, f32[48,1408]{1,0:T(8,128)S(1)}, u32[]{:S(2)}, u32[]{:S(2)}) collective-permute-start(f32[48,1408]{1,0:T(8,128)S(1)} %slice_add_fusion.12.refs_7_), channel_id=1, source_target_pairs={{0,4},{4,0},{8,12},{12,8},{16,20},{20,16},{24,28},{28,24},{1,5},{5... | collective-permute-start | bytes 811016 | tf_op jit(solution)/shard_map/ppermute | solution.py:67
  344.1 19.7 %collective-permute-start.75 = (f32[48,2816]{1,0:T(8,128)S(1)}, f32[48,2816]{1,0:T(8,128)S(1)}, u32[]{:S(2)}, u32[]{:S(2)}) collective-permute-start(f32[48,2816]{1,0:T(8,128)S(1)} %pad_maximum_fusion.18), channel_id=1, source_target_pairs={{0,16},{4,20},{8,24},{12,28},{16,0},{20,4},{24,8},{28,12},{1,17},{... | collective-permute-start | bytes 1622024 | tf_op jit(solution)/shard_map/ppermute | solution.py:67
  346.3 18.0 %collective-permute-start.67 = (f32[56,2816]{1,0:T(8,128)S(1)}, f32[56,2816]{1,0:T(8,128)S(1)}, u32[]{:S(2)}, u32[]{:S(2)}) collective-permute-start(f32[56,2816]{1,0:T(8,128)S(1)} %pad_maximum_fusion.7), channel_id=1, source_target_pairs={{0,8},{4,12},{8,0},{12,4},{16,24},{20,28},{24,16},{28,20},{1,9},{5... | collective-permute-start | bytes 1892360 | tf_op jit(solution)/shard_map/ppermute | solution.py:67
  347.0 16.8 %collective-permute-start.58 = (f32[48,1408]{1,0:T(8,128)S(1)}, f32[48,1408]{1,0:T(8,128)S(1)}, u32[]{:S(2)}, u32[]{:S(2)}) collective-permute-start(f32[48,1408]{1,0:T(8,128)S(1)} %slice_add_fusion.13.refs_1_), channel_id=1, source_target_pairs={{0,16},{4,20},{8,24},{12,28},{16,0},{20,4},{24,8},{28,12},{1,17},{... | collective-permute-start | bytes 811016 | tf_op jit(solution)/shard_map/ppermute | solution.py:67
  348.3 19.3 %collective-permute-start.53 = (f32[48,1408]{1,0:T(8,128)S(1)}, f32[48,1408]{1,0:T(8,128)S(1)}, u32[]{:S(2)}, u32[]{:S(2)}) collective-permute-start(f32[48,1408]{1,0:T(8,128)S(1)} %slice_add_fusion.14.refs_7_), channel_id=1, source_target_pairs={{0,8},{4,12},{8,0},{12,4},{16,24},{20,28},{24,16},{28,20},{1,9},{5... | collective-permute-start | bytes 811016 | tf_op jit(solution)/shard_map/ppermute | solution.py:67
  367.6 20.7 %collective-permute-start.59 = (f32[48,2816]{1,0:T(8,128)S(1)}, f32[48,2816]{1,0:T(8,128)S(1)}, u32[]{:S(2)}, u32[]{:S(2)}) collective-permute-start(f32[48,2816]{1,0:T(8,128)S(1)} %pad_maximum_fusion.17), channel_id=1, source_target_pairs={{0,8},{4,12},{8,0},{12,4},{16,24},{20,28},{24,16},{28,20},{1,9},{5... | collective-permute-start | bytes 1622024 | tf_op jit(solution)/shard_map/ppermute | solution.py:67
  369.8 18.4 %collective-permute-start.54 = (f32[48,2816]{1,0:T(8,128)S(1)}, f32[48,2816]{1,0:T(8,128)S(1)}, u32[]{:S(2)}, u32[]{:S(2)}) collective-permute-start(f32[48,2816]{1,0:T(8,128)S(1)} %pad_maximum_fusion.15), channel_id=1, source_target_pairs={{0,16},{4,20},{8,24},{12,28},{16,0},{20,4},{24,8},{28,12},{1,17},{... | collective-permute-start | bytes 1622024 | tf_op jit(solution)/shard_map/ppermute | solution.py:67
  399.4 26.7 %collective-permute-start.80 = (f32[216,384]{1,0:T(8,128)S(1)}, f32[216,384]{1,0:T(8,128)S(1)}, u32[]{:S(2)}, u32[]{:S(2)}) collective-permute-start(f32[216,384]{1,0:T(8,128)S(1)} %add.262), channel_id=1, source_target_pairs={{0,2},{1,3},{2,0},{3,1},{4,6},{5,7},{6,4},{7,5},{8,10},{9,11},{10,... | collective-permute-start | bytes 995336 | tf_op jit(solution)/shard_map/ppermute | solution.py:67
  426.1 20.5 %collective-permute-start.81 = (f32[216,384]{1,0:T(8,128)S(1)}, f32[216,384]{1,0:T(8,128)S(1)}, u32[]{:S(2)}, u32[]{:S(2)}) collective-permute-start(f32[216,384]{1,0:T(8,128)S(1)} %add.263), channel_id=1, source_target_pairs={{0,1},{1,0},{2,3},{3,2},{4,5},{5,4},{6,7},{7,6},{8,9},{9,8},{10,11... | collective-permute-start | bytes 995336 | tf_op jit(solution)/shard_map/ppermute | solution.py:67
  429.3 11.6 %collective-permute-start.92 = (f32[104,384]{1,0:T(8,128)S(1)}, f32[104,384]{1,0:T(8,128)S(1)}, u32[]{:S(2)}, u32[]{:S(2)}) collective-permute-start(f32[104,384]{1,0:T(8,128)S(1)} %add.266), channel_id=1, source_target_pairs={{0,2},{1,3},{2,0},{3,1},{4,6},{5,7},{6,4},{7,5},{8,10},{9,11},{10,... | collective-permute-start | bytes 479240 | tf_op jit(solution)/shard_map/ppermute | solution.py:67
  464.1 14.7 %collective-permute-start.100 = (f32[48,5632]{1,0:T(8,128)}, f32[48,5632]{1,0:T(8,128)}, u32[]{:S(2)}, u32[]{:S(2)}) collective-permute-start(f32[48,5632]{1,0:T(8,128)} %get-tuple-element.145), channel_id=1, source_target_pairs={{0,4},{4,0},{8,12},{12,8},{16,20},{20,16},{24,28},{28,24},{1,5},{5... | collective-permute-start | bytes 3244040 | tf_op jit(solution)/shard_map/ppermute | solution.py:67
  476.3 12.9 %collective-permute-start.121 = (f32[48,5632]{1,0:T(8,128)}, f32[48,5632]{1,0:T(8,128)S(1)}, u32[]{:S(2)}, u32[]{:S(2)}) collective-permute-start(f32[48,5632]{1,0:T(8,128)} %get-tuple-element.150), channel_id=1, source_target_pairs={{0,4},{4,0},{8,12},{12,8},{16,20},{20,16},{24,28},{28,24},{1,5},{5... | collective-permute-start | bytes 3244040 | tf_op jit(solution)/shard_map/ppermute | solution.py:67
  484.7 48.9 %collective-permute-start.101 = (f32[48,2816]{1,0:T(8,128)}, f32[48,2816]{1,0:T(8,128)}, u32[]{:S(2)}, u32[]{:S(2)}) collective-permute-start(f32[48,2816]{1,0:T(8,128)} %pad_maximum_fusion.19), channel_id=1, source_target_pairs={{0,8},{4,12},{8,0},{12,4},{16,24},{20,28},{24,16},{28,20},{1,9},{5... | collective-permute-start | bytes 1622024 | tf_op jit(solution)/shard_map/ppermute | solution.py:67
  488.3 47.4 %collective-permute-start.109 = (f32[48,2816]{1,0:T(8,128)}, f32[48,2816]{1,0:T(8,128)}, u32[]{:S(2)}, u32[]{:S(2)}) collective-permute-start(f32[48,2816]{1,0:T(8,128)} %slice.384), channel_id=1, source_target_pairs={{0,16},{4,20},{8,24},{12,28},{16,0},{20,4},{24,8},{28,12},{1,17},{... | collective-permute-start | bytes 1622024 | tf_op jit(solution)/shard_map/ppermute | solution.py:67
  492.5 45.1 %collective-permute-start.122 = (f32[48,2816]{1,0:T(8,128)}, f32[48,2816]{1,0:T(8,128)}, u32[]{:S(2)}, u32[]{:S(2)}) collective-permute-start(f32[48,2816]{1,0:T(8,128)} %slice.388), channel_id=1, source_target_pairs={{0,16},{4,20},{8,24},{12,28},{16,0},{20,4},{24,8},{28,12},{1,17},{... | collective-permute-start | bytes 1622024 | tf_op jit(solution)/shard_map/ppermute | solution.py:67
  500.4 14.3 %collective-permute-start.99 = (f32[8,128]{1,0:T(8,128)S(1)}, f32[8,128]{1,0:T(8,128)S(1)}, u32[]{:S(2)}, u32[]{:S(2)}) collective-permute-start(f32[8,128]{1,0:T(8,128)S(1)} %fusion.24), channel_id=1, source_target_pairs={{0,16},{4,20},{8,24},{12,28},{16,0},{20,4},{24,8},{28,12},{1,17},{... | collective-permute-start | bytes 12296 | tf_op jit(solution)/shard_map/ppermute | solution.py:67
  502.2 48.2 %collective-permute-start.95 = (f32[56,2816]{1,0:T(8,128)}, f32[56,2816]{1,0:T(8,128)}, u32[]{:S(2)}, u32[]{:S(2)}) collective-permute-start(f32[56,2816]{1,0:T(8,128)} %pad_maximum_fusion.8), channel_id=1, source_target_pairs={{0,8},{4,12},{8,0},{12,4},{16,24},{20,28},{24,16},{28,20},{1,9},{5... | collective-permute-start | bytes 1892360 | tf_op jit(solution)/shard_map/ppermute | solution.py:67
  536.9 15.4 %collective-permute-start.110 = (f32[48,1408]{1,0:T(8,128)S(1)}, f32[48,1408]{1,0:T(8,128)S(1)}, u32[]{:S(2)}, u32[]{:S(2)}) collective-permute-start(f32[48,1408]{1,0:T(8,128)S(1)} %slice.386), channel_id=1, source_target_pairs={{0,8},{4,12},{8,0},{12,4},{16,24},{20,28},{24,16},{28,20},{1,9},{5... | collective-permute-start | bytes 811016 | tf_op jit(solution)/shard_map/ppermute | solution.py:67
  542.7 31.2 %collective-permute-start.105 = (f32[48,1408]{1,0:T(8,128)S(1)}, f32[48,1408]{1,0:T(8,128)S(1)}, u32[]{:S(2)}, u32[]{:S(2)}) collective-permute-start(f32[48,1408]{1,0:T(8,128)S(1)} %slice_add_fusion.11.refs_0_), channel_id=1, source_target_pairs={{0,4},{4,0},{8,12},{12,8},{16,20},{20,16},{24,28},{28,24},{1,5},{5... | collective-permute-start | bytes 811016 | tf_op jit(solution)/shard_map/ppermute | solution.py:67
  542.7 30.2 %collective-permute-start.103 = (f32[48,1408]{1,0:T(8,128)S(1)}, f32[48,1408]{1,0:T(8,128)S(1)}, u32[]{:S(2)}, u32[]{:S(2)}) collective-permute-start(f32[48,1408]{1,0:T(8,128)S(1)} %slice_add_fusion.11.refs_0_), channel_id=1, source_target_pairs={{0,16},{4,20},{8,24},{12,28},{16,0},{20,4},{24,8},{28,12},{1,17},{... | collective-permute-start | bytes 811016 | tf_op jit(solution)/shard_map/ppermute | solution.py:67
  550.3 25.0 %collective-permute-start.126 = (f32[48,1408]{1,0:T(8,128)S(1)}, f32[48,1408]{1,0:T(8,128)S(1)}, u32[]{:S(2)}, u32[]{:S(2)}) collective-permute-start(f32[48,1408]{1,0:T(8,128)S(1)} %slice_add_fusion.9.refs_6_), channel_id=1, source_target_pairs={{0,4},{4,0},{8,12},{12,8},{16,20},{20,16},{24,28},{28,24},{1,5},{5... | collective-permute-start | bytes 811016 | tf_op jit(solution)/shard_map/ppermute | solution.py:67
  550.4 12.9 %collective-permute-start.124 = (f32[48,1408]{1,0:T(8,128)S(1)}, f32[48,1408]{1,0:T(8,128)S(1)}, u32[]{:S(2)}, u32[]{:S(2)}) collective-permute-start(f32[48,1408]{1,0:T(8,128)S(1)} %slice_add_fusion.9.refs_6_), channel_id=1, source_target_pairs={{0,8},{4,12},{8,0},{12,4},{16,24},{20,28},{24,16},{28,20},{1,9},{5... | collective-permute-start | bytes 811016 | tf_op jit(solution)/shard_map/ppermute | solution.py:67
  561.9 11.8 %collective-permute-start.111 = (f32[48,1408]{1,0:T(8,128)S(1)}, f32[48,1408]{1,0:T(8,128)S(1)}, u32[]{:S(2)}, u32[]{:S(2)}) collective-permute-start(f32[48,1408]{1,0:T(8,128)S(1)} %slice_add_fusion.10.refs_6_), channel_id=1, source_target_pairs={{0,8},{4,12},{8,0},{12,4},{16,24},{20,28},{24,16},{28,20},{1,9},{5... | collective-permute-start | bytes 811016 | tf_op jit(solution)/shard_map/ppermute | solution.py:67
  571.8 18.4 %collective-permute-start.125 = (f32[48,2816]{1,0:T(8,128)S(1)}, f32[48,2816]{1,0:T(8,128)S(1)}, u32[]{:S(2)}, u32[]{:S(2)}) collective-permute-start(f32[48,2816]{1,0:T(8,128)S(1)} %pad_maximum_fusion.22), channel_id=1, source_target_pairs={{0,16},{4,20},{8,24},{12,28},{16,0},{20,4},{24,8},{28,12},{1,17},{... | collective-permute-start | bytes 1622024 | tf_op jit(solution)/shard_map/ppermute | solution.py:67
  573.0 17.2 %collective-permute-start.117 = (f32[56,2816]{1,0:T(8,128)S(1)}, f32[56,2816]{1,0:T(8,128)S(1)}, u32[]{:S(2)}, u32[]{:S(2)}) collective-permute-start(f32[56,2816]{1,0:T(8,128)S(1)} %pad_maximum_fusion.9), channel_id=1, source_target_pairs={{0,8},{4,12},{8,0},{12,4},{16,24},{20,28},{24,16},{28,20},{1,9},{5... | collective-permute-start | bytes 1892360 | tf_op jit(solution)/shard_map/ppermute | solution.py:67
  573.8 24.8 %collective-permute-start.104 = (f32[48,2816]{1,0:T(8,128)S(1)}, f32[48,2816]{1,0:T(8,128)S(1)}, u32[]{:S(2)}, u32[]{:S(2)}) collective-permute-start(f32[48,2816]{1,0:T(8,128)S(1)} %pad_maximum_fusion.20), channel_id=1, source_target_pairs={{0,8},{4,12},{8,0},{12,4},{16,24},{20,28},{24,16},{28,20},{1,9},{5... | collective-permute-start | bytes 1622024 | tf_op jit(solution)/shard_map/ppermute | solution.py:67
  575.3 23.3 %collective-permute-start.112 = (f32[48,2816]{1,0:T(8,128)S(1)}, f32[48,2816]{1,0:T(8,128)S(1)}, u32[]{:S(2)}, u32[]{:S(2)}) collective-permute-start(f32[48,2816]{1,0:T(8,128)S(1)} %pad_maximum_fusion.21), channel_id=1, source_target_pairs={{0,16},{4,20},{8,24},{12,28},{16,0},{20,4},{24,8},{28,12},{1,17},{... | collective-permute-start | bytes 1622024 | tf_op jit(solution)/shard_map/ppermute | solution.py:67
  576.2 14.5 %collective-permute-start.118 = (f32[56,1408]{1,0:T(8,128)S(1)}, f32[56,1408]{1,0:T(8,128)S(1)}, u32[]{:S(2)}, u32[]{:S(2)}) collective-permute-start(f32[56,1408]{1,0:T(8,128)S(1)} %slice_add_fusion.6.refs_0_), channel_id=1, source_target_pairs={{0,4},{4,0},{8,12},{12,8},{16,20},{20,16},{24,28},{28,24},{1,5},{5... | collective-permute-start | bytes 946184 | tf_op jit(solution)/shard_map/ppermute | solution.py:67
  (124 other events, 859.2 us)
where the time goes:
time: 623 us; the launch traced here: 614 us
  waiting for transfers between devices  258 us (41%)
  Pallas kernels  173 us (28%)
  starting transfers between devices  98.1 us (16%)
  other arithmetic  53.4 us (9%)
  local copies, waits for them, and re-layouts  21.4 us (3%)
  between operations  8.74 us (1%)
    ppermute x129, waiting for transfers between devices, swap(): return lax.ppermute(x, axis, [(i, i ^ stride) for i in range(size)])  258 us
    ppermute x129, starting transfers between devices, swap(): return lax.ppermute(x, axis, [(i, i ^ stride) for i in range(size)])  98.1 us
    pallas_call x6, Pallas kernels, back(): pl.pallas_call(functools.partial(back_body, plan, pair), out_shape=outs,...  70 us
    pallas_call x4, Pallas kernels, forth(): pl.pallas_call(functools.partial(forth_body, plan, pair, step is not None...  60.8 us
    pallas_call x3, Pallas kernels, first(): pl.pallas_call(functools.partial(first_body, plan), out_shape=[jax.ShapeD...  31.7 us
    sub x1, other arithmetic, second_step(): base = residual - step1 * damping * (residual + ratio * direction)  17 us
  transfers between devices with their start and end apart: 129, of which 51 were waited for; matrix products, arithmetic and copies ran while one was open for 10% of the time, Pallas kernels for 20%

commit v1 on v0

v1 whole, which is shorter than its diff:
```python
import functools

import jax
import jax.numpy as jnp
from jax import lax
from jax.experimental import pallas as pl
from jax.experimental.pallas import tpu as pltpu
from jax.sharding import PartitionSpec as P

damping = 0.01
F32, BF16 = jnp.float32, jnp.bfloat16
LANES, ROWS8, UNIT = 128, 8, 16
NT = (((1,), (1,)), ((), ()))
NN = (((1,), (0,)), ((), ()))
VMEM_LIMIT = 52 * 1024 * 1024


def parts_of(x):
    high = x.astype(BF16)
    return high, (x - high.astype(F32)).astype(BF16)


def dot3(x, high, low, dims):
    x_high, x_low = parts_of(x)
    dot = functools.partial(lax.dot_general, dimension_numbers=dims, preferred_element_type=F32)
    return dot(x_high, high) + (dot(x_low, high) + dot(x_high, low))


def params():
    return pltpu.CompilerParams(vmem_limit_bytes=VMEM_LIMIT)


class Plan:
    def __init__(self, rows, feats, classes, n_clip, n_feat):
        self.rows, self.feats, self.classes = rows, feats, classes
        self.n_clip, self.n_feat = n_clip, n_feat
        units = classes // UNIT
        sizes = [UNIT * (units // 4 + (k < units % 4)) for k in range(4)]
        starts = [sum(sizes[:k]) for k in range(4)]
        self.chunks = list(zip(starts, sizes))
        self.pairs = [(0,), (1, 2), (3,)]
        self.turns = [(0, 0), (1, 1), (0, 0), (0, 1)]
        strides = [1 << k for k in range(1, n_clip.bit_length() - 1)]
        self.levels, block = [], feats
        while strides and block % (2 * LANES) == 0:
            self.levels.append(strides.pop(0))
            block //= 2
        self.doubled = strides
        self.block, self.nb = block, feats // block
        self.rows_step = next(n for n in (384, 256, 128, rows) if rows % n == 0)

    def pair_range(self, pair):
        first, last = self.pairs[pair][0], self.pairs[pair][-1]
        start = self.chunks[first][0]
        return start, self.chunks[last][0] + self.chunks[last][1] - start


def swap(x, axis, stride):
    size = lax.axis_size(axis)
    return lax.ppermute(x, axis, [(i, i ^ stride) for i in range(size)])


def first_body(plan, s_ref, f_ref, w_ref, *rest):
    high_ref, low_ref, send_ref, keep_ref, acc = rest[-5:]
    p = pl.program_id(0)
    high, low = parts_of(f_ref[...])
    high_ref[...] = high
    low_ref[...] = low
    part = dot3(w_ref[...], high, low, NT)

    @pl.when(p == 0)
    def _():
        acc[...] = part

    @pl.when(p > 0)
    def _():
        acc[...] += part

    @pl.when(p == plan.nb - 1)
    def _():
        half = plan.classes // 2
        bit = s_ref[2]
        send_ref[...] = acc[pl.ds(pl.multiple_of((1 - bit) * half, ROWS8), half), :]
        keep_ref[...] = acc[pl.ds(pl.multiple_of(bit * half, ROWS8), half), :]


def first(plan, where, features, weights, part, split):
    rows, block, step = plan.rows, plan.block, plan.rows_step
    half = plan.classes // 2
    operands = [features, weights]
    in_specs = [
        pl.BlockSpec((step, block), lambda p, s: (part, p ^ s[0])),
        pl.BlockSpec((plan.classes, block), lambda p, s: (0, p ^ s[0])),
    ]
    aliases = {}
    if split is not None:
        aliases = {3: 0, 4: 1}
        operands += list(split)
        in_specs += [pl.BlockSpec(memory_space=pl.ANY)] * 2
    high, low, send, keep = pl.pallas_call(
        functools.partial(first_body, plan),
        out_shape=[jax.ShapeDtypeStruct((rows, plan.feats), BF16)] * 2
        + [jax.ShapeDtypeStruct((half, step), F32)] * 2,
        grid_spec=pltpu.PrefetchScalarGridSpec(
            num_scalar_prefetch=1,
            grid=(plan.nb,),
            in_specs=in_specs,
            out_specs=[pl.BlockSpec((step, block), lambda p, s: (part, p))] * 2
            + [pl.BlockSpec((half, step), lambda p, s: (0, 0))] * 2,
            scratch_shapes=[pltpu.VMEM((plan.classes, step), F32)],
        ),
        input_output_aliases=aliases,
        compiler_params=params(),
        cost_estimate=pl.CostEstimate(
            flops=6 * plan.classes * step * plan.feats,
            bytes_accessed=4 * plan.feats * (2 * step + plan.classes),
            transcendentals=0,
        ),
        name="split_and_logits",
    )(where, *operands)
    return (high, low), (send, keep)


def back_body(plan, pair, s_ref, g_ref, high_ref, low_ref, *outs):
    core = s_ref[1]
    base = plan.pair_range(pair)[0]
    some, ends = [], []
    for c in plan.pairs[pair]:
        a, n = plan.chunks[c]
        h = n // 2
        for side in (core, 1 - core):
            some.append(g_ref[pl.ds(pl.multiple_of(a - base + side * h, ROWS8), h), :])
            ends.append((ends[-1] if ends else 0) + h)
    x = jnp.concatenate(some, axis=0)
    width = 2 * LANES
    for k in range(0, plan.block, width):
        w = min(width, plan.block - k)
        part = dot3(x, high_ref[:, k : k + w], low_ref[:, k : k + w], NN)
        for out, start, end in zip(outs, [0] + ends, ends):
            out[:, k : k + w] = part[start:end]


def back(plan, where, pair, values, high, low):
    rows, block, feats = plan.rows, plan.block, plan.feats
    n_pair = plan.pair_range(pair)[1]
    outs, specs = [], []
    for c in plan.pairs[pair]:
        h = plan.chunks[c][1] // 2
        outs += [jax.ShapeDtypeStruct((h, feats), F32)] * 2
        specs += [pl.BlockSpec((h, block), lambda p, s: (0, p))] * 2
    result = pl.pallas_call(
        functools.partial(back_body, plan, pair),
        out_shape=outs,
        grid_spec=pltpu.PrefetchScalarGridSpec(
            num_scalar_prefetch=1,
            grid=(plan.nb,),
            in_specs=[
                pl.BlockSpec((n_pair, rows), lambda p, s: (0, 0)),
                pl.BlockSpec((rows, block), lambda p, s: (0, p)),
                pl.BlockSpec((rows, block), lambda p, s: (0, p)),
            ],
            out_specs=specs,
        ),
        compiler_params=params(),
        cost_estimate=pl.CostEstimate(
            flops=6 * n_pair * rows * feats, bytes_accessed=4 * feats * (rows + n_pair), transcendentals=0
        ),
        name="back_pair",
    )(where, values, high, low)
    return [tuple(result[2 * k : 2 * k + 2]) for k in range(len(plan.pairs[pair]))]


class Pieces:
    def __init__(self, places, mine, theirs):
        self.places = (places, [tuple(p for place in places for p in place)])
        self.mine, self.theirs = mine, theirs

    def flat(self):
        return list(self.mine) + [self.theirs]


def gather_rows(plan, pair, chunks, s_ref, refs, position, target):
    core = s_ref[1]
    base = plan.pair_range(pair)[0]
    refs = list(refs)
    for c, places in zip(plan.pairs[pair], chunks):
        a, n = plan.chunks[c]
        h = n // 2
        for side, some in zip((core, 1 - core), places):
            for place in some:
                ref = refs.pop(0)
                if position in place:
                    k = place.index(position) * plan.block
                    target[pl.ds(pl.multiple_of(a - base + side * h, ROWS8), h), :] = ref[:, k : k + plan.block]


def forth_body(plan, pair, step, chunks, s_ref, *refs):
    nb = plan.nb
    refs = list(refs)
    scalar_ref = refs.pop(0) if step else None
    n_pieces = sum(len(some) for places in chunks for some in places)
    pieces, refs = refs[:n_pieces], refs[n_pieces:]
    direction_ref = refs.pop(0) if step else None
    high_ref, low_ref = refs[:2]
    n_ranges = len(tangent_ranges(plan, pair))
    target, acc, sums = refs[-3:]
    vector_ref, outs = refs[-4 - 2 * n_ranges], refs[-3 - 2 * n_ranges : -3]
    n_pair = plan.pair_range(pair)[1]
    p = pl.program_id(0)
    for position in range(nb):

        @pl.when(p == position)
        def _():
            gather_rows(plan, pair, chunks, s_ref, pieces, position, target)

    if step:
        direction = direction_ref[...]
        vector = direction - scalar_ref[0] * (target[...] + damping * direction)
    else:
        vector = -target[...]
    vector_ref[...] = vector
    part = dot3(vector, high_ref[...], low_ref[...], NT)
    square = jnp.sum(vector * vector).reshape(1, 1)
    cross = jnp.sum(vector * direction).reshape(1, 1) if step else square
    ids = lax.broadcasted_iota(jnp.int32, (ROWS8, plan.rows), 0)
    new = jnp.where(ids == 0, square, jnp.where(ids == 1, cross, 0.0))

    @pl.when(p == 0)
    def _():
        acc[:n_pair, :] = part
        sums[...] = new

    @pl.when(p > 0)
    def _():
        acc[:n_pair, :] += part
        sums[...] += new

    @pl.when(p == nb - 1)
    def _():
        acc[n_pair:, :] = sums[...]
        half = plan.rows // 2
        bit = s_ref[2]
        keep = pl.multiple_of(bit * half, LANES)
        send = pl.multiple_of((1 - bit) * half, LANES)
        for k, (a, n) in enumerate(tangent_ranges(plan, pair)):
            outs[2 * k][...] = acc[a : a + n, pl.ds(send, half)]
            outs[2 * k + 1][...] = acc[a : a + n, pl.ds(keep, half)]


def tangent_ranges(plan, pair):
    return [(0, plan.pair_range(pair)[1] + ROWS8)]


def placed(plan, pair):
    base, n_pair = plan.pair_range(pair)
    return pl.BlockSpec(
        (pl.Element(n_pair), pl.Element(plan.block)), lambda p, s: (base, (p ^ s[0]) * plan.block)
    )


def forth(plan, where, pair, pieces, high, low, vectors, step=None, direction=None):
    rows, block, feats, nb = plan.rows, plan.block, plan.feats, plan.nb
    half = rows // 2
    n_pair = plan.pair_range(pair)[1]
    operands, in_specs = [], []
    if step is not None:
        operands.append(step.reshape(1))
        in_specs.append(pl.BlockSpec(memory_space=pltpu.SMEM))
    for piece in pieces:
        for x in piece.flat():
            operands.append(x)
            in_specs.append(pl.BlockSpec(x.shape, lambda p, s: (0, 0)))
    if step is not None:
        operands.append(direction)
        in_specs.append(placed(plan, pair))
    operands += [high, low]
    in_specs += [pl.BlockSpec((rows, block), lambda p, s: (0, p))] * 2
    aliases = {}
    if vectors is not None:
        aliases = {len(operands) + 1: 0}
        operands.append(vectors)
        in_specs.append(pl.BlockSpec(memory_space=pl.ANY))
    outs, specs = [jax.ShapeDtypeStruct((plan.classes, feats), F32)], [placed(plan, pair)]
    for _, n in tangent_ranges(plan, pair):
        outs += [jax.ShapeDtypeStruct((n, half), F32)] * 2
        specs += [pl.BlockSpec((n, half), lambda p, s: (0, 0))] * 2
    result = pl.pallas_call(
        functools.partial(forth_body, plan, pair, step is not None, [piece.places for piece in pieces]),
        out_shape=outs,
        grid_spec=pltpu.PrefetchScalarGridSpec(
            num_scalar_prefetch=1,
            grid=(nb,),
            in_specs=in_specs,
            out_specs=specs,
            scratch_shapes=[
                pltpu.VMEM((n_pair, block), F32),
                pltpu.VMEM((n_pair + ROWS8, rows), F32),
                pltpu.VMEM((ROWS8, rows), F32),
            ],
        ),
        input_output_aliases=aliases,
        compiler_params=params(),
        cost_estimate=pl.CostEstimate(
            flops=6 * n_pair * rows * feats, bytes_accessed=4 * feats * (rows + 3 * n_pair), transcendentals=0
        ),
        name="forth_pair",
    )(where, *operands)
    return result[0], [tuple(result[1 + 2 * k : 3 + 2 * k]) for k in range(len(tangent_ranges(plan, pair)))]


def last_body(plan, pair, chunks, s_ref, scalar_ref, *refs):
    nb = plan.nb
    refs = list(refs)
    n_pieces = sum(len(some) for places in chunks for some in places)
    pieces = refs[:n_pieces]
    direction_ref, residual_ref = refs[n_pieces : n_pieces + 2]
    out_ref, target, along, ready, arrived, left = refs[-6:]
    base, n_pair = plan.pair_range(pair)

    def place(ref, position):
        column = pl.multiple_of((position ^ s_ref[0]) * plan.block, LANES)
        return ref.at[pl.ds(base, n_pair), pl.ds(column, plan.block)]

    reads = []
    for q in range(nb):
        reads.append(pltpu.make_async_copy(place(direction_ref, q), along.at[q], arrived.at[0, q]))
        reads.append(pltpu.make_async_copy(place(residual_ref, q), ready.at[q], arrived.at[1, q]))
    writes = [pltpu.make_async_copy(ready.at[q], place(out_ref, q), left.at[q]) for q in range(nb)]
    for read in reads:
        read.start()
    for q in range(nb):
        gather_rows(plan, pair, chunks, s_ref, pieces, q, target)
        reads[2 * q].wait()
        reads[2 * q + 1].wait()
        residual = ready[q]
        following = residual + scalar_ref[1] * along[q]
        ready[q] = residual - scalar_ref[0] * (target[...] + damping * following)
        writes[q].start()
    for write in writes:
        write.wait()


def last(plan, where, pair, scalars, pieces, direction, residual, out):
    block, nb = plan.block, plan.nb
    n_pair = plan.pair_range(pair)[1]
    operands, in_specs = [where, scalars], [pl.BlockSpec(memory_space=pltpu.SMEM)] * 2
    for piece in pieces:
        for x in piece.flat():
            operands.append(x)
            in_specs.append(pl.BlockSpec(memory_space=pltpu.VMEM))
    operands += [direction, residual]
    aliases = {}
    if out is not None:
        aliases = {len(operands): 0}
        operands.append(out)
    in_specs += [pl.BlockSpec(memory_space=pl.ANY)] * (len(operands) - len(in_specs))
    return pl.pallas_call(
        functools.partial(last_body, plan, pair, [piece.places for piece in pieces]),
        out_shape=jax.ShapeDtypeStruct((plan.classes, plan.feats), F32),
        in_specs=in_specs,
        out_specs=pl.BlockSpec(memory_space=pl.ANY),
        scratch_shapes=[
            pltpu.VMEM((n_pair, block), F32),
            pltpu.VMEM((nb, n_pair, block), F32),
            pltpu.VMEM((nb, n_pair, block), F32),
            pltpu.SemaphoreType.DMA((2, nb)),
            pltpu.SemaphoreType.DMA((nb,)),
        ],
        input_output_aliases=aliases,
        compiler_params=params(),
        cost_estimate=pl.CostEstimate(
            flops=6 * n_pair * plan.feats, bytes_accessed=16 * n_pair * plan.feats, transcendentals=0
        ),
        name="last_rows",
    )(*operands)


class Order:
    def __init__(self):
        self.token = None

    def after(self, x):
        if self.token is None:
            return x
        return lax.optimization_barrier((x, self.token))[0]

    def note(self, x):
        self.token = x


def columns(plan, x, positions):
    if list(positions) == list(range(positions[0], positions[-1] + 1)):
        return x[:, positions[0] * plan.block : (positions[-1] + 1) * plan.block]
    return jnp.concatenate([x[:, p * plan.block : (p + 1) * plan.block] for p in positions], axis=1)


class ClipSum:
    def __init__(self, plan, sides, turns):
        self.plan = plan
        self.own, other = sides
        levels = [(stride, 1 << k) for k, stride in enumerate(plan.levels)]
        down, up = (levels[::-1] if turn else levels for turn in turns)
        self.active = list(range(plan.nb))
        self.places, self.mine = [], []
        self.steps = [("core", 1, 0)]
        self.steps += [("scatter", stride, bit) for stride, bit in down]
        self.steps += [("double", stride, 0) for stride in plan.doubled]
        self.steps += [("gather", stride, bit) for stride, bit in up]
        self.kept = self.own
        self.pending = swap(other, "clip", 1)

    def done(self):
        return not self.steps

    def advance(self, order):
        kind, _, bit = self.steps.pop(0)
        got = order.after(self.pending)
        if kind == "gather":
            self.mine.append(got)
            self.places.append(tuple(p | bit for place in self.places for p in place))
        else:
            self.own = self.kept + got
            if not self.steps or self.steps[0][0] == "gather":
                self.places, self.mine = [tuple(self.active)], [self.own]
        kind, stride, bit = self.steps[0] if self.steps else ("core", 1, 0)
        if kind == "scatter":
            rest = [p for p in self.active if not p & bit]
            sent = columns(self.plan, self.own, [self.active.index(p | bit) for p in rest])
            self.kept = columns(self.plan, self.own, [self.active.index(p) for p in rest])
            self.active = rest
        elif kind == "double":
            sent = self.kept = self.own
        else:
            sent = self.mine[0] if len(self.mine) == 1 else jnp.concatenate(self.mine, axis=1)
        order.note(sent)
        self.pending = swap(sent, "clip", stride)

    def pieces(self, order):
        while not self.done():
            self.advance(order)
        return Pieces(self.places, self.mine, order.after(self.pending))


class FeatSum:
    def __init__(self, plan, halves, bit, axis):
        send, self.kept = halves
        self.bit, self.axis = bit, axis
        strides = [1 << k for k in range(plan.n_feat.bit_length() - 1)]
        self.strides = strides + [1]
        self.pending = swap(send, "feat", 1)

    def advance(self, order):
        self.strides.pop(0)
        got = order.after(self.pending)
        if self.strides:
            self.kept = self.kept + got
            self.pending = swap(self.kept, "feat", self.strides[0])
            order.note(self.kept)
        else:
            self.got = got
            order.note(got)

    def result(self, order):
        while self.strides:
            self.advance(order)
        one, two = [self.got, self.kept], [self.kept, self.got]
        return jnp.where(self.bit, jnp.concatenate(one, self.axis), jnp.concatenate(two, self.axis))


class ScalarSum:
    def __init__(self, plan, value):
        self.strides = [1 << k for k in range(plan.n_clip.bit_length() - 1)]
        self.row = jnp.broadcast_to(value, (ROWS8, LANES))
        self.pending = swap(self.row, "clip", 1)

    def advance(self, order):
        if not self.strides:
            return
        self.strides.pop(0)
        self.row = self.row + order.after(self.pending)
        order.note(self.row)
        if self.strides:
            self.pending = swap(self.row, "clip", self.strides[0])

    def result(self, order):
        while self.strides:
            self.advance(order)
        return self.row[0, 0]


def local(features, weights, labels):
    rows, feats = features.shape
    classes = weights.shape[0]
    plan = Plan(rows, feats, classes, lax.axis_size("clip"), lax.axis_size("feat"))
    total_rows = rows * plan.n_clip
    me, bit = lax.axis_index("clip"), lax.axis_index("feat") & 1
    mask = sum(((me // stride) & 1) << k for k, stride in enumerate(plan.levels))
    where = jnp.stack([jnp.asarray(mask), me & 1, bit]).astype(jnp.int32)
    order = Order()
    groups = range(len(plan.pairs))

    split, parts = None, []
    for part in range(rows // plan.rows_step):
        split, halves = first(plan, where, features, weights, part, split)
        parts.append(FeatSum(plan, halves, bit, 0))
    high, low = split
    probs, values = [], []
    for part, summed in enumerate(parts):
        logits = summed.result(Order())
        top = jnp.max(logits, axis=0, keepdims=True)
        powers = jnp.exp(logits - top)
        some = powers / jnp.sum(powers, axis=0, keepdims=True)
        mine = labels[part * plan.rows_step : (part + 1) * plan.rows_step]
        onehot = (mine[None, :] == jnp.arange(classes, dtype=jnp.int32)[:, None]).astype(F32)
        probs.append(some)
        values.append((some - onehot) / total_rows)
    probs, values = jnp.concatenate(probs, axis=1), jnp.concatenate(values, axis=1)

    def backward(values, scalar, during):
        sums = [None] * len(plan.chunks)

        def multiply(group):
            a, n = plan.pair_range(group)
            sides = back(plan, where, group, order.after(values[a : a + n]), high, low)
            for c, side in zip(plan.pairs[group], sides):
                sums[c] = ClipSum(plan, side, plan.turns[c])
            order.note(sides[-1][0])

        def go(*chunks):
            for c in chunks:
                if not sums[c].done():
                    sums[c].advance(order)

        multiply(0)
        if scalar is not None:
            scalar.advance(order)
        go(0)
        multiply(1)
        if scalar is not None:
            scalar.advance(order)
        go(0, 1, 2)
        multiply(2)
        if scalar is not None:
            scalar.advance(order)
        go(0, 2, 1, 3)
        result = during(scalar.result(order)) if scalar is not None else None
        go(0, 2, 1, 3, 2, 1, 0, 3)
        return sums, go, result

    def forward(sums, go, step=None, direction=None):
        vectors, found = None, []

        def multiply(group):
            pieces = [sums[c].pieces(order) for c in plan.pairs[group]]
            out, halves = forth(plan, where, group, pieces, high, low, vectors, step, direction)
            order.note(halves[0][0])
            found.append(FeatSum(plan, halves[0], bit, 1))
            return out

        vectors = multiply(0)
        go(3, 2, 1)
        vectors = multiply(1)
        found[0].advance(order)
        go(3)
        vectors = multiply(2)
        found[0].advance(order)
        found[1].advance(order)
        found[2].advance(order)
        found[1].advance(order)
        found[2].advance(order)
        tangents = [f.result(order) for f in found]
        inner = sum(t[-ROWS8 : 2 - ROWS8, 0] for t in tangents)
        return vectors, jnp.concatenate([t[:-ROWS8] for t in tangents], axis=0), inner

    def bend(tangent):
        weighted = probs * tangent
        bent = (weighted - probs * jnp.sum(weighted, axis=0, keepdims=True)) / total_rows
        order.note(bent)
        return bent, ScalarSum(plan, jnp.sum(bent * tangent))

    sums, go, _ = backward(values, None, None)
    direction, tangent, inner = forward(sums, go)
    norm0 = inner[0]
    bent, curvature = bend(tangent)

    sums, go, step0 = backward(bent, curvature, lambda total: norm0 / (total + damping * norm0))
    residual, fresh, inner = forward(sums, go, step0, direction)
    norm1, cross = inner[0], inner[1]
    ratio = norm1 / norm0
    bent, curvature = bend(fresh + ratio * tangent)
    length = norm1 + 2.0 * ratio * cross + ratio * ratio * norm0

    sums, go, step1 = backward(bent, curvature, lambda total: norm1 / (total + damping * length))
    moved = order.after(weights) + (step0 + step1 * ratio) * direction + step1 * residual
    order.note(moved)
    go(3, 2, 1)
    scalars, out = jnp.stack([step1, ratio]), None
    for group, members in enumerate(plan.pairs):
        pieces = [sums[c].pieces(order) for c in members]
        if group == 1:
            go(3)
        out = last(plan, where, group, scalars, pieces, direction, residual, out)
        order.note(out)
    return moved, out


def solution(mesh):
    in_specs = (P("clip", "feat"), P(None, "feat"), P("clip"))
    out_specs = (P(None, "feat"), P(None, "feat"))
    return jax.shard_map(local, mesh=mesh, in_specs=in_specs, out_specs=out_specs, check_vma=False)
```

time: 623 us -> 589 us (0.945)
  waiting for transfers between devices: 258 us -> 185 us
  Pallas kernels: 173 us -> 222 us
  other arithmetic: 53.4 us -> 37.6 us
  starting transfers between devices: 98.1 us -> 105 us
    ppermute x129 -> x102, waiting for transfers between devices: 258 us -> 185 us  [swap(): return lax.ppermute(x, axis, [(i, i ^ stride) for i in range(size)])]
    pallas_call x6 -> x9, Pallas kernels: 70 us -> 93.4 us  [back(): pl.pallas_call(functools.partial(back_body, plan, pair), out_shape=outs,...]
    pallas_call x4 -> x6, Pallas kernels: 60.8 us -> 83.4 us  [forth(): pl.pallas_call(functools.partial(forth_body, plan, pair, step is not None...]
    sub x1 -> x0, other arithmetic: 17 us -> none  [second_step(): base = residual - step1 * damping * (residual + ratio * direction)]
    ppermute x129 -> x102, starting transfers between devices: 98.1 us -> 105 us  [swap(): return lax.ppermute(x, axis, [(i, i ^ stride) for i in range(size)])]
    pallas_call x2 -> x3, Pallas kernels: 10.8 us -> 16.9 us  [last(): pl.pallas_call(functools.partial(last_body, plan, pair, [piece.places for...]
    pallas_call x3 -> x2, Pallas kernels: 31.7 us -> 27.9 us  [first(): pl.pallas_call(functools.partial(first_body, plan), out_shape=[jax.ShapeD...]
    add x62 -> x61, other arithmetic: 27 us -> 27.6 us  [the longest x1 13.7 us: local(): order.after(weights) + (step0 + step1 * ratio) * direction]
  transfers between devices with their start and end apart: 129 -> 102, of which waited for: 51 -> 46; matrix products, arithmetic and copies ran while one was open for 10% -> 7% of each run, Pallas kernels for 20% -> 30%
where the time goes in v1:
time: 589 us; the launch traced here: 580 us
  Pallas kernels  222 us (38%)
  waiting for transfers between devices  185 us (31%)
  starting transfers between devices  105 us (18%)
  other arithmetic  37.6 us (6%)
  local copies, waits for them, and re-layouts  21.8 us (4%)
  between operations  8.15 us (1%)
    ppermute x102, waiting for transfers between devices, swap(): return lax.ppermute(x, axis, [(i, i ^ stride) for i in range(size)])  185 us
    ppermute x102, starting transfers between devices, swap(): return lax.ppermute(x, axis, [(i, i ^ stride) for i in range(size)])  105 us
    pallas_call x9, Pallas kernels, back(): pl.pallas_call(functools.partial(back_body, plan, pair), out_shape=outs,...  93.4 us
    pallas_call x6, Pallas kernels, forth(): pl.pallas_call(functools.partial(forth_body, plan, pair, step is not None...  83.4 us
    pallas_call x2, Pallas kernels, first(): pl.pallas_call(functools.partial(first_body, plan), out_shape=[jax.ShapeD...  27.9 us
    pallas_call x3, Pallas kernels, last(): pl.pallas_call(functools.partial(last_body, plan, pair, [piece.places for...  16.9 us
    add x1, other arithmetic, local(): order.after(weights) + (step0 + step1 * ratio) * direction  13.7 us
    unnamed x56, local copies, waits for them, and re-layouts  12.4 us
  transfers between devices with their start and end apart: 102, of which 46 were waited for; matrix products, arithmetic and copies ran while one was open for 7% of the time, Pallas kernels for 30%

profile of v1, /device:TPU:0, one launch (start us, length us, event | category | flops | bytes accessed | tf_op | source)
XLA Modules:
  0.0 579.7 jit_solution(17137435562032957262)
XLA Ops:
  0.7 14.0 %split_and_logits.2 = (bf16[768,5632]{1,0:T(8,128)(2,1)}, bf16[768,5632]{1,0:T(8,128)(2,1)}, f32[200,384]{1,0:T(8,128)S(1)}, f32[200,384]{1,0:T(8,128)S(1)}) custom-call(s32[3]{0:T(128)S(1)} %pad_add_fusion.s_ref, f32[768,5632]{1,0:T(8,128)} %f_ref.3, f32[400,5632]{1,0:T(8,128)} %w_ref.3), custom_call_target="tpu_custom_call" | custom-call | flops 5190451200 | bytes 26312704 | tf_op jit(solution)/shard_map/split_and_logits/pallas_call | solution.py:100
  14.7 3.0 collective-permute-start
  17.7 14.0 %split_and_logits.3 = (bf16[768,5632]{1,0:T(8,128)(2,1)}, bf16[768,5632]{1,0:T(8,128)(2,1)}, f32[200,384]{1,0:T(8,128)S(1)}, f32[200,384]{1,0:T(8,128)S(1)}) custom-call(s32[3]{0:T(128)S(1)} %pad_add_fusion.s_ref, f32[768,5632]{1,0:T(8,128)} %f_ref.3, f32[400,5632]{1,0:T(8,128)} %w_ref.3, ...), custom_call_target="tpu_custom_call", output_to_operand_aliasing={{0}: (3, {}), {1}: (4, {})} | custom-call | flops 5190451200 | bytes 26312704 | tf_op jit(solution)/shard_map/split_and_logits/pallas_call | solution.py:100
  31.8 3.1 collective-permute-start.1
  34.8 12.2 %collective-permute-done.3 = f32[200,384]{1,0:T(8,128)S(1)} collective-permute-done((f32[200,384]{1,0:T(8,128)S(1)}, f32[200,384]{1,0:T(8,128)S(1)}, u32[]{:S(2)}, u32[]{:S(2)}) %collective-permute-start.3) | collective-permute-done | bytes 307232 | tf_op jit(solution)/shard_map/ppermute | solution.py:60
  47.2 10.2 %collective-permute-start.2 = (f32[200,384]{1,0:T(8,128)S(1)}, f32[200,384]{1,0:T(8,128)S(1)}, u32[]{:S(2)}, u32[]{:S(2)}) collective-permute-start(f32[200,384]{1,0:T(8,128)S(1)} %add.221), channel_id=1, source_target_pairs={{0,1},{1,0},{2,3},{3,2},{4,5},{5,4},{6,7},{7,6},{8,9},{9,8},{10,11... | collective-permute-start | bytes 921608 | tf_op jit(solution)/shard_map/ppermute | solution.py:60
  57.4 4.9 collective-permute-done.4
  62.4 3.5 collective-permute-done.2
  66.2 5.9 %collective-permute-done.5 = f32[200,384]{1,0:T(8,128)S(1)} collective-permute-done((f32[200,384]{1,0:T(8,128)S(1)}, f32[200,384]{1,0:T(8,128)S(1)}, u32[]{:S(2)}, u32[]{:S(2)}) %collective-permute-start.5) | collective-permute-done | bytes 307232 | tf_op jit(solution)/shard_map/ppermute | solution.py:60
  72.7 9.9 %back_pair.9 = (f32[56,5632]{1,0:T(8,128)S(1)}, f32[56,5632]{1,0:T(8,128)}) custom-call(s32[3]{0:T(128)S(1)} %pad_add_fusion.s_ref, f32[112,768]{1,0:T(8,128)S(1)} %pad_maximum_fusion.36.g_ref, bf16[768,5632]{1,0:T(8,128)(2,1)} %get-tuple-element.171.high_ref.refs_4_.refs_8_.refs_6_.refs_10_, ...), custom_call_target="tpu_custom_call" | custom-call | flops 2906652672 | bytes 19824640 | tf_op jit(solution)/shard_map/back_pair/pallas_call | solution.py:151
  82.7 3.1 collective-permute-done.6
  87.7 11.3 %back_pair.10 = (f32[48,5632]{1,0:T(8,128)S(1)}, f32[48,5632]{1,0:T(8,128)}, f32[48,5632]{1,0:T(8,128)}, f32[48,5632]{1,0:T(8,128)}) custom-call(s32[3]{0:T(128)S(1)} %pad_add_fusion.s_ref, f32[192,768]{1,0:T(8,128)S(1)} %pad_maximum_fusion.20.g_ref, bf16[768,5632]{1,0:T(8,128)(2,1)} %get-tuple-element.171.high_ref.refs_4_.refs_8_.refs_6_.refs_10_, ...), custom_call_target="tpu_custom_call" | custom-call | flops 4982833152 | bytes 21626880 | tf_op jit(solution)/shard_map/back_pair/pallas_call | solution.py:151
  99.5 3.0 collective-permute-done.7
  107.4 9.9 %back_pair.11 = (f32[48,5632]{1,0:T(8,128)S(1)}, f32[48,5632]{1,0:T(8,128)}) custom-call(s32[3]{0:T(128)S(1)} %pad_add_fusion.s_ref, f32[96,768]{1,0:T(8,128)S(1)} %pad_maximum_fusion.37.g_ref, bf16[768,5632]{1,0:T(8,128)(2,1)} %get-tuple-element.171.high_ref.refs_4_.refs_8_.refs_6_.refs_10_, ...), custom_call_target="tpu_custom_call" | custom-call | flops 2491416576 | bytes 19464192 | tf_op jit(solution)/shard_map/back_pair/pallas_call | solution.py:151
  120.2 4.4 collective-permute-done.13
  131.5 2.7 collective-permute-done.16
  135.8 9.9 %collective-permute-done.20 = f32[48,2816]{1,0:T(8,128)S(1)} collective-permute-done((f32[48,2816]{1,0:T(8,128)S(1)}, f32[48,2816]{1,0:T(8,128)S(1)}, u32[]{:S(2)}, u32[]{:S(2)}) %collective-permute-start.20) | collective-permute-done | bytes 540704 | tf_op jit(solution)/shard_map/ppermute | solution.py:60
  145.9 3.1 collective-permute-done.19.refs_5_
  152.9 5.8 collective-permute-done.22
  160.4 13.0 %forth_pair.6 = (f32[400,5632]{1,0:T(8,128)}, f32[120,384]{1,0:T(8,128)S(1)}, f32[120,384]{1,0:T(8,128)S(1)}) custom-call(s32[3]{0:T(128)S(1)} %pad_add_fusion.s_ref, f32[56,1408]{1,0:T(8,128)S(1)} %slice_add_fusion.5.refs_0_, f32[56,1408]{1,0:T(8,128)S(1)} %collective-permute-done.11.refs_1_, f32[56,2816]{1,0:T(8,128)S(1)} %collective-permute-done.15.refs_2_, ...), custom_call_target="tpu_custom_call" | custom-call | flops 2906652672 | bytes 24870912 | tf_op jit(solution)/shard_map/forth_pair/pallas_call | solution.py:287
  173.4 2.1 collective-permute-done.26.refs_1_
  181.7 14.4 %forth_pair.7 = (f32[400,5632]{1,0:T(8,128)}, f32[200,384]{1,0:T(8,128)S(1)}, f32[200,384]{1,0:T(8,128)S(1)}) custom-call(s32[3]{0:T(128)S(1)} %pad_add_fusion.s_ref, f32[48,1408]{1,0:T(8,128)S(1)} %slice_add_fusion.14.refs_0_, f32[48,1408]{1,0:T(8,128)S(1)} %collective-permute-done.18.refs_1_, ...), custom_call_target="tpu_custom_call", output_to_operand_aliasing={{0}: (11, {})} | custom-call | flops 4982833152 | bytes 30277632 | tf_op jit(solution)/shard_map/forth_pair/pallas_call | solution.py:287
  196.4 3.3 collective-permute-start.29
  200.7 12.6 %forth_pair.8 = (f32[400,5632]{1,0:T(8,128)}, f32[104,384]{1,0:T(8,128)S(1)}, f32[104,384]{1,0:T(8,128)S(1)}) custom-call(s32[3]{0:T(128)S(1)} %pad_add_fusion.s_ref, f32[48,1408]{1,0:T(8,128)S(1)} %slice_add_fusion.12.refs_0_, f32[48,1408]{1,0:T(8,128)S(1)} %collective-permute-done.26.refs_1_, ...), custom_call_target="tpu_custom_call", output_to_operand_aliasing={{0}: (7, {})} | custom-call | flops 2491416576 | bytes 23789568 | tf_op jit(solution)/shard_map/forth_pair/pallas_call | solution.py:287
  214.1 1.9 collective-permute-start.33
  216.1 8.4 %collective-permute-done.33 = f32[104,384]{1,0:T(8,128)S(1)} collective-permute-done((f32[104,384]{1,0:T(8,128)S(1)}, f32[104,384]{1,0:T(8,128)S(1)}, u32[]{:S(2)}, u32[]{:S(2)}) %collective-permute-start.33) | collective-permute-done | bytes 159776 | tf_op jit(solution)/shard_map/ppermute | solution.py:60
  224.5 5.2 collective-permute-done.36
  229.8 2.0 collective-permute-start.32
  232.6 11.6 %collective-permute-done.35 = f32[104,384]{1,0:T(8,128)S(1)} collective-permute-done((f32[104,384]{1,0:T(8,128)S(1)}, f32[104,384]{1,0:T(8,128)S(1)}, u32[]{:S(2)}, u32[]{:S(2)}) %collective-permute-start.35) | collective-permute-done | bytes 159776 | tf_op jit(solution)/shard_map/ppermute | solution.py:60
  244.2 3.2 collective-permute-start.38
  247.6 3.6 collective-permute-done.38
  253.0 9.9 %back_pair.12 = (f32[56,5632]{1,0:T(8,128)S(1)}, f32[56,5632]{1,0:T(8,128)}) custom-call(s32[3]{0:T(128)S(1)} %pad_add_fusion.s_ref, f32[112,768]{1,0:T(8,128)S(1)} %slice.407.g_ref, bf16[768,5632]{1,0:T(8,128)(2,1)} %get-tuple-element.171.high_ref.refs_4_.refs_8_.refs_6_.refs_10_, bf16[768,5632]{1,0:T(8,128)(2,1)} %get-tuple-element.172.low_ref.refs_5_.refs_9_.refs_7_.refs_11_), custom_call_target="tpu_custom_call" | custom-call | flops 2906652672 | bytes 19824640 | tf_op jit(solution)/shard_map/back_pair/pallas_call | solution.py:151
  264.0 1.8 collective-permute-done.39
  267.6 11.3 %back_pair.13 = (f32[48,5632]{1,0:T(8,128)S(1)}, f32[48,5632]{1,0:T(8,128)}, f32[48,5632]{1,0:T(8,128)}, f32[48,5632]{1,0:T(8,128)}) custom-call(s32[3]{0:T(128)S(1)} %pad_add_fusion.s_ref, f32[192,768]{1,0:T(8,128)S(1)} %slice.408.g_ref, bf16[768,5632]{1,0:T(8,128)(2,1)} %get-tuple-element.171.high_ref.refs_4_.refs_8_.refs_6_.refs_10_, ...), custom_call_target="tpu_custom_call" | custom-call | flops 4982833152 | bytes 21626880 | tf_op jit(solution)/shard_map/back_pair/pallas_call | solution.py:151
  280.5 2.5 collective-permute-done.40
  288.7 10.1 %back_pair.14 = (f32[48,5632]{1,0:T(8,128)S(1)}, f32[48,5632]{1,0:T(8,128)}) custom-call(s32[3]{0:T(128)S(1)} %pad_add_fusion.s_ref, f32[96,768]{1,0:T(8,128)S(1)} %slice.411.g_ref, bf16[768,5632]{1,0:T(8,128)(2,1)} %get-tuple-element.171.high_ref.refs_4_.refs_8_.refs_6_.refs_10_, bf16[768,5632]{1,0:T(8,128)(2,1)} %get-tuple-element.172.low_ref.refs_5_.refs_9_.refs_7_.refs_11_), custom_call_target="tpu_custom_call" | custom-call | flops 2491416576 | bytes 19464192 | tf_op jit(solution)/shard_map/back_pair/pallas_call | solution.py:151
  301.9 4.0 collective-permute-done.49
  312.9 2.7 collective-permute-done.52
  315.6 1.9 collective-permute-start.54
  317.4 9.7 %collective-permute-done.56 = f32[48,2816]{1,0:T(8,128)S(1)} collective-permute-done((f32[48,2816]{1,0:T(8,128)S(1)}, f32[48,2816]{1,0:T(8,128)S(1)}, u32[]{:S(2)}, u32[]{:S(2)}) %collective-permute-start.56) | collective-permute-done | bytes 540704 | tf_op jit(solution)/shard_map/ppermute | solution.py:60
  327.9 2.5 collective-permute-done.55.refs_6_
  339.3 3.6 collective-permute-done.58
  344.7 13.9 %forth_pair.9 = (f32[400,5632]{1,0:T(8,128)}, f32[120,384]{1,0:T(8,128)S(1)}, f32[120,384]{1,0:T(8,128)S(1)}) custom-call(s32[3]{0:T(128)S(1)} %pad_add_fusion.s_ref, f32[1]{0:T(128)} %bitcast.5.refs_0_, f32[56,1408]{1,0:T(8,128)S(1)} %slice_add_fusion.4.refs_1_, f32[56,1408]{1,0:T(8,128)S(1)} %collective-permute-done.47.refs_2_, ...), custom_call_target="tpu_custom_call" | custom-call | flops 2906652672 | bytes 24870912 | tf_op jit(solution)/shard_map/forth_pair/pallas_call | solution.py:287
  365.9 15.8 %forth_pair.10 = (f32[400,5632]{1,0:T(8,128)}, f32[200,384]{1,0:T(8,128)S(1)}, f32[200,384]{1,0:T(8,128)S(1)}) custom-call(s32[3]{0:T(128)S(1)} %pad_add_fusion.s_ref, f32[1]{0:T(128)} %bitcast.5.refs_0_, f32[48,1408]{1,0:T(8,128)S(1)} %slice_add_fusion.11.refs_1_, f32[48,1408]{1,0:T(8,128)S(1)} %collective-permute-done.54.refs_2_, ...), custom_call_target="tpu_custom_call", output_to_operand_aliasing={{0}: (13, {})} | custom-call | flops 4982833152 | bytes 30277632 | tf_op jit(solution)/shard_map/forth_pair/pallas_call | solution.py:287
  382.0 1.8 collective-permute-start.70
  385.8 13.7 %forth_pair.11 = (f32[400,5632]{1,0:T(8,128)}, f32[104,384]{1,0:T(8,128)S(1)}, f32[104,384]{1,0:T(8,128)S(1)}) custom-call(s32[3]{0:T(128)S(1)} %pad_add_fusion.s_ref, f32[1]{0:T(128)} %bitcast.5.refs_0_, f32[48,1408]{1,0:T(8,128)S(1)} %slice_add_fusion.9.refs_1_, f32[48,1408]{1,0:T(8,128)S(1)} %collective-permute-done.62.refs_2_, ...), custom_call_target="tpu_custom_call", output_to_operand_aliasing={{0}: (9, {})} | custom-call | flops 2491416576 | bytes 23789568 | tf_op jit(solution)/shard_map/forth_pair/pallas_call | solution.py:287
  399.5 2.3 collective-permute-start.72
  402.1 10.0 %collective-permute-done.69 = f32[104,384]{1,0:T(8,128)S(1)} collective-permute-done((f32[104,384]{1,0:T(8,128)S(1)}, f32[104,384]{1,0:T(8,128)S(1)}, u32[]{:S(2)}, u32[]{:S(2)}) %collective-permute-start.69) | collective-permute-done | bytes 159776 | tf_op jit(solution)/shard_map/ppermute | solution.py:60
  412.2 4.1 collective-permute-done.72
  416.4 2.0 collective-permute-start.68
  419.1 10.7 %collective-permute-done.71 = f32[104,384]{1,0:T(8,128)S(1)} collective-permute-done((f32[104,384]{1,0:T(8,128)S(1)}, f32[104,384]{1,0:T(8,128)S(1)}, u32[]{:S(2)}, u32[]{:S(2)}) %collective-permute-start.71) | collective-permute-done | bytes 159776 | tf_op jit(solution)/shard_map/ppermute | solution.py:60
  429.9 3.4 collective-permute-start.74
  433.4 3.1 collective-permute-done.74
  441.4 10.1 %back_pair.15 = (f32[56,5632]{1,0:T(8,128)S(1)}, f32[56,5632]{1,0:T(8,128)}) custom-call(s32[3]{0:T(128)S(1)} %pad_add_fusion.s_ref, f32[112,768]{1,0:T(8,128)S(1)} %slice.440.g_ref, bf16[768,5632]{1,0:T(8,128)(2,1)} %get-tuple-element.171.high_ref.refs_4_.refs_8_.refs_6_.refs_10_, bf16[768,5632]{1,0:T(8,128)(2,1)} %get-tuple-element.172.low_ref.refs_5_.refs_9_.refs_7_.refs_11_), custom_call_target="tpu_custom_call" | custom-call | flops 2906652672 | bytes 19824640 | tf_op jit(solution)/shard_map/back_pair/pallas_call | solution.py:151
  456.5 11.3 %back_pair.16 = (f32[48,5632]{1,0:T(8,128)S(1)}, f32[48,5632]{1,0:T(8,128)}, f32[48,5632]{1,0:T(8,128)}, f32[48,5632]{1,0:T(8,128)}) custom-call(s32[3]{0:T(128)S(1)} %pad_add_fusion.s_ref, f32[192,768]{1,0:T(8,128)S(1)} %slice.439.g_ref, bf16[768,5632]{1,0:T(8,128)(2,1)} %get-tuple-element.171.high_ref.refs_4_.refs_8_.refs_6_.refs_10_, ...), custom_call_target="tpu_custom_call" | custom-call | flops 4982833152 | bytes 21626880 | tf_op jit(solution)/shard_map/back_pair/pallas_call | solution.py:151
  483.9 9.8 %back_pair.17 = (f32[48,5632]{1,0:T(8,128)S(1)}, f32[48,5632]{1,0:T(8,128)}) custom-call(s32[3]{0:T(128)S(1)} %pad_add_fusion.s_ref, f32[96,768]{1,0:T(8,128)S(1)} %slice.438.g_ref, bf16[768,5632]{1,0:T(8,128)(2,1)} %get-tuple-element.171.high_ref.refs_4_.refs_8_.refs_6_.refs_10_, bf16[768,5632]{1,0:T(8,128)(2,1)} %get-tuple-element.172.low_ref.refs_5_.refs_9_.refs_7_.refs_11_), custom_call_target="tpu_custom_call" | custom-call | flops 2491416576 | bytes 19464192 | tf_op jit(solution)/shard_map/back_pair/pallas_call | solution.py:151
  512.3 10.1 %collective-permute-done.86 = f32[48,2816]{1,0:T(8,128)S(1)} collective-permute-done((f32[48,2816]{1,0:T(8,128)S(1)}, f32[48,2816]{1,0:T(8,128)S(1)}, u32[]{:S(2)}, u32[]{:S(2)}) %collective-permute-start.86) | collective-permute-done | bytes 540704 | tf_op jit(solution)/shard_map/ppermute | solution.py:60
  524.0 3.8 collective-permute-done.93.refs_5_
  530.5 3.2 collective-permute-done.90
  535.4 13.7 %multiply_add_fusion = f32[400,5632]{1,0:T(8,128)} fusion(f32[400,5632]{1,0:T(8,128)} %get-tuple-element.311.refs_5_.refs_9_, f32[400,5632]{1,0:T(8,128)} %w_ref.3, f32[400,5632]{1,0:T(8,128)} %get-tuple-element.255.refs_5_.refs_9_.refs_4_.refs_8_, f32[]{:T(128)} %div.68, f32[]{:T(128)S(6)} %add.287), kind=kLoop, calls=%fused_computation | loop fusion | flops 9011200 | bytes 36044808 | tf_op jit(solution)/shard_map/add | solution.py:594
  553.3 4.9 last_rows.3.refs_10_
  558.2 5.8 collective-permute-done.95.refs_2_
  566.2 7.5 %last_rows.4.refs_6_ = f32[400,5632]{1,0:T(8,128)} custom-call(s32[3]{0:T(128)S(1)} %pad_add_fusion.s_ref, f32[2]{0:T(128)S(1)} %pad_maximum_fusion.38.scalar_ref, f32[48,1408]{1,0:T(8,128)S(1)} %slice_add_fusion.8.refs_0_, f32[48,1408]{1,0:T(8,128)S(1)} %collective-permute-done.92.refs_1_, ...), custom_call_target="tpu_custom_call", output_to_operand_aliasing={{}: (12, {})} | custom-call | flops 6488064 | bytes 17301504 | tf_op jit(solution)/shard_map/last_rows/pallas_call | solution.py:357
  574.8 4.5 last_rows.5
  (373 shorter events, 131.1 us)
Async XLA Ops:
  14.7 17.0 %collective-permute-start = (f32[200,384]{1,0:T(8,128)S(1)}, f32[200,384]{1,0:T(8,128)S(1)}, u32[]{:S(2)}, u32[]{:S(2)}) collective-permute-start(f32[200,384]{1,0:T(8,128)S(1)} %get-tuple-element.162), channel_id=1, source_target_pairs={{0,1},{1,0},{2,3},{3,2},{4,5},{5,4},{6,7},{7,6},{8,9},{9,8},{10,11... | collective-permute-start | bytes 921608 | tf_op jit(solution)/shard_map/ppermute | solution.py:60
  31.7 15.3 %collective-permute-start.3 = (f32[200,384]{1,0:T(8,128)S(1)}, f32[200,384]{1,0:T(8,128)S(1)}, u32[]{:S(2)}, u32[]{:S(2)}) collective-permute-start(f32[200,384]{1,0:T(8,128)S(1)} %get-tuple-element.168), channel_id=1, source_target_pairs={{0,1},{1,0},{2,3},{3,2},{4,5},{5,4},{6,7},{7,6},{8,9},{9,8},{10,11... | collective-permute-start | bytes 921608 | tf_op jit(solution)/shard_map/ppermute | solution.py:60
  31.8 15.4 %collective-permute-start.1 = (f32[200,384]{1,0:T(8,128)S(1)}, f32[200,384]{1,0:T(8,128)S(1)}, u32[]{:S(2)}, u32[]{:S(2)}) collective-permute-start(f32[200,384]{1,0:T(8,128)S(1)} %add.220), channel_id=1, source_target_pairs={{0,2},{1,3},{2,0},{3,1},{4,6},{5,7},{6,4},{7,5},{8,10},{9,11},{10,... | collective-permute-start | bytes 921608 | tf_op jit(solution)/shard_map/ppermute | solution.py:60
  47.0 15.3 %collective-permute-start.4 = (f32[200,384]{1,0:T(8,128)S(1)}, f32[200,384]{1,0:T(8,128)S(1)}, u32[]{:S(2)}, u32[]{:S(2)}) collective-permute-start(f32[200,384]{1,0:T(8,128)S(1)} %add.222), channel_id=1, source_target_pairs={{0,2},{1,3},{2,0},{3,1},{4,6},{5,7},{6,4},{7,5},{8,10},{9,11},{10,... | collective-permute-start | bytes 921608 | tf_op jit(solution)/shard_map/ppermute | solution.py:60
  47.2 18.8 %collective-permute-start.2 = (f32[200,384]{1,0:T(8,128)S(1)}, f32[200,384]{1,0:T(8,128)S(1)}, u32[]{:S(2)}, u32[]{:S(2)}) collective-permute-start(f32[200,384]{1,0:T(8,128)S(1)} %add.221), channel_id=1, source_target_pairs={{0,1},{1,0},{2,3},{3,2},{4,5},{5,4},{6,7},{7,6},{8,9},{9,8},{10,11... | collective-permute-start | bytes 921608 | tf_op jit(solution)/shard_map/ppermute | solution.py:60
  86.1 16.3 %collective-permute-start.7 = (f32[56,2816]{1,0:T(8,128)S(1)}, f32[56,2816]{1,0:T(8,128)S(1)}, u32[]{:S(2)}, u32[]{:S(2)}) collective-permute-start(f32[56,2816]{1,0:T(8,128)S(1)} %pad_maximum_fusion.14), channel_id=1, source_target_pairs={{0,8},{4,12},{8,0},{12,4},{16,24},{20,28},{24,16},{28,20},{1,9},{5... | collective-permute-start | bytes 1892360 | tf_op jit(solution)/shard_map/ppermute | solution.py:60
  102.6 14.6 %collective-permute-start.8 = (f32[56,1408]{1,0:T(8,128)S(1)}, f32[56,1408]{1,0:T(8,128)S(1)}, u32[]{:S(2)}, u32[]{:S(2)}) collective-permute-start(f32[56,1408]{1,0:T(8,128)S(1)} %slice.384), channel_id=1, source_target_pairs={{0,16},{4,20},{8,24},{12,28},{16,0},{20,4},{24,8},{28,12},{1,17},{... | collective-permute-start | bytes 946184 | tf_op jit(solution)/shard_map/ppermute | solution.py:60
  104.4 20.2 %collective-permute-start.13 = (f32[48,2816]{1,0:T(8,128)S(1)}, f32[48,2816]{1,0:T(8,128)S(1)}, u32[]{:S(2)}, u32[]{:S(2)}) collective-permute-start(f32[48,2816]{1,0:T(8,128)S(1)} %slice.385), channel_id=1, source_target_pairs={{0,16},{4,20},{8,24},{12,28},{16,0},{20,4},{24,8},{28,12},{1,17},{... | collective-permute-start | bytes 1622024 | tf_op jit(solution)/shard_map/ppermute | solution.py:60
  105.8 13.6 %collective-permute-start.14 = (f32[48,2816]{1,0:T(8,128)S(1)}, f32[48,2816]{1,0:T(8,128)S(1)}, u32[]{:S(2)}, u32[]{:S(2)}) collective-permute-start(f32[48,2816]{1,0:T(8,128)S(1)} %pad_maximum_fusion.21), channel_id=1, source_target_pairs={{0,8},{4,12},{8,0},{12,4},{16,24},{20,28},{24,16},{28,20},{1,9},{5... | collective-permute-start | bytes 1622024 | tf_op jit(solution)/shard_map/ppermute | solution.py:60
  119.5 10.9 %collective-permute-start.17 = (f32[48,1408]{1,0:T(8,128)S(1)}, f32[48,1408]{1,0:T(8,128)S(1)}, u32[]{:S(2)}, u32[]{:S(2)}) collective-permute-start(f32[48,1408]{1,0:T(8,128)S(1)} %slice.391), channel_id=1, source_target_pairs={{0,16},{4,20},{8,24},{12,28},{16,0},{20,4},{24,8},{28,12},{1,17},{... | collective-permute-start | bytes 811016 | tf_op jit(solution)/shard_map/ppermute | solution.py:60
  126.5 19.2 %collective-permute-start.20 = (f32[48,2816]{1,0:T(8,128)S(1)}, f32[48,2816]{1,0:T(8,128)S(1)}, u32[]{:S(2)}, u32[]{:S(2)}) collective-permute-start(f32[48,2816]{1,0:T(8,128)S(1)} %pad_maximum_fusion.22), channel_id=1, source_target_pairs={{0,8},{4,12},{8,0},{12,4},{16,24},{20,28},{24,16},{28,20},{1,9},{5... | collective-permute-start | bytes 1622024 | tf_op jit(solution)/shard_map/ppermute | solution.py:60
  127.6 21.5 %collective-permute-start.15 = (f32[56,2816]{1,0:T(8,128)S(1)}, f32[56,2816]{1,0:T(8,128)S(1)}, u32[]{:S(2)}, u32[]{:S(2)}) collective-permute-start(f32[56,2816]{1,0:T(8,128)S(1)} %pad_maximum_fusion.15), channel_id=1, source_target_pairs={{0,16},{4,20},{8,24},{12,28},{16,0},{20,4},{24,8},{28,12},{1,17},{... | collective-permute-start | bytes 1892360 | tf_op jit(solution)/shard_map/ppermute | solution.py:60
  130.4 18.6 %collective-permute-start.19 = (f32[48,1408]{1,0:T(8,128)S(1)}, f32[48,1408]{1,0:T(8,128)S(1)}, u32[]{:S(2)}, u32[]{:S(2)}) collective-permute-start(f32[48,1408]{1,0:T(8,128)S(1)} %slice_add_fusion.13.refs_4_), channel_id=1, source_target_pairs={{0,8},{4,12},{8,0},{12,4},{16,24},{20,28},{24,16},{28,20},{1,9},{5... | collective-permute-start | bytes 811016 | tf_op jit(solution)/shard_map/ppermute | solution.py:60
  134.2 14.8 %collective-permute-start.18 = (f32[48,1408]{1,0:T(8,128)S(1)}, f32[48,1408]{1,0:T(8,128)S(1)}, u32[]{:S(2)}, u32[]{:S(2)}) collective-permute-start(f32[48,1408]{1,0:T(8,128)S(1)} %slice_add_fusion.14.refs_0_), channel_id=1, source_target_pairs={{0,16},{4,20},{8,24},{12,28},{16,0},{20,4},{24,8},{28,12},{1,17},{... | collective-permute-start | bytes 811016 | tf_op jit(solution)/shard_map/ppermute | solution.py:60
  150.0 25.7 %collective-permute-start.24 = (f32[48,2816]{1,0:T(8,128)S(1)}, f32[48,2816]{1,0:T(8,128)S(1)}, u32[]{:S(2)}, u32[]{:S(2)}) collective-permute-start(f32[48,2816]{1,0:T(8,128)S(1)} %pad_maximum_fusion.24), channel_id=1, source_target_pairs={{0,8},{4,12},{8,0},{12,4},{16,24},{20,28},{24,16},{28,20},{1,9},{5... | collective-permute-start | bytes 1622024 | tf_op jit(solution)/shard_map/ppermute | solution.py:60
  151.5 24.1 %collective-permute-start.25 = (f32[48,2816]{1,0:T(8,128)S(1)}, f32[48,2816]{1,0:T(8,128)S(1)}, u32[]{:S(2)}, u32[]{:S(2)}) collective-permute-start(f32[48,2816]{1,0:T(8,128)S(1)} %pad_maximum_fusion.23), channel_id=1, source_target_pairs={{0,16},{4,20},{8,24},{12,28},{16,0},{20,4},{24,8},{28,12},{1,17},{... | collective-permute-start | bytes 1622024 | tf_op jit(solution)/shard_map/ppermute | solution.py:60
  158.7 16.9 %collective-permute-start.26 = (f32[48,1408]{1,0:T(8,128)S(1)}, f32[48,1408]{1,0:T(8,128)S(1)}, u32[]{:S(2)}, u32[]{:S(2)}) collective-permute-start(f32[48,1408]{1,0:T(8,128)S(1)} %slice_add_fusion.12.refs_0_), channel_id=1, source_target_pairs={{0,16},{4,20},{8,24},{12,28},{16,0},{20,4},{24,8},{28,12},{1,17},{... | collective-permute-start | bytes 811016 | tf_op jit(solution)/shard_map/ppermute | solution.py:60
  176.9 19.2 %collective-permute-start.30 = (f32[48,2816]{1,0:T(8,128)S(1)}, f32[48,2816]{1,0:T(8,128)S(1)}, u32[]{:S(2)}, u32[]{:S(2)}) collective-permute-start(f32[48,2816]{1,0:T(8,128)S(1)} %pad_maximum_fusion.25), channel_id=1, source_target_pairs={{0,8},{4,12},{8,0},{12,4},{16,24},{20,28},{24,16},{28,20},{1,9},{5... | collective-permute-start | bytes 1622024 | tf_op jit(solution)/shard_map/ppermute | solution.py:60
  178.4 17.6 %collective-permute-start.23 = (f32[120,384]{1,0:T(8,128)S(1)}, f32[120,384]{1,0:T(8,128)S(1)}, u32[]{:S(2)}, u32[]{:S(2)}) collective-permute-start(f32[120,384]{1,0:T(8,128)S(1)} %get-tuple-element.201), channel_id=1, source_target_pairs={{0,1},{1,0},{2,3},{3,2},{4,5},{5,4},{6,7},{7,6},{8,9},{9,8},{10,11... | collective-permute-start | bytes 552968 | tf_op jit(solution)/shard_map/ppermute | solution.py:60
  196.4 17.0 %collective-permute-start.34 = (f32[200,384]{1,0:T(8,128)S(1)}, f32[200,384]{1,0:T(8,128)S(1)}, u32[]{:S(2)}, u32[]{:S(2)}) collective-permute-start(f32[200,384]{1,0:T(8,128)S(1)} %get-tuple-element.208), channel_id=1, source_target_pairs={{0,1},{1,0},{2,3},{3,2},{4,5},{5,4},{6,7},{7,6},{8,9},{9,8},{10,11... | collective-permute-start | bytes 921608 | tf_op jit(solution)/shard_map/ppermute | solution.py:60
  196.4 16.9 %collective-permute-start.29 = (f32[120,384]{1,0:T(8,128)S(1)}, f32[120,384]{1,0:T(8,128)S(1)}, u32[]{:S(2)}, u32[]{:S(2)}) collective-permute-start(f32[120,384]{1,0:T(8,128)S(1)} %add.236), channel_id=1, source_target_pairs={{0,2},{1,3},{2,0},{3,1},{4,6},{5,7},{6,4},{7,5},{8,10},{9,11},{10,... | collective-permute-start | bytes 552968 | tf_op jit(solution)/shard_map/ppermute | solution.py:60
  213.4 16.2 %collective-permute-start.36 = (f32[200,384]{1,0:T(8,128)S(1)}, f32[200,384]{1,0:T(8,128)S(1)}, u32[]{:S(2)}, u32[]{:S(2)}) collective-permute-start(f32[200,384]{1,0:T(8,128)S(1)} %add.238), channel_id=1, source_target_pairs={{0,2},{1,3},{2,0},{3,1},{4,6},{5,7},{6,4},{7,5},{8,10},{9,11},{10,... | collective-permute-start | bytes 921608 | tf_op jit(solution)/shard_map/ppermute | solution.py:60
  229.7 17.8 %collective-permute-start.37 = (f32[200,384]{1,0:T(8,128)S(1)}, f32[200,384]{1,0:T(8,128)S(1)}, u32[]{:S(2)}, u32[]{:S(2)}) collective-permute-start(f32[200,384]{1,0:T(8,128)S(1)} %add.240), channel_id=1, source_target_pairs={{0,1},{1,0},{2,3},{3,2},{4,5},{5,4},{6,7},{7,6},{8,9},{9,8},{10,11... | collective-permute-start | bytes 921608 | tf_op jit(solution)/shard_map/ppermute | solution.py:60
  229.8 17.6 %collective-permute-start.32 = (f32[120,384]{1,0:T(8,128)S(1)}, f32[120,384]{1,0:T(8,128)S(1)}, u32[]{:S(2)}, u32[]{:S(2)}) collective-permute-start(f32[120,384]{1,0:T(8,128)S(1)} %add.237), channel_id=1, source_target_pairs={{0,1},{1,0},{2,3},{3,2},{4,5},{5,4},{6,7},{7,6},{8,9},{9,8},{10,11... | collective-permute-start | bytes 552968 | tf_op jit(solution)/shard_map/ppermute | solution.py:60
  231.8 12.3 %collective-permute-start.35 = (f32[104,384]{1,0:T(8,128)S(1)}, f32[104,384]{1,0:T(8,128)S(1)}, u32[]{:S(2)}, u32[]{:S(2)}) collective-permute-start(f32[104,384]{1,0:T(8,128)S(1)} %add.239), channel_id=1, source_target_pairs={{0,2},{1,3},{2,0},{3,1},{4,6},{5,7},{6,4},{7,5},{8,10},{9,11},{10,... | collective-permute-start | bytes 479240 | tf_op jit(solution)/shard_map/ppermute | solution.py:60
  266.7 17.7 %collective-permute-start.45 = (f32[56,2816]{1,0:T(8,128)S(1)}, f32[56,2816]{1,0:T(8,128)S(1)}, u32[]{:S(2)}, u32[]{:S(2)}) collective-permute-start(f32[56,2816]{1,0:T(8,128)S(1)} %pad_maximum_fusion.16), channel_id=1, source_target_pairs={{0,8},{4,12},{8,0},{12,4},{16,24},{20,28},{24,16},{28,20},{1,9},{5... | collective-permute-start | bytes 1892360 | tf_op jit(solution)/shard_map/ppermute | solution.py:60
  283.6 15.1 %collective-permute-start.42 = (f32[8,128]{1,0:T(8,128)S(1)}, f32[8,128]{1,0:T(8,128)S(1)}, u32[]{:S(2)}, u32[]{:S(2)}) collective-permute-start(f32[8,128]{1,0:T(8,128)S(1)} %fusion.24), channel_id=1, source_target_pairs={{0,16},{4,20},{8,24},{12,28},{16,0},{20,4},{24,8},{28,12},{1,17},{... | collective-permute-start | bytes 12296 | tf_op jit(solution)/shard_map/ppermute | solution.py:60
  284.5 14.3 %collective-permute-start.46 = (f32[56,1408]{1,0:T(8,128)S(1)}, f32[56,1408]{1,0:T(8,128)S(1)}, u32[]{:S(2)}, u32[]{:S(2)}) collective-permute-start(f32[56,1408]{1,0:T(8,128)S(1)} %slice.414), channel_id=1, source_target_pairs={{0,16},{4,20},{8,24},{12,28},{16,0},{20,4},{24,8},{28,12},{1,17},{... | collective-permute-start | bytes 946184 | tf_op jit(solution)/shard_map/ppermute | solution.py:60
  286.1 19.8 %collective-permute-start.49 = (f32[48,2816]{1,0:T(8,128)S(1)}, f32[48,2816]{1,0:T(8,128)S(1)}, u32[]{:S(2)}, u32[]{:S(2)}) collective-permute-start(f32[48,2816]{1,0:T(8,128)S(1)} %slice.415), channel_id=1, source_target_pairs={{0,16},{4,20},{8,24},{12,28},{16,0},{20,4},{24,8},{28,12},{1,17},{... | collective-permute-start | bytes 1622024 | tf_op jit(solution)/shard_map/ppermute | solution.py:60
  287.6 13.6 %collective-permute-start.50 = (f32[48,2816]{1,0:T(8,128)S(1)}, f32[48,2816]{1,0:T(8,128)S(1)}, u32[]{:S(2)}, u32[]{:S(2)}) collective-permute-start(f32[48,2816]{1,0:T(8,128)S(1)} %pad_maximum_fusion.26), channel_id=1, source_target_pairs={{0,8},{4,12},{8,0},{12,4},{16,24},{20,28},{24,16},{28,20},{1,9},{5... | collective-permute-start | bytes 1622024 | tf_op jit(solution)/shard_map/ppermute | solution.py:60
  307.4 19.7 %collective-permute-start.56 = (f32[48,2816]{1,0:T(8,128)S(1)}, f32[48,2816]{1,0:T(8,128)S(1)}, u32[]{:S(2)}, u32[]{:S(2)}) collective-permute-start(f32[48,2816]{1,0:T(8,128)S(1)} %pad_maximum_fusion.27), channel_id=1, source_target_pairs={{0,8},{4,12},{8,0},{12,4},{16,24},{20,28},{24,16},{28,20},{1,9},{5... | collective-permute-start | bytes 1622024 | tf_op jit(solution)/shard_map/ppermute | solution.py:60
  309.1 23.1 %collective-permute-start.51 = (f32[56,2816]{1,0:T(8,128)S(1)}, f32[56,2816]{1,0:T(8,128)S(1)}, u32[]{:S(2)}, u32[]{:S(2)}) collective-permute-start(f32[56,2816]{1,0:T(8,128)S(1)} %pad_maximum_fusion.17), channel_id=1, source_target_pairs={{0,16},{4,20},{8,24},{12,28},{16,0},{20,4},{24,8},{28,12},{1,17},{... | collective-permute-start | bytes 1892360 | tf_op jit(solution)/shard_map/ppermute | solution.py:60
  311.8 18.7 %collective-permute-start.55 = (f32[48,1408]{1,0:T(8,128)S(1)}, f32[48,1408]{1,0:T(8,128)S(1)}, u32[]{:S(2)}, u32[]{:S(2)}) collective-permute-start(f32[48,1408]{1,0:T(8,128)S(1)} %slice_add_fusion.10.refs_5_), channel_id=1, source_target_pairs={{0,8},{4,12},{8,0},{12,4},{16,24},{20,28},{24,16},{28,20},{1,9},{5... | collective-permute-start | bytes 811016 | tf_op jit(solution)/shard_map/ppermute | solution.py:60
  315.6 15.8 %collective-permute-start.54 = (f32[48,1408]{1,0:T(8,128)S(1)}, f32[48,1408]{1,0:T(8,128)S(1)}, u32[]{:S(2)}, u32[]{:S(2)}) collective-permute-start(f32[48,1408]{1,0:T(8,128)S(1)} %slice_add_fusion.11.refs_1_), channel_id=1, source_target_pairs={{0,16},{4,20},{8,24},{12,28},{16,0},{20,4},{24,8},{28,12},{1,17},{... | collective-permute-start | bytes 811016 | tf_op jit(solution)/shard_map/ppermute | solution.py:60
  333.3 11.4 %collective-permute-start.57 = (f32[56,5632]{1,0:T(8,128)}, f32[56,5632]{1,0:T(8,128)}, u32[]{:S(2)}, u32[]{:S(2)}) collective-permute-start(f32[56,5632]{1,0:T(8,128)} %pad_maximum_fusion.1), channel_id=1, source_target_pairs={{0,4},{4,0},{8,12},{12,8},{16,20},{20,16},{24,28},{28,24},{1,5},{5... | collective-permute-start | bytes 3784712 | tf_op jit(solution)/shard_map/ppermute | solution.py:60
  336.8 23.1 %collective-permute-start.60 = (f32[48,2816]{1,0:T(8,128)}, f32[48,2816]{1,0:T(8,128)S(1)}, u32[]{:S(2)}, u32[]{:S(2)}) collective-permute-start(f32[48,2816]{1,0:T(8,128)} %pad_maximum_fusion.29), channel_id=1, source_target_pairs={{0,8},{4,12},{8,0},{12,4},{16,24},{20,28},{24,16},{28,20},{1,9},{5... | collective-permute-start | bytes 1622024 | tf_op jit(solution)/shard_map/ppermute | solution.py:60
  337.9 21.9 %collective-permute-start.61 = (f32[48,2816]{1,0:T(8,128)}, f32[48,2816]{1,0:T(8,128)S(1)}, u32[]{:S(2)}, u32[]{:S(2)}) collective-permute-start(f32[48,2816]{1,0:T(8,128)} %pad_maximum_fusion.28), channel_id=1, source_target_pairs={{0,16},{4,20},{8,24},{12,28},{16,0},{20,4},{24,8},{28,12},{1,17},{... | collective-permute-start | bytes 1622024 | tf_op jit(solution)/shard_map/ppermute | solution.py:60
  344.0 15.8 %collective-permute-start.62 = (f32[48,1408]{1,0:T(8,128)S(1)}, f32[48,1408]{1,0:T(8,128)S(1)}, u32[]{:S(2)}, u32[]{:S(2)}) collective-permute-start(f32[48,1408]{1,0:T(8,128)S(1)} %slice_add_fusion.9.refs_1_), channel_id=1, source_target_pairs={{0,16},{4,20},{8,24},{12,28},{16,0},{20,4},{24,8},{28,12},{1,17},{... | collective-permute-start | bytes 811016 | tf_op jit(solution)/shard_map/ppermute | solution.py:60
  361.2 20.6 %collective-permute-start.66 = (f32[48,2816]{1,0:T(8,128)S(1)}, f32[48,2816]{1,0:T(8,128)S(1)}, u32[]{:S(2)}, u32[]{:S(2)}) collective-permute-start(f32[48,2816]{1,0:T(8,128)S(1)} %pad_maximum_fusion.30), channel_id=1, source_target_pairs={{0,8},{4,12},{8,0},{12,4},{16,24},{20,28},{24,16},{28,20},{1,9},{5... | collective-permute-start | bytes 1622024 | tf_op jit(solution)/shard_map/ppermute | solution.py:60
  362.2 19.5 %collective-permute-start.59 = (f32[120,384]{1,0:T(8,128)S(1)}, f32[120,384]{1,0:T(8,128)S(1)}, u32[]{:S(2)}, u32[]{:S(2)}) collective-permute-start(f32[120,384]{1,0:T(8,128)S(1)} %get-tuple-element.257), channel_id=1, source_target_pairs={{0,1},{1,0},{2,3},{3,2},{4,5},{5,4},{6,7},{7,6},{8,9},{9,8},{10,11... | collective-permute-start | bytes 552968 | tf_op jit(solution)/shard_map/ppermute | solution.py:60
  382.0 17.4 %collective-permute-start.70 = (f32[200,384]{1,0:T(8,128)S(1)}, f32[200,384]{1,0:T(8,128)S(1)}, u32[]{:S(2)}, u32[]{:S(2)}) collective-permute-start(f32[200,384]{1,0:T(8,128)S(1)} %get-tuple-element.264), channel_id=1, source_target_pairs={{0,1},{1,0},{2,3},{3,2},{4,5},{5,4},{6,7},{7,6},{8,9},{9,8},{10,11... | collective-permute-start | bytes 921608 | tf_op jit(solution)/shard_map/ppermute | solution.py:60
  383.8 15.6 %collective-permute-start.65 = (f32[120,384]{1,0:T(8,128)S(1)}, f32[120,384]{1,0:T(8,128)S(1)}, u32[]{:S(2)}, u32[]{:S(2)}) collective-permute-start(f32[120,384]{1,0:T(8,128)S(1)} %add.260), channel_id=1, source_target_pairs={{0,2},{1,3},{2,0},{3,1},{4,6},{5,7},{6,4},{7,5},{8,10},{9,11},{10,... | collective-permute-start | bytes 552968 | tf_op jit(solution)/shard_map/ppermute | solution.py:60
  399.5 16.7 %collective-permute-start.72 = (f32[200,384]{1,0:T(8,128)S(1)}, f32[200,384]{1,0:T(8,128)S(1)}, u32[]{:S(2)}, u32[]{:S(2)}) collective-permute-start(f32[200,384]{1,0:T(8,128)S(1)} %add.262), channel_id=1, source_target_pairs={{0,2},{1,3},{2,0},{3,1},{4,6},{5,7},{6,4},{7,5},{8,10},{9,11},{10,... | collective-permute-start | bytes 921608 | tf_op jit(solution)/shard_map/ppermute | solution.py:60
  416.3 17.0 %collective-permute-start.73 = (f32[200,384]{1,0:T(8,128)S(1)}, f32[200,384]{1,0:T(8,128)S(1)}, u32[]{:S(2)}, u32[]{:S(2)}) collective-permute-start(f32[200,384]{1,0:T(8,128)S(1)} %add.264), channel_id=1, source_target_pairs={{0,1},{1,0},{2,3},{3,2},{4,5},{5,4},{6,7},{7,6},{8,9},{9,8},{10,11... | collective-permute-start | bytes 921608 | tf_op jit(solution)/shard_map/ppermute | solution.py:60
  416.4 16.9 %collective-permute-start.68 = (f32[120,384]{1,0:T(8,128)S(1)}, f32[120,384]{1,0:T(8,128)S(1)}, u32[]{:S(2)}, u32[]{:S(2)}) collective-permute-start(f32[120,384]{1,0:T(8,128)S(1)} %add.261), channel_id=1, source_target_pairs={{0,1},{1,0},{2,3},{3,2},{4,5},{5,4},{6,7},{7,6},{8,9},{9,8},{10,11... | collective-permute-start | bytes 552968 | tf_op jit(solution)/shard_map/ppermute | solution.py:60
  418.4 11.5 %collective-permute-start.71 = (f32[104,384]{1,0:T(8,128)S(1)}, f32[104,384]{1,0:T(8,128)S(1)}, u32[]{:S(2)}, u32[]{:S(2)}) collective-permute-start(f32[104,384]{1,0:T(8,128)S(1)} %add.263), channel_id=1, source_target_pairs={{0,2},{1,3},{2,0},{3,1},{4,6},{5,7},{6,4},{7,5},{8,10},{9,11},{10,... | collective-permute-start | bytes 479240 | tf_op jit(solution)/shard_map/ppermute | solution.py:60
  455.5 18.0 %collective-permute-start.79 = (f32[56,2816]{1,0:T(8,128)S(1)}, f32[56,2816]{1,0:T(8,128)}, u32[]{:S(2)}, u32[]{:S(2)}) collective-permute-start(f32[56,2816]{1,0:T(8,128)S(1)} %pad_maximum_fusion.18), channel_id=1, source_target_pairs={{0,8},{4,12},{8,0},{12,4},{16,24},{20,28},{24,16},{28,20},{1,9},{5... | collective-permute-start | bytes 1892360 | tf_op jit(solution)/shard_map/ppermute | solution.py:60
  467.8 12.0 %collective-permute-start.77 = (f32[48,5632]{1,0:T(8,128)}, f32[48,5632]{1,0:T(8,128)}, u32[]{:S(2)}, u32[]{:S(2)}) collective-permute-start(f32[48,5632]{1,0:T(8,128)} %get-tuple-element.287), channel_id=1, source_target_pairs={{0,4},{4,0},{8,12},{12,8},{16,20},{20,16},{24,28},{28,24},{1,5},{5... | collective-permute-start | bytes 3244040 | tf_op jit(solution)/shard_map/ppermute | solution.py:60
  472.9 20.9 %collective-permute-start.85 = (f32[8,128]{1,0:T(8,128)S(1)}, f32[8,128]{1,0:T(8,128)S(1)}, u32[]{:S(2)}, u32[]{:S(2)}) collective-permute-start(f32[8,128]{1,0:T(8,128)S(1)} %fusion.23), channel_id=1, source_target_pairs={{0,16},{4,20},{8,24},{12,28},{16,0},{20,4},{24,8},{28,12},{1,17},{... | collective-permute-start | bytes 12296 | tf_op jit(solution)/shard_map/ppermute | solution.py:60
  475.5 19.9 %collective-permute-start.84 = (f32[56,1408]{1,0:T(8,128)}, f32[56,1408]{1,0:T(8,128)}, u32[]{:S(2)}, u32[]{:S(2)}) collective-permute-start(f32[56,1408]{1,0:T(8,128)} %slice.445), channel_id=1, source_target_pairs={{0,16},{4,20},{8,24},{12,28},{16,0},{20,4},{24,8},{28,12},{1,17},{... | collective-permute-start | bytes 946184 | tf_op jit(solution)/shard_map/ppermute | solution.py:60
  479.2 21.2 %collective-permute-start.82 = (f32[48,2816]{1,0:T(8,128)}, f32[48,2816]{1,0:T(8,128)}, u32[]{:S(2)}, u32[]{:S(2)}) collective-permute-start(f32[48,2816]{1,0:T(8,128)} %slice.446), channel_id=1, source_target_pairs={{0,16},{4,20},{8,24},{12,28},{16,0},{20,4},{24,8},{28,12},{1,17},{... | collective-permute-start | bytes 1622024 | tf_op jit(solution)/shard_map/ppermute | solution.py:60
  482.9 14.8 %collective-permute-start.83 = (f32[48,2816]{1,0:T(8,128)}, f32[48,2816]{1,0:T(8,128)}, u32[]{:S(2)}, u32[]{:S(2)}) collective-permute-start(f32[48,2816]{1,0:T(8,128)} %pad_maximum_fusion.31), channel_id=1, source_target_pairs={{0,8},{4,12},{8,0},{12,4},{16,24},{20,28},{24,16},{28,20},{1,9},{5... | collective-permute-start | bytes 1622024 | tf_op jit(solution)/shard_map/ppermute | solution.py:60
  502.7 19.7 %collective-permute-start.86 = (f32[48,2816]{1,0:T(8,128)S(1)}, f32[48,2816]{1,0:T(8,128)S(1)}, u32[]{:S(2)}, u32[]{:S(2)}) collective-permute-start(f32[48,2816]{1,0:T(8,128)S(1)} %pad_maximum_fusion.32), channel_id=1, source_target_pairs={{0,8},{4,12},{8,0},{12,4},{16,24},{20,28},{24,16},{28,20},{1,9},{5... | collective-permute-start | bytes 1622024 | tf_op jit(solution)/shard_map/ppermute | solution.py:60
  504.8 25.5 %collective-permute-start.91 = (f32[56,2816]{1,0:T(8,128)S(1)}, f32[56,2816]{1,0:T(8,128)S(1)}, u32[]{:S(2)}, u32[]{:S(2)}) collective-permute-start(f32[56,2816]{1,0:T(8,128)S(1)} %pad_maximum_fusion.19), channel_id=1, source_target_pairs={{0,16},{4,20},{8,24},{12,28},{16,0},{20,4},{24,8},{28,12},{1,17},{... | collective-permute-start | bytes 1892360 | tf_op jit(solution)/shard_map/ppermute | solution.py:60
  508.3 19.5 %collective-permute-start.93 = (f32[48,1408]{1,0:T(8,128)S(1)}, f32[48,1408]{1,0:T(8,128)S(1)}, u32[]{:S(2)}, u32[]{:S(2)}) collective-permute-start(f32[48,1408]{1,0:T(8,128)S(1)} %slice_add_fusion.7.refs_4_), channel_id=1, source_target_pairs={{0,8},{4,12},{8,0},{12,4},{16,24},{20,28},{24,16},{28,20},{1,9},{5... | collective-permute-start | bytes 811016 | tf_op jit(solution)/shard_map/ppermute | solution.py:60
  510.9 18.2 %collective-permute-start.92 = (f32[48,1408]{1,0:T(8,128)S(1)}, f32[48,1408]{1,0:T(8,128)S(1)}, u32[]{:S(2)}, u32[]{:S(2)}) collective-permute-start(f32[48,1408]{1,0:T(8,128)S(1)} %slice_add_fusion.8.refs_0_), channel_id=1, source_target_pairs={{0,16},{4,20},{8,24},{12,28},{16,0},{20,4},{24,8},{28,12},{1,17},{... | collective-permute-start | bytes 811016 | tf_op jit(solution)/shard_map/ppermute | solution.py:60
  522.5 11.1 %collective-permute-start.90 = (f32[48,1408]{1,0:T(8,128)S(1)}, f32[48,1408]{1,0:T(8,128)S(1)}, u32[]{:S(2)}, u32[]{:S(2)}) collective-permute-start(f32[48,1408]{1,0:T(8,128)S(1)} %slice.462), channel_id=1, source_target_pairs={{0,16},{4,20},{8,24},{12,28},{16,0},{20,4},{24,8},{28,12},{1,17},{... | collective-permute-start | bytes 811016 | tf_op jit(solution)/shard_map/ppermute | solution.py:60
  527.8 23.6 %collective-permute-start.98 = (f32[48,2816]{1,0:T(8,128)S(1)}, f32[48,2816]{1,0:T(8,128)S(1)}, u32[]{:S(2)}, u32[]{:S(2)}) collective-permute-start(f32[48,2816]{1,0:T(8,128)S(1)} %pad_maximum_fusion.33), channel_id=1, source_target_pairs={{0,16},{4,20},{8,24},{12,28},{16,0},{20,4},{24,8},{28,12},{1,17},{... | collective-permute-start | bytes 1622024 | tf_op jit(solution)/shard_map/ppermute | solution.py:60
  529.1 22.5 %collective-permute-start.97 = (f32[48,2816]{1,0:T(8,128)S(1)}, f32[48,2816]{1,0:T(8,128)S(1)}, u32[]{:S(2)}, u32[]{:S(2)}) collective-permute-start(f32[48,2816]{1,0:T(8,128)S(1)} %pad_maximum_fusion.34), channel_id=1, source_target_pairs={{0,8},{4,12},{8,0},{12,4},{16,24},{20,28},{24,16},{28,20},{1,9},{5... | collective-permute-start | bytes 1622024 | tf_op jit(solution)/shard_map/ppermute | solution.py:60
  530.4 21.8 %collective-permute-start.96 = (f32[56,5632]{1,0:T(8,128)S(1)}, f32[56,5632]{1,0:T(8,128)S(1)}, u32[]{:S(2)}, u32[]{:S(2)}) collective-permute-start(f32[56,5632]{1,0:T(8,128)S(1)} %pad_maximum_fusion.2), channel_id=1, source_target_pairs={{0,4},{4,0},{8,12},{12,8},{16,20},{20,16},{24,28},{28,24},{1,5},{5... | collective-permute-start | bytes 3784712 | tf_op jit(solution)/shard_map/ppermute | solution.py:60
  533.7 16.6 %collective-permute-start.94 = (f32[48,1408]{1,0:T(8,128)S(1)}, f32[48,1408]{1,0:T(8,128)S(1)}, u32[]{:S(2)}, u32[]{:S(2)}) collective-permute-start(f32[48,1408]{1,0:T(8,128)S(1)} %slice_add_fusion.6.refs_0_), channel_id=1, source_target_pairs={{0,16},{4,20},{8,24},{12,28},{16,0},{20,4},{24,8},{28,12},{1,17},{... | collective-permute-start | bytes 811016 | tf_op jit(solution)/shard_map/ppermute | solution.py:60
  550.4 13.7 %collective-permute-start.95 = (f32[48,2816]{1,0:T(8,128)S(1)}, f32[48,2816]{1,0:T(8,128)S(1)}, u32[]{:S(2)}, u32[]{:S(2)}) collective-permute-start(f32[48,2816]{1,0:T(8,128)S(1)} %pad_maximum_fusion.35), channel_id=1, source_target_pairs={{0,8},{4,12},{8,0},{12,4},{16,24},{20,28},{24,16},{28,20},{1,9},{5... | collective-permute-start | bytes 1622024 | tf_op jit(solution)/shard_map/ppermute | solution.py:60
  551.5 12.7 %collective-permute-start.101 = (f32[48,5632]{1,0:T(8,128)S(1)}, f32[48,5632]{1,0:T(8,128)S(1)}, u32[]{:S(2)}, u32[]{:S(2)}) collective-permute-start(f32[48,5632]{1,0:T(8,128)S(1)} %pad_maximum_fusion.11), channel_id=1, source_target_pairs={{0,4},{4,0},{8,12},{12,8},{16,20},{20,16},{24,28},{28,24},{1,5},{5... | collective-permute-start | bytes 3244040 | tf_op jit(solution)/shard_map/ppermute | solution.py:60
  552.2 12.0 %collective-permute-start.100 = (f32[48,5632]{1,0:T(8,128)S(1)}, f32[48,5632]{1,0:T(8,128)S(1)}, u32[]{:S(2)}, u32[]{:S(2)}) collective-permute-start(f32[48,5632]{1,0:T(8,128)S(1)} %pad_maximum_fusion.12), channel_id=1, source_target_pairs={{0,4},{4,0},{8,12},{12,8},{16,20},{20,16},{24,28},{28,24},{1,5},{5... | collective-permute-start | bytes 3244040 | tf_op jit(solution)/shard_map/ppermute | solution.py:60
  (66 other events, 519.5 us)

commit v2 on v1

--- a/solution.py
+++ b/solution.py
@@ -35,11 +35,13 @@
         self.rows, self.feats, self.classes = rows, feats, classes
         self.n_clip, self.n_feat = n_clip, n_feat
         units = classes // UNIT
-        sizes = [UNIT * (units // 4 + (k < units % 4)) for k in range(4)]
+        small = units // 5
+        middle = (units - 2 * small) // 2
+        sizes = [UNIT * k for k in (units - 2 * small - middle, middle, small, small)]
         starts = [sum(sizes[:k]) for k in range(4)]
         self.chunks = list(zip(starts, sizes))
-        self.pairs = [(0,), (1, 2), (3,)]
-        self.turns = [(0, 0), (1, 1), (0, 0), (0, 1)]
+        self.pairs = [(0, 1), (2, 3)]
+        self.turns = [(0, 1), (1, 0), (0, 1), (1, 0)]
         strides = [1 << k for k in range(1, n_clip.bit_length() - 1)]
         self.levels, block = [], feats
         while strides and block % (2 * LANES) == 0:
@@ -47,7 +49,7 @@
             block //= 2
         self.doubled = strides
         self.block, self.nb = block, feats // block
-        self.rows_step = next(n for n in (384, 256, 128, rows) if rows % n == 0)
+        self.rows_step = next(n for n in (256, 128, rows) if rows % n == 0)
 
     def pair_range(self, pair):
         first, last = self.pairs[pair][0], self.pairs[pair][-1]
@@ -121,15 +123,13 @@
     return (high, low), (send, keep)
 
 
-def back_body(plan, pair, s_ref, g_ref, high_ref, low_ref, *outs):
+def back_body(plan, s_ref, g_ref, high_ref, low_ref, *outs):
     core = s_ref[1]
-    base = plan.pair_range(pair)[0]
     some, ends = [], []
-    for c in plan.pairs[pair]:
-        a, n = plan.chunks[c]
+    for a, n in plan.chunks:
         h = n // 2
         for side in (core, 1 - core):
-            some.append(g_ref[pl.ds(pl.multiple_of(a - base + side * h, ROWS8), h), :])
+            some.append(g_ref[pl.ds(pl.multiple_of(a + side * h, ROWS8), h), :])
             ends.append((ends[-1] if ends else 0) + h)
     x = jnp.concatenate(some, axis=0)
     width = 2 * LANES
@@ -140,22 +140,20 @@
             out[:, k : k + w] = part[start:end]
 
 
-def back(plan, where, pair, values, high, low):
-    rows, block, feats = plan.rows, plan.block, plan.feats
-    n_pair = plan.pair_range(pair)[1]
+def back(plan, where, values, high, low):
+    rows, block, feats, classes = plan.rows, plan.block, plan.feats, plan.classes
     outs, specs = [], []
-    for c in plan.pairs[pair]:
-        h = plan.chunks[c][1] // 2
-        outs += [jax.ShapeDtypeStruct((h, feats), F32)] * 2
-        specs += [pl.BlockSpec((h, block), lambda p, s: (0, p))] * 2
+    for _, n in plan.chunks:
+        outs += [jax.ShapeDtypeStruct((n // 2, feats), F32)] * 2
+        specs += [pl.BlockSpec((n // 2, block), lambda p, s: (0, p))] * 2
     result = pl.pallas_call(
-        functools.partial(back_body, plan, pair),
+        functools.partial(back_body, plan),
         out_shape=outs,
         grid_spec=pltpu.PrefetchScalarGridSpec(
             num_scalar_prefetch=1,
             grid=(plan.nb,),
             in_specs=[
-                pl.BlockSpec((n_pair, rows), lambda p, s: (0, 0)),
+                pl.BlockSpec((classes, rows), lambda p, s: (0, 0)),
                 pl.BlockSpec((rows, block), lambda p, s: (0, p)),
                 pl.BlockSpec((rows, block), lambda p, s: (0, p)),
             ],
@@ -163,11 +161,11 @@
         ),
         compiler_params=params(),
         cost_estimate=pl.CostEstimate(
-            flops=6 * n_pair * rows * feats, bytes_accessed=4 * feats * (rows + n_pair), transcendentals=0
+            flops=6 * classes * rows * feats, bytes_accessed=4 * feats * (rows + classes), transcendentals=0
         ),
-        name="back_pair",
+        name="back_all",
     )(where, values, high, low)
-    return [tuple(result[2 * k : 2 * k + 2]) for k in range(len(plan.pairs[pair]))]
+    return [tuple(result[2 * k : 2 * k + 2]) for k in range(len(plan.chunks))]
 
 
 class Pieces:
@@ -501,12 +499,18 @@
 
     split, parts = None, []
     for part in range(rows // plan.rows_step):
-        split, halves = first(plan, where, features, weights, part, split)
+        if part > 1:
+            parts[part - 2].advance(order)
+        split, halves = first(plan, where, order.after(features), weights, part, split)
+        order.note(halves[0])
         parts.append(FeatSum(plan, halves, bit, 0))
+    for part in range(len(parts) - 1, len(parts) - 3, -1):
+        if part > 0:
+            parts[part - 1].advance(order)
     high, low = split
     probs, values = [], []
     for part, summed in enumerate(parts):
-        logits = summed.result(Order())
+        logits = summed.result(order)
         top = jnp.max(logits, axis=0, keepdims=True)
         powers = jnp.exp(logits - top)
         some = powers / jnp.sum(powers, axis=0, keepdims=True)
@@ -516,35 +520,29 @@
         values.append((some - onehot) / total_rows)
     probs, values = jnp.concatenate(probs, axis=1), jnp.concatenate(values, axis=1)
 
-    def backward(values, scalar, during):
-        sums = [None] * len(plan.chunks)
-
-        def multiply(group):
-            a, n = plan.pair_range(group)
-            sides = back(plan, where, group, order.after(values[a : a + n]), high, low)
-            for c, side in zip(plan.pairs[group], sides):
-                sums[c] = ClipSum(plan, side, plan.turns[c])
-            order.note(sides[-1][0])
+    def backward(values, scalar=None, during=None, under=None):
+        sides = back(plan, where, order.after(values), high, low)
+        sums = [ClipSum(plan, side, plan.turns[c]) for c, side in enumerate(sides)]
+        order.note(sides[-1][0])
+        result = None
 
         def go(*chunks):
             for c in chunks:
                 if not sums[c].done():
                     sums[c].advance(order)
 
-        multiply(0)
         if scalar is not None:
             scalar.advance(order)
-        go(0)
-        multiply(1)
+        go(0, 1)
         if scalar is not None:
             scalar.advance(order)
-        go(0, 1, 2)
-        multiply(2)
+        go(0, 1, 2, 3)
         if scalar is not None:
-            scalar.advance(order)
-        go(0, 2, 1, 3)
-        result = during(scalar.result(order)) if scalar is not None else None
-        go(0, 2, 1, 3, 2, 1, 0, 3)
+            result = during(scalar.result(order))
+        go(0, 1, 0, 1, 2, 3)
+        if under is not None:
+            result = under(result)
+        go(2, 3, 0, 1, 2, 3)
         return sums, go, result
 
     def forward(sums, go, step=None, direction=None):
@@ -558,16 +556,12 @@
             return out
 
         vectors = multiply(0)
-        go(3, 2, 1)
+        go(2, 3)
+        found[0].advance(order)
         vectors = multiply(1)
         found[0].advance(order)
-        go(3)
-        vectors = multiply(2)
+        found[1].advance(order)
         found[0].advance(order)
-        found[1].advance(order)
-        found[2].advance(order)
-        found[1].advance(order)
-        found[2].advance(order)
         tangents = [f.result(order) for f in found]
         inner = sum(t[-ROWS8 : 2 - ROWS8, 0] for t in tangents)
         return vectors, jnp.concatenate([t[:-ROWS8] for t in tangents], axis=0), inner
@@ -578,7 +572,7 @@
         order.note(bent)
         return bent, ScalarSum(plan, jnp.sum(bent * tangent))
 
-    sums, go, _ = backward(values, None, None)
+    sums, go, _ = backward(values)
     direction, tangent, inner = forward(sums, go)
     norm0 = inner[0]
     bent, curvature = bend(tangent)
@@ -590,15 +584,19 @@
     bent, curvature = bend(fresh + ratio * tangent)
     length = norm1 + 2.0 * ratio * cross + ratio * ratio * norm0
 
-    sums, go, step1 = backward(bent, curvature, lambda total: norm1 / (total + damping * length))
-    moved = order.after(weights) + (step0 + step1 * ratio) * direction + step1 * residual
-    order.note(moved)
-    go(3, 2, 1)
+    def under(step1):
+        moved = order.after(weights) + (step0 + step1 * ratio) * direction + step1 * residual
+        order.note(moved)
+        return step1, moved
+
+    sums, go, (step1, moved) = backward(
+        bent, curvature, lambda total: norm1 / (total + damping * length), under
+    )
     scalars, out = jnp.stack([step1, ratio]), None
     for group, members in enumerate(plan.pairs):
         pieces = [sums[c].pieces(order) for c in members]
-        if group == 1:
-            go(3)
+        if group == 0:
+            go(2, 3)
         out = last(plan, where, group, scalars, pieces, direction, residual, out)
         order.note(out)
     return moved, out

time: 589 us -> 587 us (level)
  waiting for transfers between devices: 185 us -> 260 us
  Pallas kernels: 222 us -> 157 us
  starting transfers between devices: 105 us -> 89.2 us
  other arithmetic: 37.6 us -> 44.4 us
    ppermute x102 -> x99, waiting for transfers between devices: 185 us -> 260 us  [swap(): return lax.ppermute(x, axis, [(i, i ^ stride) for i in range(size)])]
    pallas_call x9 -> x3, Pallas kernels: 93.4 us -> 50.1 us  [back(): pl.pallas_call(functools.partial(back_body, plan), out_shape=outs, grid_s...]
    pallas_call x6 -> x4, Pallas kernels: 83.4 us -> 60.3 us  [forth(): pl.pallas_call(functools.partial(forth_body, plan, pair, step is not None...]
    ppermute x102 -> x99, starting transfers between devices: 105 us -> 89.2 us  [swap(): return lax.ppermute(x, axis, [(i, i ^ stride) for i in range(size)])]
    pallas_call x2 -> x3, Pallas kernels: 27.9 us -> 31.4 us  [first(): pl.pallas_call(functools.partial(first_body, plan), out_shape=[jax.ShapeD...]
    pallas_call x3 -> x2, Pallas kernels: 16.9 us -> 14.9 us  [last(): pl.pallas_call(functools.partial(last_body, plan, pair, [piece.places for...]
    unnamed x56 -> x72, local copies, waits for them, and re-layouts: 12.4 us -> 11.8 us
  transfers between devices with their start and end apart: 102 -> 99, of which waited for: 46 -> 40; matrix products, arithmetic and copies ran while one was open for 7% -> 7% of each run, Pallas kernels for 30% -> 16%
where the time goes in v2:
time: 587 us; the launch traced here: 578 us
  waiting for transfers between devices  260 us (44%)
  Pallas kernels  157 us (27%)
  starting transfers between devices  89.2 us (15%)
  other arithmetic  44.4 us (8%)
  local copies, waits for them, and re-layouts  19.3 us (3%)
  between operations  8.33 us (1%)
    ppermute x99, waiting for transfers between devices, swap(): return lax.ppermute(x, axis, [(i, i ^ stride) for i in range(size)])  260 us
    ppermute x99, starting transfers between devices, swap(): return lax.ppermute(x, axis, [(i, i ^ stride) for i in range(size)])  89.2 us
    pallas_call x4, Pallas kernels, forth(): pl.pallas_call(functools.partial(forth_body, plan, pair, step is not None...  60.3 us
    pallas_call x3, Pallas kernels, back(): pl.pallas_call(functools.partial(back_body, plan), out_shape=outs, grid_s...  50.1 us
    pallas_call x3, Pallas kernels, first(): pl.pallas_call(functools.partial(first_body, plan), out_shape=[jax.ShapeD...  31.4 us
    pallas_call x2, Pallas kernels, last(): pl.pallas_call(functools.partial(last_body, plan, pair, [piece.places for...  14.9 us
    add x1, other arithmetic, under(): order.after(weights) + (step0 + step1 * ratio) * direction  13.9 us
    add x36, other arithmetic, advance(): self.own = self.kept + got  13.9 us
  transfers between devices with their start and end apart: 99, of which 40 were waited for; matrix products, arithmetic and copies ran while one was open for 7% of the time, Pallas kernels for 16%

profile of v2, /device:TPU:0, one launch (start us, length us, event | category | flops | bytes accessed | tf_op | source)
XLA Modules:
  0.0 578.1 jit_solution(13977844155860643485)
XLA Ops:
  0.7 10.5 %split_and_logits.3 = (bf16[768,5632]{1,0:T(8,128)(2,1)}, bf16[768,5632]{1,0:T(8,128)(2,1)}, f32[200,256]{1,0:T(8,128)S(1)}, f32[200,256]{1,0:T(8,128)S(1)}) custom-call(s32[3]{0:T(128)S(1)} %pad_add_fusion.s_ref, f32[768,5632]{1,0:T(8,128)} %f_ref.3, f32[400,5632]{1,0:T(8,128)} %w_ref.5), custom_call_target="tpu_custom_call" | custom-call | flops 3460300800 | bytes 20545536 | tf_op jit(solution)/shard_map/split_and_logits/pallas_call | solution.py:102
  11.2 3.0 collective-permute-start
  14.2 10.5 %split_and_logits.4 = (bf16[768,5632]{1,0:T(8,128)(2,1)}, bf16[768,5632]{1,0:T(8,128)(2,1)}, f32[200,256]{1,0:T(8,128)S(1)}, f32[200,256]{1,0:T(8,128)S(1)}) custom-call(s32[3]{0:T(128)S(1)} %pad_add_fusion.s_ref, f32[768,5632]{1,0:T(8,128)} %f_ref.3, f32[400,5632]{1,0:T(8,128)} %w_ref.5, ...), custom_call_target="tpu_custom_call", output_to_operand_aliasing={{0}: (3, {}), {1}: (4, {})} | custom-call | flops 3460300800 | bytes 20545536 | tf_op jit(solution)/shard_map/split_and_logits/pallas_call | solution.py:102
  24.7 3.1 collective-permute-start.1
  27.9 10.5 %split_and_logits.5 = (bf16[768,5632]{1,0:T(8,128)(2,1)}, bf16[768,5632]{1,0:T(8,128)(2,1)}, f32[200,256]{1,0:T(8,128)S(1)}, f32[200,256]{1,0:T(8,128)S(1)}) custom-call(s32[3]{0:T(128)S(1)} %pad_add_fusion.s_ref, f32[768,5632]{1,0:T(8,128)} %f_ref.3, f32[400,5632]{1,0:T(8,128)} %w_ref.5, ...), custom_call_target="tpu_custom_call", output_to_operand_aliasing={{0}: (3, {}), {1}: (4, {})} | custom-call | flops 3460300800 | bytes 20545536 | tf_op jit(solution)/shard_map/split_and_logits/pallas_call | solution.py:102
  38.4 1.6 collective-permute-start.3
  41.1 5.9 %collective-permute-done.3 = f32[200,256]{1,0:T(8,128)S(1)} collective-permute-done((f32[200,256]{1,0:T(8,128)S(1)}, f32[200,256]{1,0:T(8,128)S(1)}, u32[]{:S(2)}, u32[]{:S(2)}) %collective-permute-start.3) | collective-permute-done | bytes 204832 | tf_op jit(solution)/shard_map/ppermute | solution.py:62
  47.0 4.1 collective-permute-done.4
  51.2 2.0 collective-permute-start.6
  53.2 5.8 %collective-permute-done.5 = f32[200,256]{1,0:T(8,128)S(1)} collective-permute-done((f32[200,256]{1,0:T(8,128)S(1)}, f32[200,256]{1,0:T(8,128)S(1)}, u32[]{:S(2)}, u32[]{:S(2)}) %collective-permute-start.5) | collective-permute-done | bytes 204832 | tf_op jit(solution)/shard_map/ppermute | solution.py:62
  59.0 2.2 collective-permute-done.6
  61.5 9.8 %collective-permute-done.7 = f32[200,256]{1,0:T(8,128)S(1)} collective-permute-done((f32[200,256]{1,0:T(8,128)S(1)}, f32[200,256]{1,0:T(8,128)S(1)}, u32[]{:S(2)}, u32[]{:S(2)}) %collective-permute-start.7) | collective-permute-done | bytes 204832 | tf_op jit(solution)/shard_map/ppermute | solution.py:62
  71.7 5.8 collective-permute-done.8
  79.2 16.7 %back_all.3 = (f32[64,5632]{1,0:T(8,128)}, f32[64,5632]{1,0:T(8,128)}, f32[56,5632]{1,0:T(8,128)}, f32[56,5632]{1,0:T(8,128)}, f32[40,5632]{1,0:T(8,128)S(1)}, /...) custom-call(s32[3]{0:T(128)S(1)} %pad_add_fusion.s_ref, f32[400,768]{1,0:T(8,128)} %pad_maximum_fusion.7.g_ref, ...), custom_call_target="tpu_custom_call" | custom-call | flops 10380902400 | bytes 26312704 | tf_op jit(solution)/shard_map/back_all/pallas_call | solution.py:149
  96.4 2.9 collective-permute-done.9
  104.7 14.6 %collective-permute-done.10 = f32[64,2816]{1,0:T(8,128)S(1)} collective-permute-done((f32[64,2816]{1,0:T(8,128)S(1)}, f32[64,2816]{1,0:T(8,128)S(1)}, u32[]{:S(2)}, u32[]{:S(2)}) %collective-permute-start.10) | collective-permute-done | bytes 720928 | tf_op jit(solution)/shard_map/ppermute | solution.py:62
  124.5 6.4 %collective-permute-done.12 = f32[64,1408]{1,0:T(8,128)S(1)} collective-permute-done((f32[64,1408]{1,0:T(8,128)S(1)}, f32[64,1408]{1,0:T(8,128)S(1)}, u32[]{:S(2)}, u32[]{:S(2)}) %collective-permute-start.12) | collective-permute-done | bytes 360480 | tf_op jit(solution)/shard_map/ppermute | solution.py:62
  133.8 12.6 %collective-permute-done.16.refs_1_ = f32[64,1408]{1,0:T(8,128)S(1)} collective-permute-done((f32[64,1408]{1,0:T(8,128)S(1)}, f32[64,1408]{1,0:T(8,128)S(1)}, u32[]{:S(2)}, u32[]{:S(2)}) %collective-permute-start.16) | collective-permute-done | bytes 360480 | tf_op jit(solution)/shard_map/ppermute | solution.py:62
  151.0 16.0 %collective-permute-done.23 = f32[40,1408]{1,0:T(8,128)S(1)} collective-permute-done((f32[40,1408]{1,0:T(8,128)S(1)}, f32[40,1408]{1,0:T(8,128)S(1)}, u32[]{:S(2)}, u32[]{:S(2)}) %collective-permute-start.23) | collective-permute-done | bytes 225312 | tf_op jit(solution)/shard_map/ppermute | solution.py:62
  172.2 4.7 collective-permute-done.26.refs_1_
  182.2 14.8 %forth_pair.4 = (f32[400,5632]{1,0:T(8,128)}, f32[248,384]{1,0:T(8,128)S(1)}, f32[248,384]{1,0:T(8,128)}) custom-call(s32[3]{0:T(128)S(1)} %pad_add_fusion.s_ref, f32[64,1408]{1,0:T(8,128)S(1)} %slice_add_fusion.8.refs_0_, f32[64,1408]{1,0:T(8,128)S(1)} %collective-permute-done.16.refs_1_, f32[64,2816]{1,0:T(8,128)} %copy-done.27, f32[64,5632]{1,0:T(8,128)} %copy-done.32, ...), custom_call_target="tpu_custom_call" | custom-call | flops 6228541440 | bytes 33521664 | tf_op jit(solution)/shard_map/forth_pair/pallas_call | solution.py:285
  198.0 10.6 %collective-permute-done.29 = f32[248,384]{1,0:T(8,128)S(1)} collective-permute-done((f32[248,384]{1,0:T(8,128)S(1)}, f32[248,384]{1,0:T(8,128)S(1)}, u32[]{:S(2)}, u32[]{:S(2)}) %collective-permute-start.29) | collective-permute-done | bytes 380960 | tf_op jit(solution)/shard_map/ppermute | solution.py:62
  210.0 13.8 %forth_pair.5 = (f32[400,5632]{1,0:T(8,128)}, f32[168,384]{1,0:T(8,128)S(1)}, f32[168,384]{1,0:T(8,128)S(1)}) custom-call(s32[3]{0:T(128)S(1)} %pad_add_fusion.s_ref, f32[40,1408]{1,0:T(8,128)S(1)} %slice_add_fusion.16.refs_0_, f32[40,1408]{1,0:T(8,128)S(1)} %collective-permute-done.26.refs_1_, ...), custom_call_target="tpu_custom_call", output_to_operand_aliasing={{0}: (11, {})} | custom-call | flops 4152360960 | bytes 28114944 | tf_op jit(solution)/shard_map/forth_pair/pallas_call | solution.py:285
  225.3 2.3 collective-permute-done.32
  227.7 5.4 collective-permute-done.36
  233.1 2.8 collective-permute-start.37
  236.0 10.0 %collective-permute-done.35 = f32[248,384]{1,0:T(8,128)S(1)} collective-permute-done((f32[248,384]{1,0:T(8,128)S(1)}, f32[248,384]{1,0:T(8,128)S(1)}, u32[]{:S(2)}, u32[]{:S(2)}) %collective-permute-start.35) | collective-permute-done | bytes 380960 | tf_op jit(solution)/shard_map/ppermute | solution.py:62
  246.0 1.7 collective-permute-done.37
  248.0 6.3 %collective-permute-done.38 = f32[168,384]{1,0:T(8,128)S(1)} collective-permute-done((f32[168,384]{1,0:T(8,128)S(1)}, f32[168,384]{1,0:T(8,128)S(1)}, u32[]{:S(2)}, u32[]{:S(2)}) %collective-permute-start.38) | collective-permute-done | bytes 258080 | tf_op jit(solution)/shard_map/ppermute | solution.py:62
  254.6 1.9 multiply_reduce_fusion.1
  256.5 16.7 %back_all.4 = (f32[64,5632]{1,0:T(8,128)}, f32[64,5632]{1,0:T(8,128)}, f32[56,5632]{1,0:T(8,128)}, f32[56,5632]{1,0:T(8,128)}, f32[40,5632]{1,0:T(8,128)S(1)}, /...) custom-call(s32[3]{0:T(128)S(1)} %pad_add_fusion.s_ref, f32[400,768]{1,0:T(8,128)} %get-tuple-element.222.g_ref, ...), custom_call_target="tpu_custom_call" | custom-call | flops 10380902400 | bytes 26312704 | tf_op jit(solution)/shard_map/back_all/pallas_call | solution.py:149
  274.4 2.0 collective-permute-done.39
  282.2 14.8 %collective-permute-done.40 = f32[8,128]{1,0:T(8,128)S(1)} collective-permute-done((f32[8,128]{1,0:T(8,128)S(1)}, f32[8,128]{1,0:T(8,128)S(1)}, u32[]{:S(2)}, u32[]{:S(2)}) %collective-permute-start.40) | collective-permute-done | bytes 4128 | tf_op jit(solution)/shard_map/ppermute | solution.py:62
  303.3 6.5 %collective-permute-done.48 = f32[64,1408]{1,0:T(8,128)S(1)} collective-permute-done((f32[64,1408]{1,0:T(8,128)S(1)}, f32[64,1408]{1,0:T(8,128)S(1)}, u32[]{:S(2)}, u32[]{:S(2)}) %collective-permute-start.48) | collective-permute-done | bytes 360480 | tf_op jit(solution)/shard_map/ppermute | solution.py:62
  312.2 13.1 %collective-permute-done.49.refs_2_ = f32[64,1408]{1,0:T(8,128)S(1)} collective-permute-done((f32[64,1408]{1,0:T(8,128)S(1)}, f32[64,1408]{1,0:T(8,128)S(1)}, u32[]{:S(2)}, u32[]{:S(2)}) %collective-permute-start.49) | collective-permute-done | bytes 360480 | tf_op jit(solution)/shard_map/ppermute | solution.py:62
  329.8 15.6 %collective-permute-done.56 = f32[40,1408]{1,0:T(8,128)S(1)} collective-permute-done((f32[40,1408]{1,0:T(8,128)S(1)}, f32[40,1408]{1,0:T(8,128)S(1)}, u32[]{:S(2)}, u32[]{:S(2)}) %collective-permute-start.56) | collective-permute-done | bytes 225312 | tf_op jit(solution)/shard_map/ppermute | solution.py:62
  354.6 2.4 collective-permute-done.59.refs_2_
  358.3 4.2 collective-permute-done.58.refs_6_
  363.1 16.5 %forth_pair.6 = (f32[400,5632]{1,0:T(8,128)}, f32[248,384]{1,0:T(8,128)S(1)}, f32[248,384]{1,0:T(8,128)}) custom-call(s32[3]{0:T(128)S(1)} %pad_add_fusion.s_ref, f32[1]{0:T(128)} %bitcast.5.refs_0_, f32[64,1408]{1,0:T(8,128)S(1)} %slice_add_fusion.7.refs_1_, f32[64,1408]{1,0:T(8,128)S(1)} %collective-permute-done.49.refs_2_, f32[64,2816]{1,0:T(8,128)} %copy-done.6, ...), custom_call_target="tpu_custom_call" | custom-call | flops 6228541440 | bytes 33521664 | tf_op jit(solution)/shard_map/forth_pair/pallas_call | solution.py:285
  380.6 10.6 %collective-permute-done.62 = f32[248,384]{1,0:T(8,128)S(1)} collective-permute-done((f32[248,384]{1,0:T(8,128)S(1)}, f32[248,384]{1,0:T(8,128)S(1)}, u32[]{:S(2)}, u32[]{:S(2)}) %collective-permute-start.62) | collective-permute-done | bytes 380960 | tf_op jit(solution)/shard_map/ppermute | solution.py:62
  392.6 15.1 %forth_pair.7 = (f32[400,5632]{1,0:T(8,128)}, f32[168,384]{1,0:T(8,128)S(1)}, f32[168,384]{1,0:T(8,128)S(1)}) custom-call(s32[3]{0:T(128)S(1)} %pad_add_fusion.s_ref, f32[1]{0:T(128)} %bitcast.5.refs_0_, f32[40,1408]{1,0:T(8,128)S(1)} %slice_add_fusion.14.refs_1_, f32[40,1408]{1,0:T(8,128)S(1)} %collective-permute-done.59.refs_2_, ...), custom_call_target="tpu_custom_call", output_to_operand_aliasing={{0}: (13, {})} | custom-call | flops 4152360960 | bytes 28114944 | tf_op jit(solution)/shard_map/forth_pair/pallas_call | solution.py:285
  410.2 6.6 %collective-permute-done.69 = f32[168,384]{1,0:T(8,128)S(1)} collective-permute-done((f32[168,384]{1,0:T(8,128)S(1)}, f32[168,384]{1,0:T(8,128)S(1)}, u32[]{:S(2)}, u32[]{:S(2)}) %collective-permute-start.69) | collective-permute-done | bytes 258080 | tf_op jit(solution)/shard_map/ppermute | solution.py:62
  416.9 3.0 collective-permute-start.70
  419.9 9.4 %collective-permute-done.68 = f32[248,384]{1,0:T(8,128)S(1)} collective-permute-done((f32[248,384]{1,0:T(8,128)S(1)}, f32[248,384]{1,0:T(8,128)S(1)}, u32[]{:S(2)}, u32[]{:S(2)}) %collective-permute-start.68) | collective-permute-done | bytes 380960 | tf_op jit(solution)/shard_map/ppermute | solution.py:62
  429.3 2.2 collective-permute-start.71
  431.6 4.7 collective-permute-done.71
  440.4 2.0 multiply_reduce_fusion
  442.4 16.7 %back_all.5 = (f32[64,5632]{1,0:T(8,128)}, f32[64,5632]{1,0:T(8,128)}, f32[56,5632]{1,0:T(8,128)}, f32[56,5632]{1,0:T(8,128)}, f32[40,5632]{1,0:T(8,128)S(1)}, /...) custom-call(s32[3]{0:T(128)S(1)} %pad_add_fusion.s_ref, f32[400,768]{1,0:T(8,128)} %get-tuple-element.270.g_ref, ...), custom_call_target="tpu_custom_call" | custom-call | flops 10380902400 | bytes 26312704 | tf_op jit(solution)/shard_map/back_all/pallas_call | solution.py:149
  460.4 1.9 collective-permute-done.76
  469.9 1.8 add.253
  471.7 1.7 collective-permute-start.77
  473.4 10.6 %collective-permute-done.79 = f32[8,128]{1,0:T(8,128)S(1)} collective-permute-done((f32[8,128]{1,0:T(8,128)S(1)}, f32[8,128]{1,0:T(8,128)S(1)}, u32[]{:S(2)}, u32[]{:S(2)}) %collective-permute-start.79) | collective-permute-done | bytes 4128 | tf_op jit(solution)/shard_map/ppermute | solution.py:62
  484.6 1.7 collective-permute-start.84
  494.4 1.6 collective-permute-start.80
  497.8 3.0 collective-permute-done.83
  504.7 11.3 %collective-permute-done.86.refs_1_ = f32[64,1408]{1,0:T(8,128)S(1)} collective-permute-done((f32[64,1408]{1,0:T(8,128)S(1)}, f32[64,1408]{1,0:T(8,128)S(1)}, u32[]{:S(2)}, u32[]{:S(2)}) %collective-permute-start.86) | collective-permute-done | bytes 360480 | tf_op jit(solution)/shard_map/ppermute | solution.py:62
  522.6 13.9 %multiply_add_fusion = f32[400,5632]{1,0:T(8,128)} fusion(f32[400,5632]{1,0:T(8,128)} %get-tuple-element.295.refs_9_, f32[400,5632]{1,0:T(8,128)} %w_ref.5, f32[400,5632]{1,0:T(8,128)} %get-tuple-element.254.refs_9_.refs_8_, f32[]{:T(128)} %div.82, f32[]{:T(128)S(6)} %add.267), kind=kLoop, calls=%fused_computation | loop fusion | flops 9011200 | bytes 36044808 | tf_op jit(solution)/shard_map/add | solution.py:588
  538.4 3.7 collective-permute-done.90.refs_2_
  543.1 2.0 collective-permute-start.92
  546.9 2.4 collective-permute-start.97
  549.4 4.8 collective-permute-done.92.refs_2_
  554.2 3.7 collective-permute-done.97.refs_6_
  560.9 8.5 %last_rows.2.refs_10_ = f32[400,5632]{1,0:T(8,128)} custom-call(s32[3]{0:T(128)S(1)} %pad_add_fusion.s_ref, f32[2]{0:T(128)S(1)} %pad_maximum_fusion.33.scalar_ref, f32[64,1408]{1,0:T(8,128)S(1)} %slice_add_fusion.6.refs_0_, f32[64,1408]{1,0:T(8,128)S(1)} %collective-permute-done.86.refs_1_, f32[64,2816]{1,0:T(8,128)} %copy-done.7, f32[64,5632]{1,0:T(8,128)} %copy-done.13, ...), custom_call_target="tpu_custom_call" | custom-call | flops 8110080 | bytes 21626880 | tf_op jit(solution)/shard_map/last_rows/pallas_call | solution.py:355
  571.2 6.4 %last_rows.3 = f32[400,5632]{1,0:T(8,128)} custom-call(s32[3]{0:T(128)S(1)} %pad_add_fusion.s_ref, f32[2]{0:T(128)S(1)} %pad_maximum_fusion.33.scalar_ref, f32[40,1408]{1,0:T(8,128)S(1)} %slice_add_fusion.13.refs_0_, f32[40,1408]{1,0:T(8,128)S(1)} %collective-permute-done.88.refs_1_, ...), custom_call_target="tpu_custom_call", output_to_operand_aliasing={{}: (12, {})} | custom-call | flops 5406720 | bytes 14417920 | tf_op jit(solution)/shard_map/last_rows/pallas_call | solution.py:355
  (361 shorter events, 110.6 us)
Async XLA Ops:
  11.2 13.5 %collective-permute-start = (f32[200,256]{1,0:T(8,128)S(1)}, f32[200,256]{1,0:T(8,128)S(1)}, u32[]{:S(2)}, u32[]{:S(2)}) collective-permute-start(f32[200,256]{1,0:T(8,128)S(1)} %get-tuple-element.156), channel_id=1, source_target_pairs={{0,1},{1,0},{2,3},{3,2},{4,5},{5,4},{6,7},{7,6},{8,9},{9,8},{10,11... | collective-permute-start | bytes 614408 | tf_op jit(solution)/shard_map/ppermute | solution.py:62
  24.7 13.6 %collective-permute-start.2 = (f32[200,256]{1,0:T(8,128)S(1)}, f32[200,256]{1,0:T(8,128)S(1)}, u32[]{:S(2)}, u32[]{:S(2)}) collective-permute-start(f32[200,256]{1,0:T(8,128)S(1)} %get-tuple-element.160), channel_id=1, source_target_pairs={{0,1},{1,0},{2,3},{3,2},{4,5},{5,4},{6,7},{7,6},{8,9},{9,8},{10,11... | collective-permute-start | bytes 614408 | tf_op jit(solution)/shard_map/ppermute | solution.py:62
  24.7 13.6 %collective-permute-start.1 = (f32[200,256]{1,0:T(8,128)S(1)}, f32[200,256]{1,0:T(8,128)S(1)}, u32[]{:S(2)}, u32[]{:S(2)}) collective-permute-start(f32[200,256]{1,0:T(8,128)S(1)} %add.206), channel_id=1, source_target_pairs={{0,2},{1,3},{2,0},{3,1},{4,6},{5,7},{6,4},{7,5},{8,10},{9,11},{10,... | collective-permute-start | bytes 614408 | tf_op jit(solution)/shard_map/ppermute | solution.py:62
  101.0 18.2 %collective-permute-start.10 = (f32[64,2816]{1,0:T(8,128)S(1)}, f32[64,2816]{1,0:T(8,128)S(1)}, u32[]{:S(2)}, u32[]{:S(2)}) collective-permute-start(f32[64,2816]{1,0:T(8,128)S(1)} %pad_maximum_fusion.15), channel_id=1, source_target_pairs={{0,8},{4,12},{8,0},{12,4},{16,24},{20,28},{24,16},{28,20},{1,9},{5... | collective-permute-start | bytes 2162696 | tf_op jit(solution)/shard_map/ppermute | solution.py:62
  102.4 20.1 %collective-permute-start.14 = (f32[40,5632]{1,0:T(8,128)S(1)}, f32[40,5632]{1,0:T(8,128)S(1)}, u32[]{:S(2)}, u32[]{:S(2)}) collective-permute-start(f32[40,5632]{1,0:T(8,128)S(1)} %get-tuple-element.189), channel_id=1, source_target_pairs={{0,4},{4,0},{8,12},{12,8},{16,20},{20,16},{24,28},{28,24},{1,5},{5... | collective-permute-start | bytes 2703368 | tf_op jit(solution)/shard_map/ppermute | solution.py:62
  102.4 20.9 %collective-permute-start.13 = (f32[40,5632]{1,0:T(8,128)S(1)}, f32[40,5632]{1,0:T(8,128)S(1)}, u32[]{:S(2)}, u32[]{:S(2)}) collective-permute-start(f32[40,5632]{1,0:T(8,128)S(1)} %copy-done.35), channel_id=1, source_target_pairs={{0,4},{4,0},{8,12},{12,8},{16,20},{20,16},{24,28},{28,24},{1,5},{5... | collective-permute-start | bytes 2703368 | tf_op jit(solution)/shard_map/ppermute | solution.py:62
  103.1 17.7 %collective-permute-start.15 = (f32[56,2816]{1,0:T(8,128)S(1)}, f32[56,2816]{1,0:T(8,128)S(1)}, u32[]{:S(2)}, u32[]{:S(2)}) collective-permute-start(f32[56,2816]{1,0:T(8,128)S(1)} %slice.311), channel_id=1, source_target_pairs={{0,16},{4,20},{8,24},{12,28},{16,0},{20,4},{24,8},{28,12},{1,17},{... | collective-permute-start | bytes 1892360 | tf_op jit(solution)/shard_map/ppermute | solution.py:62
  119.4 11.4 %collective-permute-start.12 = (f32[64,1408]{1,0:T(8,128)S(1)}, f32[64,1408]{1,0:T(8,128)S(1)}, u32[]{:S(2)}, u32[]{:S(2)}) collective-permute-start(f32[64,1408]{1,0:T(8,128)S(1)} %slice.313), channel_id=1, source_target_pairs={{0,16},{4,20},{8,24},{12,28},{16,0},{20,4},{24,8},{28,12},{1,17},{... | collective-permute-start | bytes 1081352 | tf_op jit(solution)/shard_map/ppermute | solution.py:62
  122.7 26.8 %collective-permute-start.20 = (f32[40,2816]{1,0:T(8,128)S(1)}, f32[40,2816]{1,0:T(8,128)S(1)}, u32[]{:S(2)}, u32[]{:S(2)}) collective-permute-start(f32[40,2816]{1,0:T(8,128)S(1)} %pad_maximum_fusion.24), channel_id=1, source_target_pairs={{0,8},{4,12},{8,0},{12,4},{16,24},{20,28},{24,16},{28,20},{1,9},{5... | collective-permute-start | bytes 1351688 | tf_op jit(solution)/shard_map/ppermute | solution.py:62
  123.9 26.3 %collective-permute-start.19 = (f32[40,2816]{1,0:T(8,128)S(1)}, f32[40,2816]{1,0:T(8,128)S(1)}, u32[]{:S(2)}, u32[]{:S(2)}) collective-permute-start(f32[40,2816]{1,0:T(8,128)S(1)} %slice.318), channel_id=1, source_target_pairs={{0,16},{4,20},{8,24},{12,28},{16,0},{20,4},{24,8},{28,12},{1,17},{... | collective-permute-start | bytes 1351688 | tf_op jit(solution)/shard_map/ppermute | solution.py:62
  130.9 15.6 %collective-permute-start.16 = (f32[64,1408]{1,0:T(8,128)S(1)}, f32[64,1408]{1,0:T(8,128)S(1)}, u32[]{:S(2)}, u32[]{:S(2)}) collective-permute-start(f32[64,1408]{1,0:T(8,128)S(1)} %slice_add_fusion.8.refs_0_), channel_id=1, source_target_pairs={{0,16},{4,20},{8,24},{12,28},{16,0},{20,4},{24,8},{28,12},{1,17},{... | collective-permute-start | bytes 1081352 | tf_op jit(solution)/shard_map/ppermute | solution.py:62
  132.3 15.6 %collective-permute-start.21 = (f32[56,1408]{1,0:T(8,128)S(1)}, f32[56,1408]{1,0:T(8,128)S(1)}, u32[]{:S(2)}, u32[]{:S(2)}) collective-permute-start(f32[56,1408]{1,0:T(8,128)S(1)} %slice_add_fusion.11.refs_4_), channel_id=1, source_target_pairs={{0,8},{4,12},{8,0},{12,4},{16,24},{20,28},{24,16},{28,20},{1,9},{5... | collective-permute-start | bytes 946184 | tf_op jit(solution)/shard_map/ppermute | solution.py:62
  146.5 21.4 %collective-permute-start.18 = (f32[64,2816]{1,0:T(8,128)S(1)}, f32[64,2816]{1,0:T(8,128)S(1)}, u32[]{:S(2)}, u32[]{:S(2)}) collective-permute-start(f32[64,2816]{1,0:T(8,128)S(1)} %pad_maximum_fusion.16), channel_id=1, source_target_pairs={{0,8},{4,12},{8,0},{12,4},{16,24},{20,28},{24,16},{28,20},{1,9},{5... | collective-permute-start | bytes 2162696 | tf_op jit(solution)/shard_map/ppermute | solution.py:62
  147.9 20.9 %collective-permute-start.27 = (f32[56,2816]{1,0:T(8,128)S(1)}, f32[56,2816]{1,0:T(8,128)S(1)}, u32[]{:S(2)}, u32[]{:S(2)}) collective-permute-start(f32[56,2816]{1,0:T(8,128)S(1)} %pad_maximum_fusion.21), channel_id=1, source_target_pairs={{0,16},{4,20},{8,24},{12,28},{16,0},{20,4},{24,8},{28,12},{1,17},{... | collective-permute-start | bytes 1892360 | tf_op jit(solution)/shard_map/ppermute | solution.py:62
  149.6 17.4 %collective-permute-start.23 = (f32[40,1408]{1,0:T(8,128)S(1)}, f32[40,1408]{1,0:T(8,128)S(1)}, u32[]{:S(2)}, u32[]{:S(2)}) collective-permute-start(f32[40,1408]{1,0:T(8,128)S(1)} %slice.323), channel_id=1, source_target_pairs={{0,16},{4,20},{8,24},{12,28},{16,0},{20,4},{24,8},{28,12},{1,17},{... | collective-permute-start | bytes 675848 | tf_op jit(solution)/shard_map/ppermute | solution.py:62
  150.2 17.6 %collective-permute-start.22 = (f32[40,1408]{1,0:T(8,128)S(1)}, f32[40,1408]{1,0:T(8,128)S(1)}, u32[]{:S(2)}, u32[]{:S(2)}) collective-permute-start(f32[40,1408]{1,0:T(8,128)S(1)} %slice.325), channel_id=1, source_target_pairs={{0,8},{4,12},{8,0},{12,4},{16,24},{20,28},{24,16},{28,20},{1,9},{5... | collective-permute-start | bytes 675848 | tf_op jit(solution)/shard_map/ppermute | solution.py:62
  177.0 20.0 %collective-permute-start.31 = (f32[40,2816]{1,0:T(8,128)S(1)}, f32[40,2816]{1,0:T(8,128)S(1)}, u32[]{:S(2)}, u32[]{:S(2)}) collective-permute-start(f32[40,2816]{1,0:T(8,128)S(1)} %pad_maximum_fusion.25), channel_id=1, source_target_pairs={{0,8},{4,12},{8,0},{12,4},{16,24},{20,28},{24,16},{28,20},{1,9},{5... | collective-permute-start | bytes 1351688 | tf_op jit(solution)/shard_map/ppermute | solution.py:62
  178.3 18.7 %collective-permute-start.30 = (f32[40,2816]{1,0:T(8,128)S(1)}, f32[40,2816]{1,0:T(8,128)S(1)}, u32[]{:S(2)}, u32[]{:S(2)}) collective-permute-start(f32[40,2816]{1,0:T(8,128)S(1)} %pad_maximum_fusion.26), channel_id=1, source_target_pairs={{0,16},{4,20},{8,24},{12,28},{16,0},{20,4},{24,8},{28,12},{1,17},{... | collective-permute-start | bytes 1351688 | tf_op jit(solution)/shard_map/ppermute | solution.py:62
  197.2 11.6 %collective-permute-start.34 = (f32[40,5632]{1,0:T(8,128)S(1)}, f32[40,5632]{1,0:T(8,128)S(1)}, u32[]{:S(2)}, u32[]{:S(2)}) collective-permute-start(f32[40,5632]{1,0:T(8,128)S(1)} %pad_maximum_fusion.10), channel_id=1, source_target_pairs={{0,4},{4,0},{8,12},{12,8},{16,20},{20,16},{24,28},{28,24},{1,5},{5... | collective-permute-start | bytes 2703368 | tf_op jit(solution)/shard_map/ppermute | solution.py:62
  197.2 11.5 %collective-permute-start.33 = (f32[40,5632]{1,0:T(8,128)S(1)}, f32[40,5632]{1,0:T(8,128)S(1)}, u32[]{:S(2)}, u32[]{:S(2)}) collective-permute-start(f32[40,5632]{1,0:T(8,128)S(1)} %pad_maximum_fusion.9), channel_id=1, source_target_pairs={{0,4},{4,0},{8,12},{12,8},{16,20},{20,16},{24,28},{28,24},{1,5},{5... | collective-permute-start | bytes 2703368 | tf_op jit(solution)/shard_map/ppermute | solution.py:62
  208.6 18.9 %collective-permute-start.32 = (f32[248,384]{1,0:T(8,128)S(1)}, f32[248,384]{1,0:T(8,128)S(1)}, u32[]{:S(2)}, u32[]{:S(2)}) collective-permute-start(f32[248,384]{1,0:T(8,128)S(1)} %add.224), channel_id=1, source_target_pairs={{0,2},{1,3},{2,0},{3,1},{4,6},{5,7},{6,4},{7,5},{8,10},{9,11},{10,... | collective-permute-start | bytes 1142792 | tf_op jit(solution)/shard_map/ppermute | solution.py:62
  227.6 18.4 %collective-permute-start.35 = (f32[248,384]{1,0:T(8,128)S(1)}, f32[248,384]{1,0:T(8,128)S(1)}, u32[]{:S(2)}, u32[]{:S(2)}) collective-permute-start(f32[248,384]{1,0:T(8,128)S(1)} %add.225), channel_id=1, source_target_pairs={{0,1},{1,0},{2,3},{3,2},{4,5},{5,4},{6,7},{7,6},{8,9},{9,8},{10,11... | collective-permute-start | bytes 1142792 | tf_op jit(solution)/shard_map/ppermute | solution.py:62
  233.1 14.6 %collective-permute-start.37 = (f32[168,384]{1,0:T(8,128)S(1)}, f32[168,384]{1,0:T(8,128)S(1)}, u32[]{:S(2)}, u32[]{:S(2)}) collective-permute-start(f32[168,384]{1,0:T(8,128)S(1)} %add.226), channel_id=1, source_target_pairs={{0,2},{1,3},{2,0},{3,1},{4,6},{5,7},{6,4},{7,5},{8,10},{9,11},{10,... | collective-permute-start | bytes 774152 | tf_op jit(solution)/shard_map/ppermute | solution.py:62
  278.7 19.5 %collective-permute-start.47 = (f32[64,2816]{1,0:T(8,128)S(1)}, f32[64,2816]{1,0:T(8,128)S(1)}, u32[]{:S(2)}, u32[]{:S(2)}) collective-permute-start(f32[64,2816]{1,0:T(8,128)S(1)} %pad_maximum_fusion.17), channel_id=1, source_target_pairs={{0,8},{4,12},{8,0},{12,4},{16,24},{20,28},{24,16},{28,20},{1,9},{5... | collective-permute-start | bytes 2162696 | tf_op jit(solution)/shard_map/ppermute | solution.py:62
  279.4 17.6 %collective-permute-start.40 = (f32[8,128]{1,0:T(8,128)S(1)}, f32[8,128]{1,0:T(8,128)S(1)}, u32[]{:S(2)}, u32[]{:S(2)}) collective-permute-start(f32[8,128]{1,0:T(8,128)S(1)} %broadcast_add_fusion.1), channel_id=1, source_target_pairs={{0,8},{4,12},{8,0},{12,4},{16,24},{20,28},{24,16},{28,20},{1,9},{5... | collective-permute-start | bytes 12296 | tf_op jit(solution)/shard_map/ppermute | solution.py:62
  280.8 19.9 %collective-permute-start.45 = (f32[40,5632]{1,0:T(8,128)S(1)}, f32[40,5632]{1,0:T(8,128)S(1)}, u32[]{:S(2)}, u32[]{:S(2)}) collective-permute-start(f32[40,5632]{1,0:T(8,128)S(1)} %get-tuple-element.234), channel_id=1, source_target_pairs={{0,4},{4,0},{8,12},{12,8},{16,20},{20,16},{24,28},{28,24},{1,5},{5... | collective-permute-start | bytes 2703368 | tf_op jit(solution)/shard_map/ppermute | solution.py:62
  280.8 21.6 %collective-permute-start.44 = (f32[40,5632]{1,0:T(8,128)S(1)}, f32[40,5632]{1,0:T(8,128)S(1)}, u32[]{:S(2)}, u32[]{:S(2)}) collective-permute-start(f32[40,5632]{1,0:T(8,128)S(1)} %copy-done.34), channel_id=1, source_target_pairs={{0,4},{4,0},{8,12},{12,8},{16,20},{20,16},{24,28},{28,24},{1,5},{5... | collective-permute-start | bytes 2703368 | tf_op jit(solution)/shard_map/ppermute | solution.py:62
  281.6 18.4 %collective-permute-start.46 = (f32[56,2816]{1,0:T(8,128)S(1)}, f32[56,2816]{1,0:T(8,128)S(1)}, u32[]{:S(2)}, u32[]{:S(2)}) collective-permute-start(f32[56,2816]{1,0:T(8,128)S(1)} %slice.333), channel_id=1, source_target_pairs={{0,16},{4,20},{8,24},{12,28},{16,0},{20,4},{24,8},{28,12},{1,17},{... | collective-permute-start | bytes 1892360 | tf_op jit(solution)/shard_map/ppermute | solution.py:62
  298.4 11.4 %collective-permute-start.48 = (f32[64,1408]{1,0:T(8,128)S(1)}, f32[64,1408]{1,0:T(8,128)S(1)}, u32[]{:S(2)}, u32[]{:S(2)}) collective-permute-start(f32[64,1408]{1,0:T(8,128)S(1)} %slice.337), channel_id=1, source_target_pairs={{0,16},{4,20},{8,24},{12,28},{16,0},{20,4},{24,8},{28,12},{1,17},{... | collective-permute-start | bytes 1081352 | tf_op jit(solution)/shard_map/ppermute | solution.py:62
  301.0 26.6 %collective-permute-start.53 = (f32[40,2816]{1,0:T(8,128)S(1)}, f32[40,2816]{1,0:T(8,128)S(1)}, u32[]{:S(2)}, u32[]{:S(2)}) collective-permute-start(f32[40,2816]{1,0:T(8,128)S(1)} %pad_maximum_fusion.27), channel_id=1, source_target_pairs={{0,8},{4,12},{8,0},{12,4},{16,24},{20,28},{24,16},{28,20},{1,9},{5... | collective-permute-start | bytes 1351688 | tf_op jit(solution)/shard_map/ppermute | solution.py:62
  302.6 26.1 %collective-permute-start.52 = (f32[40,2816]{1,0:T(8,128)S(1)}, f32[40,2816]{1,0:T(8,128)S(1)}, u32[]{:S(2)}, u32[]{:S(2)}) collective-permute-start(f32[40,2816]{1,0:T(8,128)S(1)} %slice.341), channel_id=1, source_target_pairs={{0,16},{4,20},{8,24},{12,28},{16,0},{20,4},{24,8},{28,12},{1,17},{... | collective-permute-start | bytes 1351688 | tf_op jit(solution)/shard_map/ppermute | solution.py:62
  309.9 15.4 %collective-permute-start.49 = (f32[64,1408]{1,0:T(8,128)S(1)}, f32[64,1408]{1,0:T(8,128)S(1)}, u32[]{:S(2)}, u32[]{:S(2)}) collective-permute-start(f32[64,1408]{1,0:T(8,128)S(1)} %slice_add_fusion.7.refs_1_), channel_id=1, source_target_pairs={{0,16},{4,20},{8,24},{12,28},{16,0},{20,4},{24,8},{28,12},{1,17},{... | collective-permute-start | bytes 1081352 | tf_op jit(solution)/shard_map/ppermute | solution.py:62
  311.5 15.0 %collective-permute-start.54 = (f32[56,1408]{1,0:T(8,128)S(1)}, f32[56,1408]{1,0:T(8,128)S(1)}, u32[]{:S(2)}, u32[]{:S(2)}) collective-permute-start(f32[56,1408]{1,0:T(8,128)S(1)} %slice_add_fusion.10.refs_5_), channel_id=1, source_target_pairs={{0,8},{4,12},{8,0},{12,4},{16,24},{20,28},{24,16},{28,20},{1,9},{5... | collective-permute-start | bytes 946184 | tf_op jit(solution)/shard_map/ppermute | solution.py:62
  325.3 21.1 %collective-permute-start.51 = (f32[64,2816]{1,0:T(8,128)S(1)}, f32[64,2816]{1,0:T(8,128)S(1)}, u32[]{:S(2)}, u32[]{:S(2)}) collective-permute-start(f32[64,2816]{1,0:T(8,128)S(1)} %pad_maximum_fusion.18), channel_id=1, source_target_pairs={{0,8},{4,12},{8,0},{12,4},{16,24},{20,28},{24,16},{28,20},{1,9},{5... | collective-permute-start | bytes 2162696 | tf_op jit(solution)/shard_map/ppermute | solution.py:62
  326.5 21.2 %collective-permute-start.60 = (f32[56,2816]{1,0:T(8,128)S(1)}, f32[56,2816]{1,0:T(8,128)S(1)}, u32[]{:S(2)}, u32[]{:S(2)}) collective-permute-start(f32[56,2816]{1,0:T(8,128)S(1)} %pad_maximum_fusion.22), channel_id=1, source_target_pairs={{0,16},{4,20},{8,24},{12,28},{16,0},{20,4},{24,8},{28,12},{1,17},{... | collective-permute-start | bytes 1892360 | tf_op jit(solution)/shard_map/ppermute | solution.py:62
  327.7 17.7 %collective-permute-start.56 = (f32[40,1408]{1,0:T(8,128)S(1)}, f32[40,1408]{1,0:T(8,128)S(1)}, u32[]{:S(2)}, u32[]{:S(2)}) collective-permute-start(f32[40,1408]{1,0:T(8,128)S(1)} %slice.347), channel_id=1, source_target_pairs={{0,16},{4,20},{8,24},{12,28},{16,0},{20,4},{24,8},{28,12},{1,17},{... | collective-permute-start | bytes 675848 | tf_op jit(solution)/shard_map/ppermute | solution.py:62
  328.8 17.5 %collective-permute-start.55 = (f32[40,1408]{1,0:T(8,128)S(1)}, f32[40,1408]{1,0:T(8,128)S(1)}, u32[]{:S(2)}, u32[]{:S(2)}) collective-permute-start(f32[40,1408]{1,0:T(8,128)S(1)} %slice.349), channel_id=1, source_target_pairs={{0,8},{4,12},{8,0},{12,4},{16,24},{20,28},{24,16},{28,20},{1,9},{5... | collective-permute-start | bytes 675848 | tf_op jit(solution)/shard_map/ppermute | solution.py:62
  347.8 15.3 %collective-permute-start.57 = (f32[64,5632]{1,0:T(8,128)}, f32[64,5632]{1,0:T(8,128)}, u32[]{:S(2)}, u32[]{:S(2)}) collective-permute-start(f32[64,5632]{1,0:T(8,128)} %pad_maximum_fusion.1), channel_id=1, source_target_pairs={{0,4},{4,0},{8,12},{12,8},{16,20},{20,16},{24,28},{28,24},{1,5},{5... | collective-permute-start | bytes 4325384 | tf_op jit(solution)/shard_map/ppermute | solution.py:62
  349.1 14.0 %collective-permute-start.61 = (f32[56,5632]{1,0:T(8,128)}, f32[56,5632]{1,0:T(8,128)}, u32[]{:S(2)}, u32[]{:S(2)}) collective-permute-start(f32[56,5632]{1,0:T(8,128)} %pad_maximum_fusion.4), channel_id=1, source_target_pairs={{0,4},{4,0},{8,12},{12,8},{16,20},{20,16},{24,28},{28,24},{1,5},{5... | collective-permute-start | bytes 3784712 | tf_op jit(solution)/shard_map/ppermute | solution.py:62
  357.1 22.5 %collective-permute-start.64 = (f32[40,2816]{1,0:T(8,128)S(1)}, f32[40,2816]{1,0:T(8,128)S(1)}, u32[]{:S(2)}, u32[]{:S(2)}) collective-permute-start(f32[40,2816]{1,0:T(8,128)S(1)} %pad_maximum_fusion.28), channel_id=1, source_target_pairs={{0,8},{4,12},{8,0},{12,4},{16,24},{20,28},{24,16},{28,20},{1,9},{5... | collective-permute-start | bytes 1351688 | tf_op jit(solution)/shard_map/ppermute | solution.py:62
  362.4 17.2 %collective-permute-start.63 = (f32[40,2816]{1,0:T(8,128)S(1)}, f32[40,2816]{1,0:T(8,128)S(1)}, u32[]{:S(2)}, u32[]{:S(2)}) collective-permute-start(f32[40,2816]{1,0:T(8,128)S(1)} %pad_maximum_fusion.29), channel_id=1, source_target_pairs={{0,16},{4,20},{8,24},{12,28},{16,0},{20,4},{24,8},{28,12},{1,17},{... | collective-permute-start | bytes 1351688 | tf_op jit(solution)/shard_map/ppermute | solution.py:62
  379.7 11.6 %collective-permute-start.67 = (f32[40,5632]{1,0:T(8,128)S(1)}, f32[40,5632]{1,0:T(8,128)S(1)}, u32[]{:S(2)}, u32[]{:S(2)}) collective-permute-start(f32[40,5632]{1,0:T(8,128)S(1)} %pad_maximum_fusion.12), channel_id=1, source_target_pairs={{0,4},{4,0},{8,12},{12,8},{16,20},{20,16},{24,28},{28,24},{1,5},{5... | collective-permute-start | bytes 2703368 | tf_op jit(solution)/shard_map/ppermute | solution.py:62
  379.8 11.5 %collective-permute-start.66 = (f32[40,5632]{1,0:T(8,128)S(1)}, f32[40,5632]{1,0:T(8,128)S(1)}, u32[]{:S(2)}, u32[]{:S(2)}) collective-permute-start(f32[40,5632]{1,0:T(8,128)S(1)} %pad_maximum_fusion.11), channel_id=1, source_target_pairs={{0,4},{4,0},{8,12},{12,8},{16,20},{20,16},{24,28},{28,24},{1,5},{5... | collective-permute-start | bytes 2703368 | tf_op jit(solution)/shard_map/ppermute | solution.py:62
  391.2 18.9 %collective-permute-start.65 = (f32[248,384]{1,0:T(8,128)S(1)}, f32[248,384]{1,0:T(8,128)S(1)}, u32[]{:S(2)}, u32[]{:S(2)}) collective-permute-start(f32[248,384]{1,0:T(8,128)S(1)} %add.245), channel_id=1, source_target_pairs={{0,2},{1,3},{2,0},{3,1},{4,6},{5,7},{6,4},{7,5},{8,10},{9,11},{10,... | collective-permute-start | bytes 1142792 | tf_op jit(solution)/shard_map/ppermute | solution.py:62
  410.2 19.1 %collective-permute-start.68 = (f32[248,384]{1,0:T(8,128)S(1)}, f32[248,384]{1,0:T(8,128)S(1)}, u32[]{:S(2)}, u32[]{:S(2)}) collective-permute-start(f32[248,384]{1,0:T(8,128)S(1)} %add.246), channel_id=1, source_target_pairs={{0,1},{1,0},{2,3},{3,2},{4,5},{5,4},{6,7},{7,6},{8,9},{9,8},{10,11... | collective-permute-start | bytes 1142792 | tf_op jit(solution)/shard_map/ppermute | solution.py:62
  416.9 12.4 %collective-permute-start.70 = (f32[168,384]{1,0:T(8,128)S(1)}, f32[168,384]{1,0:T(8,128)S(1)}, u32[]{:S(2)}, u32[]{:S(2)}) collective-permute-start(f32[168,384]{1,0:T(8,128)S(1)} %add.247), channel_id=1, source_target_pairs={{0,2},{1,3},{2,0},{3,1},{4,6},{5,7},{6,4},{7,5},{8,10},{9,11},{10,... | collective-permute-start | bytes 774152 | tf_op jit(solution)/shard_map/ppermute | solution.py:62
  465.5 20.8 %collective-permute-start.78 = (f32[64,2816]{1,0:T(8,128)}, f32[64,2816]{1,0:T(8,128)S(1)}, u32[]{:S(2)}, u32[]{:S(2)}) collective-permute-start(f32[64,2816]{1,0:T(8,128)} %pad_maximum_fusion.19), channel_id=1, source_target_pairs={{0,8},{4,12},{8,0},{12,4},{16,24},{20,28},{24,16},{28,20},{1,9},{5... | collective-permute-start | bytes 2162696 | tf_op jit(solution)/shard_map/ppermute | solution.py:62
  466.8 17.2 %collective-permute-start.79 = (f32[8,128]{1,0:T(8,128)S(1)}, f32[8,128]{1,0:T(8,128)S(1)}, u32[]{:S(2)}, u32[]{:S(2)}) collective-permute-start(f32[8,128]{1,0:T(8,128)S(1)} %broadcast_add_fusion), channel_id=1, source_target_pairs={{0,8},{4,12},{8,0},{12,4},{16,24},{20,28},{24,16},{28,20},{1,9},{5... | collective-permute-start | bytes 12296 | tf_op jit(solution)/shard_map/ppermute | solution.py:62
  469.3 22.5 %collective-permute-start.73 = (f32[40,5632]{1,0:T(8,128)S(1)}, f32[40,5632]{1,0:T(8,128)S(1)}, u32[]{:S(2)}, u32[]{:S(2)}) collective-permute-start(f32[40,5632]{1,0:T(8,128)S(1)} %get-tuple-element.274), channel_id=1, source_target_pairs={{0,4},{4,0},{8,12},{12,8},{16,20},{20,16},{24,28},{28,24},{1,5},{5... | collective-permute-start | bytes 2703368 | tf_op jit(solution)/shard_map/ppermute | solution.py:62
  469.4 24.1 %collective-permute-start.72 = (f32[40,5632]{1,0:T(8,128)}, f32[40,5632]{1,0:T(8,128)S(1)}, u32[]{:S(2)}, u32[]{:S(2)}) collective-permute-start(f32[40,5632]{1,0:T(8,128)} %get-tuple-element.272), channel_id=1, source_target_pairs={{0,4},{4,0},{8,12},{12,8},{16,20},{20,16},{24,28},{28,24},{1,5},{5... | collective-permute-start | bytes 2703368 | tf_op jit(solution)/shard_map/ppermute | solution.py:62
  471.7 17.8 %collective-permute-start.77 = (f32[56,2816]{1,0:T(8,128)S(1)}, f32[56,2816]{1,0:T(8,128)S(1)}, u32[]{:S(2)}, u32[]{:S(2)}) collective-permute-start(f32[56,2816]{1,0:T(8,128)S(1)} %slice.358), channel_id=1, source_target_pairs={{0,16},{4,20},{8,24},{12,28},{16,0},{20,4},{24,8},{28,12},{1,17},{... | collective-permute-start | bytes 1892360 | tf_op jit(solution)/shard_map/ppermute | solution.py:62
  484.6 11.4 %collective-permute-start.84 = (f32[8,128]{1,0:T(8,128)S(1)}, f32[8,128]{1,0:T(8,128)S(1)}, u32[]{:S(2)}, u32[]{:S(2)}) collective-permute-start(f32[8,128]{1,0:T(8,128)S(1)} %fusion.24), channel_id=1, source_target_pairs={{0,16},{4,20},{8,24},{12,28},{16,0},{20,4},{24,8},{28,12},{1,17},{... | collective-permute-start | bytes 12296 | tf_op jit(solution)/shard_map/ppermute | solution.py:62
  489.1 11.7 %collective-permute-start.83 = (f32[64,1408]{1,0:T(8,128)}, f32[64,1408]{1,0:T(8,128)}, u32[]{:S(2)}, u32[]{:S(2)}) collective-permute-start(f32[64,1408]{1,0:T(8,128)} %slice.361), channel_id=1, source_target_pairs={{0,16},{4,20},{8,24},{12,28},{16,0},{20,4},{24,8},{28,12},{1,17},{... | collective-permute-start | bytes 1081352 | tf_op jit(solution)/shard_map/ppermute | solution.py:62
  490.5 11.8 %collective-permute-start.82 = (f32[56,1408]{1,0:T(8,128)}, f32[56,1408]{1,0:T(8,128)}, u32[]{:S(2)}, u32[]{:S(2)}) collective-permute-start(f32[56,1408]{1,0:T(8,128)} %slice.362), channel_id=1, source_target_pairs={{0,8},{4,12},{8,0},{12,4},{16,24},{20,28},{24,16},{28,20},{1,9},{5... | collective-permute-start | bytes 946184 | tf_op jit(solution)/shard_map/ppermute | solution.py:62
  492.8 23.4 %collective-permute-start.81 = (f32[40,2816]{1,0:T(8,128)}, f32[40,2816]{1,0:T(8,128)}, u32[]{:S(2)}, u32[]{:S(2)}) collective-permute-start(f32[40,2816]{1,0:T(8,128)} %pad_maximum_fusion.30), channel_id=1, source_target_pairs={{0,8},{4,12},{8,0},{12,4},{16,24},{20,28},{24,16},{28,20},{1,9},{5... | collective-permute-start | bytes 1351688 | tf_op jit(solution)/shard_map/ppermute | solution.py:62
  494.4 23.6 %collective-permute-start.80 = (f32[40,2816]{1,0:T(8,128)}, f32[40,2816]{1,0:T(8,128)}, u32[]{:S(2)}, u32[]{:S(2)}) collective-permute-start(f32[40,2816]{1,0:T(8,128)} %slice.366), channel_id=1, source_target_pairs={{0,16},{4,20},{8,24},{12,28},{16,0},{20,4},{24,8},{28,12},{1,17},{... | collective-permute-start | bytes 1351688 | tf_op jit(solution)/shard_map/ppermute | solution.py:62
  501.8 14.2 %collective-permute-start.86 = (f32[64,1408]{1,0:T(8,128)S(1)}, f32[64,1408]{1,0:T(8,128)S(1)}, u32[]{:S(2)}, u32[]{:S(2)}) collective-permute-start(f32[64,1408]{1,0:T(8,128)S(1)} %slice_add_fusion.6.refs_0_), channel_id=1, source_target_pairs={{0,16},{4,20},{8,24},{12,28},{16,0},{20,4},{24,8},{28,12},{1,17},{... | collective-permute-start | bytes 1081352 | tf_op jit(solution)/shard_map/ppermute | solution.py:62
  503.3 12.8 %collective-permute-start.85 = (f32[56,1408]{1,0:T(8,128)S(1)}, f32[56,1408]{1,0:T(8,128)S(1)}, u32[]{:S(2)}, u32[]{:S(2)}) collective-permute-start(f32[56,1408]{1,0:T(8,128)S(1)} %slice_add_fusion.9.refs_4_), channel_id=1, source_target_pairs={{0,8},{4,12},{8,0},{12,4},{16,24},{20,28},{24,16},{28,20},{1,9},{5... | collective-permute-start | bytes 946184 | tf_op jit(solution)/shard_map/ppermute | solution.py:62
  517.3 19.2 %collective-permute-start.87 = (f32[40,1408]{1,0:T(8,128)S(1)}, f32[40,1408]{1,0:T(8,128)S(1)}, u32[]{:S(2)}, u32[]{:S(2)}) collective-permute-start(f32[40,1408]{1,0:T(8,128)S(1)} %slice.371), channel_id=1, source_target_pairs={{0,16},{4,20},{8,24},{12,28},{16,0},{20,4},{24,8},{28,12},{1,17},{... | collective-permute-start | bytes 675848 | tf_op jit(solution)/shard_map/ppermute | solution.py:62
  519.1 18.1 %collective-permute-start.91 = (f32[40,1408]{1,0:T(8,128)S(1)}, f32[40,1408]{1,0:T(8,128)S(1)}, u32[]{:S(2)}, u32[]{:S(2)}) collective-permute-start(f32[40,1408]{1,0:T(8,128)S(1)} %slice.372), channel_id=1, source_target_pairs={{0,8},{4,12},{8,0},{12,4},{16,24},{20,28},{24,16},{28,20},{1,9},{5... | collective-permute-start | bytes 675848 | tf_op jit(solution)/shard_map/ppermute | solution.py:62
  520.3 21.8 %collective-permute-start.90 = (f32[64,2816]{1,0:T(8,128)S(1)}, f32[64,2816]{1,0:T(8,128)S(1)}, u32[]{:S(2)}, u32[]{:S(2)}) collective-permute-start(f32[64,2816]{1,0:T(8,128)S(1)} %pad_maximum_fusion.20), channel_id=1, source_target_pairs={{0,8},{4,12},{8,0},{12,4},{16,24},{20,28},{24,16},{28,20},{1,9},{5... | collective-permute-start | bytes 2162696 | tf_op jit(solution)/shard_map/ppermute | solution.py:62
  521.2 21.7 %collective-permute-start.89 = (f32[56,2816]{1,0:T(8,128)S(1)}, f32[56,2816]{1,0:T(8,128)S(1)}, u32[]{:S(2)}, u32[]{:S(2)}) collective-permute-start(f32[56,2816]{1,0:T(8,128)S(1)} %pad_maximum_fusion.23), channel_id=1, source_target_pairs={{0,16},{4,20},{8,24},{12,28},{16,0},{20,4},{24,8},{28,12},{1,17},{... | collective-permute-start | bytes 1892360 | tf_op jit(solution)/shard_map/ppermute | solution.py:62
  545.1 13.6 %collective-permute-start.96 = (f32[56,5632]{1,0:T(8,128)S(1)}, f32[56,5632]{1,0:T(8,128)S(1)}, u32[]{:S(2)}, u32[]{:S(2)}) collective-permute-start(f32[56,5632]{1,0:T(8,128)S(1)} %pad_maximum_fusion.5), channel_id=1, source_target_pairs={{0,4},{4,0},{8,12},{12,8},{16,20},{20,16},{24,28},{28,24},{1,5},{5... | collective-permute-start | bytes 3784712 | tf_op jit(solution)/shard_map/ppermute | solution.py:62
  545.1 13.6 %collective-permute-start.95 = (f32[64,5632]{1,0:T(8,128)S(1)}, f32[64,5632]{1,0:T(8,128)S(1)}, u32[]{:S(2)}, u32[]{:S(2)}) collective-permute-start(f32[64,5632]{1,0:T(8,128)S(1)} %pad_maximum_fusion.2), channel_id=1, source_target_pairs={{0,4},{4,0},{8,12},{12,8},{16,20},{20,16},{24,28},{28,24},{1,5},{5... | collective-permute-start | bytes 4325384 | tf_op jit(solution)/shard_map/ppermute | solution.py:62
  (71 other events, 790.5 us)

commit v3 on v2

--- a/solution.py
+++ b/solution.py
@@ -12,7 +12,7 @@
 LANES, ROWS8, UNIT = 128, 8, 16
 NT = (((1,), (1,)), ((), ()))
 NN = (((1,), (0,)), ((), ()))
-VMEM_LIMIT = 52 * 1024 * 1024
+VMEM_LIMIT = 32 * 1024 * 1024
 
 
 def parts_of(x):
@@ -123,13 +123,15 @@
     return (high, low), (send, keep)
 
 
-def back_body(plan, s_ref, g_ref, high_ref, low_ref, *outs):
+def back_body(plan, group, s_ref, g_ref, high_ref, low_ref, *outs):
     core = s_ref[1]
+    base = plan.pair_range(group)[0]
     some, ends = [], []
-    for a, n in plan.chunks:
+    for c in plan.pairs[group]:
+        a, n = plan.chunks[c]
         h = n // 2
         for side in (core, 1 - core):
-            some.append(g_ref[pl.ds(pl.multiple_of(a + side * h, ROWS8), h), :])
+            some.append(g_ref[pl.ds(pl.multiple_of(a - base + side * h, ROWS8), h), :])
             ends.append((ends[-1] if ends else 0) + h)
     x = jnp.concatenate(some, axis=0)
     width = 2 * LANES
@@ -140,20 +142,22 @@
             out[:, k : k + w] = part[start:end]
 
 
-def back(plan, where, values, high, low):
-    rows, block, feats, classes = plan.rows, plan.block, plan.feats, plan.classes
+def back(plan, where, group, values, high, low):
+    rows, block, feats = plan.rows, plan.block, plan.feats
+    n_group = plan.pair_range(group)[1]
     outs, specs = [], []
-    for _, n in plan.chunks:
-        outs += [jax.ShapeDtypeStruct((n // 2, feats), F32)] * 2
-        specs += [pl.BlockSpec((n // 2, block), lambda p, s: (0, p))] * 2
+    for c in plan.pairs[group]:
+        h = plan.chunks[c][1] // 2
+        outs += [jax.ShapeDtypeStruct((h, feats), F32)] * 2
+        specs += [pl.BlockSpec((h, block), lambda p, s: (0, p))] * 2
     result = pl.pallas_call(
-        functools.partial(back_body, plan),
+        functools.partial(back_body, plan, group),
         out_shape=outs,
         grid_spec=pltpu.PrefetchScalarGridSpec(
             num_scalar_prefetch=1,
             grid=(plan.nb,),
             in_specs=[
-                pl.BlockSpec((classes, rows), lambda p, s: (0, 0)),
+                pl.BlockSpec((n_group, rows), lambda p, s: (0, 0), pipeline_mode=pl.Buffered(1)),
                 pl.BlockSpec((rows, block), lambda p, s: (0, p)),
                 pl.BlockSpec((rows, block), lambda p, s: (0, p)),
             ],
@@ -161,11 +165,11 @@
         ),
         compiler_params=params(),
         cost_estimate=pl.CostEstimate(
-            flops=6 * classes * rows * feats, bytes_accessed=4 * feats * (rows + classes), transcendentals=0
+            flops=6 * n_group * rows * feats, bytes_accessed=4 * feats * (rows + n_group), transcendentals=0
         ),
-        name="back_all",
+        name="back_group",
     )(where, values, high, low)
-    return [tuple(result[2 * k : 2 * k + 2]) for k in range(len(plan.chunks))]
+    return [tuple(result[2 * k : 2 * k + 2]) for k in range(len(plan.pairs[group]))]
 
 
 class Pieces:
@@ -267,7 +271,7 @@
     for piece in pieces:
         for x in piece.flat():
             operands.append(x)
-            in_specs.append(pl.BlockSpec(x.shape, lambda p, s: (0, 0)))
+            in_specs.append(pl.BlockSpec(x.shape, lambda p, s: (0, 0), pipeline_mode=pl.Buffered(1)))
     if step is not None:
         operands.append(direction)
         in_specs.append(placed(plan, pair))
@@ -521,28 +525,33 @@
     probs, values = jnp.concatenate(probs, axis=1), jnp.concatenate(values, axis=1)
 
     def backward(values, scalar=None, during=None, under=None):
-        sides = back(plan, where, order.after(values), high, low)
-        sums = [ClipSum(plan, side, plan.turns[c]) for c, side in enumerate(sides)]
-        order.note(sides[-1][0])
-        result = None
+        sums, result = [None] * len(plan.chunks), None
+
+        def multiply(group):
+            a, n = plan.pair_range(group)
+            sides = back(plan, where, group, order.after(values[a : a + n]), high, low)
+            for c, side in zip(plan.pairs[group], sides):
+                sums[c] = ClipSum(plan, side, plan.turns[c])
+            order.note(sides[-1][0])
 
         def go(*chunks):
             for c in chunks:
                 if not sums[c].done():
                     sums[c].advance(order)
 
+        multiply(0)
         if scalar is not None:
             scalar.advance(order)
         go(0, 1)
+        multiply(1)
         if scalar is not None:
             scalar.advance(order)
         go(0, 1, 2, 3)
         if scalar is not None:
             result = during(scalar.result(order))
-        go(0, 1, 0, 1, 2, 3)
         if under is not None:
             result = under(result)
-        go(2, 3, 0, 1, 2, 3)
+        go(0, 1, 2, 3, 0, 1, 2, 3, 2, 3, 0, 1)
         return sums, go, result
 
     def forward(sums, go, step=None, direction=None):
@@ -557,11 +566,9 @@
 
         vectors = multiply(0)
         go(2, 3)
-        found[0].advance(order)
         vectors = multiply(1)
-        found[0].advance(order)
-        found[1].advance(order)
-        found[0].advance(order)
+        for k in (0, 1, 0, 1):
+            found[k].advance(order)
         tangents = [f.result(order) for f in found]
         inner = sum(t[-ROWS8 : 2 - ROWS8, 0] for t in tangents)
         return vectors, jnp.concatenate([t[:-ROWS8] for t in tangents], axis=0), inner

time: 587 us -> 561 us (0.956)
  waiting for transfers between devices: 260 us -> 243 us
  Pallas kernels: 157 us -> 143 us
  local copies, waits for them, and re-layouts: 19.3 us -> 32.5 us
  other arithmetic: 44.4 us -> 37.4 us
    ppermute x99, waiting for transfers between devices: 260 us -> 243 us  [swap(): return lax.ppermute(x, axis, [(i, i ^ stride) for i in range(size)])]
    unnamed x72 -> x96, local copies, waits for them, and re-layouts: 11.8 us -> 23.3 us
    pallas_call x4, Pallas kernels: 60.3 us -> 50.9 us  [forth(): pl.pallas_call(functools.partial(forth_body, plan, pair, step is not None...]
    pallas_call x3 -> x6, Pallas kernels: 50.1 us -> 56.2 us  [back(): pl.pallas_call(functools.partial(back_body, plan, group), out_shape=outs,...]
  transfers between devices with their start and end apart: 99 -> 99, of which waited for: 40 -> 45; matrix products, arithmetic and copies ran while one was open for 7% -> 7% of each run, Pallas kernels for 16% -> 18%
where the time goes in v3:
time: 561 us; the launch traced here: 553 us
  waiting for transfers between devices  243 us (43%)
  Pallas kernels  143 us (25%)
  starting transfers between devices  88.4 us (16%)
  other arithmetic  37.4 us (7%)
  local copies, waits for them, and re-layouts  32.5 us (6%)
  between operations  8.84 us (2%)
    ppermute x99, waiting for transfers between devices, swap(): return lax.ppermute(x, axis, [(i, i ^ stride) for i in range(size)])  243 us
    ppermute x99, starting transfers between devices, swap(): return lax.ppermute(x, axis, [(i, i ^ stride) for i in range(size)])  88.4 us
    pallas_call x6, Pallas kernels, back(): pl.pallas_call(functools.partial(back_body, plan, group), out_shape=outs,...  56.2 us
    pallas_call x4, Pallas kernels, forth(): pl.pallas_call(functools.partial(forth_body, plan, pair, step is not None...  50.9 us
    pallas_call x3, Pallas kernels, first(): pl.pallas_call(functools.partial(first_body, plan), out_shape=[jax.ShapeD...  26.5 us
    unnamed x96, local copies, waits for them, and re-layouts  23.3 us
    add x1, other arithmetic, under(): order.after(weights) + (step0 + step1 * ratio) * direction  13.8 us
  transfers between devices with their start and end apart: 99, of which 45 were waited for; matrix products, arithmetic and copies ran while one was open for 7% of the time, Pallas kernels for 18%

profile of v3, /device:TPU:0, one launch (start us, length us, event | category | flops | bytes accessed | tf_op | source)
XLA Modules:
  0.0 553.0 jit_solution(4620759853245783819)
XLA Ops:
  0.7 8.8 %split_and_logits.3 = (bf16[768,5632]{1,0:T(8,128)(2,1)S(1)}, bf16[768,5632]{1,0:T(8,128)(2,1)S(1)}, f32[200,256]{1,0:T(8,128)S(1)}, f32[200,256]{1,0:T(8,128)S(1)}) custom-call(s32[3]{0:T(128)S(1)} %pad_add_fusion.s_ref, f32[768,5632]{1,0:T(8,128)} %f_ref.3, f32[400,5632]{1,0:T(8,128)} %w_ref.5), custom_call_target="tpu_custom_call" | custom-call | flops 3460300800 | bytes 20545536 | tf_op jit(solution)/shard_map/split_and_logits/pallas_call | solution.py:102
  9.6 3.1 collective-permute-start
  12.7 8.9 %split_and_logits.4 = (bf16[768,5632]{1,0:T(8,128)(2,1)S(1)}, bf16[768,5632]{1,0:T(8,128)(2,1)S(1)}, f32[200,256]{1,0:T(8,128)S(1)}, f32[200,256]{1,0:T(8,128)S(1)}) custom-call(s32[3]{0:T(128)S(1)} %pad_add_fusion.s_ref, f32[768,5632]{1,0:T(8,128)} %f_ref.3, f32[400,5632]{1,0:T(8,128)} %w_ref.5, ...), custom_call_target="tpu_custom_call", output_to_operand_aliasing={{0}: (3, {}), {1}: (4, {})} | custom-call | flops 3460300800 | bytes 20545536 | tf_op jit(solution)/shard_map/split_and_logits/pallas_call | solution.py:102
  21.7 3.1 collective-permute-start.1
  24.7 8.8 %split_and_logits.5 = (bf16[768,5632]{1,0:T(8,128)(2,1)S(1)}, bf16[768,5632]{1,0:T(8,128)(2,1)S(1)}, f32[200,256]{1,0:T(8,128)S(1)}, f32[200,256]{1,0:T(8,128)S(1)}) custom-call(s32[3]{0:T(128)S(1)} %pad_add_fusion.s_ref, f32[768,5632]{1,0:T(8,128)} %f_ref.3, f32[400,5632]{1,0:T(8,128)} %w_ref.5, ...), custom_call_target="tpu_custom_call", output_to_operand_aliasing={{0}: (3, {}), {1}: (4, {})} | custom-call | flops 3460300800 | bytes 20545536 | tf_op jit(solution)/shard_map/split_and_logits/pallas_call | solution.py:102
  33.6 3.5 copy-done
  37.1 3.3 copy-done.5
  42.5 6.1 %collective-permute-done.3 = f32[200,256]{1,0:T(8,128)S(1)} collective-permute-done((f32[200,256]{1,0:T(8,128)S(1)}, f32[200,256]{1,0:T(8,128)S(1)}, u32[]{:S(2)}, u32[]{:S(2)}) %collective-permute-start.3) | collective-permute-done | bytes 204832 | tf_op jit(solution)/shard_map/ppermute | solution.py:62
  48.6 4.6 collective-permute-done.4
  53.2 2.0 collective-permute-start.6
  55.3 6.0 %collective-permute-done.5 = f32[200,256]{1,0:T(8,128)S(1)} collective-permute-done((f32[200,256]{1,0:T(8,128)S(1)}, f32[200,256]{1,0:T(8,128)S(1)}, u32[]{:S(2)}, u32[]{:S(2)}) %collective-permute-start.5) | collective-permute-done | bytes 204832 | tf_op jit(solution)/shard_map/ppermute | solution.py:62
  61.2 2.2 collective-permute-done.6
  63.8 10.0 %collective-permute-done.7 = f32[200,256]{1,0:T(8,128)S(1)} collective-permute-done((f32[200,256]{1,0:T(8,128)S(1)}, f32[200,256]{1,0:T(8,128)S(1)}, u32[]{:S(2)}, u32[]{:S(2)}) %collective-permute-start.7) | collective-permute-done | bytes 204832 | tf_op jit(solution)/shard_map/ppermute | solution.py:62
  74.2 6.0 %collective-permute-done.8 = f32[200,256]{1,0:T(8,128)S(1)} collective-permute-done((f32[200,256]{1,0:T(8,128)S(1)}, f32[200,256]{1,0:T(8,128)S(1)}, u32[]{:S(2)}, u32[]{:S(2)}) %collective-permute-start.8) | collective-permute-done | bytes 204832 | tf_op jit(solution)/shard_map/ppermute | solution.py:62
  80.8 11.1 %back_group.6 = (f32[64,5632]{1,0:T(8,128)S(1)}, f32[64,5632]{1,0:T(8,128)S(1)}, f32[56,5632]{1,0:T(8,128)S(1)}, f32[56,5632]{1,0:T(8,128)S(1)}) custom-call(s32[3]{0:T(128)S(1)} %pad_add_fusion.s_ref, f32[240,768]{1,0:T(8,128)S(1)} %slice.331.g_ref, bf16[768,5632]{1,0:T(8,128)(2,1)S(1)} %copy-done.1, bf16[768,5632]{1,0:T(8,128)(2,1)} %copy-done.5), custom_call_target="tpu_custom_call" | custom-call | flops 6228541440 | bytes 22708224 | tf_op jit(solution)/shard_map/back_group/pallas_call | solution.py:153
  92.5 2.7 collective-permute-done.9
  95.6 1.9 collective-permute-start.10
  99.3 7.6 %back_group.7 = (f32[40,5632]{1,0:T(8,128)S(1)}, f32[40,5632]{1,0:T(8,128)S(1)}, f32[40,5632]{1,0:T(8,128)S(1)}, f32[40,5632]{1,0:T(8,128)S(1)}) custom-call(s32[3]{0:T(128)S(1)} %pad_add_fusion.s_ref, f32[160,768]{1,0:T(8,128)S(1)} %pad_maximum_fusion.24.g_ref, bf16[768,5632]{1,0:T(8,128)(2,1)S(1)} %copy-done.1, bf16[768,5632]{1,0:T(8,128)(2,1)S(1)} %bitcast.12), custom_call_target="tpu_custom_call" | custom-call | flops 4152360960 | bytes 20905984 | tf_op jit(solution)/shard_map/back_group/pallas_call | solution.py:153
  107.5 6.3 %collective-permute-done.10 = f32[64,2816]{1,0:T(8,128)S(1)} collective-permute-done((f32[64,2816]{1,0:T(8,128)S(1)}, f32[64,2816]{1,0:T(8,128)S(1)}, u32[]{:S(2)}, u32[]{:S(2)}) %collective-permute-start.10) | collective-permute-done | bytes 720928 | tf_op jit(solution)/shard_map/ppermute | solution.py:62
  118.8 6.6 %collective-permute-done.12 = f32[64,1408]{1,0:T(8,128)S(1)} collective-permute-done((f32[64,1408]{1,0:T(8,128)S(1)}, f32[64,1408]{1,0:T(8,128)S(1)}, u32[]{:S(2)}, u32[]{:S(2)}) %collective-permute-start.12) | collective-permute-done | bytes 360480 | tf_op jit(solution)/shard_map/ppermute | solution.py:62
  128.9 7.1 %collective-permute-done.18 = f32[40,2816]{1,0:T(8,128)S(1)} collective-permute-done((f32[40,2816]{1,0:T(8,128)S(1)}, f32[40,2816]{1,0:T(8,128)S(1)}, u32[]{:S(2)}, u32[]{:S(2)}) %collective-permute-start.18) | collective-permute-done | bytes 450592 | tf_op jit(solution)/shard_map/ppermute | solution.py:62
  138.3 4.4 collective-permute-done.16.refs_1_
  151.1 13.2 %collective-permute-done.25.refs_1_ = f32[40,1408]{1,0:T(8,128)S(1)} collective-permute-done((f32[40,1408]{1,0:T(8,128)S(1)}, f32[40,1408]{1,0:T(8,128)S(1)}, u32[]{:S(2)}, u32[]{:S(2)}) %collective-permute-start.25) | collective-permute-done | bytes 225312 | tf_op jit(solution)/shard_map/ppermute | solution.py:62
  168.8 2.3 collective-permute-done.28.refs_7_
  171.1 12.5 %forth_pair.4 = (f32[400,5632]{1,0:T(8,128)}, f32[248,384]{1,0:T(8,128)S(1)}, f32[248,384]{1,0:T(8,128)S(1)}) custom-call(s32[3]{0:T(128)S(1)} %pad_add_fusion.s_ref, f32[64,1408]{1,0:T(8,128)S(1)} %slice_add_fusion.8.refs_0_, f32[64,1408]{1,0:T(8,128)S(1)} %collective-permute-done.16.refs_1_, f32[64,2816]{1,0:T(8,128)S(1)} %collective-permute-done.20.refs_2_, ...), custom_call_target="tpu_custom_call" | custom-call | flops 6228541440 | bytes 33521664 | tf_op jit(solution)/shard_map/forth_pair/pallas_call | solution.py:289
  187.6 11.8 %forth_pair.5 = (f32[400,5632]{1,0:T(8,128)}, f32[168,384]{1,0:T(8,128)S(1)}, f32[168,384]{1,0:T(8,128)S(1)}) custom-call(s32[3]{0:T(128)S(1)} %pad_add_fusion.s_ref, f32[40,1408]{1,0:T(8,128)S(1)} %slice_add_fusion.16.refs_0_, f32[40,1408]{1,0:T(8,128)S(1)} %collective-permute-done.25.refs_1_, ...), custom_call_target="tpu_custom_call", output_to_operand_aliasing={{0}: (11, {})} | custom-call | flops 4152360960 | bytes 28114944 | tf_op jit(solution)/shard_map/forth_pair/pallas_call | solution.py:289
  199.9 13.9 %collective-permute-done.35 = f32[168,384]{1,0:T(8,128)S(1)} collective-permute-done((f32[168,384]{1,0:T(8,128)S(1)}, f32[168,384]{1,0:T(8,128)S(1)}, u32[]{:S(2)}, u32[]{:S(2)}) %collective-permute-start.35) | collective-permute-done | bytes 258080 | tf_op jit(solution)/shard_map/ppermute | solution.py:62
  213.8 3.5 collective-permute-start.37
  217.3 6.5 %collective-permute-done.34 = f32[248,384]{1,0:T(8,128)S(1)} collective-permute-done((f32[248,384]{1,0:T(8,128)S(1)}, f32[248,384]{1,0:T(8,128)S(1)}, u32[]{:S(2)}, u32[]{:S(2)}) %collective-permute-start.34) | collective-permute-done | bytes 380960 | tf_op jit(solution)/shard_map/ppermute | solution.py:62
  223.9 6.5 %collective-permute-done.37 = f32[168,384]{1,0:T(8,128)S(1)} collective-permute-done((f32[168,384]{1,0:T(8,128)S(1)}, f32[168,384]{1,0:T(8,128)S(1)}, u32[]{:S(2)}, u32[]{:S(2)}) %collective-permute-start.37) | collective-permute-done | bytes 258080 | tf_op jit(solution)/shard_map/ppermute | solution.py:62
  230.5 8.0 %collective-permute-done.36 = f32[248,384]{1,0:T(8,128)S(1)} collective-permute-done((f32[248,384]{1,0:T(8,128)S(1)}, f32[248,384]{1,0:T(8,128)S(1)}, u32[]{:S(2)}, u32[]{:S(2)}) %collective-permute-start.36) | collective-permute-done | bytes 380960 | tf_op jit(solution)/shard_map/ppermute | solution.py:62
  238.7 5.3 collective-permute-done.38
  245.9 10.9 %back_group.8 = (f32[64,5632]{1,0:T(8,128)S(1)}, f32[64,5632]{1,0:T(8,128)S(1)}, f32[56,5632]{1,0:T(8,128)S(1)}, f32[56,5632]{1,0:T(8,128)S(1)}) custom-call(s32[3]{0:T(128)S(1)} %pad_add_fusion.s_ref, f32[240,768]{1,0:T(8,128)S(1)} %slice.356.g_ref, bf16[768,5632]{1,0:T(8,128)(2,1)S(1)} %copy-done.1, bf16[768,5632]{1,0:T(8,128)(2,1)} %copy-done.5), custom_call_target="tpu_custom_call" | custom-call | flops 6228541440 | bytes 22708224 | tf_op jit(solution)/shard_map/back_group/pallas_call | solution.py:153
  258.3 3.7 collective-permute-done.39
  265.9 7.7 %back_group.9 = (f32[40,5632]{1,0:T(8,128)S(1)}, f32[40,5632]{1,0:T(8,128)S(1)}, f32[40,5632]{1,0:T(8,128)S(1)}, f32[40,5632]{1,0:T(8,128)S(1)}) custom-call(s32[3]{0:T(128)S(1)} %pad_add_fusion.s_ref, f32[160,768]{1,0:T(8,128)S(1)} %slice.357.g_ref, bf16[768,5632]{1,0:T(8,128)(2,1)S(1)} %copy-done.1, bf16[768,5632]{1,0:T(8,128)(2,1)S(1)} %bitcast.16), custom_call_target="tpu_custom_call" | custom-call | flops 4152360960 | bytes 20905984 | tf_op jit(solution)/shard_map/back_group/pallas_call | solution.py:153
  273.5 7.9 %collective-permute-done.40 = f32[8,128]{1,0:T(8,128)S(1)} collective-permute-done((f32[8,128]{1,0:T(8,128)S(1)}, f32[8,128]{1,0:T(8,128)S(1)}, u32[]{:S(2)}, u32[]{:S(2)}) %collective-permute-start.40) | collective-permute-done | bytes 4128 | tf_op jit(solution)/shard_map/ppermute | solution.py:62
  290.0 4.5 collective-permute-done.48
  297.9 7.2 %collective-permute-done.51 = f32[40,2816]{1,0:T(8,128)S(1)} collective-permute-done((f32[40,2816]{1,0:T(8,128)S(1)}, f32[40,2816]{1,0:T(8,128)S(1)}, u32[]{:S(2)}, u32[]{:S(2)}) %collective-permute-start.51) | collective-permute-done | bytes 450592 | tf_op jit(solution)/shard_map/ppermute | solution.py:62
  307.4 4.5 collective-permute-done.49.refs_2_
  320.1 14.0 %collective-permute-done.58.refs_2_ = f32[40,1408]{1,0:T(8,128)S(1)} collective-permute-done((f32[40,1408]{1,0:T(8,128)S(1)}, f32[40,1408]{1,0:T(8,128)S(1)}, u32[]{:S(2)}, u32[]{:S(2)}) %collective-permute-start.58) | collective-permute-done | bytes 225312 | tf_op jit(solution)/shard_map/ppermute | solution.py:62
  345.4 3.5 copy-done.2
  348.9 14.2 %forth_pair.6 = (f32[400,5632]{1,0:T(8,128)}, f32[248,384]{1,0:T(8,128)S(1)}, f32[248,384]{1,0:T(8,128)S(1)}) custom-call(s32[3]{0:T(128)S(1)} %pad_add_fusion.s_ref, f32[1]{0:T(128)} %bitcast.5.refs_0_, f32[64,1408]{1,0:T(8,128)S(1)} %slice_add_fusion.7.refs_1_, f32[64,1408]{1,0:T(8,128)S(1)} %collective-permute-done.49.refs_2_, ...), custom_call_target="tpu_custom_call" | custom-call | flops 6228541440 | bytes 33521664 | tf_op jit(solution)/shard_map/forth_pair/pallas_call | solution.py:289
  364.7 1.9 collective-permute-done.66.refs_8_
  367.9 12.4 %forth_pair.7 = (f32[400,5632]{1,0:T(8,128)}, f32[168,384]{1,0:T(8,128)S(1)}, f32[168,384]{1,0:T(8,128)S(1)}) custom-call(s32[3]{0:T(128)S(1)} %pad_add_fusion.s_ref, f32[1]{0:T(128)} %bitcast.5.refs_0_, f32[40,1408]{1,0:T(8,128)S(1)} %slice_add_fusion.14.refs_1_, f32[40,1408]{1,0:T(8,128)S(1)} %copy-done.8, ...), custom_call_target="tpu_custom_call", output_to_operand_aliasing={{0}: (13, {})} | custom-call | flops 4152360960 | bytes 28114944 | tf_op jit(solution)/shard_map/forth_pair/pallas_call | solution.py:289
  380.5 14.2 %collective-permute-done.68 = f32[168,384]{1,0:T(8,128)S(1)} collective-permute-done((f32[168,384]{1,0:T(8,128)S(1)}, f32[168,384]{1,0:T(8,128)S(1)}, u32[]{:S(2)}, u32[]{:S(2)}) %collective-permute-start.68) | collective-permute-done | bytes 258080 | tf_op jit(solution)/shard_map/ppermute | solution.py:62
  394.7 2.7 collective-permute-start.70
  397.4 2.0 collective-permute-done.67
  399.5 11.0 %collective-permute-done.70 = f32[168,384]{1,0:T(8,128)S(1)} collective-permute-done((f32[168,384]{1,0:T(8,128)S(1)}, f32[168,384]{1,0:T(8,128)S(1)}, u32[]{:S(2)}, u32[]{:S(2)}) %collective-permute-start.70) | collective-permute-done | bytes 258080 | tf_op jit(solution)/shard_map/ppermute | solution.py:62
  410.6 5.6 %collective-permute-done.69 = f32[248,384]{1,0:T(8,128)S(1)} collective-permute-done((f32[248,384]{1,0:T(8,128)S(1)}, f32[248,384]{1,0:T(8,128)S(1)}, u32[]{:S(2)}, u32[]{:S(2)}) %collective-permute-start.69) | collective-permute-done | bytes 380960 | tf_op jit(solution)/shard_map/ppermute | solution.py:62
  417.2 3.5 collective-permute-done.71
  426.2 3.5 copy-done.3
  429.7 11.5 %back_group.10 = (f32[64,5632]{1,0:T(8,128)S(1)}, f32[64,5632]{1,0:T(8,128)S(1)}, f32[56,5632]{1,0:T(8,128)S(1)}, f32[56,5632]{1,0:T(8,128)}) custom-call(s32[3]{0:T(128)S(1)} %pad_add_fusion.s_ref, f32[240,768]{1,0:T(8,128)S(1)} %slice.382.g_ref, bf16[768,5632]{1,0:T(8,128)(2,1)S(1)} %copy-done.3, bf16[768,5632]{1,0:T(8,128)(2,1)} %copy-done.5), custom_call_target="tpu_custom_call" | custom-call | flops 6228541440 | bytes 22708224 | tf_op jit(solution)/shard_map/back_group/pallas_call | solution.py:153
  442.4 3.8 collective-permute-done.72
  456.7 3.5 copy-done.4
  460.1 3.5 copy-done.6
  463.6 7.5 %back_group.11 = (f32[40,5632]{1,0:T(8,128)S(1)}, f32[40,5632]{1,0:T(8,128)S(1)}, f32[40,5632]{1,0:T(8,128)S(1)}, f32[40,5632]{1,0:T(8,128)S(1)}) custom-call(s32[3]{0:T(128)S(1)} %pad_add_fusion.s_ref, f32[160,768]{1,0:T(8,128)S(1)} %slice.383.g_ref, bf16[768,5632]{1,0:T(8,128)(2,1)S(1)} %copy-done.4, bf16[768,5632]{1,0:T(8,128)(2,1)S(1)} %copy-done.6), custom_call_target="tpu_custom_call" | custom-call | flops 4152360960 | bytes 20905984 | tf_op jit(solution)/shard_map/back_group/pallas_call | solution.py:153
  482.5 13.8 %multiply_add_fusion = f32[400,5632]{1,0:T(8,128)} fusion(f32[400,5632]{1,0:T(8,128)} %get-tuple-element.295.refs_9_, f32[400,5632]{1,0:T(8,128)} %w_ref.5, f32[400,5632]{1,0:T(8,128)} %get-tuple-element.259.refs_9_.refs_8_, f32[]{:T(128)} %div.82, f32[]{:T(128)S(6)} %add.263), kind=kLoop, calls=%fused_computation | loop fusion | flops 9011200 | bytes 36044808 | tf_op jit(solution)/shard_map/add | solution.py:595
  503.9 3.9 collective-permute-done.86.refs_1_
  510.1 2.6 collective-permute-done.84
  514.5 14.3 %collective-permute-done.88.refs_1_ = f32[40,1408]{1,0:T(8,128)S(1)} collective-permute-done((f32[40,1408]{1,0:T(8,128)S(1)}, f32[40,1408]{1,0:T(8,128)S(1)}, u32[]{:S(2)}, u32[]{:S(2)}) %collective-permute-start.88) | collective-permute-done | bytes 225312 | tf_op jit(solution)/shard_map/ppermute | solution.py:62
  529.5 4.6 collective-permute-done.93.refs_5_
  536.0 5.5 collective-permute-done.90.refs_2_
  543.4 5.6 %last_rows.2.refs_10_ = f32[400,5632]{1,0:T(8,128)} custom-call(s32[3]{0:T(128)S(1)} %pad_add_fusion.s_ref, f32[2]{0:T(128)S(1)} %pad_maximum_fusion.34.scalar_ref, f32[64,1408]{1,0:T(8,128)S(1)} %slice_add_fusion.6.refs_0_, f32[64,1408]{1,0:T(8,128)S(1)} %collective-permute-done.86.refs_1_, f32[64,2816]{1,0:T(8,128)S(1)} %collective-permute-done.92.refs_2_, ...), custom_call_target="tpu_custom_call" | custom-call | flops 8110080 | bytes 21626880 | tf_op jit(solution)/shard_map/last_rows/pallas_call | solution.py:359
  549.0 3.5 last_rows.3
  (400 shorter events, 118.6 us)
Async XLA Ops:
  9.6 12.0 %collective-permute-start = (f32[200,256]{1,0:T(8,128)S(1)}, f32[200,256]{1,0:T(8,128)S(1)}, u32[]{:S(2)}, u32[]{:S(2)}) collective-permute-start(f32[200,256]{1,0:T(8,128)S(1)} %get-tuple-element.159), channel_id=1, source_target_pairs={{0,1},{1,0},{2,3},{3,2},{4,5},{5,4},{6,7},{7,6},{8,9},{9,8},{10,11... | collective-permute-start | bytes 614408 | tf_op jit(solution)/shard_map/ppermute | solution.py:62
  21.5 18.9 %collective-permute-start.2 = (f32[200,256]{1,0:T(8,128)S(1)}, f32[200,256]{1,0:T(8,128)S(1)}, u32[]{:S(2)}, u32[]{:S(2)}) collective-permute-start(f32[200,256]{1,0:T(8,128)S(1)} %get-tuple-element.163), channel_id=1, source_target_pairs={{0,1},{1,0},{2,3},{3,2},{4,5},{5,4},{6,7},{7,6},{8,9},{9,8},{10,11... | collective-permute-start | bytes 614408 | tf_op jit(solution)/shard_map/ppermute | solution.py:62
  21.7 18.8 %collective-permute-start.1 = (f32[200,256]{1,0:T(8,128)S(1)}, f32[200,256]{1,0:T(8,128)S(1)}, u32[]{:S(2)}, u32[]{:S(2)}) collective-permute-start(f32[200,256]{1,0:T(8,128)S(1)} %add.206), channel_id=1, source_target_pairs={{0,2},{1,3},{2,0},{3,1},{4,6},{5,7},{6,4},{7,5},{8,10},{9,11},{10,... | collective-permute-start | bytes 614408 | tf_op jit(solution)/shard_map/ppermute | solution.py:62
  95.6 18.3 %collective-permute-start.10 = (f32[64,2816]{1,0:T(8,128)S(1)}, f32[64,2816]{1,0:T(8,128)S(1)}, u32[]{:S(2)}, u32[]{:S(2)}) collective-permute-start(f32[64,2816]{1,0:T(8,128)S(1)} %pad_maximum_fusion.15), channel_id=1, source_target_pairs={{0,8},{4,12},{8,0},{12,4},{16,24},{20,28},{24,16},{28,20},{1,9},{5... | collective-permute-start | bytes 2162696 | tf_op jit(solution)/shard_map/ppermute | solution.py:62
  97.7 18.1 %collective-permute-start.15 = (f32[56,2816]{1,0:T(8,128)S(1)}, f32[56,2816]{1,0:T(8,128)S(1)}, u32[]{:S(2)}, u32[]{:S(2)}) collective-permute-start(f32[56,2816]{1,0:T(8,128)S(1)} %slice.336), channel_id=1, source_target_pairs={{0,16},{4,20},{8,24},{12,28},{16,0},{20,4},{24,8},{28,12},{1,17},{... | collective-permute-start | bytes 1892360 | tf_op jit(solution)/shard_map/ppermute | solution.py:62
  107.0 11.3 %collective-permute-start.13 = (f32[40,5632]{1,0:T(8,128)S(1)}, f32[40,5632]{1,0:T(8,128)S(1)}, u32[]{:S(2)}, u32[]{:S(2)}) collective-permute-start(f32[40,5632]{1,0:T(8,128)S(1)} %get-tuple-element.191), channel_id=1, source_target_pairs={{0,4},{4,0},{8,12},{12,8},{16,20},{20,16},{24,28},{28,24},{1,5},{5... | collective-permute-start | bytes 2703368 | tf_op jit(solution)/shard_map/ppermute | solution.py:62
  114.0 11.4 %collective-permute-start.12 = (f32[64,1408]{1,0:T(8,128)S(1)}, f32[64,1408]{1,0:T(8,128)S(1)}, u32[]{:S(2)}, u32[]{:S(2)}) collective-permute-start(f32[64,1408]{1,0:T(8,128)S(1)} %slice.338), channel_id=1, source_target_pairs={{0,16},{4,20},{8,24},{12,28},{16,0},{20,4},{24,8},{28,12},{1,17},{... | collective-permute-start | bytes 1081352 | tf_op jit(solution)/shard_map/ppermute | solution.py:62
  115.9 11.3 %collective-permute-start.19 = (f32[56,1408]{1,0:T(8,128)S(1)}, f32[56,1408]{1,0:T(8,128)S(1)}, u32[]{:S(2)}, u32[]{:S(2)}) collective-permute-start(f32[56,1408]{1,0:T(8,128)S(1)} %slice.340), channel_id=1, source_target_pairs={{0,8},{4,12},{8,0},{12,4},{16,24},{20,28},{24,16},{28,20},{1,9},{5... | collective-permute-start | bytes 946184 | tf_op jit(solution)/shard_map/ppermute | solution.py:62
  117.7 18.3 %collective-permute-start.18 = (f32[40,2816]{1,0:T(8,128)S(1)}, f32[40,2816]{1,0:T(8,128)S(1)}, u32[]{:S(2)}, u32[]{:S(2)}) collective-permute-start(f32[40,2816]{1,0:T(8,128)S(1)} %pad_maximum_fusion.25), channel_id=1, source_target_pairs={{0,8},{4,12},{8,0},{12,4},{16,24},{20,28},{24,16},{28,20},{1,9},{5... | collective-permute-start | bytes 1351688 | tf_op jit(solution)/shard_map/ppermute | solution.py:62
  118.4 18.0 %collective-permute-start.17 = (f32[40,2816]{1,0:T(8,128)S(1)}, f32[40,2816]{1,0:T(8,128)S(1)}, u32[]{:S(2)}, u32[]{:S(2)}) collective-permute-start(f32[40,2816]{1,0:T(8,128)S(1)} %slice.343), channel_id=1, source_target_pairs={{0,16},{4,20},{8,24},{12,28},{16,0},{20,4},{24,8},{28,12},{1,17},{... | collective-permute-start | bytes 1351688 | tf_op jit(solution)/shard_map/ppermute | solution.py:62
  125.4 17.3 %collective-permute-start.16 = (f32[64,1408]{1,0:T(8,128)S(1)}, f32[64,1408]{1,0:T(8,128)S(1)}, u32[]{:S(2)}, u32[]{:S(2)}) collective-permute-start(f32[64,1408]{1,0:T(8,128)S(1)} %slice_add_fusion.8.refs_0_), channel_id=1, source_target_pairs={{0,16},{4,20},{8,24},{12,28},{16,0},{20,4},{24,8},{28,12},{1,17},{... | collective-permute-start | bytes 1081352 | tf_op jit(solution)/shard_map/ppermute | solution.py:62
  127.3 17.3 %collective-permute-start.23 = (f32[56,1408]{1,0:T(8,128)S(1)}, f32[56,1408]{1,0:T(8,128)S(1)}, u32[]{:S(2)}, u32[]{:S(2)}) collective-permute-start(f32[56,1408]{1,0:T(8,128)S(1)} %slice_add_fusion.11.refs_4_), channel_id=1, source_target_pairs={{0,8},{4,12},{8,0},{12,4},{16,24},{20,28},{24,16},{28,20},{1,9},{5... | collective-permute-start | bytes 946184 | tf_op jit(solution)/shard_map/ppermute | solution.py:62
  136.1 11.5 %collective-permute-start.22 = (f32[40,1408]{1,0:T(8,128)S(1)}, f32[40,1408]{1,0:T(8,128)S(1)}, u32[]{:S(2)}, u32[]{:S(2)}) collective-permute-start(f32[40,1408]{1,0:T(8,128)S(1)} %slice.348), channel_id=1, source_target_pairs={{0,16},{4,20},{8,24},{12,28},{16,0},{20,4},{24,8},{28,12},{1,17},{... | collective-permute-start | bytes 675848 | tf_op jit(solution)/shard_map/ppermute | solution.py:62
  136.5 12.9 %collective-permute-start.21 = (f32[40,1408]{1,0:T(8,128)S(1)}, f32[40,1408]{1,0:T(8,128)S(1)}, u32[]{:S(2)}, u32[]{:S(2)}) collective-permute-start(f32[40,1408]{1,0:T(8,128)S(1)} %slice.349), channel_id=1, source_target_pairs={{0,8},{4,12},{8,0},{12,4},{16,24},{20,28},{24,16},{28,20},{1,9},{5... | collective-permute-start | bytes 675848 | tf_op jit(solution)/shard_map/ppermute | solution.py:62
  142.8 23.1 %collective-permute-start.20 = (f32[64,2816]{1,0:T(8,128)S(1)}, f32[64,2816]{1,0:T(8,128)S(1)}, u32[]{:S(2)}, u32[]{:S(2)}) collective-permute-start(f32[64,2816]{1,0:T(8,128)S(1)} %pad_maximum_fusion.16), channel_id=1, source_target_pairs={{0,8},{4,12},{8,0},{12,4},{16,24},{20,28},{24,16},{28,20},{1,9},{5... | collective-permute-start | bytes 2162696 | tf_op jit(solution)/shard_map/ppermute | solution.py:62
  144.7 21.4 %collective-permute-start.27 = (f32[56,2816]{1,0:T(8,128)S(1)}, f32[56,2816]{1,0:T(8,128)S(1)}, u32[]{:S(2)}, u32[]{:S(2)}) collective-permute-start(f32[56,2816]{1,0:T(8,128)S(1)} %pad_maximum_fusion.21), channel_id=1, source_target_pairs={{0,16},{4,20},{8,24},{12,28},{16,0},{20,4},{24,8},{28,12},{1,17},{... | collective-permute-start | bytes 1892360 | tf_op jit(solution)/shard_map/ppermute | solution.py:62
  147.6 16.6 %collective-permute-start.25 = (f32[40,1408]{1,0:T(8,128)S(1)}, f32[40,1408]{1,0:T(8,128)S(1)}, u32[]{:S(2)}, u32[]{:S(2)}) collective-permute-start(f32[40,1408]{1,0:T(8,128)S(1)} %slice_add_fusion.16.refs_0_), channel_id=1, source_target_pairs={{0,16},{4,20},{8,24},{12,28},{16,0},{20,4},{24,8},{28,12},{1,17},{... | collective-permute-start | bytes 675848 | tf_op jit(solution)/shard_map/ppermute | solution.py:62
  149.5 16.4 %collective-permute-start.24 = (f32[40,1408]{1,0:T(8,128)S(1)}, f32[40,1408]{1,0:T(8,128)S(1)}, u32[]{:S(2)}, u32[]{:S(2)}) collective-permute-start(f32[40,1408]{1,0:T(8,128)S(1)} %slice_add_fusion.17.refs_4_), channel_id=1, source_target_pairs={{0,8},{4,12},{8,0},{12,4},{16,24},{20,28},{24,16},{28,20},{1,9},{5... | collective-permute-start | bytes 675848 | tf_op jit(solution)/shard_map/ppermute | solution.py:62
  166.8 16.9 %collective-permute-start.32 = (f32[40,2816]{1,0:T(8,128)S(1)}, f32[40,2816]{1,0:T(8,128)S(1)}, u32[]{:S(2)}, u32[]{:S(2)}) collective-permute-start(f32[40,2816]{1,0:T(8,128)S(1)} %pad_maximum_fusion.27), channel_id=1, source_target_pairs={{0,16},{4,20},{8,24},{12,28},{16,0},{20,4},{24,8},{28,12},{1,17},{... | collective-permute-start | bytes 1351688 | tf_op jit(solution)/shard_map/ppermute | solution.py:62
  167.1 16.5 %collective-permute-start.30 = (f32[40,2816]{1,0:T(8,128)S(1)}, f32[40,2816]{1,0:T(8,128)S(1)}, u32[]{:S(2)}, u32[]{:S(2)}) collective-permute-start(f32[40,2816]{1,0:T(8,128)S(1)} %pad_maximum_fusion.26), channel_id=1, source_target_pairs={{0,8},{4,12},{8,0},{12,4},{16,24},{20,28},{24,16},{28,20},{1,9},{5... | collective-permute-start | bytes 1351688 | tf_op jit(solution)/shard_map/ppermute | solution.py:62
  184.4 15.1 %collective-permute-start.29 = (f32[248,384]{1,0:T(8,128)S(1)}, f32[248,384]{1,0:T(8,128)S(1)}, u32[]{:S(2)}, u32[]{:S(2)}) collective-permute-start(f32[248,384]{1,0:T(8,128)S(1)} %get-tuple-element.212), channel_id=1, source_target_pairs={{0,1},{1,0},{2,3},{3,2},{4,5},{5,4},{6,7},{7,6},{8,9},{9,8},{10,11... | collective-permute-start | bytes 1142792 | tf_op jit(solution)/shard_map/ppermute | solution.py:62
  199.5 24.3 %collective-permute-start.34 = (f32[248,384]{1,0:T(8,128)S(1)}, f32[248,384]{1,0:T(8,128)S(1)}, u32[]{:S(2)}, u32[]{:S(2)}) collective-permute-start(f32[248,384]{1,0:T(8,128)S(1)} %add.224), channel_id=1, source_target_pairs={{0,2},{1,3},{2,0},{3,1},{4,6},{5,7},{6,4},{7,5},{8,10},{9,11},{10,... | collective-permute-start | bytes 1142792 | tf_op jit(solution)/shard_map/ppermute | solution.py:62
  199.6 14.2 %collective-permute-start.35 = (f32[168,384]{1,0:T(8,128)S(1)}, f32[168,384]{1,0:T(8,128)S(1)}, u32[]{:S(2)}, u32[]{:S(2)}) collective-permute-start(f32[168,384]{1,0:T(8,128)S(1)} %get-tuple-element.218), channel_id=1, source_target_pairs={{0,1},{1,0},{2,3},{3,2},{4,5},{5,4},{6,7},{7,6},{8,9},{9,8},{10,11... | collective-permute-start | bytes 774152 | tf_op jit(solution)/shard_map/ppermute | solution.py:62
  213.8 16.5 %collective-permute-start.37 = (f32[168,384]{1,0:T(8,128)S(1)}, f32[168,384]{1,0:T(8,128)S(1)}, u32[]{:S(2)}, u32[]{:S(2)}) collective-permute-start(f32[168,384]{1,0:T(8,128)S(1)} %add.225), channel_id=1, source_target_pairs={{0,2},{1,3},{2,0},{3,1},{4,6},{5,7},{6,4},{7,5},{8,10},{9,11},{10,... | collective-permute-start | bytes 774152 | tf_op jit(solution)/shard_map/ppermute | solution.py:62
  223.8 14.7 %collective-permute-start.36 = (f32[248,384]{1,0:T(8,128)S(1)}, f32[248,384]{1,0:T(8,128)S(1)}, u32[]{:S(2)}, u32[]{:S(2)}) collective-permute-start(f32[248,384]{1,0:T(8,128)S(1)} %add.226), channel_id=1, source_target_pairs={{0,1},{1,0},{2,3},{3,2},{4,5},{5,4},{6,7},{7,6},{8,9},{9,8},{10,11... | collective-permute-start | bytes 1142792 | tf_op jit(solution)/shard_map/ppermute | solution.py:62
  230.4 13.6 %collective-permute-start.38 = (f32[168,384]{1,0:T(8,128)S(1)}, f32[168,384]{1,0:T(8,128)S(1)}, u32[]{:S(2)}, u32[]{:S(2)}) collective-permute-start(f32[168,384]{1,0:T(8,128)S(1)} %add.227), channel_id=1, source_target_pairs={{0,1},{1,0},{2,3},{3,2},{4,5},{5,4},{6,7},{7,6},{8,9},{9,8},{10,11... | collective-permute-start | bytes 774152 | tf_op jit(solution)/shard_map/ppermute | solution.py:62
  263.1 19.9 %collective-permute-start.47 = (f32[64,2816]{1,0:T(8,128)S(1)}, f32[64,2816]{1,0:T(8,128)S(1)}, u32[]{:S(2)}, u32[]{:S(2)}) collective-permute-start(f32[64,2816]{1,0:T(8,128)S(1)} %pad_maximum_fusion.17), channel_id=1, source_target_pairs={{0,8},{4,12},{8,0},{12,4},{16,24},{20,28},{24,16},{28,20},{1,9},{5... | collective-permute-start | bytes 2162696 | tf_op jit(solution)/shard_map/ppermute | solution.py:62
  264.7 16.7 %collective-permute-start.40 = (f32[8,128]{1,0:T(8,128)S(1)}, f32[8,128]{1,0:T(8,128)S(1)}, u32[]{:S(2)}, u32[]{:S(2)}) collective-permute-start(f32[8,128]{1,0:T(8,128)S(1)} %broadcast_add_fusion.1), channel_id=1, source_target_pairs={{0,8},{4,12},{8,0},{12,4},{16,24},{20,28},{24,16},{28,20},{1,9},{5... | collective-permute-start | bytes 12296 | tf_op jit(solution)/shard_map/ppermute | solution.py:62
  265.5 19.4 %collective-permute-start.46 = (f32[56,2816]{1,0:T(8,128)S(1)}, f32[56,2816]{1,0:T(8,128)S(1)}, u32[]{:S(2)}, u32[]{:S(2)}) collective-permute-start(f32[56,2816]{1,0:T(8,128)S(1)} %slice.360), channel_id=1, source_target_pairs={{0,16},{4,20},{8,24},{12,28},{16,0},{20,4},{24,8},{28,12},{1,17},{... | collective-permute-start | bytes 1892360 | tf_op jit(solution)/shard_map/ppermute | solution.py:62
  283.1 11.3 %collective-permute-start.48 = (f32[64,1408]{1,0:T(8,128)S(1)}, f32[64,1408]{1,0:T(8,128)S(1)}, u32[]{:S(2)}, u32[]{:S(2)}) collective-permute-start(f32[64,1408]{1,0:T(8,128)S(1)} %slice.364), channel_id=1, source_target_pairs={{0,16},{4,20},{8,24},{12,28},{16,0},{20,4},{24,8},{28,12},{1,17},{... | collective-permute-start | bytes 1081352 | tf_op jit(solution)/shard_map/ppermute | solution.py:62
  285.0 11.3 %collective-permute-start.52 = (f32[56,1408]{1,0:T(8,128)S(1)}, f32[56,1408]{1,0:T(8,128)S(1)}, u32[]{:S(2)}, u32[]{:S(2)}) collective-permute-start(f32[56,1408]{1,0:T(8,128)S(1)} %slice.365), channel_id=1, source_target_pairs={{0,8},{4,12},{8,0},{12,4},{16,24},{20,28},{24,16},{28,20},{1,9},{5... | collective-permute-start | bytes 946184 | tf_op jit(solution)/shard_map/ppermute | solution.py:62
  286.8 18.3 %collective-permute-start.51 = (f32[40,2816]{1,0:T(8,128)S(1)}, f32[40,2816]{1,0:T(8,128)S(1)}, u32[]{:S(2)}, u32[]{:S(2)}) collective-permute-start(f32[40,2816]{1,0:T(8,128)S(1)} %pad_maximum_fusion.28), channel_id=1, source_target_pairs={{0,8},{4,12},{8,0},{12,4},{16,24},{20,28},{24,16},{28,20},{1,9},{5... | collective-permute-start | bytes 1351688 | tf_op jit(solution)/shard_map/ppermute | solution.py:62
  288.4 17.2 %collective-permute-start.50 = (f32[40,2816]{1,0:T(8,128)S(1)}, f32[40,2816]{1,0:T(8,128)S(1)}, u32[]{:S(2)}, u32[]{:S(2)}) collective-permute-start(f32[40,2816]{1,0:T(8,128)S(1)} %slice.368), channel_id=1, source_target_pairs={{0,16},{4,20},{8,24},{12,28},{16,0},{20,4},{24,8},{28,12},{1,17},{... | collective-permute-start | bytes 1351688 | tf_op jit(solution)/shard_map/ppermute | solution.py:62
  294.5 17.3 %collective-permute-start.49 = (f32[64,1408]{1,0:T(8,128)S(1)}, f32[64,1408]{1,0:T(8,128)S(1)}, u32[]{:S(2)}, u32[]{:S(2)}) collective-permute-start(f32[64,1408]{1,0:T(8,128)S(1)} %slice_add_fusion.7.refs_1_), channel_id=1, source_target_pairs={{0,16},{4,20},{8,24},{12,28},{16,0},{20,4},{24,8},{28,12},{1,17},{... | collective-permute-start | bytes 1081352 | tf_op jit(solution)/shard_map/ppermute | solution.py:62
  296.3 17.3 %collective-permute-start.56 = (f32[56,1408]{1,0:T(8,128)S(1)}, f32[56,1408]{1,0:T(8,128)S(1)}, u32[]{:S(2)}, u32[]{:S(2)}) collective-permute-start(f32[56,1408]{1,0:T(8,128)S(1)} %slice_add_fusion.10.refs_5_), channel_id=1, source_target_pairs={{0,8},{4,12},{8,0},{12,4},{16,24},{20,28},{24,16},{28,20},{1,9},{5... | collective-permute-start | bytes 946184 | tf_op jit(solution)/shard_map/ppermute | solution.py:62
  305.2 11.5 %collective-permute-start.55 = (f32[40,1408]{1,0:T(8,128)S(1)}, f32[40,1408]{1,0:T(8,128)S(1)}, u32[]{:S(2)}, u32[]{:S(2)}) collective-permute-start(f32[40,1408]{1,0:T(8,128)S(1)} %slice.374), channel_id=1, source_target_pairs={{0,16},{4,20},{8,24},{12,28},{16,0},{20,4},{24,8},{28,12},{1,17},{... | collective-permute-start | bytes 675848 | tf_op jit(solution)/shard_map/ppermute | solution.py:62
  305.6 12.8 %collective-permute-start.54 = (f32[40,1408]{1,0:T(8,128)S(1)}, f32[40,1408]{1,0:T(8,128)S(1)}, u32[]{:S(2)}, u32[]{:S(2)}) collective-permute-start(f32[40,1408]{1,0:T(8,128)S(1)} %slice.375), channel_id=1, source_target_pairs={{0,8},{4,12},{8,0},{12,4},{16,24},{20,28},{24,16},{28,20},{1,9},{5... | collective-permute-start | bytes 675848 | tf_op jit(solution)/shard_map/ppermute | solution.py:62
  311.9 24.7 %collective-permute-start.53 = (f32[64,2816]{1,0:T(8,128)S(1)}, f32[64,2816]{1,0:T(8,128)S(1)}, u32[]{:S(2)}, u32[]{:S(2)}) collective-permute-start(f32[64,2816]{1,0:T(8,128)S(1)} %pad_maximum_fusion.18), channel_id=1, source_target_pairs={{0,8},{4,12},{8,0},{12,4},{16,24},{20,28},{24,16},{28,20},{1,9},{5... | collective-permute-start | bytes 2162696 | tf_op jit(solution)/shard_map/ppermute | solution.py:62
  313.7 24.1 %collective-permute-start.60 = (f32[56,2816]{1,0:T(8,128)S(1)}, f32[56,2816]{1,0:T(8,128)S(1)}, u32[]{:S(2)}, u32[]{:S(2)}) collective-permute-start(f32[56,2816]{1,0:T(8,128)S(1)} %pad_maximum_fusion.22), channel_id=1, source_target_pairs={{0,16},{4,20},{8,24},{12,28},{16,0},{20,4},{24,8},{28,12},{1,17},{... | collective-permute-start | bytes 1892360 | tf_op jit(solution)/shard_map/ppermute | solution.py:62
  316.7 17.4 %collective-permute-start.58 = (f32[40,1408]{1,0:T(8,128)S(1)}, f32[40,1408]{1,0:T(8,128)S(1)}, u32[]{:S(2)}, u32[]{:S(2)}) collective-permute-start(f32[40,1408]{1,0:T(8,128)S(1)} %slice_add_fusion.14.refs_1_), channel_id=1, source_target_pairs={{0,16},{4,20},{8,24},{12,28},{16,0},{20,4},{24,8},{28,12},{1,17},{... | collective-permute-start | bytes 675848 | tf_op jit(solution)/shard_map/ppermute | solution.py:62
  318.5 17.2 %collective-permute-start.57 = (f32[40,1408]{1,0:T(8,128)S(1)}, f32[40,1408]{1,0:T(8,128)S(1)}, u32[]{:S(2)}, u32[]{:S(2)}) collective-permute-start(f32[40,1408]{1,0:T(8,128)S(1)} %slice_add_fusion.15.refs_5_), channel_id=1, source_target_pairs={{0,8},{4,12},{8,0},{12,4},{16,24},{20,28},{24,16},{28,20},{1,9},{5... | collective-permute-start | bytes 675848 | tf_op jit(solution)/shard_map/ppermute | solution.py:62
  342.9 20.3 %collective-permute-start.65 = (f32[40,2816]{1,0:T(8,128)}, f32[40,2816]{1,0:T(8,128)S(1)}, u32[]{:S(2)}, u32[]{:S(2)}) collective-permute-start(f32[40,2816]{1,0:T(8,128)} %pad_maximum_fusion.30), channel_id=1, source_target_pairs={{0,16},{4,20},{8,24},{12,28},{16,0},{20,4},{24,8},{28,12},{1,17},{... | collective-permute-start | bytes 1351688 | tf_op jit(solution)/shard_map/ppermute | solution.py:62
  343.9 19.2 %collective-permute-start.63 = (f32[40,2816]{1,0:T(8,128)}, f32[40,2816]{1,0:T(8,128)S(1)}, u32[]{:S(2)}, u32[]{:S(2)}) collective-permute-start(f32[40,2816]{1,0:T(8,128)} %pad_maximum_fusion.29), channel_id=1, source_target_pairs={{0,8},{4,12},{8,0},{12,4},{16,24},{20,28},{24,16},{28,20},{1,9},{5... | collective-permute-start | bytes 1351688 | tf_op jit(solution)/shard_map/ppermute | solution.py:62
  364.7 15.6 %collective-permute-start.62 = (f32[248,384]{1,0:T(8,128)S(1)}, f32[248,384]{1,0:T(8,128)S(1)}, u32[]{:S(2)}, u32[]{:S(2)}) collective-permute-start(f32[248,384]{1,0:T(8,128)S(1)} %get-tuple-element.261), channel_id=1, source_target_pairs={{0,1},{1,0},{2,3},{3,2},{4,5},{5,4},{6,7},{7,6},{8,9},{9,8},{10,11... | collective-permute-start | bytes 1142792 | tf_op jit(solution)/shard_map/ppermute | solution.py:62
  380.3 19.1 %collective-permute-start.67 = (f32[248,384]{1,0:T(8,128)S(1)}, f32[248,384]{1,0:T(8,128)S(1)}, u32[]{:S(2)}, u32[]{:S(2)}) collective-permute-start(f32[248,384]{1,0:T(8,128)S(1)} %add.245), channel_id=1, source_target_pairs={{0,2},{1,3},{2,0},{3,1},{4,6},{5,7},{6,4},{7,5},{8,10},{9,11},{10,... | collective-permute-start | bytes 1142792 | tf_op jit(solution)/shard_map/ppermute | solution.py:62
  380.4 14.3 %collective-permute-start.68 = (f32[168,384]{1,0:T(8,128)S(1)}, f32[168,384]{1,0:T(8,128)S(1)}, u32[]{:S(2)}, u32[]{:S(2)}) collective-permute-start(f32[168,384]{1,0:T(8,128)S(1)} %get-tuple-element.267), channel_id=1, source_target_pairs={{0,1},{1,0},{2,3},{3,2},{4,5},{5,4},{6,7},{7,6},{8,9},{9,8},{10,11... | collective-permute-start | bytes 774152 | tf_op jit(solution)/shard_map/ppermute | solution.py:62
  394.7 15.8 %collective-permute-start.70 = (f32[168,384]{1,0:T(8,128)S(1)}, f32[168,384]{1,0:T(8,128)S(1)}, u32[]{:S(2)}, u32[]{:S(2)}) collective-permute-start(f32[168,384]{1,0:T(8,128)S(1)} %add.246), channel_id=1, source_target_pairs={{0,2},{1,3},{2,0},{3,1},{4,6},{5,7},{6,4},{7,5},{8,10},{9,11},{10,... | collective-permute-start | bytes 774152 | tf_op jit(solution)/shard_map/ppermute | solution.py:62
  399.5 16.7 %collective-permute-start.69 = (f32[248,384]{1,0:T(8,128)S(1)}, f32[248,384]{1,0:T(8,128)S(1)}, u32[]{:S(2)}, u32[]{:S(2)}) collective-permute-start(f32[248,384]{1,0:T(8,128)S(1)} %add.247), channel_id=1, source_target_pairs={{0,1},{1,0},{2,3},{3,2},{4,5},{5,4},{6,7},{7,6},{8,9},{9,8},{10,11... | collective-permute-start | bytes 1142792 | tf_op jit(solution)/shard_map/ppermute | solution.py:62
  441.2 12.9 %collective-permute-start.74 = (f32[56,5632]{1,0:T(8,128)}, f32[56,5632]{1,0:T(8,128)}, u32[]{:S(2)}, u32[]{:S(2)}) collective-permute-start(f32[56,5632]{1,0:T(8,128)} %get-tuple-element.278), channel_id=1, source_target_pairs={{0,4},{4,0},{8,12},{12,8},{16,20},{20,16},{24,28},{28,24},{1,5},{5... | collective-permute-start | bytes 3784712 | tf_op jit(solution)/shard_map/ppermute | solution.py:62
  449.0 24.2 %collective-permute-start.80 = (f32[64,2816]{1,0:T(8,128)}, f32[64,2816]{1,0:T(8,128)}, u32[]{:S(2)}, u32[]{:S(2)}) collective-permute-start(f32[64,2816]{1,0:T(8,128)} %pad_maximum_fusion.19), channel_id=1, source_target_pairs={{0,8},{4,12},{8,0},{12,4},{16,24},{20,28},{24,16},{28,20},{1,9},{5... | collective-permute-start | bytes 2162696 | tf_op jit(solution)/shard_map/ppermute | solution.py:62
  452.5 18.5 %collective-permute-start.73 = (f32[8,128]{1,0:T(8,128)S(1)}, f32[8,128]{1,0:T(8,128)S(1)}, u32[]{:S(2)}, u32[]{:S(2)}) collective-permute-start(f32[8,128]{1,0:T(8,128)S(1)} %broadcast_add_fusion), channel_id=1, source_target_pairs={{0,8},{4,12},{8,0},{12,4},{16,24},{20,28},{24,16},{28,20},{1,9},{5... | collective-permute-start | bytes 12296 | tf_op jit(solution)/shard_map/ppermute | solution.py:62
  455.5 20.8 %collective-permute-start.79 = (f32[56,2816]{1,0:T(8,128)S(1)}, f32[56,2816]{1,0:T(8,128)S(1)}, u32[]{:S(2)}, u32[]{:S(2)}) collective-permute-start(f32[56,2816]{1,0:T(8,128)S(1)} %slice.386), channel_id=1, source_target_pairs={{0,16},{4,20},{8,24},{12,28},{16,0},{20,4},{24,8},{28,12},{1,17},{... | collective-permute-start | bytes 1892360 | tf_op jit(solution)/shard_map/ppermute | solution.py:62
  475.3 21.1 %collective-permute-start.83 = (f32[64,1408]{1,0:T(8,128)}, f32[64,1408]{1,0:T(8,128)S(1)}, u32[]{:S(2)}, u32[]{:S(2)}) collective-permute-start(f32[64,1408]{1,0:T(8,128)} %slice.390), channel_id=1, source_target_pairs={{0,16},{4,20},{8,24},{12,28},{16,0},{20,4},{24,8},{28,12},{1,17},{... | collective-permute-start | bytes 1081352 | tf_op jit(solution)/shard_map/ppermute | solution.py:62
  477.3 20.3 %collective-permute-start.82 = (f32[56,1408]{1,0:T(8,128)}, f32[56,1408]{1,0:T(8,128)}, u32[]{:S(2)}, u32[]{:S(2)}) collective-permute-start(f32[56,1408]{1,0:T(8,128)} %slice.391), channel_id=1, source_target_pairs={{0,8},{4,12},{8,0},{12,4},{16,24},{20,28},{24,16},{28,20},{1,9},{5... | collective-permute-start | bytes 946184 | tf_op jit(solution)/shard_map/ppermute | solution.py:62
  478.8 22.5 %collective-permute-start.87 = (f32[40,2816]{1,0:T(8,128)S(1)}, f32[40,2816]{1,0:T(8,128)}, u32[]{:S(2)}, u32[]{:S(2)}) collective-permute-start(f32[40,2816]{1,0:T(8,128)S(1)} %slice.394), channel_id=1, source_target_pairs={{0,16},{4,20},{8,24},{12,28},{16,0},{20,4},{24,8},{28,12},{1,17},{... | collective-permute-start | bytes 1351688 | tf_op jit(solution)/shard_map/ppermute | solution.py:62
  479.8 19.4 %collective-permute-start.81 = (f32[40,2816]{1,0:T(8,128)S(1)}, f32[40,2816]{1,0:T(8,128)}, u32[]{:S(2)}, u32[]{:S(2)}) collective-permute-start(f32[40,2816]{1,0:T(8,128)S(1)} %pad_maximum_fusion.31), channel_id=1, source_target_pairs={{0,8},{4,12},{8,0},{12,4},{16,24},{20,28},{24,16},{28,20},{1,9},{5... | collective-permute-start | bytes 1351688 | tf_op jit(solution)/shard_map/ppermute | solution.py:62
  496.4 11.4 %collective-permute-start.86 = (f32[64,1408]{1,0:T(8,128)S(1)}, f32[64,1408]{1,0:T(8,128)S(1)}, u32[]{:S(2)}, u32[]{:S(2)}) collective-permute-start(f32[64,1408]{1,0:T(8,128)S(1)} %slice_add_fusion.6.refs_0_), channel_id=1, source_target_pairs={{0,16},{4,20},{8,24},{12,28},{16,0},{20,4},{24,8},{28,12},{1,17},{... | collective-permute-start | bytes 1081352 | tf_op jit(solution)/shard_map/ppermute | solution.py:62
  500.3 12.3 %collective-permute-start.84 = (f32[40,1408]{1,0:T(8,128)S(1)}, f32[40,1408]{1,0:T(8,128)S(1)}, u32[]{:S(2)}, u32[]{:S(2)}) collective-permute-start(f32[40,1408]{1,0:T(8,128)S(1)} %slice.400), channel_id=1, source_target_pairs={{0,16},{4,20},{8,24},{12,28},{16,0},{20,4},{24,8},{28,12},{1,17},{... | collective-permute-start | bytes 675848 | tf_op jit(solution)/shard_map/ppermute | solution.py:62
  502.4 11.4 %collective-permute-start.89 = (f32[40,1408]{1,0:T(8,128)S(1)}, f32[40,1408]{1,0:T(8,128)S(1)}, u32[]{:S(2)}, u32[]{:S(2)}) collective-permute-start(f32[40,1408]{1,0:T(8,128)S(1)} %slice.402), channel_id=1, source_target_pairs={{0,8},{4,12},{8,0},{12,4},{16,24},{20,28},{24,16},{28,20},{1,9},{5... | collective-permute-start | bytes 675848 | tf_op jit(solution)/shard_map/ppermute | solution.py:62
  507.9 27.3 %collective-permute-start.92 = (f32[64,2816]{1,0:T(8,128)S(1)}, f32[64,2816]{1,0:T(8,128)S(1)}, u32[]{:S(2)}, u32[]{:S(2)}) collective-permute-start(f32[64,2816]{1,0:T(8,128)S(1)} %pad_maximum_fusion.20), channel_id=1, source_target_pairs={{0,8},{4,12},{8,0},{12,4},{16,24},{20,28},{24,16},{28,20},{1,9},{5... | collective-permute-start | bytes 2162696 | tf_op jit(solution)/shard_map/ppermute | solution.py:62
  509.1 26.3 %collective-permute-start.91 = (f32[56,2816]{1,0:T(8,128)S(1)}, f32[56,2816]{1,0:T(8,128)S(1)}, u32[]{:S(2)}, u32[]{:S(2)}) collective-permute-start(f32[56,2816]{1,0:T(8,128)S(1)} %pad_maximum_fusion.23), channel_id=1, source_target_pairs={{0,16},{4,20},{8,24},{12,28},{16,0},{20,4},{24,8},{28,12},{1,17},{... | collective-permute-start | bytes 1892360 | tf_op jit(solution)/shard_map/ppermute | solution.py:62
  512.7 16.2 %collective-permute-start.88 = (f32[40,1408]{1,0:T(8,128)S(1)}, f32[40,1408]{1,0:T(8,128)S(1)}, u32[]{:S(2)}, u32[]{:S(2)}) collective-permute-start(f32[40,1408]{1,0:T(8,128)S(1)} %slice_add_fusion.13.refs_0_), channel_id=1, source_target_pairs={{0,16},{4,20},{8,24},{12,28},{16,0},{20,4},{24,8},{28,12},{1,17},{... | collective-permute-start | bytes 675848 | tf_op jit(solution)/shard_map/ppermute | solution.py:62
  513.9 20.2 %collective-permute-start.93 = (f32[40,1408]{1,0:T(8,128)S(1)}, f32[40,1408]{1,0:T(8,128)S(1)}, u32[]{:S(2)}, u32[]{:S(2)}) collective-permute-start(f32[40,1408]{1,0:T(8,128)S(1)} %slice_add_fusion.12.refs_4_), channel_id=1, source_target_pairs={{0,8},{4,12},{8,0},{12,4},{16,24},{20,28},{24,16},{28,20},{1,9},{5... | collective-permute-start | bytes 675848 | tf_op jit(solution)/shard_map/ppermute | solution.py:62
  528.9 12.6 %collective-permute-start.90 = (f32[40,2816]{1,0:T(8,128)S(1)}, f32[40,2816]{1,0:T(8,128)S(1)}, u32[]{:S(2)}, u32[]{:S(2)}) collective-permute-start(f32[40,2816]{1,0:T(8,128)S(1)} %pad_maximum_fusion.32), channel_id=1, source_target_pairs={{0,8},{4,12},{8,0},{12,4},{16,24},{20,28},{24,16},{28,20},{1,9},{5... | collective-permute-start | bytes 1351688 | tf_op jit(solution)/shard_map/ppermute | solution.py:62
  (83 other events, 1276.3 us)

commit v4 on v3

--- a/solution.py
+++ b/solution.py
@@ -12,7 +12,7 @@
 LANES, ROWS8, UNIT = 128, 8, 16
 NT = (((1,), (1,)), ((), ()))
 NN = (((1,), (0,)), ((), ()))
-VMEM_LIMIT = 32 * 1024 * 1024
+MIB = 1024 * 1024
 
 
 def parts_of(x):
@@ -26,8 +26,8 @@
     return dot(x_high, high) + (dot(x_low, high) + dot(x_high, low))
 
 
-def params():
-    return pltpu.CompilerParams(vmem_limit_bytes=VMEM_LIMIT)
+def params(mib):
+    return pltpu.CompilerParams(vmem_limit_bytes=mib * MIB)
 
 
 class Plan:
@@ -112,7 +112,7 @@
             scratch_shapes=[pltpu.VMEM((plan.classes, step), F32)],
         ),
         input_output_aliases=aliases,
-        compiler_params=params(),
+        compiler_params=params(20),
         cost_estimate=pl.CostEstimate(
             flops=6 * plan.classes * step * plan.feats,
             bytes_accessed=4 * plan.feats * (2 * step + plan.classes),
@@ -163,7 +163,7 @@
             ],
             out_specs=specs,
         ),
-        compiler_params=params(),
+        compiler_params=params(20),
         cost_estimate=pl.CostEstimate(
             flops=6 * n_group * rows * feats, bytes_accessed=4 * feats * (rows + n_group), transcendentals=0
         ),
@@ -301,7 +301,7 @@
             ],
         ),
         input_output_aliases=aliases,
-        compiler_params=params(),
+        compiler_params=params(30),
         cost_estimate=pl.CostEstimate(
             flops=6 * n_pair * rows * feats, bytes_accessed=4 * feats * (rows + 3 * n_pair), transcendentals=0
         ),
@@ -369,7 +369,7 @@
             pltpu.SemaphoreType.DMA((nb,)),
         ],
         input_output_aliases=aliases,
-        compiler_params=params(),
+        compiler_params=params(22),
         cost_estimate=pl.CostEstimate(
             flops=6 * n_pair * plan.feats, bytes_accessed=16 * n_pair * plan.feats, transcendentals=0
         ),
@@ -508,9 +508,8 @@
         split, halves = first(plan, where, order.after(features), weights, part, split)
         order.note(halves[0])
         parts.append(FeatSum(plan, halves, bit, 0))
-    for part in range(len(parts) - 1, len(parts) - 3, -1):
-        if part > 0:
-            parts[part - 1].advance(order)
+    for summed in parts:
+        summed.advance(order)
     high, low = split
     probs, values = [], []
     for part, summed in enumerate(parts):
@@ -566,9 +565,11 @@
 
         vectors = multiply(0)
         go(2, 3)
+        found[0].advance(order)
         vectors = multiply(1)
         for k in (0, 1, 0, 1):
-            found[k].advance(order)
+            if found[k].strides:
+                found[k].advance(order)
         tangents = [f.result(order) for f in found]
         inner = sum(t[-ROWS8 : 2 - ROWS8, 0] for t in tangents)
         return vectors, jnp.concatenate([t[:-ROWS8] for t in tangents], axis=0), inner

time: 561 us -> 561 us (level)
  local copies, waits for them, and re-layouts: 32.5 us -> 49.8 us
  Pallas kernels: 143 us -> 134 us
  waiting for transfers between devices: 243 us -> 234 us
    unnamed x96 -> x70, local copies, waits for them, and re-layouts: 23.3 us -> 40.9 us
    ppermute x99, waiting for transfers between devices: 243 us -> 234 us  [swap(): return lax.ppermute(x, axis, [(i, i ^ stride) for i in range(size)])]
  transfers between devices with their start and end apart: 99 -> 99, of which waited for: 45 -> 42; matrix products, arithmetic and copies ran while one was open for 7% -> 7% of each run, Pallas kernels for 18% -> 17%
where the time goes in v4:
time: 561 us; the launch traced here: 552 us
  waiting for transfers between devices  234 us (42%)
  Pallas kernels  134 us (24%)
  starting transfers between devices  87.9 us (16%)
  local copies, waits for them, and re-layouts  49.8 us (9%)
  other arithmetic  38.1 us (7%)
  between operations  8.76 us (2%)
    ppermute x99, waiting for transfers between devices, swap(): return lax.ppermute(x, axis, [(i, i ^ stride) for i in range(size)])  234 us
    ppermute x99, starting transfers between devices, swap(): return lax.ppermute(x, axis, [(i, i ^ stride) for i in range(size)])  87.9 us
    pallas_call x6, Pallas kernels, back(): pl.pallas_call(functools.partial(back_body, plan, group), out_shape=outs,...  53.9 us
    pallas_call x4, Pallas kernels, forth(): pl.pallas_call(functools.partial(forth_body, plan, pair, step is not None...  49.6 us
    unnamed x70, local copies, waits for them, and re-layouts  40.9 us
    pallas_call x3, Pallas kernels, first(): pl.pallas_call(functools.partial(first_body, plan), out_shape=[jax.ShapeD...  22.6 us
    add x1, other arithmetic, under(): order.after(weights) + (step0 + step1 * ratio) * direction  14 us
  transfers between devices with their start and end apart: 99, of which 42 were waited for; matrix products, arithmetic and copies ran while one was open for 7% of the time, Pallas kernels for 17%

profile of v4, /device:TPU:0, one launch (start us, length us, event | category | flops | bytes accessed | tf_op | source)
XLA Modules:
  0.0 552.5 jit_solution(3442010203261631905)
XLA Ops:
  0.7 3.6 copy-done.11
  4.3 7.5 %split_and_logits.3 = (bf16[768,5632]{1,0:T(8,128)(2,1)S(1)}, bf16[768,5632]{1,0:T(8,128)(2,1)S(1)}, f32[200,256]{1,0:T(8,128)S(1)}, f32[200,256]{1,0:T(8,128)S(1)}) custom-call(s32[3]{0:T(128)S(1)} %pad_add_fusion.s_ref, f32[768,5632]{1,0:T(8,128)} %f_ref.3, f32[400,5632]{1,0:T(8,128)S(1)} %copy-done.11), custom_call_target="tpu_custom_call" | custom-call | flops 3460300800 | bytes 20545536 | tf_op jit(solution)/shard_map/split_and_logits/pallas_call | solution.py:102
  11.8 3.1 collective-permute-start
  14.9 7.5 %split_and_logits.4 = (bf16[768,5632]{1,0:T(8,128)(2,1)S(1)}, bf16[768,5632]{1,0:T(8,128)(2,1)S(1)}, f32[200,256]{1,0:T(8,128)S(1)}, f32[200,256]{1,0:T(8,128)S(1)}) custom-call(s32[3]{0:T(128)S(1)} %pad_add_fusion.s_ref, f32[768,5632]{1,0:T(8,128)} %f_ref.3, f32[400,5632]{1,0:T(8,128)S(1)} %copy-done.11, ...), custom_call_target="tpu_custom_call", output_to_operand_aliasing={{0}: (3, {}), {1}: (4, {})} | custom-call | flops 3460300800 | bytes 20545536 | tf_op jit(solution)/shard_map/split_and_logits/pallas_call | solution.py:102
  22.6 3.1 collective-permute-start.1
  25.7 7.5 %split_and_logits.5 = (bf16[768,5632]{1,0:T(8,128)(2,1)S(1)}, bf16[768,5632]{1,0:T(8,128)(2,1)S(1)}, f32[200,256]{1,0:T(8,128)S(1)}, f32[200,256]{1,0:T(8,128)S(1)}) custom-call(s32[3]{0:T(128)S(1)} %pad_add_fusion.s_ref, f32[768,5632]{1,0:T(8,128)} %f_ref.3, f32[400,5632]{1,0:T(8,128)S(1)} %copy-done.11, ...), custom_call_target="tpu_custom_call", output_to_operand_aliasing={{0}: (3, {}), {1}: (4, {})} | custom-call | flops 3460300800 | bytes 20545536 | tf_op jit(solution)/shard_map/split_and_logits/pallas_call | solution.py:102
  33.2 3.5 copy-done
  36.7 3.4 copy-done.5
  42.3 11.5 %collective-permute-done.3 = f32[200,256]{1,0:T(8,128)S(1)} collective-permute-done((f32[200,256]{1,0:T(8,128)S(1)}, f32[200,256]{1,0:T(8,128)S(1)}, u32[]{:S(2)}, u32[]{:S(2)}) %collective-permute-start.3) | collective-permute-done | bytes 204832 | tf_op jit(solution)/shard_map/ppermute | solution.py:62
  54.2 2.0 collective-permute-done.2
  57.3 7.0 %collective-permute-done.6 = f32[200,256]{1,0:T(8,128)S(1)} collective-permute-done((f32[200,256]{1,0:T(8,128)S(1)}, f32[200,256]{1,0:T(8,128)S(1)}, u32[]{:S(2)}, u32[]{:S(2)}) %collective-permute-start.6) | collective-permute-done | bytes 204832 | tf_op jit(solution)/shard_map/ppermute | solution.py:62
  65.6 4.5 collective-permute-done.8
  70.8 3.6 copy-done.6
  74.4 9.9 %back_group.6 = (f32[64,5632]{1,0:T(8,128)S(1)}, f32[64,5632]{1,0:T(8,128)S(1)}, f32[56,5632]{1,0:T(8,128)S(1)}, f32[56,5632]{1,0:T(8,128)S(1)}) custom-call(s32[3]{0:T(128)S(1)} %pad_add_fusion.s_ref, f32[240,768]{1,0:T(8,128)S(1)} %slice.331.g_ref, bf16[768,5632]{1,0:T(8,128)(2,1)S(1)} %copy-done.1, bf16[768,5632]{1,0:T(8,128)(2,1)S(1)} %copy-done.6), custom_call_target="tpu_custom_call" | custom-call | flops 6228541440 | bytes 22708224 | tf_op jit(solution)/shard_map/back_group/pallas_call | solution.py:153
  84.9 2.7 collective-permute-done.9
  91.3 7.8 %back_group.7 = (f32[40,5632]{1,0:T(8,128)S(1)}, f32[40,5632]{1,0:T(8,128)S(1)}, f32[40,5632]{1,0:T(8,128)S(1)}, f32[40,5632]{1,0:T(8,128)S(1)}) custom-call(s32[3]{0:T(128)S(1)} %pad_add_fusion.s_ref, f32[160,768]{1,0:T(8,128)S(1)} %pad_maximum_fusion.24.g_ref, bf16[768,5632]{1,0:T(8,128)(2,1)S(1)} %copy-done.1, bf16[768,5632]{1,0:T(8,128)(2,1)S(1)} %copy-done.6), custom_call_target="tpu_custom_call" | custom-call | flops 4152360960 | bytes 20905984 | tf_op jit(solution)/shard_map/back_group/pallas_call | solution.py:153
  99.7 6.5 %collective-permute-done.10 = f32[64,2816]{1,0:T(8,128)S(1)} collective-permute-done((f32[64,2816]{1,0:T(8,128)S(1)}, f32[64,2816]{1,0:T(8,128)S(1)}, u32[]{:S(2)}, u32[]{:S(2)}) %collective-permute-start.10) | collective-permute-done | bytes 720928 | tf_op jit(solution)/shard_map/ppermute | solution.py:62
  111.1 6.6 %collective-permute-done.12 = f32[64,1408]{1,0:T(8,128)S(1)} collective-permute-done((f32[64,1408]{1,0:T(8,128)S(1)}, f32[64,1408]{1,0:T(8,128)S(1)}, u32[]{:S(2)}, u32[]{:S(2)}) %collective-permute-start.12) | collective-permute-done | bytes 360480 | tf_op jit(solution)/shard_map/ppermute | solution.py:62
  121.0 7.1 %collective-permute-done.18 = f32[40,2816]{1,0:T(8,128)S(1)} collective-permute-done((f32[40,2816]{1,0:T(8,128)S(1)}, f32[40,2816]{1,0:T(8,128)S(1)}, u32[]{:S(2)}, u32[]{:S(2)}) %collective-permute-start.18) | collective-permute-done | bytes 450592 | tf_op jit(solution)/shard_map/ppermute | solution.py:62
  130.4 4.7 collective-permute-done.16.refs_1_
  143.2 13.4 %collective-permute-done.25.refs_1_ = f32[40,1408]{1,0:T(8,128)S(1)} collective-permute-done((f32[40,1408]{1,0:T(8,128)S(1)}, f32[40,1408]{1,0:T(8,128)S(1)}, u32[]{:S(2)}, u32[]{:S(2)}) %collective-permute-start.25) | collective-permute-done | bytes 225312 | tf_op jit(solution)/shard_map/ppermute | solution.py:62
  160.9 2.3 collective-permute-done.28.refs_7_
  163.2 11.8 %forth_pair.4 = (f32[400,5632]{1,0:T(8,128)}, f32[248,384]{1,0:T(8,128)S(1)}, f32[248,384]{1,0:T(8,128)S(1)}) custom-call(s32[3]{0:T(128)S(1)} %pad_add_fusion.s_ref, f32[64,1408]{1,0:T(8,128)S(1)} %slice_add_fusion.8.refs_0_, f32[64,1408]{1,0:T(8,128)S(1)} %collective-permute-done.16.refs_1_, f32[64,2816]{1,0:T(8,128)S(1)} %collective-permute-done.20.refs_2_, ...), custom_call_target="tpu_custom_call" | custom-call | flops 6228541440 | bytes 33521664 | tf_op jit(solution)/shard_map/forth_pair/pallas_call | solution.py:289
  176.6 10.0 %collective-permute-done.29 = f32[248,384]{1,0:T(8,128)S(1)} collective-permute-done((f32[248,384]{1,0:T(8,128)S(1)}, f32[248,384]{1,0:T(8,128)S(1)}, u32[]{:S(2)}, u32[]{:S(2)}) %collective-permute-start.29) | collective-permute-done | bytes 380960 | tf_op jit(solution)/shard_map/ppermute | solution.py:62
  188.1 11.8 %forth_pair.5 = (f32[400,5632]{1,0:T(8,128)}, f32[168,384]{1,0:T(8,128)S(1)}, f32[168,384]{1,0:T(8,128)S(1)}) custom-call(s32[3]{0:T(128)S(1)} %pad_add_fusion.s_ref, f32[40,1408]{1,0:T(8,128)S(1)} %slice_add_fusion.16.refs_0_, f32[40,1408]{1,0:T(8,128)S(1)} %collective-permute-done.25.refs_1_, ...), custom_call_target="tpu_custom_call", output_to_operand_aliasing={{0}: (11, {})} | custom-call | flops 4152360960 | bytes 28114944 | tf_op jit(solution)/shard_map/forth_pair/pallas_call | solution.py:289
  201.6 4.3 collective-permute-done.32
  206.1 5.4 collective-permute-done.36
  212.2 10.0 %collective-permute-done.35 = f32[248,384]{1,0:T(8,128)S(1)} collective-permute-done((f32[248,384]{1,0:T(8,128)S(1)}, f32[248,384]{1,0:T(8,128)S(1)}, u32[]{:S(2)}, u32[]{:S(2)}) %collective-permute-start.35) | collective-permute-done | bytes 380960 | tf_op jit(solution)/shard_map/ppermute | solution.py:62
  222.1 4.0 collective-permute-done.37
  226.3 7.1 %collective-permute-done.38 = f32[168,384]{1,0:T(8,128)S(1)} collective-permute-done((f32[168,384]{1,0:T(8,128)S(1)}, f32[168,384]{1,0:T(8,128)S(1)}, u32[]{:S(2)}, u32[]{:S(2)}) %collective-permute-start.38) | collective-permute-done | bytes 258080 | tf_op jit(solution)/shard_map/ppermute | solution.py:62
  234.8 3.4 copy-done.7
  238.2 9.9 %back_group.8 = (f32[64,5632]{1,0:T(8,128)S(1)}, f32[64,5632]{1,0:T(8,128)S(1)}, f32[56,5632]{1,0:T(8,128)S(1)}, f32[56,5632]{1,0:T(8,128)S(1)}) custom-call(s32[3]{0:T(128)S(1)} %pad_add_fusion.s_ref, f32[240,768]{1,0:T(8,128)S(1)} %slice.356.g_ref, bf16[768,5632]{1,0:T(8,128)(2,1)S(1)} %copy-done.1, bf16[768,5632]{1,0:T(8,128)(2,1)S(1)} %copy-done.7), custom_call_target="tpu_custom_call" | custom-call | flops 6228541440 | bytes 22708224 | tf_op jit(solution)/shard_map/back_group/pallas_call | solution.py:153
  249.6 3.7 collective-permute-done.39
  257.3 7.8 %back_group.9 = (f32[40,5632]{1,0:T(8,128)S(1)}, f32[40,5632]{1,0:T(8,128)S(1)}, f32[40,5632]{1,0:T(8,128)S(1)}, f32[40,5632]{1,0:T(8,128)S(1)}) custom-call(s32[3]{0:T(128)S(1)} %pad_add_fusion.s_ref, f32[160,768]{1,0:T(8,128)S(1)} %slice.357.g_ref, bf16[768,5632]{1,0:T(8,128)(2,1)S(1)} %copy-done.1, bf16[768,5632]{1,0:T(8,128)(2,1)S(1)} %copy-done.7), custom_call_target="tpu_custom_call" | custom-call | flops 4152360960 | bytes 20905984 | tf_op jit(solution)/shard_map/back_group/pallas_call | solution.py:153
  265.1 7.6 %collective-permute-done.40 = f32[8,128]{1,0:T(8,128)S(1)} collective-permute-done((f32[8,128]{1,0:T(8,128)S(1)}, f32[8,128]{1,0:T(8,128)S(1)}, u32[]{:S(2)}, u32[]{:S(2)}) %collective-permute-start.40) | collective-permute-done | bytes 4128 | tf_op jit(solution)/shard_map/ppermute | solution.py:62
  279.4 6.6 %collective-permute-done.48 = f32[64,1408]{1,0:T(8,128)S(1)} collective-permute-done((f32[64,1408]{1,0:T(8,128)S(1)}, f32[64,1408]{1,0:T(8,128)S(1)}, u32[]{:S(2)}, u32[]{:S(2)}) %collective-permute-start.48) | collective-permute-done | bytes 360480 | tf_op jit(solution)/shard_map/ppermute | solution.py:62
  289.3 7.2 %collective-permute-done.51 = f32[40,2816]{1,0:T(8,128)S(1)} collective-permute-done((f32[40,2816]{1,0:T(8,128)S(1)}, f32[40,2816]{1,0:T(8,128)S(1)}, u32[]{:S(2)}, u32[]{:S(2)}) %collective-permute-start.51) | collective-permute-done | bytes 450592 | tf_op jit(solution)/shard_map/ppermute | solution.py:62
  298.8 4.6 collective-permute-done.49.refs_2_
  311.5 13.9 %collective-permute-done.58.refs_2_ = f32[40,1408]{1,0:T(8,128)S(1)} collective-permute-done((f32[40,1408]{1,0:T(8,128)S(1)}, f32[40,1408]{1,0:T(8,128)S(1)}, u32[]{:S(2)}, u32[]{:S(2)}) %collective-permute-start.58) | collective-permute-done | bytes 225312 | tf_op jit(solution)/shard_map/ppermute | solution.py:62
  336.6 3.5 copy-done.2
  340.0 3.5 copy-done.8
  343.5 13.6 %forth_pair.6 = (f32[400,5632]{1,0:T(8,128)}, f32[248,384]{1,0:T(8,128)S(1)}, f32[248,384]{1,0:T(8,128)S(1)}) custom-call(s32[3]{0:T(128)S(1)} %pad_add_fusion.s_ref, f32[1]{0:T(128)} %bitcast.5.refs_0_, f32[64,1408]{1,0:T(8,128)S(1)} %slice_add_fusion.7.refs_1_, f32[64,1408]{1,0:T(8,128)S(1)} %collective-permute-done.49.refs_2_, ...), custom_call_target="tpu_custom_call" | custom-call | flops 6228541440 | bytes 33521664 | tf_op jit(solution)/shard_map/forth_pair/pallas_call | solution.py:289
  358.9 10.6 %collective-permute-done.62 = f32[248,384]{1,0:T(8,128)S(1)} collective-permute-done((f32[248,384]{1,0:T(8,128)S(1)}, f32[248,384]{1,0:T(8,128)S(1)}, u32[]{:S(2)}, u32[]{:S(2)}) %collective-permute-start.62) | collective-permute-done | bytes 380960 | tf_op jit(solution)/shard_map/ppermute | solution.py:62
  371.2 12.4 %forth_pair.7 = (f32[400,5632]{1,0:T(8,128)}, f32[168,384]{1,0:T(8,128)S(1)}, f32[168,384]{1,0:T(8,128)S(1)}) custom-call(s32[3]{0:T(128)S(1)} %pad_add_fusion.s_ref, f32[1]{0:T(128)} %bitcast.5.refs_0_, f32[40,1408]{1,0:T(8,128)S(1)} %slice_add_fusion.14.refs_1_, f32[40,1408]{1,0:T(8,128)S(1)} %collective-permute-done.58.refs_2_, ...), custom_call_target="tpu_custom_call", output_to_operand_aliasing={{0}: (13, {})} | custom-call | flops 4152360960 | bytes 28114944 | tf_op jit(solution)/shard_map/forth_pair/pallas_call | solution.py:289
  385.3 3.4 collective-permute-done.65
  388.9 5.4 collective-permute-done.69
  394.9 10.0 %collective-permute-done.68 = f32[248,384]{1,0:T(8,128)S(1)} collective-permute-done((f32[248,384]{1,0:T(8,128)S(1)}, f32[248,384]{1,0:T(8,128)S(1)}, u32[]{:S(2)}, u32[]{:S(2)}) %collective-permute-start.68) | collective-permute-done | bytes 380960 | tf_op jit(solution)/shard_map/ppermute | solution.py:62
  404.9 3.9 collective-permute-done.70
  409.2 7.0 %collective-permute-done.71 = f32[168,384]{1,0:T(8,128)S(1)} collective-permute-done((f32[168,384]{1,0:T(8,128)S(1)}, f32[168,384]{1,0:T(8,128)S(1)}, u32[]{:S(2)}, u32[]{:S(2)}) %collective-permute-start.71) | collective-permute-done | bytes 258080 | tf_op jit(solution)/shard_map/ppermute | solution.py:62
  422.4 3.5 copy-done.3
  425.8 3.5 copy-done.9
  429.3 10.9 %back_group.10 = (f32[64,5632]{1,0:T(8,128)S(1)}, f32[64,5632]{1,0:T(8,128)S(1)}, f32[56,5632]{1,0:T(8,128)S(1)}, f32[56,5632]{1,0:T(8,128)}) custom-call(s32[3]{0:T(128)S(1)} %pad_add_fusion.s_ref, f32[240,768]{1,0:T(8,128)S(1)} %slice.382.g_ref, bf16[768,5632]{1,0:T(8,128)(2,1)S(1)} %copy-done.3, bf16[768,5632]{1,0:T(8,128)(2,1)S(1)} %copy-done.9), custom_call_target="tpu_custom_call" | custom-call | flops 6228541440 | bytes 22708224 | tf_op jit(solution)/shard_map/back_group/pallas_call | solution.py:153
  441.3 3.8 collective-permute-done.72
  454.8 3.5 copy-done.4
  458.3 3.5 copy-done.10
  461.8 7.6 %back_group.11 = (f32[40,5632]{1,0:T(8,128)S(1)}, f32[40,5632]{1,0:T(8,128)S(1)}, f32[40,5632]{1,0:T(8,128)S(1)}, f32[40,5632]{1,0:T(8,128)S(1)}) custom-call(s32[3]{0:T(128)S(1)} %pad_add_fusion.s_ref, f32[160,768]{1,0:T(8,128)S(1)} %slice.383.g_ref, bf16[768,5632]{1,0:T(8,128)(2,1)S(1)} %copy-done.4, bf16[768,5632]{1,0:T(8,128)(2,1)S(1)} %copy-done.10), custom_call_target="tpu_custom_call" | custom-call | flops 4152360960 | bytes 20905984 | tf_op jit(solution)/shard_map/back_group/pallas_call | solution.py:153
  482.1 14.0 %multiply_add_fusion = f32[400,5632]{1,0:T(8,128)} fusion(f32[400,5632]{1,0:T(8,128)} %get-tuple-element.295.refs_9_, f32[400,5632]{1,0:T(8,128)} %w_ref.5, f32[400,5632]{1,0:T(8,128)} %get-tuple-element.259.refs_9_.refs_8_, f32[]{:T(128)} %div.82, f32[]{:T(128)S(6)} %add.263), kind=kLoop, calls=%fused_computation | loop fusion | flops 9011200 | bytes 36044808 | tf_op jit(solution)/shard_map/add | solution.py:596
  497.4 1.7 slice_add_fusion.9.refs_4_
  504.7 2.9 collective-permute-done.86.refs_1_
  515.2 13.3 %collective-permute-done.88.refs_1_ = f32[40,1408]{1,0:T(8,128)S(1)} collective-permute-done((f32[40,1408]{1,0:T(8,128)S(1)}, f32[40,1408]{1,0:T(8,128)S(1)}, u32[]{:S(2)}, u32[]{:S(2)}) %collective-permute-start.88) | collective-permute-done | bytes 225312 | tf_op jit(solution)/shard_map/ppermute | solution.py:62
  529.2 5.6 %collective-permute-done.93.refs_5_ = f32[40,1408]{1,0:T(8,128)S(1)} collective-permute-done((f32[40,1408]{1,0:T(8,128)S(1)}, f32[40,1408]{1,0:T(8,128)S(1)}, u32[]{:S(2)}, u32[]{:S(2)}) %collective-permute-start.93) | collective-permute-done | bytes 225312 | tf_op jit(solution)/shard_map/ppermute | solution.py:62
  536.8 5.2 collective-permute-done.90.refs_2_
  544.0 4.5 last_rows.2.refs_10_
  548.5 3.5 last_rows.3
  (371 shorter events, 125.8 us)
Async XLA Ops:
  22.4 19.7 %collective-permute-start.4 = (f32[200,256]{1,0:T(8,128)S(1)}, f32[200,256]{1,0:T(8,128)S(1)}, u32[]{:S(2)}, u32[]{:S(2)}) collective-permute-start(f32[200,256]{1,0:T(8,128)S(1)} %get-tuple-element.163), channel_id=1, source_target_pairs={{0,1},{1,0},{2,3},{3,2},{4,5},{5,4},{6,7},{7,6},{8,9},{9,8},{10,11... | collective-permute-start | bytes 614408 | tf_op jit(solution)/shard_map/ppermute | solution.py:62
  22.6 19.1 %collective-permute-start.1 = (f32[200,256]{1,0:T(8,128)S(1)}, f32[200,256]{1,0:T(8,128)S(1)}, u32[]{:S(2)}, u32[]{:S(2)}) collective-permute-start(f32[200,256]{1,0:T(8,128)S(1)} %add.206), channel_id=1, source_target_pairs={{0,2},{1,3},{2,0},{3,1},{4,6},{5,7},{6,4},{7,5},{8,10},{9,11},{10,... | collective-permute-start | bytes 614408 | tf_op jit(solution)/shard_map/ppermute | solution.py:62
  40.1 13.7 %collective-permute-start.3 = (f32[200,256]{1,0:T(8,128)S(1)}, f32[200,256]{1,0:T(8,128)S(1)}, u32[]{:S(2)}, u32[]{:S(2)}) collective-permute-start(f32[200,256]{1,0:T(8,128)S(1)} %get-tuple-element.168), channel_id=1, source_target_pairs={{0,1},{1,0},{2,3},{3,2},{4,5},{5,4},{6,7},{7,6},{8,9},{9,8},{10,11... | collective-permute-start | bytes 614408 | tf_op jit(solution)/shard_map/ppermute | solution.py:62
  41.7 14.5 %collective-permute-start.2 = (f32[200,256]{1,0:T(8,128)S(1)}, f32[200,256]{1,0:T(8,128)S(1)}, u32[]{:S(2)}, u32[]{:S(2)}) collective-permute-start(f32[200,256]{1,0:T(8,128)S(1)} %add.207), channel_id=1, source_target_pairs={{0,1},{1,0},{2,3},{3,2},{4,5},{5,4},{6,7},{7,6},{8,9},{9,8},{10,11... | collective-permute-start | bytes 614408 | tf_op jit(solution)/shard_map/ppermute | solution.py:62
  42.2 13.9 %collective-permute-start.5 = (f32[200,256]{1,0:T(8,128)S(1)}, f32[200,256]{1,0:T(8,128)S(1)}, u32[]{:S(2)}, u32[]{:S(2)}) collective-permute-start(f32[200,256]{1,0:T(8,128)S(1)} %add.208), channel_id=1, source_target_pairs={{0,2},{1,3},{2,0},{3,1},{4,6},{5,7},{6,4},{7,5},{8,10},{9,11},{10,... | collective-permute-start | bytes 614408 | tf_op jit(solution)/shard_map/ppermute | solution.py:62
  87.9 18.2 %collective-permute-start.10 = (f32[64,2816]{1,0:T(8,128)S(1)}, f32[64,2816]{1,0:T(8,128)S(1)}, u32[]{:S(2)}, u32[]{:S(2)}) collective-permute-start(f32[64,2816]{1,0:T(8,128)S(1)} %pad_maximum_fusion.15), channel_id=1, source_target_pairs={{0,8},{4,12},{8,0},{12,4},{16,24},{20,28},{24,16},{28,20},{1,9},{5... | collective-permute-start | bytes 2162696 | tf_op jit(solution)/shard_map/ppermute | solution.py:62
  89.8 18.1 %collective-permute-start.15 = (f32[56,2816]{1,0:T(8,128)S(1)}, f32[56,2816]{1,0:T(8,128)S(1)}, u32[]{:S(2)}, u32[]{:S(2)}) collective-permute-start(f32[56,2816]{1,0:T(8,128)S(1)} %slice.336), channel_id=1, source_target_pairs={{0,16},{4,20},{8,24},{12,28},{16,0},{20,4},{24,8},{28,12},{1,17},{... | collective-permute-start | bytes 1892360 | tf_op jit(solution)/shard_map/ppermute | solution.py:62
  106.3 11.4 %collective-permute-start.12 = (f32[64,1408]{1,0:T(8,128)S(1)}, f32[64,1408]{1,0:T(8,128)S(1)}, u32[]{:S(2)}, u32[]{:S(2)}) collective-permute-start(f32[64,1408]{1,0:T(8,128)S(1)} %slice.338), channel_id=1, source_target_pairs={{0,16},{4,20},{8,24},{12,28},{16,0},{20,4},{24,8},{28,12},{1,17},{... | collective-permute-start | bytes 1081352 | tf_op jit(solution)/shard_map/ppermute | solution.py:62
  108.0 11.3 %collective-permute-start.19 = (f32[56,1408]{1,0:T(8,128)S(1)}, f32[56,1408]{1,0:T(8,128)S(1)}, u32[]{:S(2)}, u32[]{:S(2)}) collective-permute-start(f32[56,1408]{1,0:T(8,128)S(1)} %slice.340), channel_id=1, source_target_pairs={{0,8},{4,12},{8,0},{12,4},{16,24},{20,28},{24,16},{28,20},{1,9},{5... | collective-permute-start | bytes 946184 | tf_op jit(solution)/shard_map/ppermute | solution.py:62
  109.8 18.3 %collective-permute-start.18 = (f32[40,2816]{1,0:T(8,128)S(1)}, f32[40,2816]{1,0:T(8,128)S(1)}, u32[]{:S(2)}, u32[]{:S(2)}) collective-permute-start(f32[40,2816]{1,0:T(8,128)S(1)} %pad_maximum_fusion.25), channel_id=1, source_target_pairs={{0,8},{4,12},{8,0},{12,4},{16,24},{20,28},{24,16},{28,20},{1,9},{5... | collective-permute-start | bytes 1351688 | tf_op jit(solution)/shard_map/ppermute | solution.py:62
  110.6 18.2 %collective-permute-start.17 = (f32[40,2816]{1,0:T(8,128)S(1)}, f32[40,2816]{1,0:T(8,128)S(1)}, u32[]{:S(2)}, u32[]{:S(2)}) collective-permute-start(f32[40,2816]{1,0:T(8,128)S(1)} %slice.343), channel_id=1, source_target_pairs={{0,16},{4,20},{8,24},{12,28},{16,0},{20,4},{24,8},{28,12},{1,17},{... | collective-permute-start | bytes 1351688 | tf_op jit(solution)/shard_map/ppermute | solution.py:62
  117.8 17.3 %collective-permute-start.16 = (f32[64,1408]{1,0:T(8,128)S(1)}, f32[64,1408]{1,0:T(8,128)S(1)}, u32[]{:S(2)}, u32[]{:S(2)}) collective-permute-start(f32[64,1408]{1,0:T(8,128)S(1)} %slice_add_fusion.8.refs_0_), channel_id=1, source_target_pairs={{0,16},{4,20},{8,24},{12,28},{16,0},{20,4},{24,8},{28,12},{1,17},{... | collective-permute-start | bytes 1081352 | tf_op jit(solution)/shard_map/ppermute | solution.py:62
  119.4 17.3 %collective-permute-start.23 = (f32[56,1408]{1,0:T(8,128)S(1)}, f32[56,1408]{1,0:T(8,128)S(1)}, u32[]{:S(2)}, u32[]{:S(2)}) collective-permute-start(f32[56,1408]{1,0:T(8,128)S(1)} %slice_add_fusion.11.refs_4_), channel_id=1, source_target_pairs={{0,8},{4,12},{8,0},{12,4},{16,24},{20,28},{24,16},{28,20},{1,9},{5... | collective-permute-start | bytes 946184 | tf_op jit(solution)/shard_map/ppermute | solution.py:62
  128.2 11.7 %collective-permute-start.22 = (f32[40,1408]{1,0:T(8,128)S(1)}, f32[40,1408]{1,0:T(8,128)S(1)}, u32[]{:S(2)}, u32[]{:S(2)}) collective-permute-start(f32[40,1408]{1,0:T(8,128)S(1)} %slice.348), channel_id=1, source_target_pairs={{0,16},{4,20},{8,24},{12,28},{16,0},{20,4},{24,8},{28,12},{1,17},{... | collective-permute-start | bytes 675848 | tf_op jit(solution)/shard_map/ppermute | solution.py:62
  128.8 12.7 %collective-permute-start.21 = (f32[40,1408]{1,0:T(8,128)S(1)}, f32[40,1408]{1,0:T(8,128)S(1)}, u32[]{:S(2)}, u32[]{:S(2)}) collective-permute-start(f32[40,1408]{1,0:T(8,128)S(1)} %slice.349), channel_id=1, source_target_pairs={{0,8},{4,12},{8,0},{12,4},{16,24},{20,28},{24,16},{28,20},{1,9},{5... | collective-permute-start | bytes 675848 | tf_op jit(solution)/shard_map/ppermute | solution.py:62
  135.1 22.9 %collective-permute-start.20 = (f32[64,2816]{1,0:T(8,128)S(1)}, f32[64,2816]{1,0:T(8,128)S(1)}, u32[]{:S(2)}, u32[]{:S(2)}) collective-permute-start(f32[64,2816]{1,0:T(8,128)S(1)} %pad_maximum_fusion.16), channel_id=1, source_target_pairs={{0,8},{4,12},{8,0},{12,4},{16,24},{20,28},{24,16},{28,20},{1,9},{5... | collective-permute-start | bytes 2162696 | tf_op jit(solution)/shard_map/ppermute | solution.py:62
  136.8 21.4 %collective-permute-start.27 = (f32[56,2816]{1,0:T(8,128)S(1)}, f32[56,2816]{1,0:T(8,128)S(1)}, u32[]{:S(2)}, u32[]{:S(2)}) collective-permute-start(f32[56,2816]{1,0:T(8,128)S(1)} %pad_maximum_fusion.21), channel_id=1, source_target_pairs={{0,16},{4,20},{8,24},{12,28},{16,0},{20,4},{24,8},{28,12},{1,17},{... | collective-permute-start | bytes 1892360 | tf_op jit(solution)/shard_map/ppermute | solution.py:62
  140.0 16.6 %collective-permute-start.25 = (f32[40,1408]{1,0:T(8,128)S(1)}, f32[40,1408]{1,0:T(8,128)S(1)}, u32[]{:S(2)}, u32[]{:S(2)}) collective-permute-start(f32[40,1408]{1,0:T(8,128)S(1)} %slice_add_fusion.16.refs_0_), channel_id=1, source_target_pairs={{0,16},{4,20},{8,24},{12,28},{16,0},{20,4},{24,8},{28,12},{1,17},{... | collective-permute-start | bytes 675848 | tf_op jit(solution)/shard_map/ppermute | solution.py:62
  141.6 16.4 %collective-permute-start.24 = (f32[40,1408]{1,0:T(8,128)S(1)}, f32[40,1408]{1,0:T(8,128)S(1)}, u32[]{:S(2)}, u32[]{:S(2)}) collective-permute-start(f32[40,1408]{1,0:T(8,128)S(1)} %slice_add_fusion.17.refs_4_), channel_id=1, source_target_pairs={{0,8},{4,12},{8,0},{12,4},{16,24},{20,28},{24,16},{28,20},{1,9},{5... | collective-permute-start | bytes 675848 | tf_op jit(solution)/shard_map/ppermute | solution.py:62
  158.9 16.2 %collective-permute-start.31 = (f32[40,2816]{1,0:T(8,128)S(1)}, f32[40,2816]{1,0:T(8,128)S(1)}, u32[]{:S(2)}, u32[]{:S(2)}) collective-permute-start(f32[40,2816]{1,0:T(8,128)S(1)} %pad_maximum_fusion.26), channel_id=1, source_target_pairs={{0,8},{4,12},{8,0},{12,4},{16,24},{20,28},{24,16},{28,20},{1,9},{5... | collective-permute-start | bytes 1351688 | tf_op jit(solution)/shard_map/ppermute | solution.py:62
  160.4 14.7 %collective-permute-start.30 = (f32[40,2816]{1,0:T(8,128)S(1)}, f32[40,2816]{1,0:T(8,128)S(1)}, u32[]{:S(2)}, u32[]{:S(2)}) collective-permute-start(f32[40,2816]{1,0:T(8,128)S(1)} %pad_maximum_fusion.27), channel_id=1, source_target_pairs={{0,16},{4,20},{8,24},{12,28},{16,0},{20,4},{24,8},{28,12},{1,17},{... | collective-permute-start | bytes 1351688 | tf_op jit(solution)/shard_map/ppermute | solution.py:62
  175.2 12.9 %collective-permute-start.34 = (f32[40,5632]{1,0:T(8,128)S(1)}, f32[40,5632]{1,0:T(8,128)S(1)}, u32[]{:S(2)}, u32[]{:S(2)}) collective-permute-start(f32[40,5632]{1,0:T(8,128)S(1)} %pad_maximum_fusion.10), channel_id=1, source_target_pairs={{0,4},{4,0},{8,12},{12,8},{16,20},{20,16},{24,28},{28,24},{1,5},{5... | collective-permute-start | bytes 2703368 | tf_op jit(solution)/shard_map/ppermute | solution.py:62
  175.4 12.7 %collective-permute-start.33 = (f32[40,5632]{1,0:T(8,128)S(1)}, f32[40,5632]{1,0:T(8,128)S(1)}, u32[]{:S(2)}, u32[]{:S(2)}) collective-permute-start(f32[40,5632]{1,0:T(8,128)S(1)} %pad_maximum_fusion.9), channel_id=1, source_target_pairs={{0,4},{4,0},{8,12},{12,8},{16,20},{20,16},{24,28},{28,24},{1,5},{5... | collective-permute-start | bytes 2703368 | tf_op jit(solution)/shard_map/ppermute | solution.py:62
  186.7 19.3 %collective-permute-start.32 = (f32[248,384]{1,0:T(8,128)S(1)}, f32[248,384]{1,0:T(8,128)S(1)}, u32[]{:S(2)}, u32[]{:S(2)}) collective-permute-start(f32[248,384]{1,0:T(8,128)S(1)} %add.224), channel_id=1, source_target_pairs={{0,2},{1,3},{2,0},{3,1},{4,6},{5,7},{6,4},{7,5},{8,10},{9,11},{10,... | collective-permute-start | bytes 1142792 | tf_op jit(solution)/shard_map/ppermute | solution.py:62
  199.9 11.6 %collective-permute-start.36 = (f32[168,384]{1,0:T(8,128)S(1)}, f32[168,384]{1,0:T(8,128)S(1)}, u32[]{:S(2)}, u32[]{:S(2)}) collective-permute-start(f32[168,384]{1,0:T(8,128)S(1)} %get-tuple-element.219), channel_id=1, source_target_pairs={{0,1},{1,0},{2,3},{3,2},{4,5},{5,4},{6,7},{7,6},{8,9},{9,8},{10,11... | collective-permute-start | bytes 774152 | tf_op jit(solution)/shard_map/ppermute | solution.py:62
  206.0 16.1 %collective-permute-start.35 = (f32[248,384]{1,0:T(8,128)S(1)}, f32[248,384]{1,0:T(8,128)S(1)}, u32[]{:S(2)}, u32[]{:S(2)}) collective-permute-start(f32[248,384]{1,0:T(8,128)S(1)} %add.225), channel_id=1, source_target_pairs={{0,1},{1,0},{2,3},{3,2},{4,5},{5,4},{6,7},{7,6},{8,9},{9,8},{10,11... | collective-permute-start | bytes 1142792 | tf_op jit(solution)/shard_map/ppermute | solution.py:62
  211.5 14.6 %collective-permute-start.37 = (f32[168,384]{1,0:T(8,128)S(1)}, f32[168,384]{1,0:T(8,128)S(1)}, u32[]{:S(2)}, u32[]{:S(2)}) collective-permute-start(f32[168,384]{1,0:T(8,128)S(1)} %add.226), channel_id=1, source_target_pairs={{0,2},{1,3},{2,0},{3,1},{4,6},{5,7},{6,4},{7,5},{8,10},{9,11},{10,... | collective-permute-start | bytes 774152 | tf_op jit(solution)/shard_map/ppermute | solution.py:62
  254.4 20.1 %collective-permute-start.47 = (f32[64,2816]{1,0:T(8,128)S(1)}, f32[64,2816]{1,0:T(8,128)S(1)}, u32[]{:S(2)}, u32[]{:S(2)}) collective-permute-start(f32[64,2816]{1,0:T(8,128)S(1)} %pad_maximum_fusion.17), channel_id=1, source_target_pairs={{0,8},{4,12},{8,0},{12,4},{16,24},{20,28},{24,16},{28,20},{1,9},{5... | collective-permute-start | bytes 2162696 | tf_op jit(solution)/shard_map/ppermute | solution.py:62
  256.0 16.7 %collective-permute-start.40 = (f32[8,128]{1,0:T(8,128)S(1)}, f32[8,128]{1,0:T(8,128)S(1)}, u32[]{:S(2)}, u32[]{:S(2)}) collective-permute-start(f32[8,128]{1,0:T(8,128)S(1)} %broadcast_add_fusion.1), channel_id=1, source_target_pairs={{0,8},{4,12},{8,0},{12,4},{16,24},{20,28},{24,16},{28,20},{1,9},{5... | collective-permute-start | bytes 12296 | tf_op jit(solution)/shard_map/ppermute | solution.py:62
  256.8 19.5 %collective-permute-start.46 = (f32[56,2816]{1,0:T(8,128)S(1)}, f32[56,2816]{1,0:T(8,128)S(1)}, u32[]{:S(2)}, u32[]{:S(2)}) collective-permute-start(f32[56,2816]{1,0:T(8,128)S(1)} %slice.360), channel_id=1, source_target_pairs={{0,16},{4,20},{8,24},{12,28},{16,0},{20,4},{24,8},{28,12},{1,17},{... | collective-permute-start | bytes 1892360 | tf_op jit(solution)/shard_map/ppermute | solution.py:62
  274.6 11.4 %collective-permute-start.48 = (f32[64,1408]{1,0:T(8,128)S(1)}, f32[64,1408]{1,0:T(8,128)S(1)}, u32[]{:S(2)}, u32[]{:S(2)}) collective-permute-start(f32[64,1408]{1,0:T(8,128)S(1)} %slice.364), channel_id=1, source_target_pairs={{0,16},{4,20},{8,24},{12,28},{16,0},{20,4},{24,8},{28,12},{1,17},{... | collective-permute-start | bytes 1081352 | tf_op jit(solution)/shard_map/ppermute | solution.py:62
  276.3 11.3 %collective-permute-start.52 = (f32[56,1408]{1,0:T(8,128)S(1)}, f32[56,1408]{1,0:T(8,128)S(1)}, u32[]{:S(2)}, u32[]{:S(2)}) collective-permute-start(f32[56,1408]{1,0:T(8,128)S(1)} %slice.365), channel_id=1, source_target_pairs={{0,8},{4,12},{8,0},{12,4},{16,24},{20,28},{24,16},{28,20},{1,9},{5... | collective-permute-start | bytes 946184 | tf_op jit(solution)/shard_map/ppermute | solution.py:62
  278.1 18.3 %collective-permute-start.51 = (f32[40,2816]{1,0:T(8,128)S(1)}, f32[40,2816]{1,0:T(8,128)S(1)}, u32[]{:S(2)}, u32[]{:S(2)}) collective-permute-start(f32[40,2816]{1,0:T(8,128)S(1)} %pad_maximum_fusion.28), channel_id=1, source_target_pairs={{0,8},{4,12},{8,0},{12,4},{16,24},{20,28},{24,16},{28,20},{1,9},{5... | collective-permute-start | bytes 1351688 | tf_op jit(solution)/shard_map/ppermute | solution.py:62
  278.8 18.3 %collective-permute-start.50 = (f32[40,2816]{1,0:T(8,128)S(1)}, f32[40,2816]{1,0:T(8,128)S(1)}, u32[]{:S(2)}, u32[]{:S(2)}) collective-permute-start(f32[40,2816]{1,0:T(8,128)S(1)} %slice.368), channel_id=1, source_target_pairs={{0,16},{4,20},{8,24},{12,28},{16,0},{20,4},{24,8},{28,12},{1,17},{... | collective-permute-start | bytes 1351688 | tf_op jit(solution)/shard_map/ppermute | solution.py:62
  286.0 17.3 %collective-permute-start.49 = (f32[64,1408]{1,0:T(8,128)S(1)}, f32[64,1408]{1,0:T(8,128)S(1)}, u32[]{:S(2)}, u32[]{:S(2)}) collective-permute-start(f32[64,1408]{1,0:T(8,128)S(1)} %slice_add_fusion.7.refs_1_), channel_id=1, source_target_pairs={{0,16},{4,20},{8,24},{12,28},{16,0},{20,4},{24,8},{28,12},{1,17},{... | collective-permute-start | bytes 1081352 | tf_op jit(solution)/shard_map/ppermute | solution.py:62
  287.7 17.3 %collective-permute-start.56 = (f32[56,1408]{1,0:T(8,128)S(1)}, f32[56,1408]{1,0:T(8,128)S(1)}, u32[]{:S(2)}, u32[]{:S(2)}) collective-permute-start(f32[56,1408]{1,0:T(8,128)S(1)} %slice_add_fusion.10.refs_5_), channel_id=1, source_target_pairs={{0,8},{4,12},{8,0},{12,4},{16,24},{20,28},{24,16},{28,20},{1,9},{5... | collective-permute-start | bytes 946184 | tf_op jit(solution)/shard_map/ppermute | solution.py:62
  296.5 11.7 %collective-permute-start.55 = (f32[40,1408]{1,0:T(8,128)S(1)}, f32[40,1408]{1,0:T(8,128)S(1)}, u32[]{:S(2)}, u32[]{:S(2)}) collective-permute-start(f32[40,1408]{1,0:T(8,128)S(1)} %slice.374), channel_id=1, source_target_pairs={{0,16},{4,20},{8,24},{12,28},{16,0},{20,4},{24,8},{28,12},{1,17},{... | collective-permute-start | bytes 675848 | tf_op jit(solution)/shard_map/ppermute | solution.py:62
  297.2 12.7 %collective-permute-start.54 = (f32[40,1408]{1,0:T(8,128)S(1)}, f32[40,1408]{1,0:T(8,128)S(1)}, u32[]{:S(2)}, u32[]{:S(2)}) collective-permute-start(f32[40,1408]{1,0:T(8,128)S(1)} %slice.375), channel_id=1, source_target_pairs={{0,8},{4,12},{8,0},{12,4},{16,24},{20,28},{24,16},{28,20},{1,9},{5... | collective-permute-start | bytes 675848 | tf_op jit(solution)/shard_map/ppermute | solution.py:62
  303.4 24.8 %collective-permute-start.53 = (f32[64,2816]{1,0:T(8,128)S(1)}, f32[64,2816]{1,0:T(8,128)S(1)}, u32[]{:S(2)}, u32[]{:S(2)}) collective-permute-start(f32[64,2816]{1,0:T(8,128)S(1)} %pad_maximum_fusion.18), channel_id=1, source_target_pairs={{0,8},{4,12},{8,0},{12,4},{16,24},{20,28},{24,16},{28,20},{1,9},{5... | collective-permute-start | bytes 2162696 | tf_op jit(solution)/shard_map/ppermute | solution.py:62
  305.1 24.4 %collective-permute-start.60 = (f32[56,2816]{1,0:T(8,128)S(1)}, f32[56,2816]{1,0:T(8,128)S(1)}, u32[]{:S(2)}, u32[]{:S(2)}) collective-permute-start(f32[56,2816]{1,0:T(8,128)S(1)} %pad_maximum_fusion.22), channel_id=1, source_target_pairs={{0,16},{4,20},{8,24},{12,28},{16,0},{20,4},{24,8},{28,12},{1,17},{... | collective-permute-start | bytes 1892360 | tf_op jit(solution)/shard_map/ppermute | solution.py:62
  308.2 17.1 %collective-permute-start.58 = (f32[40,1408]{1,0:T(8,128)S(1)}, f32[40,1408]{1,0:T(8,128)S(1)}, u32[]{:S(2)}, u32[]{:S(2)}) collective-permute-start(f32[40,1408]{1,0:T(8,128)S(1)} %slice_add_fusion.14.refs_1_), channel_id=1, source_target_pairs={{0,16},{4,20},{8,24},{12,28},{16,0},{20,4},{24,8},{28,12},{1,17},{... | collective-permute-start | bytes 675848 | tf_op jit(solution)/shard_map/ppermute | solution.py:62
  309.9 16.8 %collective-permute-start.57 = (f32[40,1408]{1,0:T(8,128)S(1)}, f32[40,1408]{1,0:T(8,128)S(1)}, u32[]{:S(2)}, u32[]{:S(2)}) collective-permute-start(f32[40,1408]{1,0:T(8,128)S(1)} %slice_add_fusion.15.refs_5_), channel_id=1, source_target_pairs={{0,8},{4,12},{8,0},{12,4},{16,24},{20,28},{24,16},{28,20},{1,9},{5... | collective-permute-start | bytes 675848 | tf_op jit(solution)/shard_map/ppermute | solution.py:62
  334.1 23.0 %collective-permute-start.64 = (f32[40,2816]{1,0:T(8,128)}, f32[40,2816]{1,0:T(8,128)S(1)}, u32[]{:S(2)}, u32[]{:S(2)}) collective-permute-start(f32[40,2816]{1,0:T(8,128)} %pad_maximum_fusion.29), channel_id=1, source_target_pairs={{0,8},{4,12},{8,0},{12,4},{16,24},{20,28},{24,16},{28,20},{1,9},{5... | collective-permute-start | bytes 1351688 | tf_op jit(solution)/shard_map/ppermute | solution.py:62
  335.7 21.5 %collective-permute-start.63 = (f32[40,2816]{1,0:T(8,128)}, f32[40,2816]{1,0:T(8,128)S(1)}, u32[]{:S(2)}, u32[]{:S(2)}) collective-permute-start(f32[40,2816]{1,0:T(8,128)} %pad_maximum_fusion.30), channel_id=1, source_target_pairs={{0,16},{4,20},{8,24},{12,28},{16,0},{20,4},{24,8},{28,12},{1,17},{... | collective-permute-start | bytes 1351688 | tf_op jit(solution)/shard_map/ppermute | solution.py:62
  358.1 13.1 %collective-permute-start.67 = (f32[40,5632]{1,0:T(8,128)S(1)}, f32[40,5632]{1,0:T(8,128)S(1)}, u32[]{:S(2)}, u32[]{:S(2)}) collective-permute-start(f32[40,5632]{1,0:T(8,128)S(1)} %pad_maximum_fusion.12), channel_id=1, source_target_pairs={{0,4},{4,0},{8,12},{12,8},{16,20},{20,16},{24,28},{28,24},{1,5},{5... | collective-permute-start | bytes 2703368 | tf_op jit(solution)/shard_map/ppermute | solution.py:62
  358.1 13.0 %collective-permute-start.66 = (f32[40,5632]{1,0:T(8,128)S(1)}, f32[40,5632]{1,0:T(8,128)S(1)}, u32[]{:S(2)}, u32[]{:S(2)}) collective-permute-start(f32[40,5632]{1,0:T(8,128)S(1)} %pad_maximum_fusion.11), channel_id=1, source_target_pairs={{0,4},{4,0},{8,12},{12,8},{16,20},{20,16},{24,28},{28,24},{1,5},{5... | collective-permute-start | bytes 2703368 | tf_op jit(solution)/shard_map/ppermute | solution.py:62
  369.5 19.2 %collective-permute-start.65 = (f32[248,384]{1,0:T(8,128)S(1)}, f32[248,384]{1,0:T(8,128)S(1)}, u32[]{:S(2)}, u32[]{:S(2)}) collective-permute-start(f32[248,384]{1,0:T(8,128)S(1)} %add.245), channel_id=1, source_target_pairs={{0,2},{1,3},{2,0},{3,1},{4,6},{5,7},{6,4},{7,5},{8,10},{9,11},{10,... | collective-permute-start | bytes 1142792 | tf_op jit(solution)/shard_map/ppermute | solution.py:62
  388.8 16.2 %collective-permute-start.68 = (f32[248,384]{1,0:T(8,128)S(1)}, f32[248,384]{1,0:T(8,128)S(1)}, u32[]{:S(2)}, u32[]{:S(2)}) collective-permute-start(f32[248,384]{1,0:T(8,128)S(1)} %add.246), channel_id=1, source_target_pairs={{0,1},{1,0},{2,3},{3,2},{4,5},{5,4},{6,7},{7,6},{8,9},{9,8},{10,11... | collective-permute-start | bytes 1142792 | tf_op jit(solution)/shard_map/ppermute | solution.py:62
  394.3 14.6 %collective-permute-start.70 = (f32[168,384]{1,0:T(8,128)S(1)}, f32[168,384]{1,0:T(8,128)S(1)}, u32[]{:S(2)}, u32[]{:S(2)}) collective-permute-start(f32[168,384]{1,0:T(8,128)S(1)} %add.247), channel_id=1, source_target_pairs={{0,2},{1,3},{2,0},{3,1},{4,6},{5,7},{6,4},{7,5},{8,10},{9,11},{10,... | collective-permute-start | bytes 774152 | tf_op jit(solution)/shard_map/ppermute | solution.py:62
  440.1 11.9 %collective-permute-start.74 = (f32[56,5632]{1,0:T(8,128)}, f32[56,5632]{1,0:T(8,128)}, u32[]{:S(2)}, u32[]{:S(2)}) collective-permute-start(f32[56,5632]{1,0:T(8,128)} %get-tuple-element.278), channel_id=1, source_target_pairs={{0,4},{4,0},{8,12},{12,8},{16,20},{20,16},{24,28},{28,24},{1,5},{5... | collective-permute-start | bytes 3784712 | tf_op jit(solution)/shard_map/ppermute | solution.py:62
  447.0 24.6 %collective-permute-start.80 = (f32[64,2816]{1,0:T(8,128)}, f32[64,2816]{1,0:T(8,128)}, u32[]{:S(2)}, u32[]{:S(2)}) collective-permute-start(f32[64,2816]{1,0:T(8,128)} %pad_maximum_fusion.19), channel_id=1, source_target_pairs={{0,8},{4,12},{8,0},{12,4},{16,24},{20,28},{24,16},{28,20},{1,9},{5... | collective-permute-start | bytes 2162696 | tf_op jit(solution)/shard_map/ppermute | solution.py:62
  450.6 18.8 %collective-permute-start.73 = (f32[8,128]{1,0:T(8,128)S(1)}, f32[8,128]{1,0:T(8,128)S(1)}, u32[]{:S(2)}, u32[]{:S(2)}) collective-permute-start(f32[8,128]{1,0:T(8,128)S(1)} %broadcast_add_fusion), channel_id=1, source_target_pairs={{0,8},{4,12},{8,0},{12,4},{16,24},{20,28},{24,16},{28,20},{1,9},{5... | collective-permute-start | bytes 12296 | tf_op jit(solution)/shard_map/ppermute | solution.py:62
  453.6 21.1 %collective-permute-start.79 = (f32[56,2816]{1,0:T(8,128)S(1)}, f32[56,2816]{1,0:T(8,128)S(1)}, u32[]{:S(2)}, u32[]{:S(2)}) collective-permute-start(f32[56,2816]{1,0:T(8,128)S(1)} %slice.386), channel_id=1, source_target_pairs={{0,16},{4,20},{8,24},{12,28},{16,0},{20,4},{24,8},{28,12},{1,17},{... | collective-permute-start | bytes 1892360 | tf_op jit(solution)/shard_map/ppermute | solution.py:62
  473.5 22.6 %collective-permute-start.83 = (f32[64,1408]{1,0:T(8,128)}, f32[64,1408]{1,0:T(8,128)S(1)}, u32[]{:S(2)}, u32[]{:S(2)}) collective-permute-start(f32[64,1408]{1,0:T(8,128)} %slice.390), channel_id=1, source_target_pairs={{0,16},{4,20},{8,24},{12,28},{16,0},{20,4},{24,8},{28,12},{1,17},{... | collective-permute-start | bytes 1081352 | tf_op jit(solution)/shard_map/ppermute | solution.py:62
  475.5 21.9 %collective-permute-start.82 = (f32[56,1408]{1,0:T(8,128)}, f32[56,1408]{1,0:T(8,128)}, u32[]{:S(2)}, u32[]{:S(2)}) collective-permute-start(f32[56,1408]{1,0:T(8,128)} %slice.391), channel_id=1, source_target_pairs={{0,8},{4,12},{8,0},{12,4},{16,24},{20,28},{24,16},{28,20},{1,9},{5... | collective-permute-start | bytes 946184 | tf_op jit(solution)/shard_map/ppermute | solution.py:62
  478.4 21.4 %collective-permute-start.81 = (f32[40,2816]{1,0:T(8,128)}, f32[40,2816]{1,0:T(8,128)}, u32[]{:S(2)}, u32[]{:S(2)}) collective-permute-start(f32[40,2816]{1,0:T(8,128)} %pad_maximum_fusion.31), channel_id=1, source_target_pairs={{0,8},{4,12},{8,0},{12,4},{16,24},{20,28},{24,16},{28,20},{1,9},{5... | collective-permute-start | bytes 1351688 | tf_op jit(solution)/shard_map/ppermute | solution.py:62
  479.9 22.2 %collective-permute-start.87 = (f32[40,2816]{1,0:T(8,128)}, f32[40,2816]{1,0:T(8,128)}, u32[]{:S(2)}, u32[]{:S(2)}) collective-permute-start(f32[40,2816]{1,0:T(8,128)} %slice.394), channel_id=1, source_target_pairs={{0,16},{4,20},{8,24},{12,28},{16,0},{20,4},{24,8},{28,12},{1,17},{... | collective-permute-start | bytes 1351688 | tf_op jit(solution)/shard_map/ppermute | solution.py:62
  496.2 11.4 %collective-permute-start.86 = (f32[64,1408]{1,0:T(8,128)S(1)}, f32[64,1408]{1,0:T(8,128)S(1)}, u32[]{:S(2)}, u32[]{:S(2)}) collective-permute-start(f32[64,1408]{1,0:T(8,128)S(1)} %slice_add_fusion.6.refs_0_), channel_id=1, source_target_pairs={{0,16},{4,20},{8,24},{12,28},{16,0},{20,4},{24,8},{28,12},{1,17},{... | collective-permute-start | bytes 1081352 | tf_op jit(solution)/shard_map/ppermute | solution.py:62
  501.0 11.5 %collective-permute-start.84 = (f32[40,1408]{1,0:T(8,128)S(1)}, f32[40,1408]{1,0:T(8,128)S(1)}, u32[]{:S(2)}, u32[]{:S(2)}) collective-permute-start(f32[40,1408]{1,0:T(8,128)S(1)} %slice.400), channel_id=1, source_target_pairs={{0,16},{4,20},{8,24},{12,28},{16,0},{20,4},{24,8},{28,12},{1,17},{... | collective-permute-start | bytes 675848 | tf_op jit(solution)/shard_map/ppermute | solution.py:62
  507.7 28.2 %collective-permute-start.92 = (f32[64,2816]{1,0:T(8,128)S(1)}, f32[64,2816]{1,0:T(8,128)S(1)}, u32[]{:S(2)}, u32[]{:S(2)}) collective-permute-start(f32[64,2816]{1,0:T(8,128)S(1)} %pad_maximum_fusion.20), channel_id=1, source_target_pairs={{0,8},{4,12},{8,0},{12,4},{16,24},{20,28},{24,16},{28,20},{1,9},{5... | collective-permute-start | bytes 2162696 | tf_op jit(solution)/shard_map/ppermute | solution.py:62
  509.7 26.4 %collective-permute-start.91 = (f32[56,2816]{1,0:T(8,128)S(1)}, f32[56,2816]{1,0:T(8,128)S(1)}, u32[]{:S(2)}, u32[]{:S(2)}) collective-permute-start(f32[56,2816]{1,0:T(8,128)S(1)} %pad_maximum_fusion.23), channel_id=1, source_target_pairs={{0,16},{4,20},{8,24},{12,28},{16,0},{20,4},{24,8},{28,12},{1,17},{... | collective-permute-start | bytes 1892360 | tf_op jit(solution)/shard_map/ppermute | solution.py:62
  512.5 16.0 %collective-permute-start.88 = (f32[40,1408]{1,0:T(8,128)S(1)}, f32[40,1408]{1,0:T(8,128)S(1)}, u32[]{:S(2)}, u32[]{:S(2)}) collective-permute-start(f32[40,1408]{1,0:T(8,128)S(1)} %slice_add_fusion.13.refs_0_), channel_id=1, source_target_pairs={{0,16},{4,20},{8,24},{12,28},{16,0},{20,4},{24,8},{28,12},{1,17},{... | collective-permute-start | bytes 675848 | tf_op jit(solution)/shard_map/ppermute | solution.py:62
  514.5 20.2 %collective-permute-start.93 = (f32[40,1408]{1,0:T(8,128)S(1)}, f32[40,1408]{1,0:T(8,128)S(1)}, u32[]{:S(2)}, u32[]{:S(2)}) collective-permute-start(f32[40,1408]{1,0:T(8,128)S(1)} %slice_add_fusion.12.refs_4_), channel_id=1, source_target_pairs={{0,8},{4,12},{8,0},{12,4},{16,24},{20,28},{24,16},{28,20},{1,9},{5... | collective-permute-start | bytes 675848 | tf_op jit(solution)/shard_map/ppermute | solution.py:62
  528.5 13.5 %collective-permute-start.90 = (f32[40,2816]{1,0:T(8,128)S(1)}, f32[40,2816]{1,0:T(8,128)S(1)}, u32[]{:S(2)}, u32[]{:S(2)}) collective-permute-start(f32[40,2816]{1,0:T(8,128)S(1)} %pad_maximum_fusion.32), channel_id=1, source_target_pairs={{0,8},{4,12},{8,0},{12,4},{16,24},{20,28},{24,16},{28,20},{1,9},{5... | collective-permute-start | bytes 1351688 | tf_op jit(solution)/shard_map/ppermute | solution.py:62
  (70 other events, 1338.4 us)

commit v5 on v4

--- a/solution.py
+++ b/solution.py
@@ -98,10 +98,10 @@
     if split is not None:
         aliases = {3: 0, 4: 1}
         operands += list(split)
-        in_specs += [pl.BlockSpec(memory_space=pl.ANY)] * 2
+        in_specs += [pl.BlockSpec(memory_space=pltpu.HBM)] * 2
     high, low, send, keep = pl.pallas_call(
         functools.partial(first_body, plan),
-        out_shape=[jax.ShapeDtypeStruct((rows, plan.feats), BF16)] * 2
+        out_shape=[pltpu.HBM((rows, plan.feats), BF16)] * 2
         + [jax.ShapeDtypeStruct((half, step), F32)] * 2,
         grid_spec=pltpu.PrefetchScalarGridSpec(
             num_scalar_prefetch=1,
@@ -112,7 +112,7 @@
             scratch_shapes=[pltpu.VMEM((plan.classes, step), F32)],
         ),
         input_output_aliases=aliases,
-        compiler_params=params(20),
+        compiler_params=params(56),
         cost_estimate=pl.CostEstimate(
             flops=6 * plan.classes * step * plan.feats,
             bytes_accessed=4 * plan.feats * (2 * step + plan.classes),
@@ -123,7 +123,38 @@
     return (high, low), (send, keep)
 
 
-def back_body(plan, group, s_ref, g_ref, high_ref, low_ref, *outs):
+def stream(plan, p, sources, buffers, sems):
+    def copies(step):
+        slot = lax.rem(step, 2)
+        place = pl.ds(pl.multiple_of(step * plan.block, LANES), plan.block)
+        return [
+            pltpu.make_async_copy(source.at[:, place], buffer.at[slot], sems.at[k, slot])
+            for k, (source, buffer) in enumerate(zip(sources, buffers))
+        ]
+
+    @pl.when(p == 0)
+    def _():
+        for copy in copies(p):
+            copy.start()
+
+    @pl.when(p + 1 < plan.nb)
+    def _():
+        for copy in copies(p + 1):
+            copy.start()
+
+    for copy in copies(p):
+        copy.wait()
+    return [buffer.at[lax.rem(p, 2)] for buffer in buffers]
+
+
+def stream_scratch(plan):
+    buffer = pltpu.VMEM((2, plan.rows, plan.block), BF16)
+    return [buffer, buffer, pltpu.SemaphoreType.DMA((2, 2))]
+
+
+def back_body(plan, group, s_ref, g_ref, high_hbm, low_hbm, *rest):
+    outs, (high_buf, low_buf, sems) = rest[:-5], rest[-3:]
+    high_ref, low_ref = stream(plan, pl.program_id(0), (high_hbm, low_hbm), (high_buf, low_buf), sems)
     core = s_ref[1]
     base = plan.pair_range(group)[0]
     some, ends = [], []
@@ -150,6 +181,9 @@
         h = plan.chunks[c][1] // 2
         outs += [jax.ShapeDtypeStruct((h, feats), F32)] * 2
         specs += [pl.BlockSpec((h, block), lambda p, s: (0, p))] * 2
+    aliases = {2: len(outs), 3: len(outs) + 1}
+    outs += [pltpu.HBM((rows, feats), BF16)] * 2
+    specs += [pl.BlockSpec(memory_space=pltpu.HBM)] * 2
     result = pl.pallas_call(
         functools.partial(back_body, plan, group),
         out_shape=outs,
@@ -158,18 +192,20 @@
             grid=(plan.nb,),
             in_specs=[
                 pl.BlockSpec((n_group, rows), lambda p, s: (0, 0), pipeline_mode=pl.Buffered(1)),
-                pl.BlockSpec((rows, block), lambda p, s: (0, p)),
-                pl.BlockSpec((rows, block), lambda p, s: (0, p)),
+                pl.BlockSpec(memory_space=pltpu.HBM),
+                pl.BlockSpec(memory_space=pltpu.HBM),
             ],
             out_specs=specs,
+            scratch_shapes=stream_scratch(plan),
         ),
+        input_output_aliases=aliases,
         compiler_params=params(20),
         cost_estimate=pl.CostEstimate(
             flops=6 * n_group * rows * feats, bytes_accessed=4 * feats * (rows + n_group), transcendentals=0
         ),
         name="back_group",
     )(where, values, high, low)
-    return [tuple(result[2 * k : 2 * k + 2]) for k in range(len(plan.pairs[group]))]
+    return [tuple(result[2 * k : 2 * k + 2]) for k in range(len(plan.pairs[group]))], tuple(result[-2:])
 
 
 class Pieces:
@@ -203,12 +239,13 @@
     n_pieces = sum(len(some) for places in chunks for some in places)
     pieces, refs = refs[:n_pieces], refs[n_pieces:]
     direction_ref = refs.pop(0) if step else None
-    high_ref, low_ref = refs[:2]
+    high_hbm, low_hbm = refs[:2]
     n_ranges = len(tangent_ranges(plan, pair))
-    target, acc, sums = refs[-3:]
-    vector_ref, outs = refs[-4 - 2 * n_ranges], refs[-3 - 2 * n_ranges : -3]
+    target, acc, sums, high_buf, low_buf, sems = refs[-6:]
+    vector_ref, outs = refs[-9 - 2 * n_ranges], refs[-8 - 2 * n_ranges : -8]
     n_pair = plan.pair_range(pair)[1]
     p = pl.program_id(0)
+    high_ref, low_ref = stream(plan, p, (high_hbm, low_hbm), (high_buf, low_buf), sems)
     for position in range(nb):
 
         @pl.when(p == position)
@@ -275,17 +312,20 @@
     if step is not None:
         operands.append(direction)
         in_specs.append(placed(plan, pair))
+    n_ranges = len(tangent_ranges(plan, pair))
+    aliases = {len(operands) + 1: 1 + 2 * n_ranges, len(operands) + 2: 2 + 2 * n_ranges}
     operands += [high, low]
-    in_specs += [pl.BlockSpec((rows, block), lambda p, s: (0, p))] * 2
-    aliases = {}
+    in_specs += [pl.BlockSpec(memory_space=pltpu.HBM)] * 2
     if vectors is not None:
-        aliases = {len(operands) + 1: 0}
+        aliases[len(operands) + 1] = 0
         operands.append(vectors)
         in_specs.append(pl.BlockSpec(memory_space=pl.ANY))
-    outs, specs = [jax.ShapeDtypeStruct((plan.classes, feats), F32)], [placed(plan, pair)]
+    outs, specs = [pltpu.HBM((plan.classes, feats), F32)], [placed(plan, pair)]
     for _, n in tangent_ranges(plan, pair):
         outs += [jax.ShapeDtypeStruct((n, half), F32)] * 2
         specs += [pl.BlockSpec((n, half), lambda p, s: (0, 0))] * 2
+    outs += [pltpu.HBM((rows, feats), BF16)] * 2
+    specs += [pl.BlockSpec(memory_space=pltpu.HBM)] * 2
     result = pl.pallas_call(
         functools.partial(forth_body, plan, pair, step is not None, [piece.places for piece in pieces]),
         out_shape=outs,
@@ -298,7 +338,8 @@
                 pltpu.VMEM((n_pair, block), F32),
                 pltpu.VMEM((n_pair + ROWS8, rows), F32),
                 pltpu.VMEM((ROWS8, rows), F32),
-            ],
+            ]
+            + stream_scratch(plan),
         ),
         input_output_aliases=aliases,
         compiler_params=params(30),
@@ -307,7 +348,7 @@
         ),
         name="forth_pair",
     )(where, *operands)
-    return result[0], [tuple(result[1 + 2 * k : 3 + 2 * k]) for k in range(len(tangent_ranges(plan, pair)))]
+    return result[0], [tuple(result[1 + 2 * k : 3 + 2 * k]) for k in range(n_ranges)], tuple(result[-2:])
 
 
 def last_body(plan, pair, chunks, s_ref, scalar_ref, *refs):
@@ -510,7 +551,7 @@
         parts.append(FeatSum(plan, halves, bit, 0))
     for summed in parts:
         summed.advance(order)
-    high, low = split
+    split = list(split)
     probs, values = [], []
     for part, summed in enumerate(parts):
         logits = summed.result(order)
@@ -528,7 +569,7 @@
 
         def multiply(group):
             a, n = plan.pair_range(group)
-            sides = back(plan, where, group, order.after(values[a : a + n]), high, low)
+            sides, split[:] = back(plan, where, group, order.after(values[a : a + n]), *split)
             for c, side in zip(plan.pairs[group], sides):
                 sums[c] = ClipSum(plan, side, plan.turns[c])
             order.note(sides[-1][0])
@@ -558,7 +599,7 @@
 
         def multiply(group):
             pieces = [sums[c].pieces(order) for c in plan.pairs[group]]
-            out, halves = forth(plan, where, group, pieces, high, low, vectors, step, direction)
+            out, halves, split[:] = forth(plan, where, group, pieces, *split, vectors, step, direction)
             order.note(halves[0][0])
             found.append(FeatSum(plan, halves[0], bit, 1))
             return out

time: 561 us -> 546 us (0.973)
  local copies, waits for them, and re-layouts: 49.8 us -> 13.6 us
  Pallas kernels: 134 us -> 161 us
    unnamed x70 -> x50, local copies, waits for them, and re-layouts: 40.9 us -> 5.75 us
    pallas_call x6, Pallas kernels: 53.9 us -> 64 us  [back(): pl.pallas_call(functools.partial(back_body, plan, group), out_shape=outs,...]
    pallas_call x3, Pallas kernels: 22.6 us -> 32.5 us  [first(): pl.pallas_call(functools.partial(first_body, plan), out_shape=[pltpu.HBM(...]
    pallas_call x4, Pallas kernels: 49.6 us -> 56.3 us  [forth(): pl.pallas_call(functools.partial(forth_body, plan, pair, step is not None...]
  transfers between devices with their start and end apart: 99 -> 99, of which waited for: 42 -> 43; matrix products, arithmetic and copies ran while one was open for 7% -> 7% of each run, Pallas kernels for 17% -> 21%
where the time goes in v5:
time: 546 us; the launch traced here: 539 us
  waiting for transfers between devices  229 us (42%)
  Pallas kernels  161 us (29%)
  starting transfers between devices  87.3 us (16%)
  other arithmetic  38.9 us (7%)
  local copies, waits for them, and re-layouts  13.6 us (2%)
  between operations  9.13 us (2%)
    ppermute x99, waiting for transfers between devices, swap(): return lax.ppermute(x, axis, [(i, i ^ stride) for i in range(size)])  229 us
    ppermute x99, starting transfers between devices, swap(): return lax.ppermute(x, axis, [(i, i ^ stride) for i in range(size)])  87.3 us
    pallas_call x6, Pallas kernels, back(): pl.pallas_call(functools.partial(back_body, plan, group), out_shape=outs,...  64 us
    pallas_call x4, Pallas kernels, forth(): pl.pallas_call(functools.partial(forth_body, plan, pair, step is not None...  56.3 us
    pallas_call x3, Pallas kernels, first(): pl.pallas_call(functools.partial(first_body, plan), out_shape=[pltpu.HBM(...  32.5 us
    add x1, other arithmetic, under(): order.after(weights) + (step0 + step1 * ratio) * direction  14.1 us
  transfers between devices with their start and end apart: 99, of which 43 were waited for; matrix products, arithmetic and copies ran while one was open for 7% of the time, Pallas kernels for 21%

profile of v5, /device:TPU:0, one launch (start us, length us, event | category | flops | bytes accessed | tf_op | source)
XLA Modules:
  0.0 539.0 jit_solution(3688972422507608428)
XLA Ops:
  1.2 10.7 %split_and_logits.3 = (bf16[768,5632]{1,0:T(8,128)(2,1)}, bf16[768,5632]{1,0:T(8,128)(2,1)}, f32[200,256]{1,0:T(8,128)}, f32[200,256]{1,0:T(8,128)}) custom-call(s32[3]{0:T(128)} %pad_add_fusion.s_ref, f32[768,5632]{1,0:T(8,128)} %f_ref.3, f32[400,5632]{1,0:T(8,128)} %w_ref.5), custom_call_target="tpu_custom_call" | custom-call | flops 3460300800 | bytes 20545536 | tf_op jit(solution)/shard_map/split_and_logits/pallas_call | solution.py:102
  12.0 3.1 collective-permute-start
  15.1 10.9 %split_and_logits.4 = (bf16[768,5632]{1,0:T(8,128)(2,1)}, bf16[768,5632]{1,0:T(8,128)(2,1)}, f32[200,256]{1,0:T(8,128)}, f32[200,256]{1,0:T(8,128)}) custom-call(s32[3]{0:T(128)} %pad_add_fusion.s_ref, f32[768,5632]{1,0:T(8,128)} %f_ref.3, f32[400,5632]{1,0:T(8,128)} %w_ref.5, ...), custom_call_target="tpu_custom_call", output_to_operand_aliasing={{0}: (3, {}), {1}: (4, {})} | custom-call | flops 3460300800 | bytes 20545536 | tf_op jit(solution)/shard_map/split_and_logits/pallas_call | solution.py:102
  26.1 3.1 collective-permute-start.1
  29.2 10.9 %split_and_logits.5 = (bf16[768,5632]{1,0:T(8,128)(2,1)}, bf16[768,5632]{1,0:T(8,128)(2,1)}, f32[200,256]{1,0:T(8,128)}, f32[200,256]{1,0:T(8,128)}) custom-call(s32[3]{0:T(128)} %pad_add_fusion.s_ref, f32[768,5632]{1,0:T(8,128)} %f_ref.3, f32[400,5632]{1,0:T(8,128)} %w_ref.5, ...), custom_call_target="tpu_custom_call", output_to_operand_aliasing={{0}: (3, {}), {1}: (4, {})} | custom-call | flops 3460300800 | bytes 20545536 | tf_op jit(solution)/shard_map/split_and_logits/pallas_call | solution.py:102
  40.1 1.6 collective-permute-start.3
  42.5 11.8 %collective-permute-done.3 = f32[200,256]{1,0:T(8,128)S(1)} collective-permute-done((f32[200,256]{1,0:T(8,128)}, f32[200,256]{1,0:T(8,128)S(1)}, u32[]{:S(2)}, u32[]{:S(2)}) %collective-permute-start.3) | collective-permute-done | bytes 204832 | tf_op jit(solution)/shard_map/ppermute | solution.py:62
  54.6 2.0 collective-permute-done.2
  57.6 6.8 %collective-permute-done.6 = f32[200,256]{1,0:T(8,128)S(1)} collective-permute-done((f32[200,256]{1,0:T(8,128)S(1)}, f32[200,256]{1,0:T(8,128)S(1)}, u32[]{:S(2)}, u32[]{:S(2)}) %collective-permute-start.6) | collective-permute-done | bytes 204832 | tf_op jit(solution)/shard_map/ppermute | solution.py:62
  65.9 4.3 collective-permute-done.8
  71.5 11.3 %back_group.6 = (f32[64,5632]{1,0:T(8,128)S(1)}, f32[64,5632]{1,0:T(8,128)S(1)}, f32[56,5632]{1,0:T(8,128)S(1)}, f32[56,5632]{1,0:T(8,128)S(1)}, bf16[768,5632]{1,0:T(8,128)(2,1)}, /*index=5*/bf16[768,5632]{1,0:T(8,128)(2,1)}) custom-call(s32[3]{0:T(128)S(1)} %copy-done.3, ...), custom_call_target="tpu_custom_call", output_to_operand_aliasing={{4}: (2, {}), {5}: (3, {})} | custom-call | flops 6228541440 | bytes 22708224 | tf_op jit(solution)/shard_map/back_group/pallas_call | solution.py:187
  83.3 2.7 collective-permute-done.9
  88.1 1.6 collective-permute-start.15
  89.7 9.8 %back_group.7 = (f32[40,5632]{1,0:T(8,128)S(1)}, f32[40,5632]{1,0:T(8,128)S(1)}, f32[40,5632]{1,0:T(8,128)S(1)}, f32[40,5632]{1,0:T(8,128)S(1)}, bf16[768,5632]{1,0:T(8,128)(2,1)}, /*index=5*/bf16[768,5632]{1,0:T(8,128)(2,1)}) custom-call(s32[3]{0:T(128)S(1)} %copy-done.3, ...), custom_call_target="tpu_custom_call", output_to_operand_aliasing={{4}: (2, {}), {5}: (3, {})} | custom-call | flops 4152360960 | bytes 20905984 | tf_op jit(solution)/shard_map/back_group/pallas_call | solution.py:187
  100.1 4.5 collective-permute-done.10
  104.7 1.6 collective-permute-start.12
  109.5 6.6 %collective-permute-done.12 = f32[64,1408]{1,0:T(8,128)S(1)} collective-permute-done((f32[64,1408]{1,0:T(8,128)S(1)}, f32[64,1408]{1,0:T(8,128)S(1)}, u32[]{:S(2)}, u32[]{:S(2)}) %collective-permute-start.12) | collective-permute-done | bytes 360480 | tf_op jit(solution)/shard_map/ppermute | solution.py:62
  119.3 7.2 %collective-permute-done.18 = f32[40,2816]{1,0:T(8,128)S(1)} collective-permute-done((f32[40,2816]{1,0:T(8,128)S(1)}, f32[40,2816]{1,0:T(8,128)S(1)}, u32[]{:S(2)}, u32[]{:S(2)}) %collective-permute-start.18) | collective-permute-done | bytes 450592 | tf_op jit(solution)/shard_map/ppermute | solution.py:62
  128.8 4.7 collective-permute-done.16.refs_1_
  136.7 1.6 collective-permute-done.22
  141.5 13.4 %collective-permute-done.25.refs_1_ = f32[40,1408]{1,0:T(8,128)S(1)} collective-permute-done((f32[40,1408]{1,0:T(8,128)S(1)}, f32[40,1408]{1,0:T(8,128)S(1)}, u32[]{:S(2)}, u32[]{:S(2)}) %collective-permute-start.25) | collective-permute-done | bytes 225312 | tf_op jit(solution)/shard_map/ppermute | solution.py:62
  159.2 2.4 collective-permute-done.28.refs_7_
  161.6 13.7 %forth_pair.4 = (f32[400,5632]{1,0:T(8,128)}, f32[248,384]{1,0:T(8,128)S(1)}, f32[248,384]{1,0:T(8,128)S(1)}, bf16[768,5632]{1,0:T(8,128)(2,1)}, bf16[768,5632]{1,0:T(8,128)(2,1)}) custom-call(s32[3]{0:T(128)S(1)} %copy-done.3, f32[64,1408]{1,0:T(8,128)S(1)} %slice_add_fusion.8.refs_0_, ...), custom_call_target="tpu_custom_call", output_to_operand_aliasing={{3}: (9, {}), {4}: (10, {})} | custom-call | flops 6228541440 | bytes 33521664 | tf_op jit(solution)/shard_map/forth_pair/pallas_call | solution.py:329
  177.1 9.8 %collective-permute-done.29 = f32[248,384]{1,0:T(8,128)S(1)} collective-permute-done((f32[248,384]{1,0:T(8,128)S(1)}, f32[248,384]{1,0:T(8,128)S(1)}, u32[]{:S(2)}, u32[]{:S(2)}) %collective-permute-start.29) | collective-permute-done | bytes 380960 | tf_op jit(solution)/shard_map/ppermute | solution.py:62
  188.5 13.3 %forth_pair.5 = (f32[400,5632]{1,0:T(8,128)}, f32[168,384]{1,0:T(8,128)S(1)}, f32[168,384]{1,0:T(8,128)S(1)}, bf16[768,5632]{1,0:T(8,128)(2,1)}, bf16[768,5632]{1,0:T(8,128)(2,1)}) custom-call(s32[3]{0:T(128)S(1)} %copy-done.3, f32[40,1408]{1,0:T(8,128)S(1)} %slice_add_fusion.16.refs_0_, ...), custom_call_target="tpu_custom_call", output_to_operand_aliasing={{3}: (9, {}), {4}: (10, {}), {0}: (11, {})} | custom-call | flops 4152360960 | bytes 28114944 | tf_op jit(solution)/shard_map/forth_pair/pallas_call | solution.py:329
  201.8 1.8 collective-permute-start.36
  203.6 2.6 collective-permute-done.32
  206.4 5.4 collective-permute-done.36
  212.6 10.1 %collective-permute-done.35 = f32[248,384]{1,0:T(8,128)S(1)} collective-permute-done((f32[248,384]{1,0:T(8,128)S(1)}, f32[248,384]{1,0:T(8,128)S(1)}, u32[]{:S(2)}, u32[]{:S(2)}) %collective-permute-start.35) | collective-permute-done | bytes 380960 | tf_op jit(solution)/shard_map/ppermute | solution.py:62
  222.7 3.7 collective-permute-done.37
  226.7 7.1 %collective-permute-done.38 = f32[168,384]{1,0:T(8,128)S(1)} collective-permute-done((f32[168,384]{1,0:T(8,128)S(1)}, f32[168,384]{1,0:T(8,128)S(1)}, u32[]{:S(2)}, u32[]{:S(2)}) %collective-permute-start.38) | collective-permute-done | bytes 258080 | tf_op jit(solution)/shard_map/ppermute | solution.py:62
  235.1 11.3 %back_group.8 = (f32[64,5632]{1,0:T(8,128)S(1)}, f32[64,5632]{1,0:T(8,128)S(1)}, f32[56,5632]{1,0:T(8,128)S(1)}, f32[56,5632]{1,0:T(8,128)S(1)}, bf16[768,5632]{1,0:T(8,128)(2,1)}, /*index=5*/bf16[768,5632]{1,0:T(8,128)(2,1)}) custom-call(s32[3]{0:T(128)S(1)} %copy-done.3, ...), custom_call_target="tpu_custom_call", output_to_operand_aliasing={{4}: (2, {}), {5}: (3, {})} | custom-call | flops 6228541440 | bytes 22708224 | tf_op jit(solution)/shard_map/back_group/pallas_call | solution.py:187
  247.7 3.8 collective-permute-done.39
  255.4 9.8 %back_group.9 = (f32[40,5632]{1,0:T(8,128)S(1)}, f32[40,5632]{1,0:T(8,128)S(1)}, f32[40,5632]{1,0:T(8,128)S(1)}, f32[40,5632]{1,0:T(8,128)S(1)}, bf16[768,5632]{1,0:T(8,128)(2,1)}, /*index=5*/bf16[768,5632]{1,0:T(8,128)(2,1)}) custom-call(s32[3]{0:T(128)S(1)} %copy-done.3, ...), custom_call_target="tpu_custom_call", output_to_operand_aliasing={{4}: (2, {}), {5}: (3, {})} | custom-call | flops 4152360960 | bytes 20905984 | tf_op jit(solution)/shard_map/back_group/pallas_call | solution.py:187
  265.2 5.6 %collective-permute-done.40 = f32[8,128]{1,0:T(8,128)S(1)} collective-permute-done((f32[8,128]{1,0:T(8,128)S(1)}, f32[8,128]{1,0:T(8,128)S(1)}, u32[]{:S(2)}, u32[]{:S(2)}) %collective-permute-start.40) | collective-permute-done | bytes 4128 | tf_op jit(solution)/shard_map/ppermute | solution.py:62
  277.4 6.6 %collective-permute-done.48 = f32[64,1408]{1,0:T(8,128)S(1)} collective-permute-done((f32[64,1408]{1,0:T(8,128)S(1)}, f32[64,1408]{1,0:T(8,128)S(1)}, u32[]{:S(2)}, u32[]{:S(2)}) %collective-permute-start.48) | collective-permute-done | bytes 360480 | tf_op jit(solution)/shard_map/ppermute | solution.py:62
  287.2 7.2 %collective-permute-done.51 = f32[40,2816]{1,0:T(8,128)S(1)} collective-permute-done((f32[40,2816]{1,0:T(8,128)S(1)}, f32[40,2816]{1,0:T(8,128)S(1)}, u32[]{:S(2)}, u32[]{:S(2)}) %collective-permute-start.51) | collective-permute-done | bytes 450592 | tf_op jit(solution)/shard_map/ppermute | solution.py:62
  296.7 4.7 collective-permute-done.49.refs_2_
  304.6 1.6 collective-permute-done.55
  309.4 13.9 %collective-permute-done.58.refs_2_ = f32[40,1408]{1,0:T(8,128)S(1)} collective-permute-done((f32[40,1408]{1,0:T(8,128)S(1)}, f32[40,1408]{1,0:T(8,128)S(1)}, u32[]{:S(2)}, u32[]{:S(2)}) %collective-permute-start.58) | collective-permute-done | bytes 225312 | tf_op jit(solution)/shard_map/ppermute | solution.py:62
  334.6 3.6 copy-done
  338.2 15.7 %forth_pair.6 = (f32[400,5632]{1,0:T(8,128)}, f32[248,384]{1,0:T(8,128)S(1)}, f32[248,384]{1,0:T(8,128)S(1)}, bf16[768,5632]{1,0:T(8,128)(2,1)}, bf16[768,5632]{1,0:T(8,128)(2,1)}) custom-call(s32[3]{0:T(128)S(1)} %copy-done.3, f32[1]{0:T(128)} %bitcast.5.refs_0_, ...), custom_call_target="tpu_custom_call", output_to_operand_aliasing={{3}: (11, {}), {4}: (12, {})} | custom-call | flops 6228541440 | bytes 33521664 | tf_op jit(solution)/shard_map/forth_pair/pallas_call | solution.py:329
  355.7 10.5 %collective-permute-done.62 = f32[248,384]{1,0:T(8,128)S(1)} collective-permute-done((f32[248,384]{1,0:T(8,128)S(1)}, f32[248,384]{1,0:T(8,128)S(1)}, u32[]{:S(2)}, u32[]{:S(2)}) %collective-permute-start.62) | collective-permute-done | bytes 380960 | tf_op jit(solution)/shard_map/ppermute | solution.py:62
  366.3 1.7 collective-permute-start.65
  368.0 13.6 %forth_pair.7 = (f32[400,5632]{1,0:T(8,128)}, f32[168,384]{1,0:T(8,128)S(1)}, f32[168,384]{1,0:T(8,128)S(1)}, bf16[768,5632]{1,0:T(8,128)(2,1)}, bf16[768,5632]{1,0:T(8,128)(2,1)}) custom-call(s32[3]{0:T(128)S(1)} %copy-done.3, f32[1]{0:T(128)} %bitcast.5.refs_0_, ...), custom_call_target="tpu_custom_call", output_to_operand_aliasing={{3}: (11, {}), {4}: (12, {}), {0}: (13, {})} | custom-call | flops 4152360960 | bytes 28114944 | tf_op jit(solution)/shard_map/forth_pair/pallas_call | solution.py:329
  381.6 1.8 collective-permute-start.69
  383.4 2.1 collective-permute-done.65
  385.7 5.4 %collective-permute-done.69 = f32[168,384]{1,0:T(8,128)S(1)} collective-permute-done((f32[168,384]{1,0:T(8,128)S(1)}, f32[168,384]{1,0:T(8,128)S(1)}, u32[]{:S(2)}, u32[]{:S(2)}) %collective-permute-start.69) | collective-permute-done | bytes 258080 | tf_op jit(solution)/shard_map/ppermute | solution.py:62
  391.8 10.6 %collective-permute-done.68 = f32[248,384]{1,0:T(8,128)S(1)} collective-permute-done((f32[248,384]{1,0:T(8,128)S(1)}, f32[248,384]{1,0:T(8,128)S(1)}, u32[]{:S(2)}, u32[]{:S(2)}) %collective-permute-start.68) | collective-permute-done | bytes 380960 | tf_op jit(solution)/shard_map/ppermute | solution.py:62
  402.3 3.4 collective-permute-done.70
  406.0 7.0 %collective-permute-done.71 = f32[168,384]{1,0:T(8,128)S(1)} collective-permute-done((f32[168,384]{1,0:T(8,128)S(1)}, f32[168,384]{1,0:T(8,128)S(1)}, u32[]{:S(2)}, u32[]{:S(2)}) %collective-permute-start.71) | collective-permute-done | bytes 258080 | tf_op jit(solution)/shard_map/ppermute | solution.py:62
  418.3 12.3 %back_group.10 = (f32[64,5632]{1,0:T(8,128)S(1)}, f32[64,5632]{1,0:T(8,128)S(1)}, f32[56,5632]{1,0:T(8,128)S(1)}, f32[56,5632]{1,0:T(8,128)}, bf16[768,5632]{1,0:T(8,128)(2,1)}, /*index=5*/bf16[768,5632]{1,0:T(8,128)(2,1)}) custom-call(s32[3]{0:T(128)S(1)} %copy-done.3, f32[240,768]{1,0:T(8,128)S(1)} %slice.382.g_ref, ...), custom_call_target="tpu_custom_call", output_to_operand_aliasing={{4}: (2, {}), {5}: (3, {})} | custom-call | flops 6228541440 | bytes 22708224 | tf_op jit(solution)/shard_map/back_group/pallas_call | solution.py:187
  432.0 3.2 collective-permute-done.72
  444.7 9.6 %back_group.11 = (f32[40,5632]{1,0:T(8,128)S(1)}, f32[40,5632]{1,0:T(8,128)S(1)}, f32[40,5632]{1,0:T(8,128)S(1)}, f32[40,5632]{1,0:T(8,128)S(1)}, bf16[768,5632]{1,0:T(8,128)(2,1)}, /*index=5*/bf16[768,5632]{1,0:T(8,128)(2,1)}) custom-call(s32[3]{0:T(128)S(1)} %copy-done.3, ...), custom_call_target="tpu_custom_call", output_to_operand_aliasing={{4}: (2, {}), {5}: (3, {})} | custom-call | flops 4152360960 | bytes 20905984 | tf_op jit(solution)/shard_map/back_group/pallas_call | solution.py:187
  454.3 2.0 collective-permute-done.73
  468.7 14.1 %multiply_add_fusion = f32[400,5632]{1,0:T(8,128)} fusion(f32[400,5632]{1,0:T(8,128)} %get-tuple-element.331.refs_9_, f32[400,5632]{1,0:T(8,128)} %w_ref.5, f32[400,5632]{1,0:T(8,128)} %get-tuple-element.287.refs_9_.refs_8_, f32[]{:T(128)} %div.82, f32[]{:T(128)S(6)} %add.263), kind=kLoop, calls=%fused_computation | loop fusion | flops 9011200 | bytes 36044808 | tf_op jit(solution)/shard_map/add | solution.py:637
  483.9 1.8 slice_add_fusion.9.refs_4_
  491.1 3.2 collective-permute-done.86.refs_1_
  497.2 1.9 collective-permute-done.84
  501.3 13.7 %collective-permute-done.88.refs_1_ = f32[40,1408]{1,0:T(8,128)S(1)} collective-permute-done((f32[40,1408]{1,0:T(8,128)S(1)}, f32[40,1408]{1,0:T(8,128)S(1)}, u32[]{:S(2)}, u32[]{:S(2)}) %collective-permute-start.88) | collective-permute-done | bytes 225312 | tf_op jit(solution)/shard_map/ppermute | solution.py:62
  515.7 5.6 %collective-permute-done.93.refs_5_ = f32[40,1408]{1,0:T(8,128)S(1)} collective-permute-done((f32[40,1408]{1,0:T(8,128)S(1)}, f32[40,1408]{1,0:T(8,128)S(1)}, u32[]{:S(2)}, u32[]{:S(2)}) %collective-permute-start.93) | collective-permute-done | bytes 225312 | tf_op jit(solution)/shard_map/ppermute | solution.py:62
  523.2 5.2 collective-permute-done.90.refs_2_
  530.6 4.5 last_rows.2.refs_10_
  535.1 3.5 last_rows.3
  (350 shorter events, 109.5 us)
Async XLA Ops:
  12.0 14.1 %collective-permute-start = (f32[200,256]{1,0:T(8,128)}, f32[200,256]{1,0:T(8,128)S(1)}, u32[]{:S(2)}, u32[]{:S(2)}) collective-permute-start(f32[200,256]{1,0:T(8,128)} %get-tuple-element.177), channel_id=1, source_target_pairs={{0,1},{1,0},{2,3},{3,2},{4,5},{5,4},{6,7},{7,6},{8,9},{9,8},{10,11... | collective-permute-start | bytes 614408 | tf_op jit(solution)/shard_map/ppermute | solution.py:62
  25.9 16.3 %collective-permute-start.4 = (f32[200,256]{1,0:T(8,128)}, f32[200,256]{1,0:T(8,128)S(1)}, u32[]{:S(2)}, u32[]{:S(2)}) collective-permute-start(f32[200,256]{1,0:T(8,128)} %get-tuple-element.181), channel_id=1, source_target_pairs={{0,1},{1,0},{2,3},{3,2},{4,5},{5,4},{6,7},{7,6},{8,9},{9,8},{10,11... | collective-permute-start | bytes 614408 | tf_op jit(solution)/shard_map/ppermute | solution.py:62
  26.1 15.6 %collective-permute-start.1 = (f32[200,256]{1,0:T(8,128)S(1)}, f32[200,256]{1,0:T(8,128)S(1)}, u32[]{:S(2)}, u32[]{:S(2)}) collective-permute-start(f32[200,256]{1,0:T(8,128)S(1)} %add.206), channel_id=1, source_target_pairs={{0,2},{1,3},{2,0},{3,1},{4,6},{5,7},{6,4},{7,5},{8,10},{9,11},{10,... | collective-permute-start | bytes 614408 | tf_op jit(solution)/shard_map/ppermute | solution.py:62
  40.1 14.2 %collective-permute-start.3 = (f32[200,256]{1,0:T(8,128)}, f32[200,256]{1,0:T(8,128)S(1)}, u32[]{:S(2)}, u32[]{:S(2)}) collective-permute-start(f32[200,256]{1,0:T(8,128)} %get-tuple-element.186), channel_id=1, source_target_pairs={{0,1},{1,0},{2,3},{3,2},{4,5},{5,4},{6,7},{7,6},{8,9},{9,8},{10,11... | collective-permute-start | bytes 614408 | tf_op jit(solution)/shard_map/ppermute | solution.py:62
  41.7 14.9 %collective-permute-start.2 = (f32[200,256]{1,0:T(8,128)S(1)}, f32[200,256]{1,0:T(8,128)S(1)}, u32[]{:S(2)}, u32[]{:S(2)}) collective-permute-start(f32[200,256]{1,0:T(8,128)S(1)} %add.207), channel_id=1, source_target_pairs={{0,1},{1,0},{2,3},{3,2},{4,5},{5,4},{6,7},{7,6},{8,9},{9,8},{10,11... | collective-permute-start | bytes 614408 | tf_op jit(solution)/shard_map/ppermute | solution.py:62
  42.3 14.3 %collective-permute-start.5 = (f32[200,256]{1,0:T(8,128)S(1)}, f32[200,256]{1,0:T(8,128)S(1)}, u32[]{:S(2)}, u32[]{:S(2)}) collective-permute-start(f32[200,256]{1,0:T(8,128)S(1)} %add.208), channel_id=1, source_target_pairs={{0,2},{1,3},{2,0},{3,1},{4,6},{5,7},{6,4},{7,5},{8,10},{9,11},{10,... | collective-permute-start | bytes 614408 | tf_op jit(solution)/shard_map/ppermute | solution.py:62
  86.3 18.2 %collective-permute-start.10 = (f32[64,2816]{1,0:T(8,128)S(1)}, f32[64,2816]{1,0:T(8,128)S(1)}, u32[]{:S(2)}, u32[]{:S(2)}) collective-permute-start(f32[64,2816]{1,0:T(8,128)S(1)} %pad_maximum_fusion.15), channel_id=1, source_target_pairs={{0,8},{4,12},{8,0},{12,4},{16,24},{20,28},{24,16},{28,20},{1,9},{5... | collective-permute-start | bytes 2162696 | tf_op jit(solution)/shard_map/ppermute | solution.py:62
  88.1 18.1 %collective-permute-start.15 = (f32[56,2816]{1,0:T(8,128)S(1)}, f32[56,2816]{1,0:T(8,128)S(1)}, u32[]{:S(2)}, u32[]{:S(2)}) collective-permute-start(f32[56,2816]{1,0:T(8,128)S(1)} %slice.336), channel_id=1, source_target_pairs={{0,16},{4,20},{8,24},{12,28},{16,0},{20,4},{24,8},{28,12},{1,17},{... | collective-permute-start | bytes 1892360 | tf_op jit(solution)/shard_map/ppermute | solution.py:62
  104.7 11.4 %collective-permute-start.12 = (f32[64,1408]{1,0:T(8,128)S(1)}, f32[64,1408]{1,0:T(8,128)S(1)}, u32[]{:S(2)}, u32[]{:S(2)}) collective-permute-start(f32[64,1408]{1,0:T(8,128)S(1)} %slice.338), channel_id=1, source_target_pairs={{0,16},{4,20},{8,24},{12,28},{16,0},{20,4},{24,8},{28,12},{1,17},{... | collective-permute-start | bytes 1081352 | tf_op jit(solution)/shard_map/ppermute | solution.py:62
  106.4 11.3 %collective-permute-start.19 = (f32[56,1408]{1,0:T(8,128)S(1)}, f32[56,1408]{1,0:T(8,128)S(1)}, u32[]{:S(2)}, u32[]{:S(2)}) collective-permute-start(f32[56,1408]{1,0:T(8,128)S(1)} %slice.340), channel_id=1, source_target_pairs={{0,8},{4,12},{8,0},{12,4},{16,24},{20,28},{24,16},{28,20},{1,9},{5... | collective-permute-start | bytes 946184 | tf_op jit(solution)/shard_map/ppermute | solution.py:62
  108.2 18.3 %collective-permute-start.18 = (f32[40,2816]{1,0:T(8,128)S(1)}, f32[40,2816]{1,0:T(8,128)S(1)}, u32[]{:S(2)}, u32[]{:S(2)}) collective-permute-start(f32[40,2816]{1,0:T(8,128)S(1)} %pad_maximum_fusion.25), channel_id=1, source_target_pairs={{0,8},{4,12},{8,0},{12,4},{16,24},{20,28},{24,16},{28,20},{1,9},{5... | collective-permute-start | bytes 1351688 | tf_op jit(solution)/shard_map/ppermute | solution.py:62
  109.0 18.2 %collective-permute-start.17 = (f32[40,2816]{1,0:T(8,128)S(1)}, f32[40,2816]{1,0:T(8,128)S(1)}, u32[]{:S(2)}, u32[]{:S(2)}) collective-permute-start(f32[40,2816]{1,0:T(8,128)S(1)} %slice.343), channel_id=1, source_target_pairs={{0,16},{4,20},{8,24},{12,28},{16,0},{20,4},{24,8},{28,12},{1,17},{... | collective-permute-start | bytes 1351688 | tf_op jit(solution)/shard_map/ppermute | solution.py:62
  116.1 17.3 %collective-permute-start.16 = (f32[64,1408]{1,0:T(8,128)S(1)}, f32[64,1408]{1,0:T(8,128)S(1)}, u32[]{:S(2)}, u32[]{:S(2)}) collective-permute-start(f32[64,1408]{1,0:T(8,128)S(1)} %slice_add_fusion.8.refs_0_), channel_id=1, source_target_pairs={{0,16},{4,20},{8,24},{12,28},{16,0},{20,4},{24,8},{28,12},{1,17},{... | collective-permute-start | bytes 1081352 | tf_op jit(solution)/shard_map/ppermute | solution.py:62
  117.8 17.3 %collective-permute-start.23 = (f32[56,1408]{1,0:T(8,128)S(1)}, f32[56,1408]{1,0:T(8,128)S(1)}, u32[]{:S(2)}, u32[]{:S(2)}) collective-permute-start(f32[56,1408]{1,0:T(8,128)S(1)} %slice_add_fusion.11.refs_4_), channel_id=1, source_target_pairs={{0,8},{4,12},{8,0},{12,4},{16,24},{20,28},{24,16},{28,20},{1,9},{5... | collective-permute-start | bytes 946184 | tf_op jit(solution)/shard_map/ppermute | solution.py:62
  126.6 11.7 %collective-permute-start.22 = (f32[40,1408]{1,0:T(8,128)S(1)}, f32[40,1408]{1,0:T(8,128)S(1)}, u32[]{:S(2)}, u32[]{:S(2)}) collective-permute-start(f32[40,1408]{1,0:T(8,128)S(1)} %slice.348), channel_id=1, source_target_pairs={{0,16},{4,20},{8,24},{12,28},{16,0},{20,4},{24,8},{28,12},{1,17},{... | collective-permute-start | bytes 675848 | tf_op jit(solution)/shard_map/ppermute | solution.py:62
  127.3 12.7 %collective-permute-start.21 = (f32[40,1408]{1,0:T(8,128)S(1)}, f32[40,1408]{1,0:T(8,128)S(1)}, u32[]{:S(2)}, u32[]{:S(2)}) collective-permute-start(f32[40,1408]{1,0:T(8,128)S(1)} %slice.349), channel_id=1, source_target_pairs={{0,8},{4,12},{8,0},{12,4},{16,24},{20,28},{24,16},{28,20},{1,9},{5... | collective-permute-start | bytes 675848 | tf_op jit(solution)/shard_map/ppermute | solution.py:62
  133.5 22.9 %collective-permute-start.20 = (f32[64,2816]{1,0:T(8,128)S(1)}, f32[64,2816]{1,0:T(8,128)S(1)}, u32[]{:S(2)}, u32[]{:S(2)}) collective-permute-start(f32[64,2816]{1,0:T(8,128)S(1)} %pad_maximum_fusion.16), channel_id=1, source_target_pairs={{0,8},{4,12},{8,0},{12,4},{16,24},{20,28},{24,16},{28,20},{1,9},{5... | collective-permute-start | bytes 2162696 | tf_op jit(solution)/shard_map/ppermute | solution.py:62
  135.1 21.5 %collective-permute-start.27 = (f32[56,2816]{1,0:T(8,128)S(1)}, f32[56,2816]{1,0:T(8,128)S(1)}, u32[]{:S(2)}, u32[]{:S(2)}) collective-permute-start(f32[56,2816]{1,0:T(8,128)S(1)} %pad_maximum_fusion.21), channel_id=1, source_target_pairs={{0,16},{4,20},{8,24},{12,28},{16,0},{20,4},{24,8},{28,12},{1,17},{... | collective-permute-start | bytes 1892360 | tf_op jit(solution)/shard_map/ppermute | solution.py:62
  138.3 16.6 %collective-permute-start.25 = (f32[40,1408]{1,0:T(8,128)S(1)}, f32[40,1408]{1,0:T(8,128)S(1)}, u32[]{:S(2)}, u32[]{:S(2)}) collective-permute-start(f32[40,1408]{1,0:T(8,128)S(1)} %slice_add_fusion.16.refs_0_), channel_id=1, source_target_pairs={{0,16},{4,20},{8,24},{12,28},{16,0},{20,4},{24,8},{28,12},{1,17},{... | collective-permute-start | bytes 675848 | tf_op jit(solution)/shard_map/ppermute | solution.py:62
  140.0 16.4 %collective-permute-start.24 = (f32[40,1408]{1,0:T(8,128)S(1)}, f32[40,1408]{1,0:T(8,128)S(1)}, u32[]{:S(2)}, u32[]{:S(2)}) collective-permute-start(f32[40,1408]{1,0:T(8,128)S(1)} %slice_add_fusion.17.refs_4_), channel_id=1, source_target_pairs={{0,8},{4,12},{8,0},{12,4},{16,24},{20,28},{24,16},{28,20},{1,9},{5... | collective-permute-start | bytes 675848 | tf_op jit(solution)/shard_map/ppermute | solution.py:62
  157.2 18.0 %collective-permute-start.31 = (f32[40,2816]{1,0:T(8,128)S(1)}, f32[40,2816]{1,0:T(8,128)S(1)}, u32[]{:S(2)}, u32[]{:S(2)}) collective-permute-start(f32[40,2816]{1,0:T(8,128)S(1)} %pad_maximum_fusion.26), channel_id=1, source_target_pairs={{0,8},{4,12},{8,0},{12,4},{16,24},{20,28},{24,16},{28,20},{1,9},{5... | collective-permute-start | bytes 1351688 | tf_op jit(solution)/shard_map/ppermute | solution.py:62
  158.7 16.6 %collective-permute-start.30 = (f32[40,2816]{1,0:T(8,128)S(1)}, f32[40,2816]{1,0:T(8,128)S(1)}, u32[]{:S(2)}, u32[]{:S(2)}) collective-permute-start(f32[40,2816]{1,0:T(8,128)S(1)} %pad_maximum_fusion.27), channel_id=1, source_target_pairs={{0,16},{4,20},{8,24},{12,28},{16,0},{20,4},{24,8},{28,12},{1,17},{... | collective-permute-start | bytes 1351688 | tf_op jit(solution)/shard_map/ppermute | solution.py:62
  175.4 13.1 %collective-permute-start.34 = (f32[40,5632]{1,0:T(8,128)S(1)}, f32[40,5632]{1,0:T(8,128)S(1)}, u32[]{:S(2)}, u32[]{:S(2)}) collective-permute-start(f32[40,5632]{1,0:T(8,128)S(1)} %pad_maximum_fusion.10), channel_id=1, source_target_pairs={{0,4},{4,0},{8,12},{12,8},{16,20},{20,16},{24,28},{28,24},{1,5},{5... | collective-permute-start | bytes 2703368 | tf_op jit(solution)/shard_map/ppermute | solution.py:62
  175.6 12.9 %collective-permute-start.33 = (f32[40,5632]{1,0:T(8,128)S(1)}, f32[40,5632]{1,0:T(8,128)S(1)}, u32[]{:S(2)}, u32[]{:S(2)}) collective-permute-start(f32[40,5632]{1,0:T(8,128)S(1)} %pad_maximum_fusion.9), channel_id=1, source_target_pairs={{0,4},{4,0},{8,12},{12,8},{16,20},{20,16},{24,28},{28,24},{1,5},{5... | collective-permute-start | bytes 2703368 | tf_op jit(solution)/shard_map/ppermute | solution.py:62
  186.9 19.3 %collective-permute-start.32 = (f32[248,384]{1,0:T(8,128)S(1)}, f32[248,384]{1,0:T(8,128)S(1)}, u32[]{:S(2)}, u32[]{:S(2)}) collective-permute-start(f32[248,384]{1,0:T(8,128)S(1)} %add.224), channel_id=1, source_target_pairs={{0,2},{1,3},{2,0},{3,1},{4,6},{5,7},{6,4},{7,5},{8,10},{9,11},{10,... | collective-permute-start | bytes 1142792 | tf_op jit(solution)/shard_map/ppermute | solution.py:62
  206.3 16.4 %collective-permute-start.35 = (f32[248,384]{1,0:T(8,128)S(1)}, f32[248,384]{1,0:T(8,128)S(1)}, u32[]{:S(2)}, u32[]{:S(2)}) collective-permute-start(f32[248,384]{1,0:T(8,128)S(1)} %add.225), channel_id=1, source_target_pairs={{0,1},{1,0},{2,3},{3,2},{4,5},{5,4},{6,7},{7,6},{8,9},{9,8},{10,11... | collective-permute-start | bytes 1142792 | tf_op jit(solution)/shard_map/ppermute | solution.py:62
  211.8 14.6 %collective-permute-start.37 = (f32[168,384]{1,0:T(8,128)S(1)}, f32[168,384]{1,0:T(8,128)S(1)}, u32[]{:S(2)}, u32[]{:S(2)}) collective-permute-start(f32[168,384]{1,0:T(8,128)S(1)} %add.226), channel_id=1, source_target_pairs={{0,2},{1,3},{2,0},{3,1},{4,6},{5,7},{6,4},{7,5},{8,10},{9,11},{10,... | collective-permute-start | bytes 774152 | tf_op jit(solution)/shard_map/ppermute | solution.py:62
  252.5 20.0 %collective-permute-start.47 = (f32[64,2816]{1,0:T(8,128)S(1)}, f32[64,2816]{1,0:T(8,128)S(1)}, u32[]{:S(2)}, u32[]{:S(2)}) collective-permute-start(f32[64,2816]{1,0:T(8,128)S(1)} %pad_maximum_fusion.17), channel_id=1, source_target_pairs={{0,8},{4,12},{8,0},{12,4},{16,24},{20,28},{24,16},{28,20},{1,9},{5... | collective-permute-start | bytes 2162696 | tf_op jit(solution)/shard_map/ppermute | solution.py:62
  254.1 16.7 %collective-permute-start.40 = (f32[8,128]{1,0:T(8,128)S(1)}, f32[8,128]{1,0:T(8,128)S(1)}, u32[]{:S(2)}, u32[]{:S(2)}) collective-permute-start(f32[8,128]{1,0:T(8,128)S(1)} %broadcast_add_fusion.1), channel_id=1, source_target_pairs={{0,8},{4,12},{8,0},{12,4},{16,24},{20,28},{24,16},{28,20},{1,9},{5... | collective-permute-start | bytes 12296 | tf_op jit(solution)/shard_map/ppermute | solution.py:62
  254.9 19.3 %collective-permute-start.46 = (f32[56,2816]{1,0:T(8,128)S(1)}, f32[56,2816]{1,0:T(8,128)S(1)}, u32[]{:S(2)}, u32[]{:S(2)}) collective-permute-start(f32[56,2816]{1,0:T(8,128)S(1)} %slice.360), channel_id=1, source_target_pairs={{0,16},{4,20},{8,24},{12,28},{16,0},{20,4},{24,8},{28,12},{1,17},{... | collective-permute-start | bytes 1892360 | tf_op jit(solution)/shard_map/ppermute | solution.py:62
  272.6 11.4 %collective-permute-start.48 = (f32[64,1408]{1,0:T(8,128)S(1)}, f32[64,1408]{1,0:T(8,128)S(1)}, u32[]{:S(2)}, u32[]{:S(2)}) collective-permute-start(f32[64,1408]{1,0:T(8,128)S(1)} %slice.364), channel_id=1, source_target_pairs={{0,16},{4,20},{8,24},{12,28},{16,0},{20,4},{24,8},{28,12},{1,17},{... | collective-permute-start | bytes 1081352 | tf_op jit(solution)/shard_map/ppermute | solution.py:62
  274.3 11.3 %collective-permute-start.52 = (f32[56,1408]{1,0:T(8,128)S(1)}, f32[56,1408]{1,0:T(8,128)S(1)}, u32[]{:S(2)}, u32[]{:S(2)}) collective-permute-start(f32[56,1408]{1,0:T(8,128)S(1)} %slice.365), channel_id=1, source_target_pairs={{0,8},{4,12},{8,0},{12,4},{16,24},{20,28},{24,16},{28,20},{1,9},{5... | collective-permute-start | bytes 946184 | tf_op jit(solution)/shard_map/ppermute | solution.py:62
  276.1 18.3 %collective-permute-start.51 = (f32[40,2816]{1,0:T(8,128)S(1)}, f32[40,2816]{1,0:T(8,128)S(1)}, u32[]{:S(2)}, u32[]{:S(2)}) collective-permute-start(f32[40,2816]{1,0:T(8,128)S(1)} %pad_maximum_fusion.28), channel_id=1, source_target_pairs={{0,8},{4,12},{8,0},{12,4},{16,24},{20,28},{24,16},{28,20},{1,9},{5... | collective-permute-start | bytes 1351688 | tf_op jit(solution)/shard_map/ppermute | solution.py:62
  276.8 18.2 %collective-permute-start.50 = (f32[40,2816]{1,0:T(8,128)S(1)}, f32[40,2816]{1,0:T(8,128)S(1)}, u32[]{:S(2)}, u32[]{:S(2)}) collective-permute-start(f32[40,2816]{1,0:T(8,128)S(1)} %slice.368), channel_id=1, source_target_pairs={{0,16},{4,20},{8,24},{12,28},{16,0},{20,4},{24,8},{28,12},{1,17},{... | collective-permute-start | bytes 1351688 | tf_op jit(solution)/shard_map/ppermute | solution.py:62
  284.0 17.3 %collective-permute-start.49 = (f32[64,1408]{1,0:T(8,128)S(1)}, f32[64,1408]{1,0:T(8,128)S(1)}, u32[]{:S(2)}, u32[]{:S(2)}) collective-permute-start(f32[64,1408]{1,0:T(8,128)S(1)} %slice_add_fusion.7.refs_1_), channel_id=1, source_target_pairs={{0,16},{4,20},{8,24},{12,28},{16,0},{20,4},{24,8},{28,12},{1,17},{... | collective-permute-start | bytes 1081352 | tf_op jit(solution)/shard_map/ppermute | solution.py:62
  285.6 17.3 %collective-permute-start.56 = (f32[56,1408]{1,0:T(8,128)S(1)}, f32[56,1408]{1,0:T(8,128)S(1)}, u32[]{:S(2)}, u32[]{:S(2)}) collective-permute-start(f32[56,1408]{1,0:T(8,128)S(1)} %slice_add_fusion.10.refs_5_), channel_id=1, source_target_pairs={{0,8},{4,12},{8,0},{12,4},{16,24},{20,28},{24,16},{28,20},{1,9},{5... | collective-permute-start | bytes 946184 | tf_op jit(solution)/shard_map/ppermute | solution.py:62
  294.5 11.7 %collective-permute-start.55 = (f32[40,1408]{1,0:T(8,128)S(1)}, f32[40,1408]{1,0:T(8,128)S(1)}, u32[]{:S(2)}, u32[]{:S(2)}) collective-permute-start(f32[40,1408]{1,0:T(8,128)S(1)} %slice.374), channel_id=1, source_target_pairs={{0,16},{4,20},{8,24},{12,28},{16,0},{20,4},{24,8},{28,12},{1,17},{... | collective-permute-start | bytes 675848 | tf_op jit(solution)/shard_map/ppermute | solution.py:62
  295.1 12.7 %collective-permute-start.54 = (f32[40,1408]{1,0:T(8,128)S(1)}, f32[40,1408]{1,0:T(8,128)S(1)}, u32[]{:S(2)}, u32[]{:S(2)}) collective-permute-start(f32[40,1408]{1,0:T(8,128)S(1)} %slice.375), channel_id=1, source_target_pairs={{0,8},{4,12},{8,0},{12,4},{16,24},{20,28},{24,16},{28,20},{1,9},{5... | collective-permute-start | bytes 675848 | tf_op jit(solution)/shard_map/ppermute | solution.py:62
  301.4 24.8 %collective-permute-start.53 = (f32[64,2816]{1,0:T(8,128)S(1)}, f32[64,2816]{1,0:T(8,128)S(1)}, u32[]{:S(2)}, u32[]{:S(2)}) collective-permute-start(f32[64,2816]{1,0:T(8,128)S(1)} %pad_maximum_fusion.18), channel_id=1, source_target_pairs={{0,8},{4,12},{8,0},{12,4},{16,24},{20,28},{24,16},{28,20},{1,9},{5... | collective-permute-start | bytes 2162696 | tf_op jit(solution)/shard_map/ppermute | solution.py:62
  303.0 24.4 %collective-permute-start.60 = (f32[56,2816]{1,0:T(8,128)S(1)}, f32[56,2816]{1,0:T(8,128)S(1)}, u32[]{:S(2)}, u32[]{:S(2)}) collective-permute-start(f32[56,2816]{1,0:T(8,128)S(1)} %pad_maximum_fusion.22), channel_id=1, source_target_pairs={{0,16},{4,20},{8,24},{12,28},{16,0},{20,4},{24,8},{28,12},{1,17},{... | collective-permute-start | bytes 1892360 | tf_op jit(solution)/shard_map/ppermute | solution.py:62
  306.2 17.1 %collective-permute-start.58 = (f32[40,1408]{1,0:T(8,128)S(1)}, f32[40,1408]{1,0:T(8,128)S(1)}, u32[]{:S(2)}, u32[]{:S(2)}) collective-permute-start(f32[40,1408]{1,0:T(8,128)S(1)} %slice_add_fusion.14.refs_1_), channel_id=1, source_target_pairs={{0,16},{4,20},{8,24},{12,28},{16,0},{20,4},{24,8},{28,12},{1,17},{... | collective-permute-start | bytes 675848 | tf_op jit(solution)/shard_map/ppermute | solution.py:62
  307.8 16.8 %collective-permute-start.57 = (f32[40,1408]{1,0:T(8,128)S(1)}, f32[40,1408]{1,0:T(8,128)S(1)}, u32[]{:S(2)}, u32[]{:S(2)}) collective-permute-start(f32[40,1408]{1,0:T(8,128)S(1)} %slice_add_fusion.15.refs_5_), channel_id=1, source_target_pairs={{0,8},{4,12},{8,0},{12,4},{16,24},{20,28},{24,16},{28,20},{1,9},{5... | collective-permute-start | bytes 675848 | tf_op jit(solution)/shard_map/ppermute | solution.py:62
  332.1 21.7 %collective-permute-start.64 = (f32[40,2816]{1,0:T(8,128)}, f32[40,2816]{1,0:T(8,128)S(1)}, u32[]{:S(2)}, u32[]{:S(2)}) collective-permute-start(f32[40,2816]{1,0:T(8,128)} %pad_maximum_fusion.29), channel_id=1, source_target_pairs={{0,8},{4,12},{8,0},{12,4},{16,24},{20,28},{24,16},{28,20},{1,9},{5... | collective-permute-start | bytes 1351688 | tf_op jit(solution)/shard_map/ppermute | solution.py:62
  333.7 20.3 %collective-permute-start.63 = (f32[40,2816]{1,0:T(8,128)}, f32[40,2816]{1,0:T(8,128)S(1)}, u32[]{:S(2)}, u32[]{:S(2)}) collective-permute-start(f32[40,2816]{1,0:T(8,128)} %pad_maximum_fusion.30), channel_id=1, source_target_pairs={{0,16},{4,20},{8,24},{12,28},{16,0},{20,4},{24,8},{28,12},{1,17},{... | collective-permute-start | bytes 1351688 | tf_op jit(solution)/shard_map/ppermute | solution.py:62
  354.9 13.1 %collective-permute-start.67 = (f32[40,5632]{1,0:T(8,128)S(1)}, f32[40,5632]{1,0:T(8,128)S(1)}, u32[]{:S(2)}, u32[]{:S(2)}) collective-permute-start(f32[40,5632]{1,0:T(8,128)S(1)} %pad_maximum_fusion.12), channel_id=1, source_target_pairs={{0,4},{4,0},{8,12},{12,8},{16,20},{20,16},{24,28},{28,24},{1,5},{5... | collective-permute-start | bytes 2703368 | tf_op jit(solution)/shard_map/ppermute | solution.py:62
  354.9 13.1 %collective-permute-start.66 = (f32[40,5632]{1,0:T(8,128)S(1)}, f32[40,5632]{1,0:T(8,128)S(1)}, u32[]{:S(2)}, u32[]{:S(2)}) collective-permute-start(f32[40,5632]{1,0:T(8,128)S(1)} %pad_maximum_fusion.11), channel_id=1, source_target_pairs={{0,4},{4,0},{8,12},{12,8},{16,20},{20,16},{24,28},{28,24},{1,5},{5... | collective-permute-start | bytes 2703368 | tf_op jit(solution)/shard_map/ppermute | solution.py:62
  366.3 19.2 %collective-permute-start.65 = (f32[248,384]{1,0:T(8,128)S(1)}, f32[248,384]{1,0:T(8,128)S(1)}, u32[]{:S(2)}, u32[]{:S(2)}) collective-permute-start(f32[248,384]{1,0:T(8,128)S(1)} %add.245), channel_id=1, source_target_pairs={{0,2},{1,3},{2,0},{3,1},{4,6},{5,7},{6,4},{7,5},{8,10},{9,11},{10,... | collective-permute-start | bytes 1142792 | tf_op jit(solution)/shard_map/ppermute | solution.py:62
  385.6 16.7 %collective-permute-start.68 = (f32[248,384]{1,0:T(8,128)S(1)}, f32[248,384]{1,0:T(8,128)S(1)}, u32[]{:S(2)}, u32[]{:S(2)}) collective-permute-start(f32[248,384]{1,0:T(8,128)S(1)} %add.246), channel_id=1, source_target_pairs={{0,1},{1,0},{2,3},{3,2},{4,5},{5,4},{6,7},{7,6},{8,9},{9,8},{10,11... | collective-permute-start | bytes 1142792 | tf_op jit(solution)/shard_map/ppermute | solution.py:62
  391.1 14.6 %collective-permute-start.70 = (f32[168,384]{1,0:T(8,128)S(1)}, f32[168,384]{1,0:T(8,128)S(1)}, u32[]{:S(2)}, u32[]{:S(2)}) collective-permute-start(f32[168,384]{1,0:T(8,128)S(1)} %add.247), channel_id=1, source_target_pairs={{0,2},{1,3},{2,0},{3,1},{4,6},{5,7},{6,4},{7,5},{8,10},{9,11},{10,... | collective-permute-start | bytes 774152 | tf_op jit(solution)/shard_map/ppermute | solution.py:62
  437.8 20.9 %collective-permute-start.80 = (f32[64,2816]{1,0:T(8,128)}, f32[64,2816]{1,0:T(8,128)}, u32[]{:S(2)}, u32[]{:S(2)}) collective-permute-start(f32[64,2816]{1,0:T(8,128)} %pad_maximum_fusion.19), channel_id=1, source_target_pairs={{0,8},{4,12},{8,0},{12,4},{16,24},{20,28},{24,16},{28,20},{1,9},{5... | collective-permute-start | bytes 2162696 | tf_op jit(solution)/shard_map/ppermute | solution.py:62
  440.4 16.0 %collective-permute-start.73 = (f32[8,128]{1,0:T(8,128)S(1)}, f32[8,128]{1,0:T(8,128)S(1)}, u32[]{:S(2)}, u32[]{:S(2)}) collective-permute-start(f32[8,128]{1,0:T(8,128)S(1)} %broadcast_add_fusion), channel_id=1, source_target_pairs={{0,8},{4,12},{8,0},{12,4},{16,24},{20,28},{24,16},{28,20},{1,9},{5... | collective-permute-start | bytes 12296 | tf_op jit(solution)/shard_map/ppermute | solution.py:62
  443.6 18.1 %collective-permute-start.79 = (f32[56,2816]{1,0:T(8,128)S(1)}, f32[56,2816]{1,0:T(8,128)S(1)}, u32[]{:S(2)}, u32[]{:S(2)}) collective-permute-start(f32[56,2816]{1,0:T(8,128)S(1)} %slice.386), channel_id=1, source_target_pairs={{0,16},{4,20},{8,24},{12,28},{16,0},{20,4},{24,8},{28,12},{1,17},{... | collective-permute-start | bytes 1892360 | tf_op jit(solution)/shard_map/ppermute | solution.py:62
  460.7 22.1 %collective-permute-start.83 = (f32[64,1408]{1,0:T(8,128)}, f32[64,1408]{1,0:T(8,128)S(1)}, u32[]{:S(2)}, u32[]{:S(2)}) collective-permute-start(f32[64,1408]{1,0:T(8,128)} %slice.390), channel_id=1, source_target_pairs={{0,16},{4,20},{8,24},{12,28},{16,0},{20,4},{24,8},{28,12},{1,17},{... | collective-permute-start | bytes 1081352 | tf_op jit(solution)/shard_map/ppermute | solution.py:62
  462.5 21.4 %collective-permute-start.82 = (f32[56,1408]{1,0:T(8,128)}, f32[56,1408]{1,0:T(8,128)}, u32[]{:S(2)}, u32[]{:S(2)}) collective-permute-start(f32[56,1408]{1,0:T(8,128)} %slice.391), channel_id=1, source_target_pairs={{0,8},{4,12},{8,0},{12,4},{16,24},{20,28},{24,16},{28,20},{1,9},{5... | collective-permute-start | bytes 946184 | tf_op jit(solution)/shard_map/ppermute | solution.py:62
  464.7 21.6 %collective-permute-start.81 = (f32[40,2816]{1,0:T(8,128)}, f32[40,2816]{1,0:T(8,128)}, u32[]{:S(2)}, u32[]{:S(2)}) collective-permute-start(f32[40,2816]{1,0:T(8,128)} %pad_maximum_fusion.31), channel_id=1, source_target_pairs={{0,8},{4,12},{8,0},{12,4},{16,24},{20,28},{24,16},{28,20},{1,9},{5... | collective-permute-start | bytes 1351688 | tf_op jit(solution)/shard_map/ppermute | solution.py:62
  466.2 22.2 %collective-permute-start.87 = (f32[40,2816]{1,0:T(8,128)S(1)}, f32[40,2816]{1,0:T(8,128)}, u32[]{:S(2)}, u32[]{:S(2)}) collective-permute-start(f32[40,2816]{1,0:T(8,128)S(1)} %slice.394), channel_id=1, source_target_pairs={{0,16},{4,20},{8,24},{12,28},{16,0},{20,4},{24,8},{28,12},{1,17},{... | collective-permute-start | bytes 1351688 | tf_op jit(solution)/shard_map/ppermute | solution.py:62
  482.9 11.4 %collective-permute-start.86 = (f32[64,1408]{1,0:T(8,128)S(1)}, f32[64,1408]{1,0:T(8,128)S(1)}, u32[]{:S(2)}, u32[]{:S(2)}) collective-permute-start(f32[64,1408]{1,0:T(8,128)S(1)} %slice_add_fusion.6.refs_0_), channel_id=1, source_target_pairs={{0,16},{4,20},{8,24},{12,28},{16,0},{20,4},{24,8},{28,12},{1,17},{... | collective-permute-start | bytes 1081352 | tf_op jit(solution)/shard_map/ppermute | solution.py:62
  487.5 11.7 %collective-permute-start.84 = (f32[40,1408]{1,0:T(8,128)S(1)}, f32[40,1408]{1,0:T(8,128)S(1)}, u32[]{:S(2)}, u32[]{:S(2)}) collective-permute-start(f32[40,1408]{1,0:T(8,128)S(1)} %slice.400), channel_id=1, source_target_pairs={{0,16},{4,20},{8,24},{12,28},{16,0},{20,4},{24,8},{28,12},{1,17},{... | collective-permute-start | bytes 675848 | tf_op jit(solution)/shard_map/ppermute | solution.py:62
  489.6 11.5 %collective-permute-start.89 = (f32[40,1408]{1,0:T(8,128)S(1)}, f32[40,1408]{1,0:T(8,128)S(1)}, u32[]{:S(2)}, u32[]{:S(2)}) collective-permute-start(f32[40,1408]{1,0:T(8,128)S(1)} %slice.402), channel_id=1, source_target_pairs={{0,8},{4,12},{8,0},{12,4},{16,24},{20,28},{24,16},{28,20},{1,9},{5... | collective-permute-start | bytes 675848 | tf_op jit(solution)/shard_map/ppermute | solution.py:62
  494.4 28.0 %collective-permute-start.92 = (f32[64,2816]{1,0:T(8,128)S(1)}, f32[64,2816]{1,0:T(8,128)S(1)}, u32[]{:S(2)}, u32[]{:S(2)}) collective-permute-start(f32[64,2816]{1,0:T(8,128)S(1)} %pad_maximum_fusion.20), channel_id=1, source_target_pairs={{0,8},{4,12},{8,0},{12,4},{16,24},{20,28},{24,16},{28,20},{1,9},{5... | collective-permute-start | bytes 2162696 | tf_op jit(solution)/shard_map/ppermute | solution.py:62
  496.2 26.3 %collective-permute-start.91 = (f32[56,2816]{1,0:T(8,128)S(1)}, f32[56,2816]{1,0:T(8,128)S(1)}, u32[]{:S(2)}, u32[]{:S(2)}) collective-permute-start(f32[56,2816]{1,0:T(8,128)S(1)} %pad_maximum_fusion.23), channel_id=1, source_target_pairs={{0,16},{4,20},{8,24},{12,28},{16,0},{20,4},{24,8},{28,12},{1,17},{... | collective-permute-start | bytes 1892360 | tf_op jit(solution)/shard_map/ppermute | solution.py:62
  499.2 15.9 %collective-permute-start.88 = (f32[40,1408]{1,0:T(8,128)S(1)}, f32[40,1408]{1,0:T(8,128)S(1)}, u32[]{:S(2)}, u32[]{:S(2)}) collective-permute-start(f32[40,1408]{1,0:T(8,128)S(1)} %slice_add_fusion.13.refs_0_), channel_id=1, source_target_pairs={{0,16},{4,20},{8,24},{12,28},{16,0},{20,4},{24,8},{28,12},{1,17},{... | collective-permute-start | bytes 675848 | tf_op jit(solution)/shard_map/ppermute | solution.py:62
  501.1 20.2 %collective-permute-start.93 = (f32[40,1408]{1,0:T(8,128)S(1)}, f32[40,1408]{1,0:T(8,128)S(1)}, u32[]{:S(2)}, u32[]{:S(2)}) collective-permute-start(f32[40,1408]{1,0:T(8,128)S(1)} %slice_add_fusion.12.refs_4_), channel_id=1, source_target_pairs={{0,8},{4,12},{8,0},{12,4},{16,24},{20,28},{24,16},{28,20},{1,9},{5... | collective-permute-start | bytes 675848 | tf_op jit(solution)/shard_map/ppermute | solution.py:62
  515.1 13.2 %collective-permute-start.90 = (f32[40,2816]{1,0:T(8,128)S(1)}, f32[40,2816]{1,0:T(8,128)S(1)}, u32[]{:S(2)}, u32[]{:S(2)}) collective-permute-start(f32[40,2816]{1,0:T(8,128)S(1)} %pad_maximum_fusion.32), channel_id=1, source_target_pairs={{0,8},{4,12},{8,0},{12,4},{16,24},{20,28},{24,16},{28,20},{1,9},{5... | collective-permute-start | bytes 1351688 | tf_op jit(solution)/shard_map/ppermute | solution.py:62
  (60 other events, 1220.9 us)

commit v6 on v5

--- a/solution.py
+++ b/solution.py
@@ -342,7 +342,7 @@
             + stream_scratch(plan),
         ),
         input_output_aliases=aliases,
-        compiler_params=params(30),
+        compiler_params=params(46),
         cost_estimate=pl.CostEstimate(
             flops=6 * n_pair * rows * feats, bytes_accessed=4 * feats * (rows + 3 * n_pair), transcendentals=0
         ),

time: 546 us -> 542 us (level)
  no operation moved by 1% of the time
where the time goes in v6:
time: 542 us; the launch traced here: 534 us
  waiting for transfers between devices  226 us (42%)
  Pallas kernels  163 us (30%)
  starting transfers between devices  88.7 us (16%)
  other arithmetic  38.7 us (7%)
  local copies, waits for them, and re-layouts  9.91 us (2%)
  between operations  8.43 us (2%)
    ppermute x99, waiting for transfers between devices, swap(): return lax.ppermute(x, axis, [(i, i ^ stride) for i in range(size)])  226 us
    ppermute x99, starting transfers between devices, swap(): return lax.ppermute(x, axis, [(i, i ^ stride) for i in range(size)])  88.7 us
    pallas_call x6, Pallas kernels, back(): pl.pallas_call(functools.partial(back_body, plan, group), out_shape=outs,...  64 us
    pallas_call x4, Pallas kernels, forth(): pl.pallas_call(functools.partial(forth_body, plan, pair, step is not None...  58.3 us
    pallas_call x3, Pallas kernels, first(): pl.pallas_call(functools.partial(first_body, plan), out_shape=[pltpu.HBM(...  32.5 us
    add x1, other arithmetic, under(): order.after(weights) + (step0 + step1 * ratio) * direction  14.1 us
  transfers between devices with their start and end apart: 99, of which 43 were waited for; matrix products, arithmetic and copies ran while one was open for 7% of the time, Pallas kernels for 21%

profile of v6, /device:TPU:0, one launch (start us, length us, event | category | flops | bytes accessed | tf_op | source)
XLA Modules:
  0.0 534.2 jit_solution(12219376497259990511)
XLA Ops:
  1.2 10.7 %split_and_logits.3 = (bf16[768,5632]{1,0:T(8,128)(2,1)}, bf16[768,5632]{1,0:T(8,128)(2,1)}, f32[200,256]{1,0:T(8,128)}, f32[200,256]{1,0:T(8,128)}) custom-call(s32[3]{0:T(128)} %pad_add_fusion.s_ref, f32[768,5632]{1,0:T(8,128)} %f_ref.3, f32[400,5632]{1,0:T(8,128)} %w_ref.5), custom_call_target="tpu_custom_call" | custom-call | flops 3460300800 | bytes 20545536 | tf_op jit(solution)/shard_map/split_and_logits/pallas_call | solution.py:102
  11.9 3.1 collective-permute-start
  15.0 10.9 %split_and_logits.4 = (bf16[768,5632]{1,0:T(8,128)(2,1)}, bf16[768,5632]{1,0:T(8,128)(2,1)}, f32[200,256]{1,0:T(8,128)}, f32[200,256]{1,0:T(8,128)}) custom-call(s32[3]{0:T(128)} %pad_add_fusion.s_ref, f32[768,5632]{1,0:T(8,128)} %f_ref.3, f32[400,5632]{1,0:T(8,128)} %w_ref.5, ...), custom_call_target="tpu_custom_call", output_to_operand_aliasing={{0}: (3, {}), {1}: (4, {})} | custom-call | flops 3460300800 | bytes 20545536 | tf_op jit(solution)/shard_map/split_and_logits/pallas_call | solution.py:102
  26.0 3.1 collective-permute-start.1
  29.1 10.9 %split_and_logits.5 = (bf16[768,5632]{1,0:T(8,128)(2,1)}, bf16[768,5632]{1,0:T(8,128)(2,1)}, f32[200,256]{1,0:T(8,128)}, f32[200,256]{1,0:T(8,128)}) custom-call(s32[3]{0:T(128)} %pad_add_fusion.s_ref, f32[768,5632]{1,0:T(8,128)} %f_ref.3, f32[400,5632]{1,0:T(8,128)} %w_ref.5, ...), custom_call_target="tpu_custom_call", output_to_operand_aliasing={{0}: (3, {}), {1}: (4, {})} | custom-call | flops 3460300800 | bytes 20545536 | tf_op jit(solution)/shard_map/split_and_logits/pallas_call | solution.py:102
  40.0 1.6 collective-permute-start.3
  42.4 11.8 %collective-permute-done.3 = f32[200,256]{1,0:T(8,128)S(1)} collective-permute-done((f32[200,256]{1,0:T(8,128)}, f32[200,256]{1,0:T(8,128)S(1)}, u32[]{:S(2)}, u32[]{:S(2)}) %collective-permute-start.3) | collective-permute-done | bytes 204832 | tf_op jit(solution)/shard_map/ppermute | solution.py:62
  54.5 2.0 collective-permute-done.2
  57.5 6.8 %collective-permute-done.6 = f32[200,256]{1,0:T(8,128)S(1)} collective-permute-done((f32[200,256]{1,0:T(8,128)S(1)}, f32[200,256]{1,0:T(8,128)S(1)}, u32[]{:S(2)}, u32[]{:S(2)}) %collective-permute-start.6) | collective-permute-done | bytes 204832 | tf_op jit(solution)/shard_map/ppermute | solution.py:62
  65.9 4.3 collective-permute-done.8
  71.4 11.3 %back_group.6 = (f32[64,5632]{1,0:T(8,128)S(1)}, f32[64,5632]{1,0:T(8,128)S(1)}, f32[56,5632]{1,0:T(8,128)S(1)}, f32[56,5632]{1,0:T(8,128)S(1)}, bf16[768,5632]{1,0:T(8,128)(2,1)}, /*index=5*/bf16[768,5632]{1,0:T(8,128)(2,1)}) custom-call(s32[3]{0:T(128)S(1)} %copy-done.2, ...), custom_call_target="tpu_custom_call", output_to_operand_aliasing={{4}: (2, {}), {5}: (3, {})} | custom-call | flops 6228541440 | bytes 22708224 | tf_op jit(solution)/shard_map/back_group/pallas_call | solution.py:187
  83.2 2.7 collective-permute-done.9
  89.6 9.8 %back_group.7 = (f32[40,5632]{1,0:T(8,128)S(1)}, f32[40,5632]{1,0:T(8,128)S(1)}, f32[40,5632]{1,0:T(8,128)S(1)}, f32[40,5632]{1,0:T(8,128)S(1)}, bf16[768,5632]{1,0:T(8,128)(2,1)}, /*index=5*/bf16[768,5632]{1,0:T(8,128)(2,1)}) custom-call(s32[3]{0:T(128)S(1)} %copy-done.2, ...), custom_call_target="tpu_custom_call", output_to_operand_aliasing={{4}: (2, {}), {5}: (3, {})} | custom-call | flops 4152360960 | bytes 20905984 | tf_op jit(solution)/shard_map/back_group/pallas_call | solution.py:187
  100.0 4.5 collective-permute-done.10
  109.4 6.6 %collective-permute-done.12 = f32[64,1408]{1,0:T(8,128)S(1)} collective-permute-done((f32[64,1408]{1,0:T(8,128)S(1)}, f32[64,1408]{1,0:T(8,128)S(1)}, u32[]{:S(2)}, u32[]{:S(2)}) %collective-permute-start.12) | collective-permute-done | bytes 360480 | tf_op jit(solution)/shard_map/ppermute | solution.py:62
  119.3 7.2 %collective-permute-done.18 = f32[40,2816]{1,0:T(8,128)S(1)} collective-permute-done((f32[40,2816]{1,0:T(8,128)S(1)}, f32[40,2816]{1,0:T(8,128)S(1)}, u32[]{:S(2)}, u32[]{:S(2)}) %collective-permute-start.18) | collective-permute-done | bytes 450592 | tf_op jit(solution)/shard_map/ppermute | solution.py:62
  128.7 4.7 collective-permute-done.16.refs_1_
  141.5 13.4 %collective-permute-done.25.refs_1_ = f32[40,1408]{1,0:T(8,128)S(1)} collective-permute-done((f32[40,1408]{1,0:T(8,128)S(1)}, f32[40,1408]{1,0:T(8,128)S(1)}, u32[]{:S(2)}, u32[]{:S(2)}) %collective-permute-start.25) | collective-permute-done | bytes 225312 | tf_op jit(solution)/shard_map/ppermute | solution.py:62
  159.2 2.4 collective-permute-done.28.refs_7_
  161.5 13.7 %forth_pair.4 = (f32[400,5632]{1,0:T(8,128)}, f32[248,384]{1,0:T(8,128)S(1)}, f32[248,384]{1,0:T(8,128)S(1)}, bf16[768,5632]{1,0:T(8,128)(2,1)}, bf16[768,5632]{1,0:T(8,128)(2,1)}) custom-call(s32[3]{0:T(128)S(1)} %copy-done.2, f32[64,1408]{1,0:T(8,128)S(1)} %slice_add_fusion.8.refs_0_, ...), custom_call_target="tpu_custom_call", output_to_operand_aliasing={{3}: (9, {}), {4}: (10, {})} | custom-call | flops 6228541440 | bytes 33521664 | tf_op jit(solution)/shard_map/forth_pair/pallas_call | solution.py:329
  177.0 9.8 %collective-permute-done.29 = f32[248,384]{1,0:T(8,128)S(1)} collective-permute-done((f32[248,384]{1,0:T(8,128)S(1)}, f32[248,384]{1,0:T(8,128)S(1)}, u32[]{:S(2)}, u32[]{:S(2)}) %collective-permute-start.29) | collective-permute-done | bytes 380960 | tf_op jit(solution)/shard_map/ppermute | solution.py:62
  188.5 13.3 %forth_pair.5 = (f32[400,5632]{1,0:T(8,128)}, f32[168,384]{1,0:T(8,128)S(1)}, f32[168,384]{1,0:T(8,128)S(1)}, bf16[768,5632]{1,0:T(8,128)(2,1)}, bf16[768,5632]{1,0:T(8,128)(2,1)}) custom-call(s32[3]{0:T(128)S(1)} %copy-done.2, f32[40,1408]{1,0:T(8,128)S(1)} %slice_add_fusion.16.refs_0_, ...), custom_call_target="tpu_custom_call", output_to_operand_aliasing={{3}: (9, {}), {4}: (10, {}), {0}: (11, {})} | custom-call | flops 4152360960 | bytes 28114944 | tf_op jit(solution)/shard_map/forth_pair/pallas_call | solution.py:329
  201.8 1.8 collective-permute-start.36
  203.6 2.6 collective-permute-done.32
  206.3 5.4 %collective-permute-done.36 = f32[168,384]{1,0:T(8,128)S(1)} collective-permute-done((f32[168,384]{1,0:T(8,128)S(1)}, f32[168,384]{1,0:T(8,128)S(1)}, u32[]{:S(2)}, u32[]{:S(2)}) %collective-permute-start.36) | collective-permute-done | bytes 258080 | tf_op jit(solution)/shard_map/ppermute | solution.py:62
  212.6 10.0 %collective-permute-done.35 = f32[248,384]{1,0:T(8,128)S(1)} collective-permute-done((f32[248,384]{1,0:T(8,128)S(1)}, f32[248,384]{1,0:T(8,128)S(1)}, u32[]{:S(2)}, u32[]{:S(2)}) %collective-permute-start.35) | collective-permute-done | bytes 380960 | tf_op jit(solution)/shard_map/ppermute | solution.py:62
  222.6 3.7 collective-permute-done.37
  226.6 7.1 %collective-permute-done.38 = f32[168,384]{1,0:T(8,128)S(1)} collective-permute-done((f32[168,384]{1,0:T(8,128)S(1)}, f32[168,384]{1,0:T(8,128)S(1)}, u32[]{:S(2)}, u32[]{:S(2)}) %collective-permute-start.38) | collective-permute-done | bytes 258080 | tf_op jit(solution)/shard_map/ppermute | solution.py:62
  235.1 11.3 %back_group.8 = (f32[64,5632]{1,0:T(8,128)S(1)}, f32[64,5632]{1,0:T(8,128)S(1)}, f32[56,5632]{1,0:T(8,128)S(1)}, f32[56,5632]{1,0:T(8,128)S(1)}, bf16[768,5632]{1,0:T(8,128)(2,1)}, /*index=5*/bf16[768,5632]{1,0:T(8,128)(2,1)}) custom-call(s32[3]{0:T(128)S(1)} %copy-done.2, ...), custom_call_target="tpu_custom_call", output_to_operand_aliasing={{4}: (2, {}), {5}: (3, {})} | custom-call | flops 6228541440 | bytes 22708224 | tf_op jit(solution)/shard_map/back_group/pallas_call | solution.py:187
  247.7 3.8 collective-permute-done.39
  255.4 9.7 %back_group.9 = (f32[40,5632]{1,0:T(8,128)S(1)}, f32[40,5632]{1,0:T(8,128)S(1)}, f32[40,5632]{1,0:T(8,128)S(1)}, f32[40,5632]{1,0:T(8,128)S(1)}, bf16[768,5632]{1,0:T(8,128)(2,1)}, /*index=5*/bf16[768,5632]{1,0:T(8,128)(2,1)}) custom-call(s32[3]{0:T(128)S(1)} %copy-done.2, ...), custom_call_target="tpu_custom_call", output_to_operand_aliasing={{4}: (2, {}), {5}: (3, {})} | custom-call | flops 4152360960 | bytes 20905984 | tf_op jit(solution)/shard_map/back_group/pallas_call | solution.py:187
  265.2 5.6 %collective-permute-done.40 = f32[8,128]{1,0:T(8,128)S(1)} collective-permute-done((f32[8,128]{1,0:T(8,128)S(1)}, f32[8,128]{1,0:T(8,128)S(1)}, u32[]{:S(2)}, u32[]{:S(2)}) %collective-permute-start.40) | collective-permute-done | bytes 4128 | tf_op jit(solution)/shard_map/ppermute | solution.py:62
  274.3 1.6 collective-permute-start.52
  277.4 6.6 %collective-permute-done.48 = f32[64,1408]{1,0:T(8,128)S(1)} collective-permute-done((f32[64,1408]{1,0:T(8,128)S(1)}, f32[64,1408]{1,0:T(8,128)S(1)}, u32[]{:S(2)}, u32[]{:S(2)}) %collective-permute-start.48) | collective-permute-done | bytes 360480 | tf_op jit(solution)/shard_map/ppermute | solution.py:62
  285.7 1.6 collective-permute-start.56
  287.3 7.1 %collective-permute-done.51 = f32[40,2816]{1,0:T(8,128)S(1)} collective-permute-done((f32[40,2816]{1,0:T(8,128)S(1)}, f32[40,2816]{1,0:T(8,128)S(1)}, u32[]{:S(2)}, u32[]{:S(2)}) %collective-permute-start.51) | collective-permute-done | bytes 450592 | tf_op jit(solution)/shard_map/ppermute | solution.py:62
  296.7 4.7 collective-permute-done.49.refs_2_
  303.0 1.6 collective-permute-start.60
  307.9 1.6 collective-permute-start.57
  309.5 13.9 %collective-permute-done.58.refs_2_ = f32[40,1408]{1,0:T(8,128)S(1)} collective-permute-done((f32[40,1408]{1,0:T(8,128)S(1)}, f32[40,1408]{1,0:T(8,128)S(1)}, u32[]{:S(2)}, u32[]{:S(2)}) %collective-permute-start.58) | collective-permute-done | bytes 225312 | tf_op jit(solution)/shard_map/ppermute | solution.py:62
  334.4 16.6 %forth_pair.6 = (f32[400,5632]{1,0:T(8,128)}, f32[248,384]{1,0:T(8,128)S(1)}, f32[248,384]{1,0:T(8,128)S(1)}, bf16[768,5632]{1,0:T(8,128)(2,1)}, bf16[768,5632]{1,0:T(8,128)(2,1)}) custom-call(s32[3]{0:T(128)S(1)} %copy-done.2, f32[1]{0:T(128)} %bitcast.5.refs_0_, ...), custom_call_target="tpu_custom_call", output_to_operand_aliasing={{3}: (11, {}), {4}: (12, {})} | custom-call | flops 6228541440 | bytes 33521664 | tf_op jit(solution)/shard_map/forth_pair/pallas_call | solution.py:329
  352.9 10.5 %collective-permute-done.62 = f32[248,384]{1,0:T(8,128)S(1)} collective-permute-done((f32[248,384]{1,0:T(8,128)S(1)}, f32[248,384]{1,0:T(8,128)S(1)}, u32[]{:S(2)}, u32[]{:S(2)}) %collective-permute-start.62) | collective-permute-done | bytes 380960 | tf_op jit(solution)/shard_map/ppermute | solution.py:62
  363.4 1.6 collective-permute-start.65
  365.1 14.7 %forth_pair.7 = (f32[400,5632]{1,0:T(8,128)}, f32[168,384]{1,0:T(8,128)S(1)}, f32[168,384]{1,0:T(8,128)S(1)}, bf16[768,5632]{1,0:T(8,128)(2,1)}, bf16[768,5632]{1,0:T(8,128)(2,1)}) custom-call(s32[3]{0:T(128)S(1)} %copy-done.2, f32[1]{0:T(128)} %bitcast.5.refs_0_, ...), custom_call_target="tpu_custom_call", output_to_operand_aliasing={{3}: (11, {}), {4}: (12, {}), {0}: (13, {})} | custom-call | flops 4152360960 | bytes 28114944 | tf_op jit(solution)/shard_map/forth_pair/pallas_call | solution.py:329
  379.8 1.8 collective-permute-start.69
  382.8 6.3 %collective-permute-done.69 = f32[168,384]{1,0:T(8,128)S(1)} collective-permute-done((f32[168,384]{1,0:T(8,128)S(1)}, f32[168,384]{1,0:T(8,128)S(1)}, u32[]{:S(2)}, u32[]{:S(2)}) %collective-permute-start.69) | collective-permute-done | bytes 258080 | tf_op jit(solution)/shard_map/ppermute | solution.py:62
  390.2 11.3 %collective-permute-done.68 = f32[248,384]{1,0:T(8,128)S(1)} collective-permute-done((f32[248,384]{1,0:T(8,128)S(1)}, f32[248,384]{1,0:T(8,128)S(1)}, u32[]{:S(2)}, u32[]{:S(2)}) %collective-permute-start.68) | collective-permute-done | bytes 380960 | tf_op jit(solution)/shard_map/ppermute | solution.py:62
  402.7 6.1 %collective-permute-done.71 = f32[168,384]{1,0:T(8,128)S(1)} collective-permute-done((f32[168,384]{1,0:T(8,128)S(1)}, f32[168,384]{1,0:T(8,128)S(1)}, u32[]{:S(2)}, u32[]{:S(2)}) %collective-permute-start.71) | collective-permute-done | bytes 258080 | tf_op jit(solution)/shard_map/ppermute | solution.py:62
  413.9 12.3 %back_group.10 = (f32[64,5632]{1,0:T(8,128)S(1)}, f32[64,5632]{1,0:T(8,128)S(1)}, f32[56,5632]{1,0:T(8,128)S(1)}, f32[56,5632]{1,0:T(8,128)}, bf16[768,5632]{1,0:T(8,128)(2,1)}, /*index=5*/bf16[768,5632]{1,0:T(8,128)(2,1)}) custom-call(s32[3]{0:T(128)S(1)} %copy-done.2, f32[240,768]{1,0:T(8,128)S(1)} %slice.382.g_ref, ...), custom_call_target="tpu_custom_call", output_to_operand_aliasing={{4}: (2, {}), {5}: (3, {})} | custom-call | flops 6228541440 | bytes 22708224 | tf_op jit(solution)/shard_map/back_group/pallas_call | solution.py:187
  427.6 3.2 collective-permute-done.72
  435.7 1.7 collective-permute-start.73
  439.9 9.6 %back_group.11 = (f32[40,5632]{1,0:T(8,128)S(1)}, f32[40,5632]{1,0:T(8,128)S(1)}, f32[40,5632]{1,0:T(8,128)S(1)}, f32[40,5632]{1,0:T(8,128)S(1)}, bf16[768,5632]{1,0:T(8,128)(2,1)}, /*index=5*/bf16[768,5632]{1,0:T(8,128)(2,1)}) custom-call(s32[3]{0:T(128)S(1)} %copy-done.2, ...), custom_call_target="tpu_custom_call", output_to_operand_aliasing={{4}: (2, {}), {5}: (3, {})} | custom-call | flops 4152360960 | bytes 20905984 | tf_op jit(solution)/shard_map/back_group/pallas_call | solution.py:187
  449.5 2.4 collective-permute-done.73
  460.1 1.6 collective-permute-start.81
  463.9 14.1 %multiply_add_fusion = f32[400,5632]{1,0:T(8,128)} fusion(f32[400,5632]{1,0:T(8,128)} %get-tuple-element.331.refs_9_, f32[400,5632]{1,0:T(8,128)} %w_ref.5, f32[400,5632]{1,0:T(8,128)} %get-tuple-element.287.refs_9_.refs_8_, f32[]{:T(128)} %div.82, f32[]{:T(128)S(6)} %add.263), kind=kLoop, calls=%fused_computation | loop fusion | flops 9011200 | bytes 36044808 | tf_op jit(solution)/shard_map/add | solution.py:637
  479.3 1.7 slice_add_fusion.9.refs_4_
  484.8 1.7 collective-permute-start.89
  486.5 3.0 collective-permute-done.86.refs_1_
  492.6 1.8 collective-permute-done.84
  496.7 13.6 %collective-permute-done.88.refs_1_ = f32[40,1408]{1,0:T(8,128)S(1)} collective-permute-done((f32[40,1408]{1,0:T(8,128)S(1)}, f32[40,1408]{1,0:T(8,128)S(1)}, u32[]{:S(2)}, u32[]{:S(2)}) %collective-permute-start.88) | collective-permute-done | bytes 225312 | tf_op jit(solution)/shard_map/ppermute | solution.py:62
  510.8 5.8 %collective-permute-done.93.refs_5_ = f32[40,1408]{1,0:T(8,128)S(1)} collective-permute-done((f32[40,1408]{1,0:T(8,128)S(1)}, f32[40,1408]{1,0:T(8,128)S(1)}, u32[]{:S(2)}, u32[]{:S(2)}) %collective-permute-start.93) | collective-permute-done | bytes 225312 | tf_op jit(solution)/shard_map/ppermute | solution.py:62
  518.6 5.2 collective-permute-done.90.refs_2_
  525.8 4.5 last_rows.2.refs_10_
  530.3 3.5 last_rows.3
  (348 shorter events, 107.1 us)
Async XLA Ops:
  11.9 14.1 %collective-permute-start = (f32[200,256]{1,0:T(8,128)}, f32[200,256]{1,0:T(8,128)S(1)}, u32[]{:S(2)}, u32[]{:S(2)}) collective-permute-start(f32[200,256]{1,0:T(8,128)} %get-tuple-element.177), channel_id=1, source_target_pairs={{0,1},{1,0},{2,3},{3,2},{4,5},{5,4},{6,7},{7,6},{8,9},{9,8},{10,11... | collective-permute-start | bytes 614408 | tf_op jit(solution)/shard_map/ppermute | solution.py:62
  25.9 16.3 %collective-permute-start.4 = (f32[200,256]{1,0:T(8,128)}, f32[200,256]{1,0:T(8,128)S(1)}, u32[]{:S(2)}, u32[]{:S(2)}) collective-permute-start(f32[200,256]{1,0:T(8,128)} %get-tuple-element.181), channel_id=1, source_target_pairs={{0,1},{1,0},{2,3},{3,2},{4,5},{5,4},{6,7},{7,6},{8,9},{9,8},{10,11... | collective-permute-start | bytes 614408 | tf_op jit(solution)/shard_map/ppermute | solution.py:62
  26.0 15.6 %collective-permute-start.1 = (f32[200,256]{1,0:T(8,128)S(1)}, f32[200,256]{1,0:T(8,128)S(1)}, u32[]{:S(2)}, u32[]{:S(2)}) collective-permute-start(f32[200,256]{1,0:T(8,128)S(1)} %add.206), channel_id=1, source_target_pairs={{0,2},{1,3},{2,0},{3,1},{4,6},{5,7},{6,4},{7,5},{8,10},{9,11},{10,... | collective-permute-start | bytes 614408 | tf_op jit(solution)/shard_map/ppermute | solution.py:62
  40.0 14.2 %collective-permute-start.3 = (f32[200,256]{1,0:T(8,128)}, f32[200,256]{1,0:T(8,128)S(1)}, u32[]{:S(2)}, u32[]{:S(2)}) collective-permute-start(f32[200,256]{1,0:T(8,128)} %get-tuple-element.186), channel_id=1, source_target_pairs={{0,1},{1,0},{2,3},{3,2},{4,5},{5,4},{6,7},{7,6},{8,9},{9,8},{10,11... | collective-permute-start | bytes 614408 | tf_op jit(solution)/shard_map/ppermute | solution.py:62
  41.7 14.8 %collective-permute-start.2 = (f32[200,256]{1,0:T(8,128)S(1)}, f32[200,256]{1,0:T(8,128)S(1)}, u32[]{:S(2)}, u32[]{:S(2)}) collective-permute-start(f32[200,256]{1,0:T(8,128)S(1)} %add.207), channel_id=1, source_target_pairs={{0,1},{1,0},{2,3},{3,2},{4,5},{5,4},{6,7},{7,6},{8,9},{9,8},{10,11... | collective-permute-start | bytes 614408 | tf_op jit(solution)/shard_map/ppermute | solution.py:62
  42.3 14.3 %collective-permute-start.5 = (f32[200,256]{1,0:T(8,128)S(1)}, f32[200,256]{1,0:T(8,128)S(1)}, u32[]{:S(2)}, u32[]{:S(2)}) collective-permute-start(f32[200,256]{1,0:T(8,128)S(1)} %add.208), channel_id=1, source_target_pairs={{0,2},{1,3},{2,0},{3,1},{4,6},{5,7},{6,4},{7,5},{8,10},{9,11},{10,... | collective-permute-start | bytes 614408 | tf_op jit(solution)/shard_map/ppermute | solution.py:62
  86.3 18.2 %collective-permute-start.10 = (f32[64,2816]{1,0:T(8,128)S(1)}, f32[64,2816]{1,0:T(8,128)S(1)}, u32[]{:S(2)}, u32[]{:S(2)}) collective-permute-start(f32[64,2816]{1,0:T(8,128)S(1)} %pad_maximum_fusion.15), channel_id=1, source_target_pairs={{0,8},{4,12},{8,0},{12,4},{16,24},{20,28},{24,16},{28,20},{1,9},{5... | collective-permute-start | bytes 2162696 | tf_op jit(solution)/shard_map/ppermute | solution.py:62
  88.1 18.1 %collective-permute-start.15 = (f32[56,2816]{1,0:T(8,128)S(1)}, f32[56,2816]{1,0:T(8,128)S(1)}, u32[]{:S(2)}, u32[]{:S(2)}) collective-permute-start(f32[56,2816]{1,0:T(8,128)S(1)} %slice.336), channel_id=1, source_target_pairs={{0,16},{4,20},{8,24},{12,28},{16,0},{20,4},{24,8},{28,12},{1,17},{... | collective-permute-start | bytes 1892360 | tf_op jit(solution)/shard_map/ppermute | solution.py:62
  104.6 11.4 %collective-permute-start.12 = (f32[64,1408]{1,0:T(8,128)S(1)}, f32[64,1408]{1,0:T(8,128)S(1)}, u32[]{:S(2)}, u32[]{:S(2)}) collective-permute-start(f32[64,1408]{1,0:T(8,128)S(1)} %slice.338), channel_id=1, source_target_pairs={{0,16},{4,20},{8,24},{12,28},{16,0},{20,4},{24,8},{28,12},{1,17},{... | collective-permute-start | bytes 1081352 | tf_op jit(solution)/shard_map/ppermute | solution.py:62
  106.3 11.3 %collective-permute-start.19 = (f32[56,1408]{1,0:T(8,128)S(1)}, f32[56,1408]{1,0:T(8,128)S(1)}, u32[]{:S(2)}, u32[]{:S(2)}) collective-permute-start(f32[56,1408]{1,0:T(8,128)S(1)} %slice.340), channel_id=1, source_target_pairs={{0,8},{4,12},{8,0},{12,4},{16,24},{20,28},{24,16},{28,20},{1,9},{5... | collective-permute-start | bytes 946184 | tf_op jit(solution)/shard_map/ppermute | solution.py:62
  108.1 18.3 %collective-permute-start.18 = (f32[40,2816]{1,0:T(8,128)S(1)}, f32[40,2816]{1,0:T(8,128)S(1)}, u32[]{:S(2)}, u32[]{:S(2)}) collective-permute-start(f32[40,2816]{1,0:T(8,128)S(1)} %pad_maximum_fusion.25), channel_id=1, source_target_pairs={{0,8},{4,12},{8,0},{12,4},{16,24},{20,28},{24,16},{28,20},{1,9},{5... | collective-permute-start | bytes 1351688 | tf_op jit(solution)/shard_map/ppermute | solution.py:62
  108.9 18.2 %collective-permute-start.17 = (f32[40,2816]{1,0:T(8,128)S(1)}, f32[40,2816]{1,0:T(8,128)S(1)}, u32[]{:S(2)}, u32[]{:S(2)}) collective-permute-start(f32[40,2816]{1,0:T(8,128)S(1)} %slice.343), channel_id=1, source_target_pairs={{0,16},{4,20},{8,24},{12,28},{16,0},{20,4},{24,8},{28,12},{1,17},{... | collective-permute-start | bytes 1351688 | tf_op jit(solution)/shard_map/ppermute | solution.py:62
  116.1 17.3 %collective-permute-start.16 = (f32[64,1408]{1,0:T(8,128)S(1)}, f32[64,1408]{1,0:T(8,128)S(1)}, u32[]{:S(2)}, u32[]{:S(2)}) collective-permute-start(f32[64,1408]{1,0:T(8,128)S(1)} %slice_add_fusion.8.refs_0_), channel_id=1, source_target_pairs={{0,16},{4,20},{8,24},{12,28},{16,0},{20,4},{24,8},{28,12},{1,17},{... | collective-permute-start | bytes 1081352 | tf_op jit(solution)/shard_map/ppermute | solution.py:62
  117.7 17.3 %collective-permute-start.23 = (f32[56,1408]{1,0:T(8,128)S(1)}, f32[56,1408]{1,0:T(8,128)S(1)}, u32[]{:S(2)}, u32[]{:S(2)}) collective-permute-start(f32[56,1408]{1,0:T(8,128)S(1)} %slice_add_fusion.11.refs_4_), channel_id=1, source_target_pairs={{0,8},{4,12},{8,0},{12,4},{16,24},{20,28},{24,16},{28,20},{1,9},{5... | collective-permute-start | bytes 946184 | tf_op jit(solution)/shard_map/ppermute | solution.py:62
  126.5 11.7 %collective-permute-start.22 = (f32[40,1408]{1,0:T(8,128)S(1)}, f32[40,1408]{1,0:T(8,128)S(1)}, u32[]{:S(2)}, u32[]{:S(2)}) collective-permute-start(f32[40,1408]{1,0:T(8,128)S(1)} %slice.348), channel_id=1, source_target_pairs={{0,16},{4,20},{8,24},{12,28},{16,0},{20,4},{24,8},{28,12},{1,17},{... | collective-permute-start | bytes 675848 | tf_op jit(solution)/shard_map/ppermute | solution.py:62
  127.2 12.7 %collective-permute-start.21 = (f32[40,1408]{1,0:T(8,128)S(1)}, f32[40,1408]{1,0:T(8,128)S(1)}, u32[]{:S(2)}, u32[]{:S(2)}) collective-permute-start(f32[40,1408]{1,0:T(8,128)S(1)} %slice.349), channel_id=1, source_target_pairs={{0,8},{4,12},{8,0},{12,4},{16,24},{20,28},{24,16},{28,20},{1,9},{5... | collective-permute-start | bytes 675848 | tf_op jit(solution)/shard_map/ppermute | solution.py:62
  133.5 22.9 %collective-permute-start.20 = (f32[64,2816]{1,0:T(8,128)S(1)}, f32[64,2816]{1,0:T(8,128)S(1)}, u32[]{:S(2)}, u32[]{:S(2)}) collective-permute-start(f32[64,2816]{1,0:T(8,128)S(1)} %pad_maximum_fusion.16), channel_id=1, source_target_pairs={{0,8},{4,12},{8,0},{12,4},{16,24},{20,28},{24,16},{28,20},{1,9},{5... | collective-permute-start | bytes 2162696 | tf_op jit(solution)/shard_map/ppermute | solution.py:62
  135.1 21.4 %collective-permute-start.27 = (f32[56,2816]{1,0:T(8,128)S(1)}, f32[56,2816]{1,0:T(8,128)S(1)}, u32[]{:S(2)}, u32[]{:S(2)}) collective-permute-start(f32[56,2816]{1,0:T(8,128)S(1)} %pad_maximum_fusion.21), channel_id=1, source_target_pairs={{0,16},{4,20},{8,24},{12,28},{16,0},{20,4},{24,8},{28,12},{1,17},{... | collective-permute-start | bytes 1892360 | tf_op jit(solution)/shard_map/ppermute | solution.py:62
  138.3 16.6 %collective-permute-start.25 = (f32[40,1408]{1,0:T(8,128)S(1)}, f32[40,1408]{1,0:T(8,128)S(1)}, u32[]{:S(2)}, u32[]{:S(2)}) collective-permute-start(f32[40,1408]{1,0:T(8,128)S(1)} %slice_add_fusion.16.refs_0_), channel_id=1, source_target_pairs={{0,16},{4,20},{8,24},{12,28},{16,0},{20,4},{24,8},{28,12},{1,17},{... | collective-permute-start | bytes 675848 | tf_op jit(solution)/shard_map/ppermute | solution.py:62
  139.9 16.4 %collective-permute-start.24 = (f32[40,1408]{1,0:T(8,128)S(1)}, f32[40,1408]{1,0:T(8,128)S(1)}, u32[]{:S(2)}, u32[]{:S(2)}) collective-permute-start(f32[40,1408]{1,0:T(8,128)S(1)} %slice_add_fusion.17.refs_4_), channel_id=1, source_target_pairs={{0,8},{4,12},{8,0},{12,4},{16,24},{20,28},{24,16},{28,20},{1,9},{5... | collective-permute-start | bytes 675848 | tf_op jit(solution)/shard_map/ppermute | solution.py:62
  157.2 18.0 %collective-permute-start.31 = (f32[40,2816]{1,0:T(8,128)S(1)}, f32[40,2816]{1,0:T(8,128)S(1)}, u32[]{:S(2)}, u32[]{:S(2)}) collective-permute-start(f32[40,2816]{1,0:T(8,128)S(1)} %pad_maximum_fusion.26), channel_id=1, source_target_pairs={{0,8},{4,12},{8,0},{12,4},{16,24},{20,28},{24,16},{28,20},{1,9},{5... | collective-permute-start | bytes 1351688 | tf_op jit(solution)/shard_map/ppermute | solution.py:62
  158.7 16.6 %collective-permute-start.30 = (f32[40,2816]{1,0:T(8,128)S(1)}, f32[40,2816]{1,0:T(8,128)S(1)}, u32[]{:S(2)}, u32[]{:S(2)}) collective-permute-start(f32[40,2816]{1,0:T(8,128)S(1)} %pad_maximum_fusion.27), channel_id=1, source_target_pairs={{0,16},{4,20},{8,24},{12,28},{16,0},{20,4},{24,8},{28,12},{1,17},{... | collective-permute-start | bytes 1351688 | tf_op jit(solution)/shard_map/ppermute | solution.py:62
  175.3 13.1 %collective-permute-start.34 = (f32[40,5632]{1,0:T(8,128)S(1)}, f32[40,5632]{1,0:T(8,128)S(1)}, u32[]{:S(2)}, u32[]{:S(2)}) collective-permute-start(f32[40,5632]{1,0:T(8,128)S(1)} %pad_maximum_fusion.10), channel_id=1, source_target_pairs={{0,4},{4,0},{8,12},{12,8},{16,20},{20,16},{24,28},{28,24},{1,5},{5... | collective-permute-start | bytes 2703368 | tf_op jit(solution)/shard_map/ppermute | solution.py:62
  175.5 12.9 %collective-permute-start.33 = (f32[40,5632]{1,0:T(8,128)S(1)}, f32[40,5632]{1,0:T(8,128)S(1)}, u32[]{:S(2)}, u32[]{:S(2)}) collective-permute-start(f32[40,5632]{1,0:T(8,128)S(1)} %pad_maximum_fusion.9), channel_id=1, source_target_pairs={{0,4},{4,0},{8,12},{12,8},{16,20},{20,16},{24,28},{28,24},{1,5},{5... | collective-permute-start | bytes 2703368 | tf_op jit(solution)/shard_map/ppermute | solution.py:62
  186.9 19.3 %collective-permute-start.32 = (f32[248,384]{1,0:T(8,128)S(1)}, f32[248,384]{1,0:T(8,128)S(1)}, u32[]{:S(2)}, u32[]{:S(2)}) collective-permute-start(f32[248,384]{1,0:T(8,128)S(1)} %add.224), channel_id=1, source_target_pairs={{0,2},{1,3},{2,0},{3,1},{4,6},{5,7},{6,4},{7,5},{8,10},{9,11},{10,... | collective-permute-start | bytes 1142792 | tf_op jit(solution)/shard_map/ppermute | solution.py:62
  206.2 16.4 %collective-permute-start.35 = (f32[248,384]{1,0:T(8,128)S(1)}, f32[248,384]{1,0:T(8,128)S(1)}, u32[]{:S(2)}, u32[]{:S(2)}) collective-permute-start(f32[248,384]{1,0:T(8,128)S(1)} %add.225), channel_id=1, source_target_pairs={{0,1},{1,0},{2,3},{3,2},{4,5},{5,4},{6,7},{7,6},{8,9},{9,8},{10,11... | collective-permute-start | bytes 1142792 | tf_op jit(solution)/shard_map/ppermute | solution.py:62
  211.7 14.6 %collective-permute-start.37 = (f32[168,384]{1,0:T(8,128)S(1)}, f32[168,384]{1,0:T(8,128)S(1)}, u32[]{:S(2)}, u32[]{:S(2)}) collective-permute-start(f32[168,384]{1,0:T(8,128)S(1)} %add.226), channel_id=1, source_target_pairs={{0,2},{1,3},{2,0},{3,1},{4,6},{5,7},{6,4},{7,5},{8,10},{9,11},{10,... | collective-permute-start | bytes 774152 | tf_op jit(solution)/shard_map/ppermute | solution.py:62
  252.5 20.1 %collective-permute-start.47 = (f32[64,2816]{1,0:T(8,128)S(1)}, f32[64,2816]{1,0:T(8,128)S(1)}, u32[]{:S(2)}, u32[]{:S(2)}) collective-permute-start(f32[64,2816]{1,0:T(8,128)S(1)} %pad_maximum_fusion.17), channel_id=1, source_target_pairs={{0,8},{4,12},{8,0},{12,4},{16,24},{20,28},{24,16},{28,20},{1,9},{5... | collective-permute-start | bytes 2162696 | tf_op jit(solution)/shard_map/ppermute | solution.py:62
  254.1 16.7 %collective-permute-start.40 = (f32[8,128]{1,0:T(8,128)S(1)}, f32[8,128]{1,0:T(8,128)S(1)}, u32[]{:S(2)}, u32[]{:S(2)}) collective-permute-start(f32[8,128]{1,0:T(8,128)S(1)} %broadcast_add_fusion.1), channel_id=1, source_target_pairs={{0,8},{4,12},{8,0},{12,4},{16,24},{20,28},{24,16},{28,20},{1,9},{5... | collective-permute-start | bytes 12296 | tf_op jit(solution)/shard_map/ppermute | solution.py:62
  254.8 19.4 %collective-permute-start.46 = (f32[56,2816]{1,0:T(8,128)S(1)}, f32[56,2816]{1,0:T(8,128)S(1)}, u32[]{:S(2)}, u32[]{:S(2)}) collective-permute-start(f32[56,2816]{1,0:T(8,128)S(1)} %slice.360), channel_id=1, source_target_pairs={{0,16},{4,20},{8,24},{12,28},{16,0},{20,4},{24,8},{28,12},{1,17},{... | collective-permute-start | bytes 1892360 | tf_op jit(solution)/shard_map/ppermute | solution.py:62
  272.6 11.4 %collective-permute-start.48 = (f32[64,1408]{1,0:T(8,128)S(1)}, f32[64,1408]{1,0:T(8,128)S(1)}, u32[]{:S(2)}, u32[]{:S(2)}) collective-permute-start(f32[64,1408]{1,0:T(8,128)S(1)} %slice.364), channel_id=1, source_target_pairs={{0,16},{4,20},{8,24},{12,28},{16,0},{20,4},{24,8},{28,12},{1,17},{... | collective-permute-start | bytes 1081352 | tf_op jit(solution)/shard_map/ppermute | solution.py:62
  274.3 11.3 %collective-permute-start.52 = (f32[56,1408]{1,0:T(8,128)S(1)}, f32[56,1408]{1,0:T(8,128)S(1)}, u32[]{:S(2)}, u32[]{:S(2)}) collective-permute-start(f32[56,1408]{1,0:T(8,128)S(1)} %slice.365), channel_id=1, source_target_pairs={{0,8},{4,12},{8,0},{12,4},{16,24},{20,28},{24,16},{28,20},{1,9},{5... | collective-permute-start | bytes 946184 | tf_op jit(solution)/shard_map/ppermute | solution.py:62
  276.1 18.3 %collective-permute-start.51 = (f32[40,2816]{1,0:T(8,128)S(1)}, f32[40,2816]{1,0:T(8,128)S(1)}, u32[]{:S(2)}, u32[]{:S(2)}) collective-permute-start(f32[40,2816]{1,0:T(8,128)S(1)} %pad_maximum_fusion.28), channel_id=1, source_target_pairs={{0,8},{4,12},{8,0},{12,4},{16,24},{20,28},{24,16},{28,20},{1,9},{5... | collective-permute-start | bytes 1351688 | tf_op jit(solution)/shard_map/ppermute | solution.py:62
  276.8 18.2 %collective-permute-start.50 = (f32[40,2816]{1,0:T(8,128)S(1)}, f32[40,2816]{1,0:T(8,128)S(1)}, u32[]{:S(2)}, u32[]{:S(2)}) collective-permute-start(f32[40,2816]{1,0:T(8,128)S(1)} %slice.368), channel_id=1, source_target_pairs={{0,16},{4,20},{8,24},{12,28},{16,0},{20,4},{24,8},{28,12},{1,17},{... | collective-permute-start | bytes 1351688 | tf_op jit(solution)/shard_map/ppermute | solution.py:62
  284.1 17.3 %collective-permute-start.49 = (f32[64,1408]{1,0:T(8,128)S(1)}, f32[64,1408]{1,0:T(8,128)S(1)}, u32[]{:S(2)}, u32[]{:S(2)}) collective-permute-start(f32[64,1408]{1,0:T(8,128)S(1)} %slice_add_fusion.7.refs_1_), channel_id=1, source_target_pairs={{0,16},{4,20},{8,24},{12,28},{16,0},{20,4},{24,8},{28,12},{1,17},{... | collective-permute-start | bytes 1081352 | tf_op jit(solution)/shard_map/ppermute | solution.py:62
  285.7 17.3 %collective-permute-start.56 = (f32[56,1408]{1,0:T(8,128)S(1)}, f32[56,1408]{1,0:T(8,128)S(1)}, u32[]{:S(2)}, u32[]{:S(2)}) collective-permute-start(f32[56,1408]{1,0:T(8,128)S(1)} %slice_add_fusion.10.refs_5_), channel_id=1, source_target_pairs={{0,8},{4,12},{8,0},{12,4},{16,24},{20,28},{24,16},{28,20},{1,9},{5... | collective-permute-start | bytes 946184 | tf_op jit(solution)/shard_map/ppermute | solution.py:62
  294.5 11.7 %collective-permute-start.55 = (f32[40,1408]{1,0:T(8,128)S(1)}, f32[40,1408]{1,0:T(8,128)S(1)}, u32[]{:S(2)}, u32[]{:S(2)}) collective-permute-start(f32[40,1408]{1,0:T(8,128)S(1)} %slice.374), channel_id=1, source_target_pairs={{0,16},{4,20},{8,24},{12,28},{16,0},{20,4},{24,8},{28,12},{1,17},{... | collective-permute-start | bytes 675848 | tf_op jit(solution)/shard_map/ppermute | solution.py:62
  295.2 12.7 %collective-permute-start.54 = (f32[40,1408]{1,0:T(8,128)S(1)}, f32[40,1408]{1,0:T(8,128)S(1)}, u32[]{:S(2)}, u32[]{:S(2)}) collective-permute-start(f32[40,1408]{1,0:T(8,128)S(1)} %slice.375), channel_id=1, source_target_pairs={{0,8},{4,12},{8,0},{12,4},{16,24},{20,28},{24,16},{28,20},{1,9},{5... | collective-permute-start | bytes 675848 | tf_op jit(solution)/shard_map/ppermute | solution.py:62
  301.4 24.8 %collective-permute-start.53 = (f32[64,2816]{1,0:T(8,128)S(1)}, f32[64,2816]{1,0:T(8,128)S(1)}, u32[]{:S(2)}, u32[]{:S(2)}) collective-permute-start(f32[64,2816]{1,0:T(8,128)S(1)} %pad_maximum_fusion.18), channel_id=1, source_target_pairs={{0,8},{4,12},{8,0},{12,4},{16,24},{20,28},{24,16},{28,20},{1,9},{5... | collective-permute-start | bytes 2162696 | tf_op jit(solution)/shard_map/ppermute | solution.py:62
  303.0 24.3 %collective-permute-start.60 = (f32[56,2816]{1,0:T(8,128)S(1)}, f32[56,2816]{1,0:T(8,128)S(1)}, u32[]{:S(2)}, u32[]{:S(2)}) collective-permute-start(f32[56,2816]{1,0:T(8,128)S(1)} %pad_maximum_fusion.22), channel_id=1, source_target_pairs={{0,16},{4,20},{8,24},{12,28},{16,0},{20,4},{24,8},{28,12},{1,17},{... | collective-permute-start | bytes 1892360 | tf_op jit(solution)/shard_map/ppermute | solution.py:62
  306.2 17.1 %collective-permute-start.58 = (f32[40,1408]{1,0:T(8,128)S(1)}, f32[40,1408]{1,0:T(8,128)S(1)}, u32[]{:S(2)}, u32[]{:S(2)}) collective-permute-start(f32[40,1408]{1,0:T(8,128)S(1)} %slice_add_fusion.14.refs_1_), channel_id=1, source_target_pairs={{0,16},{4,20},{8,24},{12,28},{16,0},{20,4},{24,8},{28,12},{1,17},{... | collective-permute-start | bytes 675848 | tf_op jit(solution)/shard_map/ppermute | solution.py:62
  307.9 16.8 %collective-permute-start.57 = (f32[40,1408]{1,0:T(8,128)S(1)}, f32[40,1408]{1,0:T(8,128)S(1)}, u32[]{:S(2)}, u32[]{:S(2)}) collective-permute-start(f32[40,1408]{1,0:T(8,128)S(1)} %slice_add_fusion.15.refs_5_), channel_id=1, source_target_pairs={{0,8},{4,12},{8,0},{12,4},{16,24},{20,28},{24,16},{28,20},{1,9},{5... | collective-permute-start | bytes 675848 | tf_op jit(solution)/shard_map/ppermute | solution.py:62
  331.9 19.1 %collective-permute-start.64 = (f32[40,2816]{1,0:T(8,128)}, f32[40,2816]{1,0:T(8,128)S(1)}, u32[]{:S(2)}, u32[]{:S(2)}) collective-permute-start(f32[40,2816]{1,0:T(8,128)} %pad_maximum_fusion.29), channel_id=1, source_target_pairs={{0,8},{4,12},{8,0},{12,4},{16,24},{20,28},{24,16},{28,20},{1,9},{5... | collective-permute-start | bytes 1351688 | tf_op jit(solution)/shard_map/ppermute | solution.py:62
  333.5 17.6 %collective-permute-start.63 = (f32[40,2816]{1,0:T(8,128)}, f32[40,2816]{1,0:T(8,128)S(1)}, u32[]{:S(2)}, u32[]{:S(2)}) collective-permute-start(f32[40,2816]{1,0:T(8,128)} %pad_maximum_fusion.30), channel_id=1, source_target_pairs={{0,16},{4,20},{8,24},{12,28},{16,0},{20,4},{24,8},{28,12},{1,17},{... | collective-permute-start | bytes 1351688 | tf_op jit(solution)/shard_map/ppermute | solution.py:62
  352.0 13.1 %collective-permute-start.67 = (f32[40,5632]{1,0:T(8,128)S(1)}, f32[40,5632]{1,0:T(8,128)S(1)}, u32[]{:S(2)}, u32[]{:S(2)}) collective-permute-start(f32[40,5632]{1,0:T(8,128)S(1)} %pad_maximum_fusion.12), channel_id=1, source_target_pairs={{0,4},{4,0},{8,12},{12,8},{16,20},{20,16},{24,28},{28,24},{1,5},{5... | collective-permute-start | bytes 2703368 | tf_op jit(solution)/shard_map/ppermute | solution.py:62
  352.1 13.0 %collective-permute-start.66 = (f32[40,5632]{1,0:T(8,128)S(1)}, f32[40,5632]{1,0:T(8,128)S(1)}, u32[]{:S(2)}, u32[]{:S(2)}) collective-permute-start(f32[40,5632]{1,0:T(8,128)S(1)} %pad_maximum_fusion.11), channel_id=1, source_target_pairs={{0,4},{4,0},{8,12},{12,8},{16,20},{20,16},{24,28},{28,24},{1,5},{5... | collective-permute-start | bytes 2703368 | tf_op jit(solution)/shard_map/ppermute | solution.py:62
  363.4 19.2 %collective-permute-start.65 = (f32[248,384]{1,0:T(8,128)S(1)}, f32[248,384]{1,0:T(8,128)S(1)}, u32[]{:S(2)}, u32[]{:S(2)}) collective-permute-start(f32[248,384]{1,0:T(8,128)S(1)} %add.245), channel_id=1, source_target_pairs={{0,2},{1,3},{2,0},{3,1},{4,6},{5,7},{6,4},{7,5},{8,10},{9,11},{10,... | collective-permute-start | bytes 1142792 | tf_op jit(solution)/shard_map/ppermute | solution.py:62
  382.7 18.7 %collective-permute-start.68 = (f32[248,384]{1,0:T(8,128)S(1)}, f32[248,384]{1,0:T(8,128)S(1)}, u32[]{:S(2)}, u32[]{:S(2)}) collective-permute-start(f32[248,384]{1,0:T(8,128)S(1)} %add.246), channel_id=1, source_target_pairs={{0,1},{1,0},{2,3},{3,2},{4,5},{5,4},{6,7},{7,6},{8,9},{9,8},{10,11... | collective-permute-start | bytes 1142792 | tf_op jit(solution)/shard_map/ppermute | solution.py:62
  389.1 12.8 %collective-permute-start.70 = (f32[168,384]{1,0:T(8,128)S(1)}, f32[168,384]{1,0:T(8,128)S(1)}, u32[]{:S(2)}, u32[]{:S(2)}) collective-permute-start(f32[168,384]{1,0:T(8,128)S(1)} %add.247), channel_id=1, source_target_pairs={{0,2},{1,3},{2,0},{3,1},{4,6},{5,7},{6,4},{7,5},{8,10},{9,11},{10,... | collective-permute-start | bytes 774152 | tf_op jit(solution)/shard_map/ppermute | solution.py:62
  433.4 20.7 %collective-permute-start.80 = (f32[64,2816]{1,0:T(8,128)}, f32[64,2816]{1,0:T(8,128)}, u32[]{:S(2)}, u32[]{:S(2)}) collective-permute-start(f32[64,2816]{1,0:T(8,128)} %pad_maximum_fusion.19), channel_id=1, source_target_pairs={{0,8},{4,12},{8,0},{12,4},{16,24},{20,28},{24,16},{28,20},{1,9},{5... | collective-permute-start | bytes 2162696 | tf_op jit(solution)/shard_map/ppermute | solution.py:62
  435.7 16.2 %collective-permute-start.73 = (f32[8,128]{1,0:T(8,128)S(1)}, f32[8,128]{1,0:T(8,128)S(1)}, u32[]{:S(2)}, u32[]{:S(2)}) collective-permute-start(f32[8,128]{1,0:T(8,128)S(1)} %broadcast_add_fusion), channel_id=1, source_target_pairs={{0,8},{4,12},{8,0},{12,4},{16,24},{20,28},{24,16},{28,20},{1,9},{5... | collective-permute-start | bytes 12296 | tf_op jit(solution)/shard_map/ppermute | solution.py:62
  438.9 18.2 %collective-permute-start.79 = (f32[56,2816]{1,0:T(8,128)S(1)}, f32[56,2816]{1,0:T(8,128)S(1)}, u32[]{:S(2)}, u32[]{:S(2)}) collective-permute-start(f32[56,2816]{1,0:T(8,128)S(1)} %slice.386), channel_id=1, source_target_pairs={{0,16},{4,20},{8,24},{12,28},{16,0},{20,4},{24,8},{28,12},{1,17},{... | collective-permute-start | bytes 1892360 | tf_op jit(solution)/shard_map/ppermute | solution.py:62
  456.1 22.0 %collective-permute-start.83 = (f32[64,1408]{1,0:T(8,128)}, f32[64,1408]{1,0:T(8,128)S(1)}, u32[]{:S(2)}, u32[]{:S(2)}) collective-permute-start(f32[64,1408]{1,0:T(8,128)} %slice.390), channel_id=1, source_target_pairs={{0,16},{4,20},{8,24},{12,28},{16,0},{20,4},{24,8},{28,12},{1,17},{... | collective-permute-start | bytes 1081352 | tf_op jit(solution)/shard_map/ppermute | solution.py:62
  458.0 21.3 %collective-permute-start.82 = (f32[56,1408]{1,0:T(8,128)}, f32[56,1408]{1,0:T(8,128)}, u32[]{:S(2)}, u32[]{:S(2)}) collective-permute-start(f32[56,1408]{1,0:T(8,128)} %slice.391), channel_id=1, source_target_pairs={{0,8},{4,12},{8,0},{12,4},{16,24},{20,28},{24,16},{28,20},{1,9},{5... | collective-permute-start | bytes 946184 | tf_op jit(solution)/shard_map/ppermute | solution.py:62
  460.1 21.3 %collective-permute-start.81 = (f32[40,2816]{1,0:T(8,128)}, f32[40,2816]{1,0:T(8,128)}, u32[]{:S(2)}, u32[]{:S(2)}) collective-permute-start(f32[40,2816]{1,0:T(8,128)} %pad_maximum_fusion.31), channel_id=1, source_target_pairs={{0,8},{4,12},{8,0},{12,4},{16,24},{20,28},{24,16},{28,20},{1,9},{5... | collective-permute-start | bytes 1351688 | tf_op jit(solution)/shard_map/ppermute | solution.py:62
  461.7 22.0 %collective-permute-start.87 = (f32[40,2816]{1,0:T(8,128)S(1)}, f32[40,2816]{1,0:T(8,128)}, u32[]{:S(2)}, u32[]{:S(2)}) collective-permute-start(f32[40,2816]{1,0:T(8,128)S(1)} %slice.394), channel_id=1, source_target_pairs={{0,16},{4,20},{8,24},{12,28},{16,0},{20,4},{24,8},{28,12},{1,17},{... | collective-permute-start | bytes 1351688 | tf_op jit(solution)/shard_map/ppermute | solution.py:62
  478.1 11.4 %collective-permute-start.86 = (f32[64,1408]{1,0:T(8,128)S(1)}, f32[64,1408]{1,0:T(8,128)S(1)}, u32[]{:S(2)}, u32[]{:S(2)}) collective-permute-start(f32[64,1408]{1,0:T(8,128)S(1)} %slice_add_fusion.6.refs_0_), channel_id=1, source_target_pairs={{0,16},{4,20},{8,24},{12,28},{16,0},{20,4},{24,8},{28,12},{1,17},{... | collective-permute-start | bytes 1081352 | tf_op jit(solution)/shard_map/ppermute | solution.py:62
  482.5 11.8 %collective-permute-start.84 = (f32[40,1408]{1,0:T(8,128)S(1)}, f32[40,1408]{1,0:T(8,128)S(1)}, u32[]{:S(2)}, u32[]{:S(2)}) collective-permute-start(f32[40,1408]{1,0:T(8,128)S(1)} %slice.400), channel_id=1, source_target_pairs={{0,16},{4,20},{8,24},{12,28},{16,0},{20,4},{24,8},{28,12},{1,17},{... | collective-permute-start | bytes 675848 | tf_op jit(solution)/shard_map/ppermute | solution.py:62
  484.8 11.4 %collective-permute-start.89 = (f32[40,1408]{1,0:T(8,128)S(1)}, f32[40,1408]{1,0:T(8,128)S(1)}, u32[]{:S(2)}, u32[]{:S(2)}) collective-permute-start(f32[40,1408]{1,0:T(8,128)S(1)} %slice.402), channel_id=1, source_target_pairs={{0,8},{4,12},{8,0},{12,4},{16,24},{20,28},{24,16},{28,20},{1,9},{5... | collective-permute-start | bytes 675848 | tf_op jit(solution)/shard_map/ppermute | solution.py:62
  489.6 28.1 %collective-permute-start.92 = (f32[64,2816]{1,0:T(8,128)S(1)}, f32[64,2816]{1,0:T(8,128)S(1)}, u32[]{:S(2)}, u32[]{:S(2)}) collective-permute-start(f32[64,2816]{1,0:T(8,128)S(1)} %pad_maximum_fusion.20), channel_id=1, source_target_pairs={{0,8},{4,12},{8,0},{12,4},{16,24},{20,28},{24,16},{28,20},{1,9},{5... | collective-permute-start | bytes 2162696 | tf_op jit(solution)/shard_map/ppermute | solution.py:62
  491.5 26.4 %collective-permute-start.91 = (f32[56,2816]{1,0:T(8,128)S(1)}, f32[56,2816]{1,0:T(8,128)S(1)}, u32[]{:S(2)}, u32[]{:S(2)}) collective-permute-start(f32[56,2816]{1,0:T(8,128)S(1)} %pad_maximum_fusion.23), channel_id=1, source_target_pairs={{0,16},{4,20},{8,24},{12,28},{16,0},{20,4},{24,8},{28,12},{1,17},{... | collective-permute-start | bytes 1892360 | tf_op jit(solution)/shard_map/ppermute | solution.py:62
  494.4 15.9 %collective-permute-start.88 = (f32[40,1408]{1,0:T(8,128)S(1)}, f32[40,1408]{1,0:T(8,128)S(1)}, u32[]{:S(2)}, u32[]{:S(2)}) collective-permute-start(f32[40,1408]{1,0:T(8,128)S(1)} %slice_add_fusion.13.refs_0_), channel_id=1, source_target_pairs={{0,16},{4,20},{8,24},{12,28},{16,0},{20,4},{24,8},{28,12},{1,17},{... | collective-permute-start | bytes 675848 | tf_op jit(solution)/shard_map/ppermute | solution.py:62
  496.3 20.2 %collective-permute-start.93 = (f32[40,1408]{1,0:T(8,128)S(1)}, f32[40,1408]{1,0:T(8,128)S(1)}, u32[]{:S(2)}, u32[]{:S(2)}) collective-permute-start(f32[40,1408]{1,0:T(8,128)S(1)} %slice_add_fusion.12.refs_4_), channel_id=1, source_target_pairs={{0,8},{4,12},{8,0},{12,4},{16,24},{20,28},{24,16},{28,20},{1,9},{5... | collective-permute-start | bytes 675848 | tf_op jit(solution)/shard_map/ppermute | solution.py:62
  510.3 13.4 %collective-permute-start.90 = (f32[40,2816]{1,0:T(8,128)S(1)}, f32[40,2816]{1,0:T(8,128)S(1)}, u32[]{:S(2)}, u32[]{:S(2)}) collective-permute-start(f32[40,2816]{1,0:T(8,128)S(1)} %pad_maximum_fusion.32), channel_id=1, source_target_pairs={{0,8},{4,12},{8,0},{12,4},{16,24},{20,28},{24,16},{28,20},{1,9},{5... | collective-permute-start | bytes 1351688 | tf_op jit(solution)/shard_map/ppermute | solution.py:62
  (59 other events, 1209.7 us)
